TPU v7x, 32 devices: a whole 2x2x4 slice. The times are simulated.
32 devices in a mesh: dp: 4 (over y, core), cent: 8 (over z, x).
Axes of the slice: x: 2, y: 2, z: 4, core: 2. Of those that a mesh axis runs over, the one named last changes fastest.
Arguments:
- passages: bfloat16 [4096, 768], P(('dp', 'cent')), may hold values from -10 to 10
- queries: bfloat16 [128, 768], P(('dp', 'cent')), may hold values from -10 to 10
- init_centroids: float32 [2048, 768], P('cent'), may hold values from -12 to 12
- pattern: int32 [128, 4], replicated, may hold values from 0 to 31, all different within a row
- positive_offset: int32 [128], replicated, may hold values from 0 to 127
Outputs:
- centroids: float32 [2048, 768], P('cent')
- loss: float32 [128], P(('dp', 'cent'))
Inputs may be any that keep to these rules, and one draw needn't show every extreme that they name: `pattern`: each row names 4 different blocks.
All inputs are finite; a program needn't handle non-finite values.
Results may differ from a plain program's by a relative error of at most 0.0055.
Values may be sent and summed in bfloat16 or wider, within the bound.
No kernel may reach another device: no remote copies, remote signals or barrier semaphores. Data moves between devices by JAX's collectives and lax.ppermute only.
A program may use at most 64 MiB of HBM per device.

v0:
```python
import jax
import jax.numpy as jnp
from jax import lax
from jax.sharding import PartitionSpec as P

BLOCK = 128
ITERS = 2


sharpness = 0.05
sharpening_factor = 0.05
prior_weight = 1.0


def merged(value, axis, join):
    pieces = jax.tree.map(lambda part: lax.all_gather(part, axis), value)
    head = jax.tree.map(lambda part: part[0], pieces)
    tail = jax.tree.map(lambda part: part[1:], pieces)
    so_far, _ = lax.scan(lambda so_far, section: (join(so_far, section), None), head, tail)
    return so_far


def combine_query(first, second):
    upper = jnp.maximum(first[0], second[0])
    total = first[1] * jnp.exp(first[0] - upper) + second[1] * jnp.exp(second[0] - upper)
    return (upper, total, first[2] + second[2])


def on_device(passages, queries, init_centroids, pattern, positive_offset):
    gathered = lax.all_gather(passages, "cent", axis=0, tiled=True)
    cluster_means = init_centroids
    for step_index in range(ITERS):
        centers_half = cluster_means.astype(jnp.bfloat16)
        cluster_center_norms = jnp.sum(cluster_means * cluster_means, axis=1)
        unnormalized_log_odds = sharpness * (
            2.0 * jnp.dot(gathered, centers_half.T, preferred_element_type=jnp.float32)
            - cluster_center_norms[None, :]
        )
        row_max = lax.pmax(jnp.max(unnormalized_log_odds, axis=1), "cent")
        weights_exp = jnp.exp(unnormalized_log_odds - row_max[:, None])
        row_total = lax.psum(jnp.sum(weights_exp, axis=1), "cent")
        resp = weights_exp / row_total[:, None]
        numer = lax.dot_general(
            resp.astype(jnp.bfloat16),
            gathered,
            (((0,), (0,)), ((), ())),
            preferred_element_type=jnp.float32,
        )
        counts = jnp.sum(resp, axis=0)
        numer, counts = lax.psum((numer, counts), "dp")
        cluster_means = (numer + prior_weight * cluster_means) / (counts[:, None] + prior_weight)
    query_collection = lax.all_gather(queries, ("dp", "cent"), axis=0, tiled=True)
    local_rows = passages.shape[0]
    linear = lax.axis_index(("dp", "cent"))
    first_row = linear * local_rows
    local_blocks = first_row // BLOCK + jnp.arange(local_rows // BLOCK, dtype=jnp.int32)
    paired_entries = jnp.any(pattern[:, :, None] == local_blocks[None, None, :], axis=1)
    allowed = jnp.repeat(paired_entries, BLOCK, axis=1)
    affinity_matrix = (
        jnp.dot(query_collection, passages.T, preferred_element_type=jnp.float32)
        * sharpening_factor
    )
    target_col = pattern[:, 0] * BLOCK + positive_offset - first_row
    columns = jnp.arange(local_rows, dtype=jnp.int32)
    positive = jnp.sum(
        jnp.where(columns[None, :] == target_col[:, None], affinity_matrix, 0.0), axis=1
    )
    local_max = jnp.max(jnp.where(allowed, affinity_matrix, -1e30), axis=1)
    local_total = jnp.sum(
        jnp.where(allowed, jnp.exp(affinity_matrix - local_max[:, None]), 0.0), axis=1
    )
    query_max, query_total, positive_all = merged(
        (local_max, local_total, positive), ("dp", "cent"), combine_query
    )
    whole_loss = jnp.log(query_total) + query_max - positive_all
    own_count = queries.shape[0]
    own_loss = lax.dynamic_slice_in_dim(whole_loss, linear * own_count, own_count, 0)
    return (cluster_means, own_loss)


def solution(mesh):
    placed = (P(("dp", "cent"), None), P(("dp", "cent"), None), P("cent", None), P(), P())
    return jax.shard_map(
        on_device,
        mesh=mesh,
        in_specs=placed,
        out_specs=(P("cent", None), P(("dp", "cent"))),
        check_vma=False,
    )
```

profile of v0, /device:TPU:0, one launch (start us, length us, event | category | flops | bytes accessed | tf_op | source)
XLA Modules:
  0.0 434.7 jit_solution(5352959012850848209)
XLA Ops:
  7.2 0.7 all-gather.9.cloned.1.call-update
  7.9 0.0 all-reduce.3.cloned.1.call-start
  8.0 71.6 %all-gather.3 = bf16[32,4,768]{2,1,0:T(4,128)(2,1)S(1)} all-gather(bf16[1,4,768]{2,1,0:T(4,128)(2,1)} %bitcast.51), channel_id=1, replica_groups=mesh['dp'=4,'cent'=8] {'dp','cent'}, dimensions={0}, use_global_device_ids=true | all-gather | bytes 202752 | tf_op jit(solution)/shard_map/all_gather | solution.py:52
  79.6 0.1 reshape.42
  79.6 0.7 compare_reduce_fusion
  80.3 1.2 select_reduce_fusion.2
  81.5 63.0 %all-gather.4 = f32[32,1,128]{2,1,0:T(1,128)S(1)} all-gather(f32[1,1,128]{2,1,0:T(1,128)S(1)} %bitcast.52), channel_id=2, replica_groups=mesh['dp'=4,'cent'=8] {'dp','cent'}, dimensions={0}, use_global_device_ids=true | all-gather | bytes 16896 | tf_op jit(solution)/shard_map/all_gather | solution.py:16
  144.5 0.7 fusion.25
  145.2 65.1 %all-gather.5 = f32[32,1,128]{2,1,0:T(1,128)S(1)} all-gather(f32[1,1,128]{2,1,0:T(1,128)S(1)} %bitcast.54), channel_id=3, replica_groups=mesh['dp'=4,'cent'=8] {'dp','cent'}, dimensions={0}, use_global_device_ids=true | all-gather | bytes 16896 | tf_op jit(solution)/shard_map/all_gather | solution.py:16
  210.4 63.0 %all-gather.6 = f32[32,1,128]{2,1,0:T(1,128)S(1)} all-gather(f32[1,1,128]{2,1,0:T(1,128)S(1)} %bitcast.53), channel_id=4, replica_groups=mesh['dp'=4,'cent'=8] {'dp','cent'}, dimensions={0}, use_global_device_ids=true | all-gather | bytes 16896 | tf_op jit(solution)/shard_map/all_gather | solution.py:16
  273.4 1.3 while.14
  274.7 0.6 dynamic_slice.13
  275.3 0.1 multiply_reduce_fusion.1
  275.5 2.1 fusion.27
  277.6 19.4 %pmax.14 = f32[1024]{0:T(1024)S(1)} all-reduce(f32[1024]{0:T(1024)S(1)} %get-tuple-element.65), channel_id=1, replica_groups=mesh['dp'=4,'cent'=8] {'cent'}, use_global_device_ids=true, to_apply=%region_2.0 | all-reduce | flops 1024 | bytes 8192 | tf_op jit(solution)/shard_map/pmax | solution.py:39
  297.0 0.2 fusion.12
  297.2 17.2 %psum.42 = f32[1024]{0:T(1024)S(1)} all-reduce(f32[1024]{0:T(1024)S(1)} %fusion.12), channel_id=1, replica_groups=mesh['dp'=4,'cent'=8] {'cent'}, use_global_device_ids=true, to_apply=%region_4.0 | all-reduce | flops 1024 | bytes 8192 | tf_op jit(solution)/shard_map/psum | solution.py:41
  314.3 1.5 fusion.17
  315.8 0.0 all-reduce.5.cloned.1.call-start
  315.9 0.3 fusion.23
  316.1 5.9 %psum.44 = f32[256]{0:T(256)S(1)} all-reduce(f32[256]{0:T(256)S(1)} %fusion.23), channel_id=1, replica_groups=mesh['dp'=4,'cent'=8] {'dp'}, use_global_device_ids=true, to_apply=%region_7.0 | all-reduce | flops 256 | bytes 2048 | tf_op jit(solution)/shard_map/psum | solution.py:50
  322.0 26.4 %all-reduce.3.cloned.1.call-done = f32[256,768]{1,0:T(8,128)} async-done(((f32[256,768]{1,0:T(8,128)}), f32[256,768]{1,0:T(8,128)}) %all-reduce.3.cloned.1.call-update) | async-done | bytes 786448 | tf_op jit(solution)/shard_map/psum | solution.py:50
  348.4 1.4 multiply_reduce_fusion
  349.8 2.0 fusion.28
  351.8 21.4 %pmax.15 = f32[1024]{0:T(1024)S(1)} all-reduce(f32[1024]{0:T(1024)S(1)} %get-tuple-element.67), channel_id=1, replica_groups=mesh['dp'=4,'cent'=8] {'cent'}, use_global_device_ids=true, to_apply=%region_10.0 | all-reduce | flops 1024 | bytes 8192 | tf_op jit(solution)/shard_map/pmax | solution.py:39
  373.2 0.2 fusion.13
  373.3 17.1 %psum.45 = f32[1024]{0:T(1024)S(1)} all-reduce(f32[1024]{0:T(1024)S(1)} %fusion.13), channel_id=1, replica_groups=mesh['dp'=4,'cent'=8] {'cent'}, use_global_device_ids=true, to_apply=%region_12.0 | all-reduce | flops 1024 | bytes 8192 | tf_op jit(solution)/shard_map/psum | solution.py:41
  390.5 2.9 fusion.15
  393.4 0.3 fusion.21
  393.6 6.0 %psum.47 = f32[256]{0:T(256)S(1)} all-reduce(f32[256]{0:T(256)S(1)} %fusion.21), channel_id=1, replica_groups=mesh['dp'=4,'cent'=8] {'dp'}, use_global_device_ids=true, to_apply=%region_15.0 | all-reduce | flops 256 | bytes 2048 | tf_op jit(solution)/shard_map/psum | solution.py:50
  399.6 26.4 %all-reduce.5.cloned.1.call-done = f32[256,768]{1,0:T(8,128)} async-done(((f32[256,768]{1,0:T(8,128)}), f32[256,768]{1,0:T(8,128)}) %all-reduce.5.cloned.1.call-update) | async-done | bytes 786448 | tf_op jit(solution)/shard_map/psum | solution.py:50
  426.0 2.1 add_divide_fusion
  (52 shorter events, 1.1 us)
Async XLA Ops:
  7.2 268.2 %copy-start = (f32[256,768]{1,0:T(8,128)S(1)}, f32[256,768]{1,0:T(8,128)}, u32[]{:S(2)}) copy-start(f32[256,768]{1,0:T(8,128)} %param.9) | copy-start | bytes 2359300
  7.2 268.3 %all-gather.9.cloned.1.call-start = ((), (), s32[]{:S(2)}) async-start(), calls=%async_computation | async-start | bytes 1769472 | tf_op jit(solution)/shard_map/all_gather | solution.py:30
  7.9 340.5 %all-reduce.3.cloned.1.call-start = ((), (), s32[]{:S(2)}) async-start(), calls=%async_computation.1 | async-start | bytes 1572864 | tf_op jit(solution)/shard_map/psum | solution.py:50
  275.5 38.9 %copy-start.1 = (bf16[1024,768]{1,0:T(8,128)(2,1)S(1)}, bf16[1024,768]{1,0:T(8,128)(2,1)}, u32[]{:S(2)}) copy-start(bf16[1024,768]{1,0:T(8,128)(2,1)} %all-gather.9.cloned.1.call-done) | copy-start | bytes 4718596
  315.8 110.1 %all-reduce.5.cloned.1.call-start = ((), (), s32[]{:S(2)}) async-start(), calls=%async_computation.2 | async-start | bytes 1572864 | tf_op jit(solution)/shard_map/psum | solution.py:50
Sparse Core Ops, SparseCore 0:
  10.2 47.3 all-gather.8
  316.0 32.3 all-reduce.2
  393.5 32.4 all-reduce.4
where the time goes:
time: 435 us
  blocking collectives  350 us (80%)
  waiting for transfers between devices  53.5 us (12%)
  between operations  13.9 us (3%)
  matrix products  9.67 us (2%)
  other arithmetic  6.87 us (2%)
    all_gather x3, blocking collectives, merged(): pieces = jax.tree.map(lambda part: lax.all_gather(part, axis), value)  191 us
    all_gather x1, blocking collectives, on_device(): lax.all_gather(queries, ('dp', 'cent'), axis=0, tiled=True)  71.6 us
    psum x2, waiting for transfers between devices, on_device(): numer, counts = lax.psum((numer, counts), 'dp')  52.7 us
    pmax x2, blocking collectives, on_device(): row_max = lax.pmax(jnp.max(unnormalized_log_odds, axis=1), 'cent')  40.7 us
    psum x2, blocking collectives, on_device(): row_total = lax.psum(jnp.sum(weights_exp, axis=1), 'cent')  34.3 us
    psum x2, blocking collectives, on_device(): numer, counts = lax.psum((numer, counts), 'dp')  11.9 us
  transfers between devices with their start and end apart: 3, of which 2 were waited for; matrix products, arithmetic and copies ran while one was open for 1% of the time, Pallas kernels for 0%

commit v1 on v0

v1 whole, which is shorter than its diff:
```python
import jax
import jax.numpy as jnp
from jax import lax
from jax.sharding import PartitionSpec as P

BLOCK = 128
ITERS = 2
SHARPNESS = 0.05
SCALE = 0.05
PRIOR = 1.0
FAR = -1e30


def swap(value, axis, bit):
    size = lax.axis_size(axis)
    return lax.ppermute(value, axis, [(i, i ^ bit) for i in range(size)])


def bits_of(size):
    return [1 << k for k in range(size.bit_length() - 1)]


def doubled(value, axis, order):
    for bit in order:
        value = jnp.stack([value, swap(value, axis, bit)])
    return value


def join_lse(first, second):
    top = jnp.maximum(first, second)
    return top + jnp.log(1.0 + jnp.exp(jnp.minimum(first, second) - top))


def on_device(passages, queries, init_centroids, pattern, positive_offset):
    n_dp, n_cent = lax.axis_size("dp"), lax.axis_size("cent")
    dp, cent = lax.axis_index("dp"), lax.axis_index("cent")
    dp_bits, cent_bits = bits_of(n_dp), bits_of(n_cent)
    rows, width = passages.shape
    own_queries = queries.shape[0]

    half = rows // 2
    orders = [cent_bits[1:] + cent_bits[:1], cent_bits]
    parts = [
        doubled(passages[:half], "cent", orders[0]),
        doubled(passages[half:], "cent", orders[1]),
    ]
    held = [part.reshape(-1, width) for part in parts]

    asked = queries
    for bit in dp_bits:
        other = swap(asked, "dp", bit)
        low = (dp & bit) == 0
        asked = jnp.concatenate([jnp.where(low, asked, other), jnp.where(low, other, asked)])

    core = dp & 1
    means = init_centroids
    kept = means.shape[0] // 2
    for step in range(ITERS):
        centers_half = means.astype(jnp.bfloat16)
        norms = jnp.sum(means * means, axis=1)
        odds, stats = [], []
        for index in range(2):
            logits = SHARPNESS * (
                2.0
                * lax.dot_general(
                    centers_half, held[index], (((1,), (1,)), ((), ())), preferred_element_type=jnp.float32
                )
                - norms[:, None]
            )
            top = jnp.max(logits, axis=0)
            odds.append(logits)
            stats.append(top + jnp.log(jnp.sum(jnp.exp(logits - top[None, :]), axis=0)))
        shape = (2,) * len(cent_bits) + (half,)
        views = []
        for index in range(2):
            view = stats[index].reshape(shape)
            axes = [len(cent_bits) - 1 - orders[index].index(bit) for bit in cent_bits]
            views.append(jnp.transpose(view, axes + [len(cent_bits)]))
        lse = jnp.concatenate(views, axis=-1)
        for position, bit in enumerate(cent_bits):
            lse = join_lse(lse, jnp.flip(swap(lse, "cent", bit), axis=position))
        numer, counts = 0.0, 0.0
        for index in range(2):
            view = lse[..., index * half : (index + 1) * half]
            axes = [cent_bits.index(bit) for bit in reversed(orders[index])]
            total = jnp.transpose(view, axes + [len(cent_bits)]).reshape(-1)
            resp = jnp.exp(odds[index] - total[None, :])
            counts = counts + jnp.sum(resp, axis=1)
            numer = numer + jnp.dot(
                resp.astype(jnp.bfloat16), held[index], preferred_element_type=jnp.float32
            )
        for bit in dp_bits:
            counts = counts + swap(counts, "dp", bit)
        pair = numer.reshape(2, kept, width)
        mine = lax.dynamic_index_in_dim(pair, core, 0, keepdims=False)
        mine = mine + swap(lax.dynamic_index_in_dim(pair, 1 - core, 0, keepdims=False), "dp", 1)
        for bit in dp_bits[1:]:
            sent = mine.astype(jnp.bfloat16)
            mine = sent.astype(jnp.float32) + swap(sent, "dp", bit).astype(jnp.float32)
        prior = lax.dynamic_slice_in_dim(means, core * kept, kept, 0)
        weight = lax.dynamic_slice_in_dim(counts, core * kept, kept, 0)
        fresh = (mine + PRIOR * prior) / (weight[:, None] + PRIOR)
        other = swap(fresh, "dp", 1)
        means = jnp.concatenate([jnp.where(core == 0, fresh, other), jnp.where(core == 0, other, fresh)])

    losses = []
    ids = ((jnp.arange(n_dp) * n_cent + cent) * own_queries)[:, None] + jnp.arange(own_queries)[None, :]
    ids = ids.reshape(-1)
    picks = pattern[ids]
    target = picks[:, 0] * BLOCK + positive_offset[ids]
    partial, positive = None, 0.0
    for index in range(2):
        where_bits = jnp.zeros((2,) * len(cent_bits), jnp.int32) + cent
        for bit in cent_bits:
            axis = len(cent_bits) - 1 - orders[index].index(bit)
            flag = lax.broadcasted_iota(jnp.int32, where_bits.shape, axis) * bit
            where_bits = where_bits ^ flag
        owner = (dp * n_cent + where_bits)[..., None] * rows
        column = (owner + index * half + jnp.arange(half, dtype=jnp.int32)).reshape(-1)
        scores = SCALE * lax.dot_general(
            asked, held[index], (((1,), (1,)), ((), ())), preferred_element_type=jnp.float32
        )
        allowed = jnp.any(picks[:, :, None] == (column // BLOCK)[None, None, :], axis=1)
        top = jnp.max(jnp.where(allowed, scores, FAR), axis=1)
        total = jnp.sum(jnp.where(allowed, jnp.exp(scores - top[:, None]), 0.0), axis=1)
        losses.append((top, total))
        positive = positive + jnp.sum(jnp.where(column[None, :] == target[:, None], scores, 0.0), axis=1)
    top = jnp.maximum(losses[0][0], losses[1][0])
    total = sum(t * jnp.exp(m - top) for m, t in losses)
    found = jnp.stack([jnp.where(total > 0.0, top + jnp.log(jnp.maximum(total, 1e-37)), FAR), positive])
    for bit in dp_bits:
        other = swap(found, "dp", bit)
        found = jnp.stack([join_lse(found[0], other[0]), found[1] + other[1]])
    whole = found[0] - found[1]
    loss = lax.dynamic_slice_in_dim(whole, dp * own_queries, own_queries, 0)
    return means, loss


def solution(mesh):
    placed = (P(("dp", "cent"), None), P(("dp", "cent"), None), P("cent", None), P(), P())
    return jax.shard_map(
        on_device,
        mesh=mesh,
        in_specs=placed,
        out_specs=(P("cent", None), P(("dp", "cent"))),
        check_vma=False,
    )
```

time: 435 us -> 109 us (0.25)
  blocking collectives: 350 us -> 0 us
  starting transfers between devices: 0.12 us -> 27.9 us
  between operations: 13.9 us -> 0.97 us
  waiting for transfers between devices: 53.5 us -> 60.9 us
  local copies, waits for them, and re-layouts: 0.67 us -> 6.76 us
  matrix products: 9.67 us -> 4.07 us
    all_gather x4 -> x0, blocking collectives: 263 us -> none  [the longest x3 191 us: merged(): pieces = jax.tree.map(lambda part: lax.all_gather(part, axis), value)]
    ppermute x0 -> x26, waiting for transfers between devices: none -> 60.9 us  [swap(): return lax.ppermute(value, axis, [(i, i ^ bit) for i in range(size)])]
    psum x2 -> x0, waiting for transfers between devices: 52.7 us -> none  [on_device(): numer, counts = lax.psum((numer, counts), 'dp')]
    psum x4 -> x0, blocking collectives: 46.1 us -> none  [the longest x2 34.3 us: on_device(): row_total = lax.psum(jnp.sum(weights_exp, axis=1), 'cent')]
    pmax x2 -> x0, blocking collectives: 40.7 us -> none  [on_device(): row_max = lax.pmax(jnp.max(unnormalized_log_odds, axis=1), 'cent')]
    ppermute x0 -> x26, starting transfers between devices: none -> 27.9 us  [swap(): return lax.ppermute(value, axis, [(i, i ^ bit) for i in range(size)])]
    dot_general x5 -> x10, matrix products: 9.67 us -> 4.07 us  [the longest x4 1.7 us: on_device(): lax.dot_general(centers_half, held[index], (((1,), (1,)), ((), ())), pref...]
  transfers between devices with their start and end apart: 3 -> 26, of which waited for: 2 -> 17; matrix products, arithmetic and copies ran while one was open for 1% -> 13% of each run, Pallas kernels for 0% -> 0%
where the time goes in v1:
time: 109 us
  waiting for transfers between devices  60.9 us (56%)
  starting transfers between devices  27.9 us (26%)
  other arithmetic  8.5 us (8%)
  local copies, waits for them, and re-layouts  6.76 us (6%)
  matrix products  4.07 us (4%)
    ppermute x26, waiting for transfers between devices, swap(): return lax.ppermute(value, axis, [(i, i ^ bit) for i in range(size)])  60.9 us
    ppermute x26, starting transfers between devices, swap(): return lax.ppermute(value, axis, [(i, i ^ bit) for i in range(size)])  27.9 us
  transfers between devices with their start and end apart: 26, of which 17 were waited for; matrix products, arithmetic and copies ran while one was open for 13% of the time, Pallas kernels for 0%

profile of v1, /device:TPU:0, one launch (start us, length us, event | category | flops | bytes accessed | tf_op | source)
XLA Modules:
  0.0 109.1 jit_solution(7542043841877577692)
XLA Ops:
  1.2 1.0 slice_bitcast_fusion.5
  2.1 2.7 %collective-permute-start = (bf16[64,768]{1,0:T(8,128)(2,1)S(1)}, bf16[64,768]{1,0:T(8,128)(2,1)S(1)}, u32[]{:S(2)}, u32[]{:S(2)}) collective-permute-start(bf16[64,768]{1,0:T(8,128)(2,1)S(1)} %get-tuple-element.21), channel_id=1, source_target_pairs={{0,2},{1,3},{2,0},{3,1},{4,6},{5,7},{6,4},{7,5},{8,10},{9,11},{10,... | collective-permute-start | bytes 294920 | tf_op jit(solution)/shard_map/ppermute | solution.py:16
  4.8 1.5 %collective-permute-start.3 = (bf16[64,768]{1,0:T(8,128)(2,1)S(1)}, bf16[64,768]{1,0:T(8,128)(2,1)S(1)}, u32[]{:S(2)}, u32[]{:S(2)}) collective-permute-start(bf16[64,768]{1,0:T(8,128)(2,1)S(1)} %get-tuple-element.20), channel_id=1, source_target_pairs={{0,1},{1,0},{2,3},{3,2},{4,5},{5,4},{6,7},{7,6},{8,9},{9,8},{10,11... | collective-permute-start | bytes 294920 | tf_op jit(solution)/shard_map/ppermute | solution.py:16
  6.3 1.3 %multiply_reduce_fusion.1 = f32[256]{0:T(256)S(1)} fusion(f32[256,768]{1,0:T(8,128)} %param.7), kind=kLoop, calls=%fused_computation.25 | loop fusion | flops 392960 | bytes 787456 | tf_op jit(solution)/shard_map/reduce_sum | solution.py:60
  8.3 2.8 %collective-permute-start.1 = (bf16[2,64,768]{2,1,0:T(8,128)(2,1)S(1)}, bf16[2,64,768]{2,1,0:T(8,128)(2,1)S(1)}, u32[]{:S(2)}, u32[]{:S(2)}) collective-permute-start(bf16[2,64,768]{2,1,0:T(8,128)(2,1)S(1)} %get-tuple-element.17), channel_id=1, source_target_pairs={{0,4},{1,5},{2,6},{3,7},{4,0},{5,1},{6,2},{7,3},{8,12},{9,13},{10,... | collective-permute-start | bytes 589832 | tf_op jit(solution)/shard_map/ppermute | solution.py:16
  11.2 9.0 %collective-permute-done.1 = bf16[2,64,768]{2,1,0:T(8,128)(2,1)S(1)} collective-permute-done((bf16[2,64,768]{2,1,0:T(8,128)(2,1)S(1)}, bf16[2,64,768]{2,1,0:T(8,128)(2,1)S(1)}, u32[]{:S(2)}, u32[]{:S(2)}) %collective-permute-start.1) | collective-permute-done | bytes 196640 | tf_op jit(solution)/shard_map/ppermute | solution.py:16
  20.2 1.5 %collective-permute-start.2 = (bf16[2,2,64,768]{3,2,1,0:T(8,128)(2,1)S(1)}, bf16[2,2,64,768]{3,2,1,0:T(8,128)(2,1)S(1)}, u32[]{:S(2)}, u32[]{:S(2)}) collective-permute-start(bf16[2,2,64,768]{3,2,1,0:T(8,128)(2,1)S(1)} %get-tuple-element.13), channel_id=1, source_target_pairs={{0,1},{1,0},{2,3},{3,2},{4,5},{5,4},{6,7},{7,6},{8,9},{9,8},{10,11... | collective-permute-start | bytes 1179656 | tf_op jit(solution)/shard_map/ppermute | solution.py:16
  22.6 4.9 %collective-permute-done.4 = bf16[2,64,768]{2,1,0:T(8,128)(2,1)S(1)} collective-permute-done((bf16[2,64,768]{2,1,0:T(8,128)(2,1)S(1)}, bf16[2,64,768]{2,1,0:T(8,128)(2,1)S(1)}, u32[]{:S(2)}, u32[]{:S(2)}) %collective-permute-start.4) | collective-permute-done | bytes 196640 | tf_op jit(solution)/shard_map/ppermute | solution.py:16
  28.3 3.2 %collective-permute-start.5 = (bf16[2,2,64,768]{3,2,1,0:T(8,128)(2,1)}, bf16[2,2,64,768]{3,2,1,0:T(8,128)(2,1)}, u32[]{:S(2)}, u32[]{:S(2)}) collective-permute-start(bf16[2,2,64,768]{3,2,1,0:T(8,128)(2,1)} %get-tuple-element.15), channel_id=1, source_target_pairs={{0,4},{1,5},{2,6},{3,7},{4,0},{5,1},{6,2},{7,3},{8,12},{9,13},{10,... | collective-permute-start | bytes 1179656 | tf_op jit(solution)/shard_map/ppermute | solution.py:16
  31.6 1.1 copy-done.1
  33.3 15.4 %collective-permute-done.5 = bf16[2,2,64,768]{3,2,1,0:T(8,128)(2,1)} collective-permute-done((bf16[2,2,64,768]{3,2,1,0:T(8,128)(2,1)}, bf16[2,2,64,768]{3,2,1,0:T(8,128)(2,1)}, u32[]{:S(2)}, u32[]{:S(2)}) %collective-permute-start.5) | collective-permute-done | bytes 393248 | tf_op jit(solution)/shard_map/ppermute | solution.py:16
  48.7 1.1 pad_maximum_fusion.2
  51.2 2.9 %collective-permute-done.6 = f32[2,2,2,128]{3,1,2,0:T(2,128)S(1)} collective-permute-done((f32[2,2,2,128]{3,1,2,0:T(2,128)S(1)}, f32[2,2,2,128]{3,1,2,0:T(2,128)S(1)}, u32[]{:S(2)}, u32[]{:S(2)}) %collective-permute-start.6) | collective-permute-done | bytes 4128 | tf_op jit(solution)/shard_map/ppermute | solution.py:16
  55.0 2.8 %collective-permute-done.7 = f32[2,2,2,128]{3,1,2,0:T(2,128)S(1)} collective-permute-done((f32[2,2,2,128]{3,1,2,0:T(2,128)S(1)}, f32[2,2,2,128]{3,1,2,0:T(2,128)S(1)}, u32[]{:S(2)}, u32[]{:S(2)}) %collective-permute-start.7) | collective-permute-done | bytes 4128 | tf_op jit(solution)/shard_map/ppermute | solution.py:16
  57.9 2.1 %collective-permute-start.8 = (f32[2,2,2,128]{3,1,2,0:T(2,128)S(1)}, f32[2,2,2,128]{3,1,2,0:T(2,128)S(1)}, u32[]{:S(2)}, u32[]{:S(2)}) collective-permute-start(f32[2,2,2,128]{3,1,2,0:T(2,128)S(1)} %log_add_fusion.4), channel_id=1, source_target_pairs={{0,4},{1,5},{2,6},{3,7},{4,0},{5,1},{6,2},{7,3},{8,12},{9,13},{10,... | collective-permute-start | bytes 12296 | tf_op jit(solution)/shard_map/ppermute | solution.py:16
  61.5 0.9 collective-permute-done.8
  63.5 0.8 dynamic-slice_bitcast_fusion.1
  66.1 1.6 %collective-permute-start.12 = (f32[256]{0:T(256)S(1)}, f32[256]{0:T(256)S(1)}, u32[]{:S(2)}, u32[]{:S(2)}) collective-permute-start(f32[256]{0:T(256)S(1)} %add.357), channel_id=1, source_target_pairs={{0,16},{8,24},{16,0},{24,8},{1,17},{9,25},{17,1},{25,9},{2,18},{10... | collective-permute-start | bytes 3080 | tf_op jit(solution)/shard_map/ppermute | solution.py:16
  67.7 1.2 %fusion.21 = bf16[128,768]{1,0:T(8,128)(2,1)S(1)} fusion(f32[128,768]{1,0:T(8,128)} %collective-permute-done.9, f32[2,128,768]{2,1,0:T(8,128)} %bitcast.140, s32[]{:T(128)S(6)} %select_n.123), kind=kLoop, calls=%fused_computation.51 | loop fusion | flops 196608 | bytes 983044 | tf_op jit(solution)/shard_map/convert_element_type | solution.py:98
  69.8 5.8 %collective-permute-done.10 = bf16[128,768]{1,0:T(8,128)(2,1)S(1)} collective-permute-done((bf16[128,768]{1,0:T(8,128)(2,1)S(1)}, bf16[128,768]{1,0:T(8,128)(2,1)S(1)}, u32[]{:S(2)}, u32[]{:S(2)}) %collective-permute-start.10) | collective-permute-done | bytes 196640 | tf_op jit(solution)/shard_map/ppermute | solution.py:16
  76.5 3.1 %collective-permute-done.23 = bf16[8,768]{1,0:T(8,128)(2,1)S(1)} collective-permute-done((bf16[8,768]{1,0:T(8,128)(2,1)S(1)}, bf16[8,768]{1,0:T(8,128)(2,1)S(1)}, u32[]{:S(2)}, u32[]{:S(2)}) %collective-permute-start.23) | collective-permute-done | bytes 12320 | tf_op jit(solution)/shard_map/ppermute | solution.py:16
  82.1 2.7 %collective-permute-done.14 = f32[2,2,2,128]{3,1,2,0:T(2,128)S(1)} collective-permute-done((f32[2,2,2,128]{3,1,2,0:T(2,128)S(1)}, f32[2,2,2,128]{3,1,2,0:T(2,128)S(1)}, u32[]{:S(2)}, u32[]{:S(2)}) %collective-permute-start.14) | collective-permute-done | bytes 4128 | tf_op jit(solution)/shard_map/ppermute | solution.py:16
  84.9 1.2 %collective-permute-start.15 = (f32[2,2,2,128]{3,1,2,0:T(2,128)S(1)}, f32[2,2,2,128]{3,1,2,0:T(2,128)S(1)}, u32[]{:S(2)}, u32[]{:S(2)}) collective-permute-start(f32[2,2,2,128]{3,1,2,0:T(2,128)S(1)} %log_add_fusion.2), channel_id=1, source_target_pairs={{0,2},{1,3},{2,0},{3,1},{4,6},{5,7},{6,4},{7,5},{8,10},{9,11},{10,... | collective-permute-start | bytes 12296 | tf_op jit(solution)/shard_map/ppermute | solution.py:16
  86.5 2.0 %collective-permute-done.15 = f32[2,2,2,128]{3,1,2,0:T(2,128)S(1)} collective-permute-done((f32[2,2,2,128]{3,1,2,0:T(2,128)S(1)}, f32[2,2,2,128]{3,1,2,0:T(2,128)S(1)}, u32[]{:S(2)}, u32[]{:S(2)}) %collective-permute-start.15) | collective-permute-done | bytes 4128 | tf_op jit(solution)/shard_map/ppermute | solution.py:16
  88.6 2.1 %collective-permute-start.16 = (f32[2,2,2,128]{3,1,2,0:T(2,128)S(1)}, f32[2,2,2,128]{3,1,2,0:T(2,128)S(1)}, u32[]{:S(2)}, u32[]{:S(2)}) collective-permute-start(f32[2,2,2,128]{3,1,2,0:T(2,128)S(1)} %log_add_fusion.1), channel_id=1, source_target_pairs={{0,4},{1,5},{2,6},{3,7},{4,0},{5,1},{6,2},{7,3},{8,12},{9,13},{10,... | collective-permute-start | bytes 12296 | tf_op jit(solution)/shard_map/ppermute | solution.py:16
  91.0 2.2 %collective-permute-done.16 = f32[2,2,2,128]{3,1,2,0:T(2,128)S(1)} collective-permute-done((f32[2,2,2,128]{3,1,2,0:T(2,128)S(1)}, f32[2,2,2,128]{3,1,2,0:T(2,128)S(1)}, u32[]{:S(2)}, u32[]{:S(2)}) %collective-permute-start.16) | collective-permute-done | bytes 4128 | tf_op jit(solution)/shard_map/ppermute | solution.py:16
  96.6 1.6 %collective-permute-start.18 = (bf16[128,768]{1,0:T(8,128)(2,1)S(1)}, bf16[128,768]{1,0:T(8,128)(2,1)S(1)}, u32[]{:S(2)}, u32[]{:S(2)}) collective-permute-start(bf16[128,768]{1,0:T(8,128)(2,1)S(1)} %fusion.20), channel_id=1, source_target_pairs={{0,16},{8,24},{16,0},{24,8},{1,17},{9,25},{17,1},{25,9},{2,18},{10... | collective-permute-start | bytes 589832 | tf_op jit(solution)/shard_map/ppermute | solution.py:16
  98.2 1.4 %collective-permute-done.20 = f32[256]{0:T(256)S(1)} collective-permute-done((f32[256]{0:T(256)S(1)}, f32[256]{0:T(256)S(1)}, u32[]{:S(2)}, u32[]{:S(2)}) %collective-permute-start.20) | collective-permute-done | bytes 1056 | tf_op jit(solution)/shard_map/ppermute | solution.py:16
  99.7 3.8 %collective-permute-done.18 = bf16[128,768]{1,0:T(8,128)(2,1)S(1)} collective-permute-done((bf16[128,768]{1,0:T(8,128)(2,1)S(1)}, bf16[128,768]{1,0:T(8,128)(2,1)S(1)}, u32[]{:S(2)}, u32[]{:S(2)}) %collective-permute-start.18) | collective-permute-done | bytes 196640 | tf_op jit(solution)/shard_map/ppermute | solution.py:16
  103.8 1.6 %collective-permute-start.25 = (f32[2,16]{1,0:T(2,128)S(1)}, f32[2,16]{1,0:T(2,128)S(1)}, u32[]{:S(2)}, u32[]{:S(2)}) collective-permute-start(f32[2,16]{1,0:T(2,128)S(1)} %pad_maximum_fusion.15), channel_id=1, source_target_pairs={{0,16},{8,24},{16,0},{24,8},{1,17},{9,25},{17,1},{25,9},{2,18},{10... | collective-permute-start | bytes 392 | tf_op jit(solution)/shard_map/ppermute | solution.py:16
  105.4 2.1 %collective-permute-done.25 = f32[2,16]{1,0:T(2,128)S(1)} collective-permute-done((f32[2,16]{1,0:T(2,128)S(1)}, f32[2,16]{1,0:T(2,128)S(1)}, u32[]{:S(2)}, u32[]{:S(2)}) %collective-permute-start.25) | collective-permute-done | bytes 160 | tf_op jit(solution)/shard_map/ppermute | solution.py:16
  108.1 0.9 pad_maximum_fusion.3
  (133 shorter events, 19.8 us)
Async XLA Ops:
  0.6 64.7 %copy-start = (s32[128]{0:T(128)S(1)}, s32[128]{0:T(128)}, u32[]{:S(2)}) copy-start(s32[128]{0:T(128)} %param.9) | copy-start | bytes 1540
  0.6 68.8 %collective-permute-start.22 = (bf16[4,768]{1,0:T(4,128)(2,1)}, bf16[4,768]{1,0:T(4,128)(2,1)S(1)}, u32[]{:S(2)}, u32[]{:S(2)}) collective-permute-start(bf16[4,768]{1,0:T(4,128)(2,1)} %param.6), channel_id=1, source_target_pairs={{0,8},{8,0},{16,24},{24,16},{1,9},{9,1},{17,25},{25,17},{2,10},{10... | collective-permute-start | bytes 18440 | tf_op jit(solution)/shard_map/ppermute | solution.py:16
  2.1 6.1 %collective-permute-start = (bf16[64,768]{1,0:T(8,128)(2,1)S(1)}, bf16[64,768]{1,0:T(8,128)(2,1)S(1)}, u32[]{:S(2)}, u32[]{:S(2)}) collective-permute-start(bf16[64,768]{1,0:T(8,128)(2,1)S(1)} %get-tuple-element.21), channel_id=1, source_target_pairs={{0,2},{1,3},{2,0},{3,1},{4,6},{5,7},{6,4},{7,5},{8,10},{9,11},{10,... | collective-permute-start | bytes 294920 | tf_op jit(solution)/shard_map/ppermute | solution.py:16
  4.8 17.0 %collective-permute-start.3 = (bf16[64,768]{1,0:T(8,128)(2,1)S(1)}, bf16[64,768]{1,0:T(8,128)(2,1)S(1)}, u32[]{:S(2)}, u32[]{:S(2)}) collective-permute-start(bf16[64,768]{1,0:T(8,128)(2,1)S(1)} %get-tuple-element.20), channel_id=1, source_target_pairs={{0,1},{1,0},{2,3},{3,2},{4,5},{5,4},{6,7},{7,6},{8,9},{9,8},{10,11... | collective-permute-start | bytes 294920 | tf_op jit(solution)/shard_map/ppermute | solution.py:16
  8.3 11.9 %collective-permute-start.1 = (bf16[2,64,768]{2,1,0:T(8,128)(2,1)S(1)}, bf16[2,64,768]{2,1,0:T(8,128)(2,1)S(1)}, u32[]{:S(2)}, u32[]{:S(2)}) collective-permute-start(bf16[2,64,768]{2,1,0:T(8,128)(2,1)S(1)} %get-tuple-element.17), channel_id=1, source_target_pairs={{0,4},{1,5},{2,6},{3,7},{4,0},{5,1},{6,2},{7,3},{8,12},{9,13},{10,... | collective-permute-start | bytes 589832 | tf_op jit(solution)/shard_map/ppermute | solution.py:16
  20.2 11.3 %collective-permute-start.2 = (bf16[2,2,64,768]{3,2,1,0:T(8,128)(2,1)S(1)}, bf16[2,2,64,768]{3,2,1,0:T(8,128)(2,1)S(1)}, u32[]{:S(2)}, u32[]{:S(2)}) collective-permute-start(bf16[2,2,64,768]{3,2,1,0:T(8,128)(2,1)S(1)} %get-tuple-element.13), channel_id=1, source_target_pairs={{0,1},{1,0},{2,3},{3,2},{4,5},{5,4},{6,7},{7,6},{8,9},{9,8},{10,11... | collective-permute-start | bytes 1179656 | tf_op jit(solution)/shard_map/ppermute | solution.py:16
  21.8 5.7 %collective-permute-start.4 = (bf16[2,64,768]{2,1,0:T(8,128)(2,1)S(1)}, bf16[2,64,768]{2,1,0:T(8,128)(2,1)S(1)}, u32[]{:S(2)}, u32[]{:S(2)}) collective-permute-start(bf16[2,64,768]{2,1,0:T(8,128)(2,1)S(1)} %get-tuple-element.23), channel_id=1, source_target_pairs={{0,2},{1,3},{2,0},{3,1},{4,6},{5,7},{6,4},{7,5},{8,10},{9,11},{10,... | collective-permute-start | bytes 589832 | tf_op jit(solution)/shard_map/ppermute | solution.py:16
  28.3 20.4 %collective-permute-start.5 = (bf16[2,2,64,768]{3,2,1,0:T(8,128)(2,1)}, bf16[2,2,64,768]{3,2,1,0:T(8,128)(2,1)}, u32[]{:S(2)}, u32[]{:S(2)}) collective-permute-start(bf16[2,2,64,768]{3,2,1,0:T(8,128)(2,1)} %get-tuple-element.15), channel_id=1, source_target_pairs={{0,4},{1,5},{2,6},{3,7},{4,0},{5,1},{6,2},{7,3},{8,12},{9,13},{10,... | collective-permute-start | bytes 1179656 | tf_op jit(solution)/shard_map/ppermute | solution.py:16
  31.5 1.1 %copy-start.1 = (f32[256,768]{1,0:T(8,128)S(1)}, f32[256,768]{1,0:T(8,128)}, u32[]{:S(2)}) copy-start(f32[256,768]{1,0:T(8,128)} %param.7) | copy-start | bytes 2359300
  50.5 3.6 %collective-permute-start.6 = (f32[2,2,2,128]{3,1,2,0:T(2,128)S(1)}, f32[2,2,2,128]{3,1,2,0:T(2,128)S(1)}, u32[]{:S(2)}, u32[]{:S(2)}) collective-permute-start(f32[2,2,2,128]{3,1,2,0:T(2,128)S(1)} %pad_maximum_fusion.12), channel_id=1, source_target_pairs={{0,1},{1,0},{2,3},{3,2},{4,5},{5,4},{6,7},{7,6},{8,9},{9,8},{10,11... | collective-permute-start | bytes 12296 | tf_op jit(solution)/shard_map/ppermute | solution.py:16
  54.2 3.7 %collective-permute-start.7 = (f32[2,2,2,128]{3,1,2,0:T(2,128)S(1)}, f32[2,2,2,128]{3,1,2,0:T(2,128)S(1)}, u32[]{:S(2)}, u32[]{:S(2)}) collective-permute-start(f32[2,2,2,128]{3,1,2,0:T(2,128)S(1)} %log_add_fusion.5), channel_id=1, source_target_pairs={{0,2},{1,3},{2,0},{3,1},{4,6},{5,7},{6,4},{7,5},{8,10},{9,11},{10,... | collective-permute-start | bytes 12296 | tf_op jit(solution)/shard_map/ppermute | solution.py:16
  57.9 4.6 %collective-permute-start.8 = (f32[2,2,2,128]{3,1,2,0:T(2,128)S(1)}, f32[2,2,2,128]{3,1,2,0:T(2,128)S(1)}, u32[]{:S(2)}, u32[]{:S(2)}) collective-permute-start(f32[2,2,2,128]{3,1,2,0:T(2,128)S(1)} %log_add_fusion.4), channel_id=1, source_target_pairs={{0,4},{1,5},{2,6},{3,7},{4,0},{5,1},{6,2},{7,3},{8,12},{9,13},{10,... | collective-permute-start | bytes 12296 | tf_op jit(solution)/shard_map/ppermute | solution.py:16
  60.1 0.7 copy-start.4
  63.5 1.1 %copy-start.2 = (f32[256,768]{1,0:T(8,128)}, f32[256,768]{1,0:T(8,128)S(1)}, u32[]{:S(2)}) copy-start(f32[256,768]{1,0:T(8,128)S(1)} %convolution_add_fusion.1) | copy-start | bytes 2359300
  64.4 3.3 %collective-permute-start.9 = (f32[128,768]{1,0:T(8,128)}, f32[128,768]{1,0:T(8,128)}, u32[]{:S(2)}, u32[]{:S(2)}) collective-permute-start(f32[128,768]{1,0:T(8,128)} %dynamic-slice_bitcast_fusion.1), channel_id=1, source_target_pairs={{0,8},{8,0},{16,24},{24,16},{1,9},{9,1},{17,25},{25,17},{2,10},{10... | collective-permute-start | bytes 1179656 | tf_op jit(solution)/shard_map/ppermute | solution.py:16
  64.6 1.4 %collective-permute-start.11 = (f32[256]{0:T(256)S(1)}, f32[256]{0:T(256)S(1)}, u32[]{:S(2)}, u32[]{:S(2)}) collective-permute-start(f32[256]{0:T(256)S(1)} %add.356), channel_id=1, source_target_pairs={{0,8},{8,0},{16,24},{24,16},{1,9},{9,1},{17,25},{25,17},{2,10},{10... | collective-permute-start | bytes 3080 | tf_op jit(solution)/shard_map/ppermute | solution.py:16
  66.1 3.3 %copy-start.3 = (bf16[4,768]{1,0:T(4,128)(2,1)S(1)}, bf16[4,768]{1,0:T(4,128)(2,1)}, u32[]{:S(2)}) copy-start(bf16[4,768]{1,0:T(4,128)(2,1)} %param.6) | copy-start | bytes 18436
  66.1 3.6 %collective-permute-start.12 = (f32[256]{0:T(256)S(1)}, f32[256]{0:T(256)S(1)}, u32[]{:S(2)}, u32[]{:S(2)}) collective-permute-start(f32[256]{0:T(256)S(1)} %add.357), channel_id=1, source_target_pairs={{0,16},{8,24},{16,0},{24,8},{1,17},{9,25},{17,1},{25,9},{2,18},{10... | collective-permute-start | bytes 3080 | tf_op jit(solution)/shard_map/ppermute | solution.py:16
  68.9 6.8 %collective-permute-start.10 = (bf16[128,768]{1,0:T(8,128)(2,1)S(1)}, bf16[128,768]{1,0:T(8,128)(2,1)S(1)}, u32[]{:S(2)}, u32[]{:S(2)}) collective-permute-start(bf16[128,768]{1,0:T(8,128)(2,1)S(1)} %fusion.21), channel_id=1, source_target_pairs={{0,16},{8,24},{16,0},{24,8},{1,17},{9,25},{17,1},{25,9},{2,18},{10... | collective-permute-start | bytes 589832 | tf_op jit(solution)/shard_map/ppermute | solution.py:16
  75.8 3.9 %collective-permute-start.13 = (f32[128,768]{1,0:T(8,128)S(1)}, f32[128,768]{1,0:T(8,128)S(1)}, u32[]{:S(2)}, u32[]{:S(2)}) collective-permute-start(f32[128,768]{1,0:T(8,128)S(1)} %add_divide_fusion), channel_id=1, source_target_pairs={{0,8},{8,0},{16,24},{24,16},{1,9},{9,1},{17,25},{25,17},{2,10},{10... | collective-permute-start | bytes 1179656 | tf_op jit(solution)/shard_map/ppermute | solution.py:16
  75.8 3.8 %collective-permute-start.23 = (bf16[8,768]{1,0:T(8,128)(2,1)S(1)}, bf16[8,768]{1,0:T(8,128)(2,1)S(1)}, u32[]{:S(2)}, u32[]{:S(2)}) collective-permute-start(bf16[8,768]{1,0:T(8,128)(2,1)S(1)} %pad_maximum_fusion.11), channel_id=1, source_target_pairs={{0,16},{8,24},{16,0},{24,8},{1,17},{9,25},{17,1},{25,9},{2,18},{10... | collective-permute-start | bytes 36872 | tf_op jit(solution)/shard_map/ppermute | solution.py:16
  81.2 3.6 %collective-permute-start.14 = (f32[2,2,2,128]{3,1,2,0:T(2,128)S(1)}, f32[2,2,2,128]{3,1,2,0:T(2,128)S(1)}, u32[]{:S(2)}, u32[]{:S(2)}) collective-permute-start(f32[2,2,2,128]{3,1,2,0:T(2,128)S(1)} %pad_maximum_fusion.13), channel_id=1, source_target_pairs={{0,1},{1,0},{2,3},{3,2},{4,5},{5,4},{6,7},{7,6},{8,9},{9,8},{10,11... | collective-permute-start | bytes 12296 | tf_op jit(solution)/shard_map/ppermute | solution.py:16
  84.9 3.7 %collective-permute-start.15 = (f32[2,2,2,128]{3,1,2,0:T(2,128)S(1)}, f32[2,2,2,128]{3,1,2,0:T(2,128)S(1)}, u32[]{:S(2)}, u32[]{:S(2)}) collective-permute-start(f32[2,2,2,128]{3,1,2,0:T(2,128)S(1)} %log_add_fusion.2), channel_id=1, source_target_pairs={{0,2},{1,3},{2,0},{3,1},{4,6},{5,7},{6,4},{7,5},{8,10},{9,11},{10,... | collective-permute-start | bytes 12296 | tf_op jit(solution)/shard_map/ppermute | solution.py:16
  88.6 4.6 %collective-permute-start.16 = (f32[2,2,2,128]{3,1,2,0:T(2,128)S(1)}, f32[2,2,2,128]{3,1,2,0:T(2,128)S(1)}, u32[]{:S(2)}, u32[]{:S(2)}) collective-permute-start(f32[2,2,2,128]{3,1,2,0:T(2,128)S(1)} %log_add_fusion.1), channel_id=1, source_target_pairs={{0,4},{1,5},{2,6},{3,7},{4,0},{5,1},{6,2},{7,3},{8,12},{9,13},{10,... | collective-permute-start | bytes 12296 | tf_op jit(solution)/shard_map/ppermute | solution.py:16
  94.3 2.3 %collective-permute-start.17 = (f32[128,768]{1,0:T(8,128)S(1)}, f32[128,768]{1,0:T(8,128)S(1)}, u32[]{:S(2)}, u32[]{:S(2)}) collective-permute-start(f32[128,768]{1,0:T(8,128)S(1)} %dynamic-slice_bitcast_fusion), channel_id=1, source_target_pairs={{0,8},{8,0},{16,24},{24,16},{1,9},{9,1},{17,25},{25,17},{2,10},{10... | collective-permute-start | bytes 1179656 | tf_op jit(solution)/shard_map/ppermute | solution.py:16
  94.7 1.4 %collective-permute-start.19 = (f32[256]{0:T(256)S(1)}, f32[256]{0:T(256)S(1)}, u32[]{:S(2)}, u32[]{:S(2)}) collective-permute-start(f32[256]{0:T(256)S(1)} %add.374), channel_id=1, source_target_pairs={{0,8},{8,0},{16,24},{24,16},{1,9},{9,1},{17,25},{25,17},{2,10},{10... | collective-permute-start | bytes 3080 | tf_op jit(solution)/shard_map/ppermute | solution.py:16
  96.1 3.6 %collective-permute-start.20 = (f32[256]{0:T(256)S(1)}, f32[256]{0:T(256)S(1)}, u32[]{:S(2)}, u32[]{:S(2)}) collective-permute-start(f32[256]{0:T(256)S(1)} %add.375), channel_id=1, source_target_pairs={{0,16},{8,24},{16,0},{24,8},{1,17},{9,25},{17,1},{25,9},{2,18},{10... | collective-permute-start | bytes 3080 | tf_op jit(solution)/shard_map/ppermute | solution.py:16
  96.6 6.9 %collective-permute-start.18 = (bf16[128,768]{1,0:T(8,128)(2,1)S(1)}, bf16[128,768]{1,0:T(8,128)(2,1)S(1)}, u32[]{:S(2)}, u32[]{:S(2)}) collective-permute-start(bf16[128,768]{1,0:T(8,128)(2,1)S(1)} %fusion.20), channel_id=1, source_target_pairs={{0,16},{8,24},{16,0},{24,8},{1,17},{9,25},{17,1},{25,9},{2,18},{10... | collective-permute-start | bytes 589832 | tf_op jit(solution)/shard_map/ppermute | solution.py:16
  98.2 5.5 %collective-permute-start.24 = (f32[2,16]{1,0:T(2,128)S(1)}, f32[2,16]{1,0:T(2,128)S(1)}, u32[]{:S(2)}, u32[]{:S(2)}) collective-permute-start(f32[2,16]{1,0:T(2,128)S(1)} %pad_maximum_fusion.14), channel_id=1, source_target_pairs={{0,8},{8,0},{16,24},{24,16},{1,9},{9,1},{17,25},{25,17},{2,10},{10... | collective-permute-start | bytes 392 | tf_op jit(solution)/shard_map/ppermute | solution.py:16
  103.7 4.4 %collective-permute-start.21 = (f32[128,768]{1,0:T(8,128)S(1)}, f32[128,768]{1,0:T(8,128)S(1)}, u32[]{:S(2)}, u32[]{:S(2)}) collective-permute-start(f32[128,768]{1,0:T(8,128)S(1)} %fusion.19), channel_id=1, source_target_pairs={{0,8},{8,0},{16,24},{24,16},{1,9},{9,1},{17,25},{25,17},{2,10},{10... | collective-permute-start | bytes 1179656 | tf_op jit(solution)/shard_map/ppermute | solution.py:16
  103.8 3.6 %collective-permute-start.25 = (f32[2,16]{1,0:T(2,128)S(1)}, f32[2,16]{1,0:T(2,128)S(1)}, u32[]{:S(2)}, u32[]{:S(2)}) collective-permute-start(f32[2,16]{1,0:T(2,128)S(1)} %pad_maximum_fusion.15), channel_id=1, source_target_pairs={{0,16},{8,24},{16,0},{24,8},{1,17},{9,25},{17,1},{25,9},{2,18},{10... | collective-permute-start | bytes 392 | tf_op jit(solution)/shard_map/ppermute | solution.py:16

commit v2 on v1

--- a/solution.py
+++ b/solution.py
@@ -20,10 +20,20 @@
     return [1 << k for k in range(size.bit_length() - 1)]
 
 
-def doubled(value, axis, order):
-    for bit in order:
-        value = jnp.stack([value, swap(value, axis, bit)])
-    return value
+def gathered_pieces(value, axis, size):
+    pieces = {0: value}
+    half = value.shape[0] // 2
+    for mask in sorted(range(1, size), key=lambda m: (bin(m).count("1"), -m)):
+        low = mask & -mask
+        if bin(mask).count("1") < 3:
+            pieces[mask] = swap(pieces[mask ^ low], axis, low)
+        else:
+            rest = mask ^ low
+            second = rest & -rest
+            pieces[mask] = jnp.concatenate(
+                [swap(pieces[mask ^ low][:half], axis, low), swap(pieces[mask ^ second][half:], axis, second)]
+            )
+    return pieces
 
 
 def join_lse(first, second):
@@ -38,13 +48,11 @@
     rows, width = passages.shape
     own_queries = queries.shape[0]
 
-    half = rows // 2
-    orders = [cent_bits[1:] + cent_bits[:1], cent_bits]
-    parts = [
-        doubled(passages[:half], "cent", orders[0]),
-        doubled(passages[half:], "cent", orders[1]),
+    pieces = gathered_pieces(passages, "cent", n_cent)
+    half = n_cent // 2
+    held = [
+        jnp.concatenate([pieces[mask] for mask in range(start, start + half)]) for start in (0, half)
     ]
-    held = [part.reshape(-1, width) for part in parts]
 
     asked = queries
     for bit in dp_bits:
@@ -70,21 +78,14 @@
             top = jnp.max(logits, axis=0)
             odds.append(logits)
             stats.append(top + jnp.log(jnp.sum(jnp.exp(logits - top[None, :]), axis=0)))
-        shape = (2,) * len(cent_bits) + (half,)
-        views = []
-        for index in range(2):
-            view = stats[index].reshape(shape)
-            axes = [len(cent_bits) - 1 - orders[index].index(bit) for bit in cent_bits]
-            views.append(jnp.transpose(view, axes + [len(cent_bits)]))
-        lse = jnp.concatenate(views, axis=-1)
-        for position, bit in enumerate(cent_bits):
+        lse = jnp.concatenate(stats).reshape((2,) * len(cent_bits) + (rows,))
+        for bit in cent_bits:
+            position = len(cent_bits) - 1 - cent_bits.index(bit)
             lse = join_lse(lse, jnp.flip(swap(lse, "cent", bit), axis=position))
+        total = lse.reshape(2, half * rows)
         numer, counts = 0.0, 0.0
         for index in range(2):
-            view = lse[..., index * half : (index + 1) * half]
-            axes = [cent_bits.index(bit) for bit in reversed(orders[index])]
-            total = jnp.transpose(view, axes + [len(cent_bits)]).reshape(-1)
-            resp = jnp.exp(odds[index] - total[None, :])
+            resp = jnp.exp(odds[index] - total[index][None, :])
             counts = counts + jnp.sum(resp, axis=1)
             numer = numer + jnp.dot(
                 resp.astype(jnp.bfloat16), held[index], preferred_element_type=jnp.float32
@@ -110,13 +111,9 @@
     target = picks[:, 0] * BLOCK + positive_offset[ids]
     partial, positive = None, 0.0
     for index in range(2):
-        where_bits = jnp.zeros((2,) * len(cent_bits), jnp.int32) + cent
-        for bit in cent_bits:
-            axis = len(cent_bits) - 1 - orders[index].index(bit)
-            flag = lax.broadcasted_iota(jnp.int32, where_bits.shape, axis) * bit
-            where_bits = where_bits ^ flag
-        owner = (dp * n_cent + where_bits)[..., None] * rows
-        column = (owner + index * half + jnp.arange(half, dtype=jnp.int32)).reshape(-1)
+        masks = jnp.arange(index * half, (index + 1) * half, dtype=jnp.int32)
+        owner = (dp * n_cent + (cent ^ masks)) * rows
+        column = (owner[:, None] + jnp.arange(rows, dtype=jnp.int32)[None, :]).reshape(-1)
         scores = SCALE * lax.dot_general(
             asked, held[index], (((1,), (1,)), ((), ())), preferred_element_type=jnp.float32
         )

time: 109 us -> 88 us (0.81)
  waiting for transfers between devices: 60.9 us -> 45.1 us
  local copies, waits for them, and re-layouts: 6.76 us -> 3.97 us
  other arithmetic: 8.5 us -> 6.15 us
    ppermute x26 -> x28, waiting for transfers between devices: 60.9 us -> 45.1 us  [swap(): return lax.ppermute(value, axis, [(i, i ^ bit) for i in range(size)])]
    another operation x6 -> x0, other arithmetic: 2.05 us -> none  [doubled(): value = jnp.stack([value, swap(value, axis, bit)])]
    ppermute x26 -> x28, starting transfers between devices: 27.9 us -> 27.4 us  [swap(): return lax.ppermute(value, axis, [(i, i ^ bit) for i in range(size)])]
  transfers between devices with their start and end apart: 26 -> 28, of which waited for: 17 -> 19; matrix products, arithmetic and copies ran while one was open for 13% -> 12% of each run, Pallas kernels for 0% -> 0%
where the time goes in v2:
time: 88 us; the launch traced here: 87.8 us
  waiting for transfers between devices  45.1 us (51%)
  starting transfers between devices  27.4 us (31%)
  other arithmetic  6.15 us (7%)
  matrix products  4.07 us (5%)
  local copies, waits for them, and re-layouts  3.97 us (5%)
  between operations  1.08 us (1%)
    ppermute x28, waiting for transfers between devices, swap(): return lax.ppermute(value, axis, [(i, i ^ bit) for i in range(size)])  45.1 us
    ppermute x28, starting transfers between devices, swap(): return lax.ppermute(value, axis, [(i, i ^ bit) for i in range(size)])  27.4 us
  transfers between devices with their start and end apart: 28, of which 19 were waited for; matrix products, arithmetic and copies ran while one was open for 12% of the time, Pallas kernels for 0%

profile of v2, /device:TPU:0, one launch (start us, length us, event | category | flops | bytes accessed | tf_op | source)
XLA Modules:
  0.0 87.8 jit_solution(5087387318187203429)
XLA Ops:
  0.6 3.1 %collective-permute-start.1 = (bf16[128,768]{1,0:T(8,128)(2,1)}, bf16[128,768]{1,0:T(8,128)(2,1)S(1)}, u32[]{:S(2)}, u32[]{:S(2)}) collective-permute-start(bf16[128,768]{1,0:T(8,128)(2,1)} %param.5), channel_id=1, source_target_pairs={{0,2},{1,3},{2,0},{3,1},{4,6},{5,7},{6,4},{7,5},{8,10},{9,11},{10,... | collective-permute-start | bytes 589832 | tf_op jit(solution)/shard_map/ppermute | solution.py:16
  3.7 1.5 %collective-permute-start = (bf16[128,768]{1,0:T(8,128)(2,1)}, bf16[128,768]{1,0:T(8,128)(2,1)S(1)}, u32[]{:S(2)}, u32[]{:S(2)}) collective-permute-start(bf16[128,768]{1,0:T(8,128)(2,1)} %param.5), channel_id=1, source_target_pairs={{0,1},{1,0},{2,3},{3,2},{4,5},{5,4},{6,7},{7,6},{8,9},{9,8},{10,11... | collective-permute-start | bytes 589832 | tf_op jit(solution)/shard_map/ppermute | solution.py:16
  5.2 2.6 %collective-permute-start.3 = (bf16[128,768]{1,0:T(8,128)(2,1)}, bf16[128,768]{1,0:T(8,128)(2,1)S(1)}, u32[]{:S(2)}, u32[]{:S(2)}) collective-permute-start(bf16[128,768]{1,0:T(8,128)(2,1)} %param.5), channel_id=1, source_target_pairs={{0,4},{1,5},{2,6},{3,7},{4,0},{5,1},{6,2},{7,3},{8,12},{9,13},{10,... | collective-permute-start | bytes 589832 | tf_op jit(solution)/shard_map/ppermute | solution.py:16
  7.8 1.3 %multiply_reduce_fusion.1 = f32[256]{0:T(256)S(1)} fusion(f32[256,768]{1,0:T(8,128)} %param.7), kind=kLoop, calls=%fused_computation.23 | loop fusion | flops 392960 | bytes 787456 | tf_op jit(solution)/shard_map/reduce_sum | solution.py:68
  9.3 7.5 %collective-permute-done.3 = bf16[128,768]{1,0:T(8,128)(2,1)S(1)} collective-permute-done((bf16[128,768]{1,0:T(8,128)(2,1)}, bf16[128,768]{1,0:T(8,128)(2,1)S(1)}, u32[]{:S(2)}, u32[]{:S(2)}) %collective-permute-start.3) | collective-permute-done | bytes 196640 | tf_op jit(solution)/shard_map/ppermute | solution.py:16
  17.4 1.4 %collective-permute-start.2 = (bf16[128,768]{1,0:T(8,128)(2,1)S(1)}, bf16[128,768]{1,0:T(8,128)(2,1)S(1)}, u32[]{:S(2)}, u32[]{:S(2)}) collective-permute-start(bf16[128,768]{1,0:T(8,128)(2,1)S(1)} %collective-permute-done.1), channel_id=1, source_target_pairs={{0,1},{1,0},{2,3},{3,2},{4,5},{5,4},{6,7},{7,6},{8,9},{9,8},{10,11... | collective-permute-start | bytes 589832 | tf_op jit(solution)/shard_map/ppermute | solution.py:16
  18.9 3.9 %collective-permute-done.5 = bf16[128,768]{1,0:T(8,128)(2,1)S(1)} collective-permute-done((bf16[128,768]{1,0:T(8,128)(2,1)S(1)}, bf16[128,768]{1,0:T(8,128)(2,1)S(1)}, u32[]{:S(2)}, u32[]{:S(2)}) %collective-permute-start.5) | collective-permute-done | bytes 196640 | tf_op jit(solution)/shard_map/ppermute | solution.py:16
  23.0 1.6 %collective-permute-done.4 = bf16[128,768]{1,0:T(8,128)(2,1)S(1)} collective-permute-done((bf16[128,768]{1,0:T(8,128)(2,1)S(1)}, bf16[128,768]{1,0:T(8,128)(2,1)S(1)}, u32[]{:S(2)}, u32[]{:S(2)}) %collective-permute-start.4) | collective-permute-done | bytes 196640 | tf_op jit(solution)/shard_map/ppermute | solution.py:16
  24.6 1.0 %collective-permute-start.7 = (bf16[64,768]{1,0:T(8,128)(2,1)S(1)}, bf16[64,768]{1,0:T(8,128)(2,1)S(1)}, u32[]{:S(2)}, u32[]{:S(2)}) collective-permute-start(bf16[64,768]{1,0:T(8,128)(2,1)S(1)} %slice.53), channel_id=1, source_target_pairs={{0,2},{1,3},{2,0},{3,1},{4,6},{5,7},{6,4},{7,5},{8,10},{9,11},{10,... | collective-permute-start | bytes 294920 | tf_op jit(solution)/shard_map/ppermute | solution.py:16
  25.6 1.4 %collective-permute-done.2 = bf16[128,768]{1,0:T(8,128)(2,1)S(1)} collective-permute-done((bf16[128,768]{1,0:T(8,128)(2,1)S(1)}, bf16[128,768]{1,0:T(8,128)(2,1)S(1)}, u32[]{:S(2)}, u32[]{:S(2)}) %collective-permute-start.2) | collective-permute-done | bytes 196640 | tf_op jit(solution)/shard_map/ppermute | solution.py:16
  28.0 1.3 %collective-permute-done.7 = bf16[64,768]{1,0:T(8,128)(2,1)S(1)} collective-permute-done((bf16[64,768]{1,0:T(8,128)(2,1)S(1)}, bf16[64,768]{1,0:T(8,128)(2,1)S(1)}, u32[]{:S(2)}, u32[]{:S(2)}) %collective-permute-start.7) | collective-permute-done | bytes 98336 | tf_op jit(solution)/shard_map/ppermute | solution.py:16
  30.7 2.8 %collective-permute-done.8 = f32[2,2,2,128]{3,2,1,0:T(2,128)S(1)} collective-permute-done((f32[2,2,2,128]{3,2,1,0:T(2,128)S(1)}, f32[2,2,2,128]{3,2,1,0:T(2,128)S(1)}, u32[]{:S(2)}, u32[]{:S(2)}) %collective-permute-start.8) | collective-permute-done | bytes 4128 | tf_op jit(solution)/shard_map/ppermute | solution.py:16
  33.6 1.0 %collective-permute-start.9 = (f32[2,2,2,128]{3,2,1,0:T(2,128)S(1)}, f32[2,2,2,128]{3,2,1,0:T(2,128)S(1)}, u32[]{:S(2)}, u32[]{:S(2)}) collective-permute-start(f32[2,2,2,128]{3,2,1,0:T(2,128)S(1)} %log_add_fusion.5), channel_id=1, source_target_pairs={{0,2},{1,3},{2,0},{3,1},{4,6},{5,7},{6,4},{7,5},{8,10},{9,11},{10,... | collective-permute-start | bytes 12296 | tf_op jit(solution)/shard_map/ppermute | solution.py:16
  34.7 2.6 %collective-permute-done.9 = f32[2,2,2,128]{3,2,1,0:T(2,128)S(1)} collective-permute-done((f32[2,2,2,128]{3,2,1,0:T(2,128)S(1)}, f32[2,2,2,128]{3,2,1,0:T(2,128)S(1)}, u32[]{:S(2)}, u32[]{:S(2)}) %collective-permute-start.9) | collective-permute-done | bytes 4128 | tf_op jit(solution)/shard_map/ppermute | solution.py:16
  37.3 3.0 %collective-permute-start.10 = (f32[2,2,2,128]{3,2,1,0:T(2,128)S(1)}, f32[2,2,2,128]{3,2,1,0:T(2,128)S(1)}, u32[]{:S(2)}, u32[]{:S(2)}) collective-permute-start(f32[2,2,2,128]{3,2,1,0:T(2,128)S(1)} %log_add_fusion.4), channel_id=1, source_target_pairs={{0,4},{1,5},{2,6},{3,7},{4,0},{5,1},{6,2},{7,3},{8,12},{9,13},{10,... | collective-permute-start | bytes 12296 | tf_op jit(solution)/shard_map/ppermute | solution.py:16
  42.7 0.8 dynamic-slice_bitcast_fusion.1
  45.3 1.6 %collective-permute-start.14 = (f32[256]{0:T(256)S(1)}, f32[256]{0:T(256)S(1)}, u32[]{:S(2)}, u32[]{:S(2)}) collective-permute-start(f32[256]{0:T(256)S(1)} %add.376), channel_id=1, source_target_pairs={{0,16},{8,24},{16,0},{24,8},{1,17},{9,25},{17,1},{25,9},{2,18},{10... | collective-permute-start | bytes 3080 | tf_op jit(solution)/shard_map/ppermute | solution.py:16
  46.9 1.2 %fusion.21 = bf16[128,768]{1,0:T(8,128)(2,1)S(1)} fusion(f32[128,768]{1,0:T(8,128)} %collective-permute-done.11, f32[2,128,768]{2,1,0:T(8,128)} %bitcast.142, s32[]{:T(128)S(6)} %select_n.123), kind=kLoop, calls=%fused_computation.47 | loop fusion | flops 196608 | bytes 983044 | tf_op jit(solution)/shard_map/convert_element_type | solution.py:99
  49.1 5.8 %collective-permute-done.12 = bf16[128,768]{1,0:T(8,128)(2,1)S(1)} collective-permute-done((bf16[128,768]{1,0:T(8,128)(2,1)S(1)}, bf16[128,768]{1,0:T(8,128)(2,1)S(1)}, u32[]{:S(2)}, u32[]{:S(2)}) %collective-permute-start.12) | collective-permute-done | bytes 196640 | tf_op jit(solution)/shard_map/ppermute | solution.py:16
  55.8 3.1 %collective-permute-done.25 = bf16[8,768]{1,0:T(8,128)(2,1)S(1)} collective-permute-done((bf16[8,768]{1,0:T(8,128)(2,1)S(1)}, bf16[8,768]{1,0:T(8,128)(2,1)S(1)}, u32[]{:S(2)}, u32[]{:S(2)}) %collective-permute-start.25) | collective-permute-done | bytes 12320 | tf_op jit(solution)/shard_map/ppermute | solution.py:16
  61.3 2.5 %collective-permute-done.16 = f32[2,2,2,128]{3,2,1,0:T(2,128)S(1)} collective-permute-done((f32[2,2,2,128]{3,2,1,0:T(2,128)S(1)}, f32[2,2,2,128]{3,2,1,0:T(2,128)S(1)}, u32[]{:S(2)}, u32[]{:S(2)}) %collective-permute-start.16) | collective-permute-done | bytes 4128 | tf_op jit(solution)/shard_map/ppermute | solution.py:16
  63.9 0.9 %collective-permute-start.17 = (f32[2,2,2,128]{3,2,1,0:T(2,128)S(1)}, f32[2,2,2,128]{3,2,1,0:T(2,128)S(1)}, u32[]{:S(2)}, u32[]{:S(2)}) collective-permute-start(f32[2,2,2,128]{3,2,1,0:T(2,128)S(1)} %log_add_fusion.2), channel_id=1, source_target_pairs={{0,2},{1,3},{2,0},{3,1},{4,6},{5,7},{6,4},{7,5},{8,10},{9,11},{10,... | collective-permute-start | bytes 12296 | tf_op jit(solution)/shard_map/ppermute | solution.py:16
  65.3 2.3 %collective-permute-done.17 = f32[2,2,2,128]{3,2,1,0:T(2,128)S(1)} collective-permute-done((f32[2,2,2,128]{3,2,1,0:T(2,128)S(1)}, f32[2,2,2,128]{3,2,1,0:T(2,128)S(1)}, u32[]{:S(2)}, u32[]{:S(2)}) %collective-permute-start.17) | collective-permute-done | bytes 4128 | tf_op jit(solution)/shard_map/ppermute | solution.py:16
  67.6 3.0 %collective-permute-start.18 = (f32[2,2,2,128]{3,2,1,0:T(2,128)S(1)}, f32[2,2,2,128]{3,2,1,0:T(2,128)S(1)}, u32[]{:S(2)}, u32[]{:S(2)}) collective-permute-start(f32[2,2,2,128]{3,2,1,0:T(2,128)S(1)} %log_add_fusion.1), channel_id=1, source_target_pairs={{0,4},{1,5},{2,6},{3,7},{4,0},{5,1},{6,2},{7,3},{8,12},{9,13},{10,... | collective-permute-start | bytes 12296 | tf_op jit(solution)/shard_map/ppermute | solution.py:16
  70.8 1.4 %collective-permute-done.18 = f32[2,2,2,128]{3,2,1,0:T(2,128)S(1)} collective-permute-done((f32[2,2,2,128]{3,2,1,0:T(2,128)S(1)}, f32[2,2,2,128]{3,2,1,0:T(2,128)S(1)}, u32[]{:S(2)}, u32[]{:S(2)}) %collective-permute-start.18) | collective-permute-done | bytes 4128 | tf_op jit(solution)/shard_map/ppermute | solution.py:16
  74.0 0.8 collective-permute-done.21
  75.4 1.6 %collective-permute-start.20 = (bf16[128,768]{1,0:T(8,128)(2,1)S(1)}, bf16[128,768]{1,0:T(8,128)(2,1)S(1)}, u32[]{:S(2)}, u32[]{:S(2)}) collective-permute-start(bf16[128,768]{1,0:T(8,128)(2,1)S(1)} %fusion.20), channel_id=1, source_target_pairs={{0,16},{8,24},{16,0},{24,8},{1,17},{9,25},{17,1},{25,9},{2,18},{10... | collective-permute-start | bytes 589832 | tf_op jit(solution)/shard_map/ppermute | solution.py:16
  77.0 1.4 %collective-permute-done.22 = f32[256]{0:T(256)S(1)} collective-permute-done((f32[256]{0:T(256)S(1)}, f32[256]{0:T(256)S(1)}, u32[]{:S(2)}, u32[]{:S(2)}) %collective-permute-start.22) | collective-permute-done | bytes 1056 | tf_op jit(solution)/shard_map/ppermute | solution.py:16
  78.5 3.8 %collective-permute-done.20 = bf16[128,768]{1,0:T(8,128)(2,1)S(1)} collective-permute-done((bf16[128,768]{1,0:T(8,128)(2,1)S(1)}, bf16[128,768]{1,0:T(8,128)(2,1)S(1)}, u32[]{:S(2)}, u32[]{:S(2)}) %collective-permute-start.20) | collective-permute-done | bytes 196640 | tf_op jit(solution)/shard_map/ppermute | solution.py:16
  82.6 1.6 %collective-permute-start.27 = (f32[2,16]{1,0:T(2,128)S(1)}, f32[2,16]{1,0:T(2,128)S(1)}, u32[]{:S(2)}, u32[]{:S(2)}) collective-permute-start(f32[2,16]{1,0:T(2,128)S(1)} %pad_maximum_fusion.9), channel_id=1, source_target_pairs={{0,16},{8,24},{16,0},{24,8},{1,17},{9,25},{17,1},{25,9},{2,18},{10... | collective-permute-start | bytes 392 | tf_op jit(solution)/shard_map/ppermute | solution.py:16
  84.1 2.1 %collective-permute-done.27 = f32[2,16]{1,0:T(2,128)S(1)} collective-permute-done((f32[2,16]{1,0:T(2,128)S(1)}, f32[2,16]{1,0:T(2,128)S(1)}, u32[]{:S(2)}, u32[]{:S(2)}) %collective-permute-start.27) | collective-permute-done | bytes 160 | tf_op jit(solution)/shard_map/ppermute | solution.py:16
  86.9 0.9 %pad_maximum_fusion.1 = f32[256,768]{1,0:T(8,128)} fusion(f32[128,768]{1,0:T(8,128)S(1)} %get-tuple-element.9, f32[128,768]{1,0:T(8,128)S(1)} %get-tuple-element.8), kind=kLoop, calls=%fused_computation.21 | loop fusion | flops 196608 | bytes 1572864 | tf_op jit(solution)/shard_map/concatenate | solution.py:105
  (126 shorter events, 16.2 us)
Async XLA Ops:
  0.6 43.9 %copy-start = (s32[128]{0:T(128)S(1)}, s32[128]{0:T(128)}, u32[]{:S(2)}) copy-start(s32[128]{0:T(128)} %param.9) | copy-start | bytes 1540
  0.6 16.8 %collective-permute-start.1 = (bf16[128,768]{1,0:T(8,128)(2,1)}, bf16[128,768]{1,0:T(8,128)(2,1)S(1)}, u32[]{:S(2)}, u32[]{:S(2)}) collective-permute-start(bf16[128,768]{1,0:T(8,128)(2,1)} %param.5), channel_id=1, source_target_pairs={{0,2},{1,3},{2,0},{3,1},{4,6},{5,7},{6,4},{7,5},{8,10},{9,11},{10,... | collective-permute-start | bytes 589832 | tf_op jit(solution)/shard_map/ppermute | solution.py:16
  3.7 15.1 %collective-permute-start = (bf16[128,768]{1,0:T(8,128)(2,1)}, bf16[128,768]{1,0:T(8,128)(2,1)S(1)}, u32[]{:S(2)}, u32[]{:S(2)}) collective-permute-start(bf16[128,768]{1,0:T(8,128)(2,1)} %param.5), channel_id=1, source_target_pairs={{0,1},{1,0},{2,3},{3,2},{4,5},{5,4},{6,7},{7,6},{8,9},{9,8},{10,11... | collective-permute-start | bytes 589832 | tf_op jit(solution)/shard_map/ppermute | solution.py:16
  5.2 11.5 %collective-permute-start.3 = (bf16[128,768]{1,0:T(8,128)(2,1)}, bf16[128,768]{1,0:T(8,128)(2,1)S(1)}, u32[]{:S(2)}, u32[]{:S(2)}) collective-permute-start(bf16[128,768]{1,0:T(8,128)(2,1)} %param.5), channel_id=1, source_target_pairs={{0,4},{1,5},{2,6},{3,7},{4,0},{5,1},{6,2},{7,3},{8,12},{9,13},{10,... | collective-permute-start | bytes 589832 | tf_op jit(solution)/shard_map/ppermute | solution.py:16
  7.8 40.9 %collective-permute-start.24 = (bf16[4,768]{1,0:T(4,128)(2,1)}, bf16[4,768]{1,0:T(4,128)(2,1)S(1)}, u32[]{:S(2)}, u32[]{:S(2)}) collective-permute-start(bf16[4,768]{1,0:T(4,128)(2,1)} %param.6), channel_id=1, source_target_pairs={{0,8},{8,0},{16,24},{24,16},{1,9},{9,1},{17,25},{25,17},{2,10},{10... | collective-permute-start | bytes 18440 | tf_op jit(solution)/shard_map/ppermute | solution.py:16
  7.8 1.4 %copy-start.3 = (bf16[128,768]{1,0:T(8,128)(2,1)S(1)}, bf16[128,768]{1,0:T(8,128)(2,1)}, u32[]{:S(2)}) copy-start(bf16[128,768]{1,0:T(8,128)(2,1)} %param.5) | copy-start | bytes 589828
  16.8 6.0 %collective-permute-start.5 = (bf16[128,768]{1,0:T(8,128)(2,1)S(1)}, bf16[128,768]{1,0:T(8,128)(2,1)S(1)}, u32[]{:S(2)}, u32[]{:S(2)}) collective-permute-start(bf16[128,768]{1,0:T(8,128)(2,1)S(1)} %collective-permute-done.3), channel_id=1, source_target_pairs={{0,2},{1,3},{2,0},{3,1},{4,6},{5,7},{6,4},{7,5},{8,10},{9,11},{10,... | collective-permute-start | bytes 589832 | tf_op jit(solution)/shard_map/ppermute | solution.py:16
  16.8 7.8 %collective-permute-start.4 = (bf16[128,768]{1,0:T(8,128)(2,1)S(1)}, bf16[128,768]{1,0:T(8,128)(2,1)S(1)}, u32[]{:S(2)}, u32[]{:S(2)}) collective-permute-start(bf16[128,768]{1,0:T(8,128)(2,1)S(1)} %collective-permute-done.3), channel_id=1, source_target_pairs={{0,1},{1,0},{2,3},{3,2},{4,5},{5,4},{6,7},{7,6},{8,9},{9,8},{10,11... | collective-permute-start | bytes 589832 | tf_op jit(solution)/shard_map/ppermute | solution.py:16
  17.4 9.5 %collective-permute-start.2 = (bf16[128,768]{1,0:T(8,128)(2,1)S(1)}, bf16[128,768]{1,0:T(8,128)(2,1)S(1)}, u32[]{:S(2)}, u32[]{:S(2)}) collective-permute-start(bf16[128,768]{1,0:T(8,128)(2,1)S(1)} %collective-permute-done.1), channel_id=1, source_target_pairs={{0,1},{1,0},{2,3},{3,2},{4,5},{5,4},{6,7},{7,6},{8,9},{9,8},{10,11... | collective-permute-start | bytes 589832 | tf_op jit(solution)/shard_map/ppermute | solution.py:16
  18.8 8.1 %copy-start.1 = (f32[256,768]{1,0:T(8,128)S(1)}, f32[256,768]{1,0:T(8,128)}, u32[]{:S(2)}) copy-start(f32[256,768]{1,0:T(8,128)} %param.7) | copy-start | bytes 2359300
  22.8 5.2 %collective-permute-start.6 = (bf16[64,768]{1,0:T(8,128)(2,1)S(1)}, bf16[64,768]{1,0:T(8,128)(2,1)S(1)}, u32[]{:S(2)}, u32[]{:S(2)}) collective-permute-start(bf16[64,768]{1,0:T(8,128)(2,1)S(1)} %slice.52), channel_id=1, source_target_pairs={{0,1},{1,0},{2,3},{3,2},{4,5},{5,4},{6,7},{7,6},{8,9},{9,8},{10,11... | collective-permute-start | bytes 294920 | tf_op jit(solution)/shard_map/ppermute | solution.py:16
  24.6 4.7 %collective-permute-start.7 = (bf16[64,768]{1,0:T(8,128)(2,1)S(1)}, bf16[64,768]{1,0:T(8,128)(2,1)S(1)}, u32[]{:S(2)}, u32[]{:S(2)}) collective-permute-start(bf16[64,768]{1,0:T(8,128)(2,1)S(1)} %slice.53), channel_id=1, source_target_pairs={{0,2},{1,3},{2,0},{3,1},{4,6},{5,7},{6,4},{7,5},{8,10},{9,11},{10,... | collective-permute-start | bytes 294920 | tf_op jit(solution)/shard_map/ppermute | solution.py:16
  29.9 3.7 %collective-permute-start.8 = (f32[2,2,2,128]{3,2,1,0:T(2,128)S(1)}, f32[2,2,2,128]{3,2,1,0:T(2,128)S(1)}, u32[]{:S(2)}, u32[]{:S(2)}) collective-permute-start(f32[2,2,2,128]{3,2,1,0:T(2,128)S(1)} %pad_maximum_fusion.6), channel_id=1, source_target_pairs={{0,1},{1,0},{2,3},{3,2},{4,5},{5,4},{6,7},{7,6},{8,9},{9,8},{10,11... | collective-permute-start | bytes 12296 | tf_op jit(solution)/shard_map/ppermute | solution.py:16
  33.6 3.7 %collective-permute-start.9 = (f32[2,2,2,128]{3,2,1,0:T(2,128)S(1)}, f32[2,2,2,128]{3,2,1,0:T(2,128)S(1)}, u32[]{:S(2)}, u32[]{:S(2)}) collective-permute-start(f32[2,2,2,128]{3,2,1,0:T(2,128)S(1)} %log_add_fusion.5), channel_id=1, source_target_pairs={{0,2},{1,3},{2,0},{3,1},{4,6},{5,7},{6,4},{7,5},{8,10},{9,11},{10,... | collective-permute-start | bytes 12296 | tf_op jit(solution)/shard_map/ppermute | solution.py:16
  37.3 4.6 %collective-permute-start.10 = (f32[2,2,2,128]{3,2,1,0:T(2,128)S(1)}, f32[2,2,2,128]{3,2,1,0:T(2,128)S(1)}, u32[]{:S(2)}, u32[]{:S(2)}) collective-permute-start(f32[2,2,2,128]{3,2,1,0:T(2,128)S(1)} %log_add_fusion.4), channel_id=1, source_target_pairs={{0,4},{1,5},{2,6},{3,7},{4,0},{5,1},{6,2},{7,3},{8,12},{9,13},{10,... | collective-permute-start | bytes 12296 | tf_op jit(solution)/shard_map/ppermute | solution.py:16
  43.6 3.4 %collective-permute-start.11 = (f32[128,768]{1,0:T(8,128)}, f32[128,768]{1,0:T(8,128)}, u32[]{:S(2)}, u32[]{:S(2)}) collective-permute-start(f32[128,768]{1,0:T(8,128)} %dynamic-slice_bitcast_fusion.1), channel_id=1, source_target_pairs={{0,8},{8,0},{16,24},{24,16},{1,9},{9,1},{17,25},{25,17},{2,10},{10... | collective-permute-start | bytes 1179656 | tf_op jit(solution)/shard_map/ppermute | solution.py:16
  43.9 1.4 %collective-permute-start.13 = (f32[256]{0:T(256)S(1)}, f32[256]{0:T(256)S(1)}, u32[]{:S(2)}, u32[]{:S(2)}) collective-permute-start(f32[256]{0:T(256)S(1)} %add.375), channel_id=1, source_target_pairs={{0,8},{8,0},{16,24},{24,16},{1,9},{9,1},{17,25},{25,17},{2,10},{10... | collective-permute-start | bytes 3080 | tf_op jit(solution)/shard_map/ppermute | solution.py:16
  45.3 3.3 %copy-start.4 = (bf16[4,768]{1,0:T(4,128)(2,1)S(1)}, bf16[4,768]{1,0:T(4,128)(2,1)}, u32[]{:S(2)}) copy-start(bf16[4,768]{1,0:T(4,128)(2,1)} %param.6) | copy-start | bytes 18436
  45.3 3.6 %collective-permute-start.14 = (f32[256]{0:T(256)S(1)}, f32[256]{0:T(256)S(1)}, u32[]{:S(2)}, u32[]{:S(2)}) collective-permute-start(f32[256]{0:T(256)S(1)} %add.376), channel_id=1, source_target_pairs={{0,16},{8,24},{16,0},{24,8},{1,17},{9,25},{17,1},{25,9},{2,18},{10... | collective-permute-start | bytes 3080 | tf_op jit(solution)/shard_map/ppermute | solution.py:16
  48.1 6.8 %collective-permute-start.12 = (bf16[128,768]{1,0:T(8,128)(2,1)S(1)}, bf16[128,768]{1,0:T(8,128)(2,1)S(1)}, u32[]{:S(2)}, u32[]{:S(2)}) collective-permute-start(bf16[128,768]{1,0:T(8,128)(2,1)S(1)} %fusion.21), channel_id=1, source_target_pairs={{0,16},{8,24},{16,0},{24,8},{1,17},{9,25},{17,1},{25,9},{2,18},{10... | collective-permute-start | bytes 589832 | tf_op jit(solution)/shard_map/ppermute | solution.py:16
  55.0 3.9 %collective-permute-start.15 = (f32[128,768]{1,0:T(8,128)S(1)}, f32[128,768]{1,0:T(8,128)S(1)}, u32[]{:S(2)}, u32[]{:S(2)}) collective-permute-start(f32[128,768]{1,0:T(8,128)S(1)} %add_divide_fusion), channel_id=1, source_target_pairs={{0,8},{8,0},{16,24},{24,16},{1,9},{9,1},{17,25},{25,17},{2,10},{10... | collective-permute-start | bytes 1179656 | tf_op jit(solution)/shard_map/ppermute | solution.py:16
  55.1 3.8 %collective-permute-start.25 = (bf16[8,768]{1,0:T(8,128)(2,1)S(1)}, bf16[8,768]{1,0:T(8,128)(2,1)S(1)}, u32[]{:S(2)}, u32[]{:S(2)}) collective-permute-start(bf16[8,768]{1,0:T(8,128)(2,1)S(1)} %pad_maximum_fusion.5), channel_id=1, source_target_pairs={{0,16},{8,24},{16,0},{24,8},{1,17},{9,25},{17,1},{25,9},{2,18},{10... | collective-permute-start | bytes 36872 | tf_op jit(solution)/shard_map/ppermute | solution.py:16
  60.2 3.7 %collective-permute-start.16 = (f32[2,2,2,128]{3,2,1,0:T(2,128)S(1)}, f32[2,2,2,128]{3,2,1,0:T(2,128)S(1)}, u32[]{:S(2)}, u32[]{:S(2)}) collective-permute-start(f32[2,2,2,128]{3,2,1,0:T(2,128)S(1)} %pad_maximum_fusion.7), channel_id=1, source_target_pairs={{0,1},{1,0},{2,3},{3,2},{4,5},{5,4},{6,7},{7,6},{8,9},{9,8},{10,11... | collective-permute-start | bytes 12296 | tf_op jit(solution)/shard_map/ppermute | solution.py:16
  63.9 3.7 %collective-permute-start.17 = (f32[2,2,2,128]{3,2,1,0:T(2,128)S(1)}, f32[2,2,2,128]{3,2,1,0:T(2,128)S(1)}, u32[]{:S(2)}, u32[]{:S(2)}) collective-permute-start(f32[2,2,2,128]{3,2,1,0:T(2,128)S(1)} %log_add_fusion.2), channel_id=1, source_target_pairs={{0,2},{1,3},{2,0},{3,1},{4,6},{5,7},{6,4},{7,5},{8,10},{9,11},{10,... | collective-permute-start | bytes 12296 | tf_op jit(solution)/shard_map/ppermute | solution.py:16
  67.6 4.6 %collective-permute-start.18 = (f32[2,2,2,128]{3,2,1,0:T(2,128)S(1)}, f32[2,2,2,128]{3,2,1,0:T(2,128)S(1)}, u32[]{:S(2)}, u32[]{:S(2)}) collective-permute-start(f32[2,2,2,128]{3,2,1,0:T(2,128)S(1)} %log_add_fusion.1), channel_id=1, source_target_pairs={{0,4},{1,5},{2,6},{3,7},{4,0},{5,1},{6,2},{7,3},{8,12},{9,13},{10,... | collective-permute-start | bytes 12296 | tf_op jit(solution)/shard_map/ppermute | solution.py:16
  73.0 2.3 %collective-permute-start.19 = (f32[128,768]{1,0:T(8,128)S(1)}, f32[128,768]{1,0:T(8,128)S(1)}, u32[]{:S(2)}, u32[]{:S(2)}) collective-permute-start(f32[128,768]{1,0:T(8,128)S(1)} %dynamic-slice_bitcast_fusion), channel_id=1, source_target_pairs={{0,8},{8,0},{16,24},{24,16},{1,9},{9,1},{17,25},{25,17},{2,10},{10... | collective-permute-start | bytes 1179656 | tf_op jit(solution)/shard_map/ppermute | solution.py:16
  73.4 1.4 %collective-permute-start.21 = (f32[256]{0:T(256)S(1)}, f32[256]{0:T(256)S(1)}, u32[]{:S(2)}, u32[]{:S(2)}) collective-permute-start(f32[256]{0:T(256)S(1)} %add.393), channel_id=1, source_target_pairs={{0,8},{8,0},{16,24},{24,16},{1,9},{9,1},{17,25},{25,17},{2,10},{10... | collective-permute-start | bytes 3080 | tf_op jit(solution)/shard_map/ppermute | solution.py:16
  74.8 3.6 %collective-permute-start.22 = (f32[256]{0:T(256)S(1)}, f32[256]{0:T(256)S(1)}, u32[]{:S(2)}, u32[]{:S(2)}) collective-permute-start(f32[256]{0:T(256)S(1)} %add.394), channel_id=1, source_target_pairs={{0,16},{8,24},{16,0},{24,8},{1,17},{9,25},{17,1},{25,9},{2,18},{10... | collective-permute-start | bytes 3080 | tf_op jit(solution)/shard_map/ppermute | solution.py:16
  75.4 6.9 %collective-permute-start.20 = (bf16[128,768]{1,0:T(8,128)(2,1)S(1)}, bf16[128,768]{1,0:T(8,128)(2,1)S(1)}, u32[]{:S(2)}, u32[]{:S(2)}) collective-permute-start(bf16[128,768]{1,0:T(8,128)(2,1)S(1)} %fusion.20), channel_id=1, source_target_pairs={{0,16},{8,24},{16,0},{24,8},{1,17},{9,25},{17,1},{25,9},{2,18},{10... | collective-permute-start | bytes 589832 | tf_op jit(solution)/shard_map/ppermute | solution.py:16
  77.0 5.5 %collective-permute-start.26 = (f32[2,16]{1,0:T(2,128)S(1)}, f32[2,16]{1,0:T(2,128)S(1)}, u32[]{:S(2)}, u32[]{:S(2)}) collective-permute-start(f32[2,16]{1,0:T(2,128)S(1)} %pad_maximum_fusion.8), channel_id=1, source_target_pairs={{0,8},{8,0},{16,24},{24,16},{1,9},{9,1},{17,25},{25,17},{2,10},{10... | collective-permute-start | bytes 392 | tf_op jit(solution)/shard_map/ppermute | solution.py:16
  82.4 4.4 %collective-permute-start.23 = (f32[128,768]{1,0:T(8,128)S(1)}, f32[128,768]{1,0:T(8,128)S(1)}, u32[]{:S(2)}, u32[]{:S(2)}) collective-permute-start(f32[128,768]{1,0:T(8,128)S(1)} %fusion.19), channel_id=1, source_target_pairs={{0,8},{8,0},{16,24},{24,16},{1,9},{9,1},{17,25},{25,17},{2,10},{10... | collective-permute-start | bytes 1179656 | tf_op jit(solution)/shard_map/ppermute | solution.py:16
  82.6 3.6 %collective-permute-start.27 = (f32[2,16]{1,0:T(2,128)S(1)}, f32[2,16]{1,0:T(2,128)S(1)}, u32[]{:S(2)}, u32[]{:S(2)}) collective-permute-start(f32[2,16]{1,0:T(2,128)S(1)} %pad_maximum_fusion.9), channel_id=1, source_target_pairs={{0,16},{8,24},{16,0},{24,8},{1,17},{9,25},{17,1},{25,9},{2,18},{10... | collective-permute-start | bytes 392 | tf_op jit(solution)/shard_map/ppermute | solution.py:16
  (2 other events, 1.8 us)

commit v3 on v2

v3 whole, which is shorter than its diff:
```python
import jax
import jax.numpy as jnp
from jax import lax
from jax.sharding import PartitionSpec as P

BLOCK = 128
ITERS = 2
SHARPNESS = 0.05
SCALE = 0.05
PRIOR = 1.0
FAR = -1e30


def swap(value, axis, bit):
    size = lax.axis_size(axis)
    return lax.ppermute(value, axis, [(i, i ^ bit) for i in range(size)])


def bits_of(size):
    return [1 << k for k in range(size.bit_length() - 1)]


def in_order(mine, other, flag):
    return jnp.concatenate([jnp.where(flag == 0, mine, other), jnp.where(flag == 0, other, mine)])


def gathered_pieces(value, later, axis, size):
    far = size // 2
    half = value.shape[0] // 2
    pieces = {0: later}
    for mask in sorted(range(1, size), key=lambda m: (bin(m).count("1"), -m)):
        low = mask & -mask
        rest = mask ^ low
        if rest & (rest - 1):
            second = rest & -rest
            pieces[mask] = jnp.concatenate(
                [swap(pieces[rest][:half], axis, low), swap(pieces[mask ^ second][half:], axis, second)]
            )
        else:
            pieces[mask] = swap(value if mask == far else pieces[rest], axis, low)
    return pieces


def in_three(value):
    parts = []
    for _ in range(3):
        top = lax.reduce_precision(value, 8, 7)
        parts.append(top.astype(jnp.bfloat16))
        value = value - top
    return parts


def join_lse(first, second):
    top = jnp.maximum(first, second)
    return top + jnp.log(1.0 + jnp.exp(jnp.minimum(first, second) - top))


def on_device(passages, queries, init_centroids, pattern, positive_offset):
    n_dp, n_cent = lax.axis_size("dp"), lax.axis_size("cent")
    dp, cent = lax.axis_index("dp"), lax.axis_index("cent")
    dp_bits, cent_bits = bits_of(n_dp), bits_of(n_cent)
    core = dp & 1
    rows, width = passages.shape
    own_queries = queries.shape[0]
    half = n_cent // 2

    asked = swap(queries, "dp", dp_bits[0])
    asked, later = lax.optimization_barrier((asked, passages))

    pieces = gathered_pieces(passages, later, "cent", n_cent)
    pieces[1], means = lax.optimization_barrier((pieces[1], init_centroids))
    near = jnp.concatenate([pieces[mask] for mask in range(half)])
    far = jnp.concatenate([pieces[mask] for mask in range(half, n_cent)])
    held = [near, far]

    def loss_partials(asked, pattern, positive_offset, dp, cent):
        mine = (n_dp, n_cent, own_queries)
        picks = lax.dynamic_index_in_dim(pattern.reshape(mine + (-1,)), cent, 1, keepdims=False)
        picks = picks.reshape(n_dp * own_queries, -1)
        offset = lax.dynamic_index_in_dim(positive_offset.reshape(mine), cent, 1, keepdims=False).reshape(-1)
        target = picks[:, 0] * BLOCK + offset
        partials, positive = [], 0.0
        for index, group in enumerate(held):
            masks = jnp.arange(index * half, (index + 1) * half, dtype=jnp.int32)
            owner = (dp * n_cent + (cent ^ masks)) * rows
            column = (owner[:, None] + jnp.arange(rows, dtype=jnp.int32)[None, :]).reshape(-1)
            scores = SCALE * lax.dot_general(
                asked, group, (((1,), (1,)), ((), ())), preferred_element_type=jnp.float32
            )
            allowed = jnp.any(picks[:, :, None] == (column // BLOCK)[None, None, :], axis=1)
            top = jnp.max(jnp.where(allowed, scores, FAR), axis=1)
            total = jnp.sum(jnp.where(allowed, jnp.exp(scores - top[:, None]), 0.0), axis=1)
            partials.append(jnp.where(total > 0.0, top + jnp.log(jnp.maximum(total, 1e-37)), FAR))
            positive = positive + jnp.sum(jnp.where(column[None, :] == target[:, None], scores, 0.0), axis=1)
        return positive, join_lse(*partials)

    centers = means.shape[0]
    kept = centers // 2
    first = core == 0
    asks = n_dp * own_queries
    for step in range(ITERS):
        last = step == ITERS - 1
        centers_half = means.astype(jnp.bfloat16)
        norms = jnp.sum(means * means, axis=1)
        odds, stats = [], []
        for group in held:
            logits = SHARPNESS * (
                2.0
                * lax.dot_general(
                    centers_half, group, (((1,), (1,)), ((), ())), preferred_element_type=jnp.float32
                )
                - norms[:, None]
            )
            top = jnp.max(logits, axis=0)
            odds.append(logits)
            stats.append(top + jnp.log(jnp.sum(jnp.exp(logits - top[None, :]), axis=0)))
        lse = jnp.concatenate(stats).reshape((2,) * len(cent_bits) + (rows,))
        for bit in cent_bits:
            position = len(cent_bits) - 1 - cent_bits.index(bit)
            lse = join_lse(lse, jnp.flip(swap(lse, "cent", bit), axis=position))
            if last and bit == cent_bits[0]:
                inputs = (lse, asked, pattern, positive_offset, dp, cent)
                lse, *inputs = lax.optimization_barrier(inputs)
                positive, found = loss_partials(*inputs)
        lse = lse.reshape(2, half * rows)
        resps, counts = [], 0.0
        for index in range(2):
            resp = jnp.exp(odds[index] - lse[index][None, :])
            counts = counts + jnp.sum(resp, axis=1)
            resps.append(resp.astype(jnp.bfloat16))

        if step == 0:
            asked = in_order(queries, asked, core)
        line = jnp.where(first, counts[:kept], counts[kept:])
        rest = jnp.where(first, counts[kept:], counts[:kept])
        if last:
            line = jnp.concatenate([line, positive, found])
            rest = jnp.concatenate([rest, positive, found])

        def join_lines(line, other):
            cut = kept + asks
            if not last:
                return line + other
            return jnp.concatenate([line[:cut] + other[:cut], join_lse(line[cut:], other[cut:])])

        cut = width // 2
        totals = []
        for part in range(2):
            numer = 0.0
            for index in range(2):
                numer = numer + jnp.dot(
                    resps[index], held[index][:, part * cut : (part + 1) * cut], preferred_element_type=jnp.float32
                )
            if part == 0:
                numer, resps = lax.optimization_barrier((numer, resps))
            total = jnp.where(first, numer[:kept], numer[kept:])
            sent = jnp.where(first, numer[kept:], numer[:kept])
            if part == 0:
                sent = jnp.concatenate([sent, jnp.pad(rest[None, :], ((0, 7), (0, cut - rest.shape[0])))])
            other = swap(sent, "dp", dp_bits[0])
            totals.append(total + other[:kept])
            if part == 0:
                line = join_lines(line, other[kept, : line.shape[0]])
        for bit in dp_bits[1:]:
            for part in range(2):
                sent = totals[part].astype(jnp.bfloat16)
                packed = sent
                if part == 0:
                    parts = [jnp.pad(p[None, :], ((0, 0), (0, cut - p.shape[0]))) for p in in_three(line)]
                    packed = jnp.concatenate([packed] + parts)
                    if step == 0:
                        packed = jnp.concatenate([packed, asked[:, :cut], asked[:, cut:]])
                    packed = jnp.pad(packed, ((0, -packed.shape[0] % 8), (0, 0)))
                other = swap(packed, "dp", bit)
                totals[part] = sent.astype(jnp.float32) + other[:kept].astype(jnp.float32)
                if part == 0:
                    three = other[kept : kept + 3, : line.shape[0]].astype(jnp.float32)
                    line = join_lines(line, (three[0] + three[1]) + three[2])
                    if step == 0:
                        more = other[kept + 3 : kept + 3 + 2 * asked.shape[0]]
                        more = jnp.concatenate([more[: asked.shape[0]], more[asked.shape[0] :]], axis=1)
                        asked = in_order(asked, more, dp & bit)
        if last:
            whole = line[kept + asks :] - line[kept : kept + asks]
            loss = lax.dynamic_slice_in_dim(whole, dp * own_queries, own_queries, 0)
        prior = jnp.where(first, means[:kept], means[kept:])
        fresh = []
        for part in range(2):
            mine = (totals[part] + PRIOR * prior[:, part * cut : (part + 1) * cut]) / (line[:kept, None] + PRIOR)
            fresh.append(in_order(mine, swap(mine, "dp", dp_bits[0]), core))
        means = jnp.concatenate(fresh, axis=1)
    return means, loss


def solution(mesh):
    placed = (P(("dp", "cent"), None), P(("dp", "cent"), None), P("cent", None), P(), P())
    return jax.shard_map(
        on_device,
        mesh=mesh,
        in_specs=placed,
        out_specs=(P("cent", None), P(("dp", "cent"))),
        check_vma=False,
    )
```

time: 88 us -> 79.9 us (0.908)
  waiting for transfers between devices: 45.1 us -> 33.8 us
  starting transfers between devices: 27.4 us -> 31.8 us
  other arithmetic: 6.15 us -> 4.96 us
    ppermute x28 -> x27, waiting for transfers between devices: 45.1 us -> 33.8 us  [swap(): return lax.ppermute(value, axis, [(i, i ^ bit) for i in range(size)])]
    ppermute x28 -> x27, starting transfers between devices: 27.4 us -> 31.8 us  [swap(): return lax.ppermute(value, axis, [(i, i ^ bit) for i in range(size)])]
    gather x4 -> x0, local copies, waits for them, and re-layouts: 1.38 us -> none  [the longest x2 0.74 us: on_device(): target = picks[:, 0] * BLOCK + positive_offset[ids]]
    reduce_sum x2, other arithmetic: 1.43 us -> 0.28 us  [on_device(): norms = jnp.sum(means * means, axis=1)]
    convert_element_type x2 -> x8, other arithmetic: 1.19 us -> 0.23 us  [the longest x4 0.14 us: on_device(): sent = totals[part].astype(jnp.bfloat16)]
    select_n x7 -> x15, other arithmetic: 0.34 us -> 1.23 us  [the longest x2 0.83 us: on_device(): prior = jnp.where(first, means[:kept], means[kept:])]
    dot_general x10 -> x14, matrix products: 4.07 us -> 4.87 us  [the longest x8 2.33 us: on_device(): jnp.dot(resps[index], held[index][:, part * cut:(part + 1) * cut], prefer...]
  transfers between devices with their start and end apart: 28 -> 27, of which waited for: 19 -> 23; matrix products, arithmetic and copies ran while one was open for 12% -> 8% of each run, Pallas kernels for 0% -> 0%
where the time goes in v3:
time: 79.9 us; the launch traced here: 79.7 us
  waiting for transfers between devices  33.8 us (42%)
  starting transfers between devices  31.8 us (40%)
  other arithmetic  4.96 us (6%)
  matrix products  4.87 us (6%)
  local copies, waits for them, and re-layouts  3.2 us (4%)
  between operations  1.16 us (1%)
    ppermute x27, waiting for transfers between devices, swap(): return lax.ppermute(value, axis, [(i, i ^ bit) for i in range(size)])  33.8 us
    ppermute x27, starting transfers between devices, swap(): return lax.ppermute(value, axis, [(i, i ^ bit) for i in range(size)])  31.8 us
    dot_general x8, matrix products, on_device(): jnp.dot(resps[index], held[index][:, part * cut:(part + 1) * cut], prefer...  2.33 us
    unnamed x17, local copies, waits for them, and re-layouts  1.72 us
    dot_general x4, matrix products, on_device(): lax.dot_general(centers_half, group, (((1,), (1,)), ((), ())), preferred_...  1.69 us
  transfers between devices with their start and end apart: 27, of which 23 were waited for; matrix products, arithmetic and copies ran while one was open for 8% of the time, Pallas kernels for 0%

profile of v3, /device:TPU:0, one launch (start us, length us, event | category | flops | bytes accessed | tf_op | source)
XLA Modules:
  0.0 79.7 jit_solution(1200635825726134597)
XLA Ops:
  0.6 4.1 %collective-permute-start.4 = (bf16[128,768]{1,0:T(8,128)(2,1)}, bf16[128,768]{1,0:T(8,128)(2,1)S(1)}, u32[]{:S(2)}, u32[]{:S(2)}) collective-permute-start(bf16[128,768]{1,0:T(8,128)(2,1)} %param.5), channel_id=1, source_target_pairs={{0,4},{1,5},{2,6},{3,7},{4,0},{5,1},{6,2},{7,3},{8,12},{9,13},{10,... | collective-permute-start | bytes 589832 | tf_op jit(solution)/shard_map/ppermute | solution.py:16
  4.7 1.4 %collective-permute-done = bf16[4,768]{1,0:T(4,128)(2,1)S(1)} collective-permute-done((bf16[4,768]{1,0:T(4,128)(2,1)}, bf16[4,768]{1,0:T(4,128)(2,1)S(1)}, u32[]{:S(2)}, u32[]{:S(2)}) %collective-permute-start) | collective-permute-done | bytes 6176 | tf_op jit(solution)/shard_map/ppermute | solution.py:16
  6.1 1.6 %collective-permute-start.2 = (bf16[128,768]{1,0:T(8,128)(2,1)}, bf16[128,768]{1,0:T(8,128)(2,1)S(1)}, u32[]{:S(2)}, u32[]{:S(2)}) collective-permute-start(bf16[128,768]{1,0:T(8,128)(2,1)} %param.5), channel_id=1, source_target_pairs={{0,2},{1,3},{2,0},{3,1},{4,6},{5,7},{6,4},{7,5},{8,10},{9,11},{10,... | collective-permute-start | bytes 589832 | tf_op jit(solution)/shard_map/ppermute | solution.py:16
  7.7 1.5 %collective-permute-start.1 = (bf16[128,768]{1,0:T(8,128)(2,1)}, bf16[128,768]{1,0:T(8,128)(2,1)S(1)}, u32[]{:S(2)}, u32[]{:S(2)}) collective-permute-start(bf16[128,768]{1,0:T(8,128)(2,1)} %param.5), channel_id=1, source_target_pairs={{0,1},{1,0},{2,3},{3,2},{4,5},{5,4},{6,7},{7,6},{8,9},{9,8},{10,11... | collective-permute-start | bytes 589832 | tf_op jit(solution)/shard_map/ppermute | solution.py:16
  9.2 1.0 %constant_dynamic-update-slice_fusion.3 = bf16[512,768]{1,0:T(8,128)(2,1)S(1)} fusion(bf16[128,768]{1,0:T(8,128)(2,1)} %param.5), kind=kLoop, calls=%fused_computation.110 | loop fusion | bytes 393216
  10.2 4.0 %collective-permute-done.4 = bf16[128,768]{1,0:T(8,128)(2,1)S(1)} collective-permute-done((bf16[128,768]{1,0:T(8,128)(2,1)}, bf16[128,768]{1,0:T(8,128)(2,1)S(1)}, u32[]{:S(2)}, u32[]{:S(2)}) %collective-permute-start.4) | collective-permute-done | bytes 196640 | tf_op jit(solution)/shard_map/ppermute | solution.py:16
  14.2 0.8 collective-permute-start.6
  14.9 1.5 %collective-permute-start.5 = (bf16[128,768]{1,0:T(8,128)(2,1)S(1)}, bf16[128,768]{1,0:T(8,128)(2,1)S(1)}, u32[]{:S(2)}, u32[]{:S(2)}) collective-permute-start(bf16[128,768]{1,0:T(8,128)(2,1)S(1)} %collective-permute-done.4), channel_id=1, source_target_pairs={{0,1},{1,0},{2,3},{3,2},{4,5},{5,4},{6,7},{7,6},{8,9},{9,8},{10,11... | collective-permute-start | bytes 589832 | tf_op jit(solution)/shard_map/ppermute | solution.py:16
  16.6 1.8 %collective-permute-start.3 = (bf16[128,768]{1,0:T(8,128)(2,1)S(1)}, bf16[128,768]{1,0:T(8,128)(2,1)S(1)}, u32[]{:S(2)}, u32[]{:S(2)}) collective-permute-start(bf16[128,768]{1,0:T(8,128)(2,1)S(1)} %collective-permute-done.2), channel_id=1, source_target_pairs={{0,1},{1,0},{2,3},{3,2},{4,5},{5,4},{6,7},{7,6},{8,9},{9,8},{10,11... | collective-permute-start | bytes 589832 | tf_op jit(solution)/shard_map/ppermute | solution.py:16
  18.6 2.0 %collective-permute-done.6 = bf16[128,768]{1,0:T(8,128)(2,1)S(1)} collective-permute-done((bf16[128,768]{1,0:T(8,128)(2,1)S(1)}, bf16[128,768]{1,0:T(8,128)(2,1)S(1)}, u32[]{:S(2)}, u32[]{:S(2)}) %collective-permute-start.6) | collective-permute-done | bytes 196640 | tf_op jit(solution)/shard_map/ppermute | solution.py:16
  20.6 1.6 %collective-permute-start.7 = (bf16[64,768]{1,0:T(8,128)(2,1)S(1)}, bf16[64,768]{1,0:T(8,128)(2,1)S(1)}, u32[]{:S(2)}, u32[]{:S(2)}) collective-permute-start(bf16[64,768]{1,0:T(8,128)(2,1)S(1)} %slice.259), channel_id=1, source_target_pairs={{0,1},{1,0},{2,3},{3,2},{4,5},{5,4},{6,7},{7,6},{8,9},{9,8},{10,11... | collective-permute-start | bytes 294920 | tf_op jit(solution)/shard_map/ppermute | solution.py:16
  22.7 1.4 %collective-permute-start.8 = (bf16[64,768]{1,0:T(8,128)(2,1)S(1)}, bf16[64,768]{1,0:T(8,128)(2,1)S(1)}, u32[]{:S(2)}, u32[]{:S(2)}) collective-permute-start(bf16[64,768]{1,0:T(8,128)(2,1)S(1)} %slice.260), channel_id=1, source_target_pairs={{0,2},{1,3},{2,0},{3,1},{4,6},{5,7},{6,4},{7,5},{8,10},{9,11},{10,... | collective-permute-start | bytes 294920 | tf_op jit(solution)/shard_map/ppermute | solution.py:16
  24.1 2.6 %collective-permute-done.3 = bf16[128,768]{1,0:T(8,128)(2,1)S(1)} collective-permute-done((bf16[128,768]{1,0:T(8,128)(2,1)S(1)}, bf16[128,768]{1,0:T(8,128)(2,1)S(1)}, u32[]{:S(2)}, u32[]{:S(2)}) %collective-permute-start.3) | collective-permute-done | bytes 196640 | tf_op jit(solution)/shard_map/ppermute | solution.py:16
  28.4 1.6 %collective-permute-start.9 = (f32[2,2,2,128]{3,2,1,0:T(2,128)S(1)}, f32[2,2,2,128]{3,2,1,0:T(2,128)S(1)}, u32[]{:S(2)}, u32[]{:S(2)}) collective-permute-start(f32[2,2,2,128]{3,2,1,0:T(2,128)S(1)} %pad_maximum_fusion.3), channel_id=1, source_target_pairs={{0,1},{1,0},{2,3},{3,2},{4,5},{5,4},{6,7},{7,6},{8,9},{9,8},{10,11... | collective-permute-start | bytes 12296 | tf_op jit(solution)/shard_map/ppermute | solution.py:16
  30.0 2.1 %collective-permute-done.9 = f32[2,2,2,128]{3,2,1,0:T(2,128)S(1)} collective-permute-done((f32[2,2,2,128]{3,2,1,0:T(2,128)S(1)}, f32[2,2,2,128]{3,2,1,0:T(2,128)S(1)}, u32[]{:S(2)}, u32[]{:S(2)}) %collective-permute-start.9) | collective-permute-done | bytes 4128 | tf_op jit(solution)/shard_map/ppermute | solution.py:16
  32.1 1.0 %collective-permute-start.10 = (f32[2,2,2,128]{3,2,1,0:T(2,128)S(1)}, f32[2,2,2,128]{3,2,1,0:T(2,128)S(1)}, u32[]{:S(2)}, u32[]{:S(2)}) collective-permute-start(f32[2,2,2,128]{3,2,1,0:T(2,128)S(1)} %log_add_fusion.5), channel_id=1, source_target_pairs={{0,2},{1,3},{2,0},{3,1},{4,6},{5,7},{6,4},{7,5},{8,10},{9,11},{10,... | collective-permute-start | bytes 12296 | tf_op jit(solution)/shard_map/ppermute | solution.py:16
  33.1 2.7 %collective-permute-done.10 = f32[2,2,2,128]{3,2,1,0:T(2,128)S(1)} collective-permute-done((f32[2,2,2,128]{3,2,1,0:T(2,128)S(1)}, f32[2,2,2,128]{3,2,1,0:T(2,128)S(1)}, u32[]{:S(2)}, u32[]{:S(2)}) %collective-permute-start.10) | collective-permute-done | bytes 4128 | tf_op jit(solution)/shard_map/ppermute | solution.py:16
  35.8 3.3 %collective-permute-start.11 = (f32[2,2,2,128]{3,2,1,0:T(2,128)S(1)}, f32[2,2,2,128]{3,2,1,0:T(2,128)S(1)}, u32[]{:S(2)}, u32[]{:S(2)}) collective-permute-start(f32[2,2,2,128]{3,2,1,0:T(2,128)S(1)} %log_add_fusion.4), channel_id=1, source_target_pairs={{0,4},{1,5},{2,6},{3,7},{4,0},{5,1},{6,2},{7,3},{8,12},{9,13},{10,... | collective-permute-start | bytes 12296 | tf_op jit(solution)/shard_map/ppermute | solution.py:16
  39.2 0.8 slice_select_fusion.1
  40.0 0.8 %collective-permute-done.11 = f32[2,2,2,128]{3,2,1,0:T(2,128)S(1)} collective-permute-done((f32[2,2,2,128]{3,2,1,0:T(2,128)S(1)}, f32[2,2,2,128]{3,2,1,0:T(2,128)S(1)}, u32[]{:S(2)}, u32[]{:S(2)}) %collective-permute-start.11) | collective-permute-done | bytes 4128 | tf_op jit(solution)/shard_map/ppermute | solution.py:16
  43.7 1.6 %collective-permute-start.13 = (bf16[152,384]{1,0:T(8,128)(2,1)S(1)}, bf16[152,384]{1,0:T(8,128)(2,1)S(1)}, u32[]{:S(2)}, u32[]{:S(2)}) collective-permute-start(bf16[152,384]{1,0:T(8,128)(2,1)S(1)} %pad.40), channel_id=1, source_target_pairs={{0,16},{8,24},{16,0},{24,8},{1,17},{9,25},{17,1},{25,9},{2,18},{10... | collective-permute-start | bytes 350216 | tf_op jit(solution)/shard_map/ppermute | solution.py:16
  45.9 3.9 %collective-permute-done.13 = bf16[152,384]{1,0:T(8,128)(2,1)S(1)} collective-permute-done((bf16[152,384]{1,0:T(8,128)(2,1)S(1)}, bf16[152,384]{1,0:T(8,128)(2,1)S(1)}, u32[]{:S(2)}, u32[]{:S(2)}) %collective-permute-start.13) | collective-permute-done | bytes 116768 | tf_op jit(solution)/shard_map/ppermute | solution.py:16
  49.8 1.3 %collective-permute-done.16 = bf16[128,384]{1,0:T(8,128)(2,1)S(1)} collective-permute-done((bf16[128,384]{1,0:T(8,128)(2,1)S(1)}, bf16[128,384]{1,0:T(8,128)(2,1)S(1)}, u32[]{:S(2)}, u32[]{:S(2)}) %collective-permute-start.16) | collective-permute-done | bytes 98336 | tf_op jit(solution)/shard_map/ppermute | solution.py:16
  51.8 0.9 %collective-permute-done.14 = f32[128,384]{1,0:T(8,128)S(1)} collective-permute-done((f32[128,384]{1,0:T(8,128)S(1)}, f32[128,384]{1,0:T(8,128)S(1)}, u32[]{:S(2)}, u32[]{:S(2)}) %collective-permute-start.14) | collective-permute-done | bytes 196640 | tf_op jit(solution)/shard_map/ppermute | solution.py:16
  54.3 1.5 %collective-permute-start.18 = (f32[2,2,2,128]{3,2,1,0:T(2,128)S(1)}, f32[2,2,2,128]{3,2,1,0:T(2,128)S(1)}, u32[]{:S(2)}, u32[]{:S(2)}) collective-permute-start(f32[2,2,2,128]{3,2,1,0:T(2,128)S(1)} %pad_maximum_fusion.4), channel_id=1, source_target_pairs={{0,1},{1,0},{2,3},{3,2},{4,5},{5,4},{6,7},{7,6},{8,9},{9,8},{10,11... | collective-permute-start | bytes 12296 | tf_op jit(solution)/shard_map/ppermute | solution.py:16
  55.9 2.1 %collective-permute-done.18 = f32[2,2,2,128]{3,2,1,0:T(2,128)S(1)} collective-permute-done((f32[2,2,2,128]{3,2,1,0:T(2,128)S(1)}, f32[2,2,2,128]{3,2,1,0:T(2,128)S(1)}, u32[]{:S(2)}, u32[]{:S(2)}) %collective-permute-start.18) | collective-permute-done | bytes 4128 | tf_op jit(solution)/shard_map/ppermute | solution.py:16
  62.0 3.0 %collective-permute-start.20 = (f32[2,2,2,128]{3,2,1,0:T(2,128)S(1)}, f32[2,2,2,128]{3,2,1,0:T(2,128)S(1)}, u32[]{:S(2)}, u32[]{:S(2)}) collective-permute-start(f32[2,2,2,128]{3,2,1,0:T(2,128)S(1)} %log_add_fusion.1), channel_id=1, source_target_pairs={{0,4},{1,5},{2,6},{3,7},{4,0},{5,1},{6,2},{7,3},{8,12},{9,13},{10,... | collective-permute-start | bytes 12296 | tf_op jit(solution)/shard_map/ppermute | solution.py:16
  64.9 1.6 %collective-permute-done.20 = f32[2,2,2,128]{3,2,1,0:T(2,128)S(1)} collective-permute-done((f32[2,2,2,128]{3,2,1,0:T(2,128)S(1)}, f32[2,2,2,128]{3,2,1,0:T(2,128)S(1)}, u32[]{:S(2)}, u32[]{:S(2)}) %collective-permute-start.20) | collective-permute-done | bytes 4128 | tf_op jit(solution)/shard_map/ppermute | solution.py:16
  69.7 1.6 %collective-permute-start.22 = (bf16[136,384]{1,0:T(8,128)(2,1)S(1)}, bf16[136,384]{1,0:T(8,128)(2,1)S(1)}, u32[]{:S(2)}, u32[]{:S(2)}) collective-permute-start(bf16[136,384]{1,0:T(8,128)(2,1)S(1)} %pad.45), channel_id=1, source_target_pairs={{0,16},{8,24},{16,0},{24,8},{1,17},{9,25},{17,1},{25,9},{2,18},{10... | collective-permute-start | bytes 313352 | tf_op jit(solution)/shard_map/ppermute | solution.py:16
  71.9 3.6 %collective-permute-done.22 = bf16[136,384]{1,0:T(8,128)(2,1)S(1)} collective-permute-done((bf16[136,384]{1,0:T(8,128)(2,1)S(1)}, bf16[136,384]{1,0:T(8,128)(2,1)S(1)}, u32[]{:S(2)}, u32[]{:S(2)}) %collective-permute-start.22) | collective-permute-done | bytes 104480 | tf_op jit(solution)/shard_map/ppermute | solution.py:16
  75.6 1.3 %collective-permute-done.25 = bf16[128,384]{1,0:T(8,128)(2,1)S(1)} collective-permute-done((bf16[128,384]{1,0:T(8,128)(2,1)S(1)}, bf16[128,384]{1,0:T(8,128)(2,1)S(1)}, u32[]{:S(2)}, u32[]{:S(2)}) %collective-permute-start.25) | collective-permute-done | bytes 98336 | tf_op jit(solution)/shard_map/ppermute | solution.py:16
  78.8 0.9 %maximum_maximum_fusion.1 = f32[256,768]{1,0:T(8,128)} fusion(f32[128,384]{1,0:T(8,128)S(1)} %get-tuple-element.63, f32[128,384]{1,0:T(8,128)S(1)} %get-tuple-element.62, f32[128,384]{1,0:T(8,128)S(1)} %get-tuple-element.61, f32[128,384]{1,0:T(8,128)S(1)} %get-tuple-element.60), kind=kLoop, calls=%fused_computation.19 | loop fusion | flops 589824 | bytes 1572864 | tf_op jit(solution)/shard_map/concatenate | solution.py:191
  (149 shorter events, 18.0 us)
Async XLA Ops:
  0.6 13.5 %collective-permute-start.4 = (bf16[128,768]{1,0:T(8,128)(2,1)}, bf16[128,768]{1,0:T(8,128)(2,1)S(1)}, u32[]{:S(2)}, u32[]{:S(2)}) collective-permute-start(bf16[128,768]{1,0:T(8,128)(2,1)} %param.5), channel_id=1, source_target_pairs={{0,4},{1,5},{2,6},{3,7},{4,0},{5,1},{6,2},{7,3},{8,12},{9,13},{10,... | collective-permute-start | bytes 589832 | tf_op jit(solution)/shard_map/ppermute | solution.py:16
  4.7 1.4 %collective-permute-start = (bf16[4,768]{1,0:T(4,128)(2,1)}, bf16[4,768]{1,0:T(4,128)(2,1)S(1)}, u32[]{:S(2)}, u32[]{:S(2)}) collective-permute-start(bf16[4,768]{1,0:T(4,128)(2,1)} %param.6), channel_id=1, source_target_pairs={{0,8},{8,0},{16,24},{24,16},{1,9},{9,1},{17,25},{25,17},{2,10},{10... | collective-permute-start | bytes 18440 | tf_op jit(solution)/shard_map/ppermute | solution.py:16
  4.7 13.7 %copy-start = (f32[256,768]{1,0:T(8,128)S(1)}, f32[256,768]{1,0:T(8,128)}, u32[]{:S(2)}) copy-start(f32[256,768]{1,0:T(8,128)} %param.7) | copy-start | bytes 2359300
  6.1 10.5 %collective-permute-start.2 = (bf16[128,768]{1,0:T(8,128)(2,1)}, bf16[128,768]{1,0:T(8,128)(2,1)S(1)}, u32[]{:S(2)}, u32[]{:S(2)}) collective-permute-start(bf16[128,768]{1,0:T(8,128)(2,1)} %param.5), channel_id=1, source_target_pairs={{0,2},{1,3},{2,0},{3,1},{4,6},{5,7},{6,4},{7,5},{8,10},{9,11},{10,... | collective-permute-start | bytes 589832 | tf_op jit(solution)/shard_map/ppermute | solution.py:16
  7.7 8.8 %collective-permute-start.1 = (bf16[128,768]{1,0:T(8,128)(2,1)}, bf16[128,768]{1,0:T(8,128)(2,1)S(1)}, u32[]{:S(2)}, u32[]{:S(2)}) collective-permute-start(bf16[128,768]{1,0:T(8,128)(2,1)} %param.5), channel_id=1, source_target_pairs={{0,1},{1,0},{2,3},{3,2},{4,5},{5,4},{6,7},{7,6},{8,9},{9,8},{10,11... | collective-permute-start | bytes 589832 | tf_op jit(solution)/shard_map/ppermute | solution.py:16
  14.2 6.4 %collective-permute-start.6 = (bf16[128,768]{1,0:T(8,128)(2,1)S(1)}, bf16[128,768]{1,0:T(8,128)(2,1)S(1)}, u32[]{:S(2)}, u32[]{:S(2)}) collective-permute-start(bf16[128,768]{1,0:T(8,128)(2,1)S(1)} %collective-permute-done.4), channel_id=1, source_target_pairs={{0,2},{1,3},{2,0},{3,1},{4,6},{5,7},{6,4},{7,5},{8,10},{9,11},{10,... | collective-permute-start | bytes 589832 | tf_op jit(solution)/shard_map/ppermute | solution.py:16
  14.9 7.8 %collective-permute-start.5 = (bf16[128,768]{1,0:T(8,128)(2,1)S(1)}, bf16[128,768]{1,0:T(8,128)(2,1)S(1)}, u32[]{:S(2)}, u32[]{:S(2)}) collective-permute-start(bf16[128,768]{1,0:T(8,128)(2,1)S(1)} %collective-permute-done.4), channel_id=1, source_target_pairs={{0,1},{1,0},{2,3},{3,2},{4,5},{5,4},{6,7},{7,6},{8,9},{9,8},{10,11... | collective-permute-start | bytes 589832 | tf_op jit(solution)/shard_map/ppermute | solution.py:16
  16.6 10.1 %collective-permute-start.3 = (bf16[128,768]{1,0:T(8,128)(2,1)S(1)}, bf16[128,768]{1,0:T(8,128)(2,1)S(1)}, u32[]{:S(2)}, u32[]{:S(2)}) collective-permute-start(bf16[128,768]{1,0:T(8,128)(2,1)S(1)} %collective-permute-done.2), channel_id=1, source_target_pairs={{0,1},{1,0},{2,3},{3,2},{4,5},{5,4},{6,7},{7,6},{8,9},{9,8},{10,11... | collective-permute-start | bytes 589832 | tf_op jit(solution)/shard_map/ppermute | solution.py:16
  20.6 7.2 %collective-permute-start.7 = (bf16[64,768]{1,0:T(8,128)(2,1)S(1)}, bf16[64,768]{1,0:T(8,128)(2,1)S(1)}, u32[]{:S(2)}, u32[]{:S(2)}) collective-permute-start(bf16[64,768]{1,0:T(8,128)(2,1)S(1)} %slice.259), channel_id=1, source_target_pairs={{0,1},{1,0},{2,3},{3,2},{4,5},{5,4},{6,7},{7,6},{8,9},{9,8},{10,11... | collective-permute-start | bytes 294920 | tf_op jit(solution)/shard_map/ppermute | solution.py:16
  22.7 5.1 %collective-permute-start.8 = (bf16[64,768]{1,0:T(8,128)(2,1)S(1)}, bf16[64,768]{1,0:T(8,128)(2,1)S(1)}, u32[]{:S(2)}, u32[]{:S(2)}) collective-permute-start(bf16[64,768]{1,0:T(8,128)(2,1)S(1)} %slice.260), channel_id=1, source_target_pairs={{0,2},{1,3},{2,0},{3,1},{4,6},{5,7},{6,4},{7,5},{8,10},{9,11},{10,... | collective-permute-start | bytes 294920 | tf_op jit(solution)/shard_map/ppermute | solution.py:16
  28.4 1.6 %copy-start.2 = (bf16[4,768]{1,0:T(4,128)(2,1)S(1)}, bf16[4,768]{1,0:T(4,128)(2,1)}, u32[]{:S(2)}) copy-start(bf16[4,768]{1,0:T(4,128)(2,1)} %param.6) | copy-start | bytes 18436
  28.4 3.7 %collective-permute-start.9 = (f32[2,2,2,128]{3,2,1,0:T(2,128)S(1)}, f32[2,2,2,128]{3,2,1,0:T(2,128)S(1)}, u32[]{:S(2)}, u32[]{:S(2)}) collective-permute-start(f32[2,2,2,128]{3,2,1,0:T(2,128)S(1)} %pad_maximum_fusion.3), channel_id=1, source_target_pairs={{0,1},{1,0},{2,3},{3,2},{4,5},{5,4},{6,7},{7,6},{8,9},{9,8},{10,11... | collective-permute-start | bytes 12296 | tf_op jit(solution)/shard_map/ppermute | solution.py:16
  32.1 3.7 %collective-permute-start.10 = (f32[2,2,2,128]{3,2,1,0:T(2,128)S(1)}, f32[2,2,2,128]{3,2,1,0:T(2,128)S(1)}, u32[]{:S(2)}, u32[]{:S(2)}) collective-permute-start(f32[2,2,2,128]{3,2,1,0:T(2,128)S(1)} %log_add_fusion.5), channel_id=1, source_target_pairs={{0,2},{1,3},{2,0},{3,1},{4,6},{5,7},{6,4},{7,5},{8,10},{9,11},{10,... | collective-permute-start | bytes 12296 | tf_op jit(solution)/shard_map/ppermute | solution.py:16
  35.8 5.0 %collective-permute-start.11 = (f32[2,2,2,128]{3,2,1,0:T(2,128)S(1)}, f32[2,2,2,128]{3,2,1,0:T(2,128)S(1)}, u32[]{:S(2)}, u32[]{:S(2)}) collective-permute-start(f32[2,2,2,128]{3,2,1,0:T(2,128)S(1)} %log_add_fusion.4), channel_id=1, source_target_pairs={{0,4},{1,5},{2,6},{3,7},{4,0},{5,1},{6,2},{7,3},{8,12},{9,13},{10,... | collective-permute-start | bytes 12296 | tf_op jit(solution)/shard_map/ppermute | solution.py:16
  41.7 1.5 %collective-permute-start.12 = (f32[136,384]{1,0:T(8,128)S(1)}, f32[136,384]{1,0:T(8,128)S(1)}, u32[]{:S(2)}, u32[]{:S(2)}) collective-permute-start(f32[136,384]{1,0:T(8,128)S(1)} %select_maximum_fusion.1), channel_id=1, source_target_pairs={{0,8},{8,0},{16,24},{24,16},{1,9},{9,1},{17,25},{25,17},{2,10},{10... | collective-permute-start | bytes 626696 | tf_op jit(solution)/shard_map/ppermute | solution.py:16
  42.4 2.8 %collective-permute-start.15 = (f32[128,384]{1,0:T(8,128)S(1)}, f32[128,384]{1,0:T(8,128)S(1)}, u32[]{:S(2)}, u32[]{:S(2)}) collective-permute-start(f32[128,384]{1,0:T(8,128)S(1)} %slice_select_fusion.3), channel_id=1, source_target_pairs={{0,8},{8,0},{16,24},{24,16},{1,9},{9,1},{17,25},{25,17},{2,10},{10... | collective-permute-start | bytes 589832 | tf_op jit(solution)/shard_map/ppermute | solution.py:16
  43.7 7.4 %copy-start.1 = (f32[128,768]{1,0:T(8,128)S(1)}, f32[128,768]{1,0:T(8,128)}, u32[]{:S(2)}) copy-start(f32[128,768]{1,0:T(8,128)} %slice_select_fusion.1) | copy-start | bytes 1179652
  43.7 6.1 %collective-permute-start.13 = (bf16[152,384]{1,0:T(8,128)(2,1)S(1)}, bf16[152,384]{1,0:T(8,128)(2,1)S(1)}, u32[]{:S(2)}, u32[]{:S(2)}) collective-permute-start(bf16[152,384]{1,0:T(8,128)(2,1)S(1)} %pad.40), channel_id=1, source_target_pairs={{0,16},{8,24},{16,0},{24,8},{1,17},{9,25},{17,1},{25,9},{2,18},{10... | collective-permute-start | bytes 350216 | tf_op jit(solution)/shard_map/ppermute | solution.py:16
  45.3 5.8 %collective-permute-start.16 = (bf16[128,384]{1,0:T(8,128)(2,1)S(1)}, bf16[128,384]{1,0:T(8,128)(2,1)S(1)}, u32[]{:S(2)}, u32[]{:S(2)}) collective-permute-start(bf16[128,384]{1,0:T(8,128)(2,1)S(1)} %add_convert_fusion.1), channel_id=1, source_target_pairs={{0,16},{8,24},{16,0},{24,8},{1,17},{9,25},{17,1},{25,9},{2,18},{10... | collective-permute-start | bytes 294920 | tf_op jit(solution)/shard_map/ppermute | solution.py:16
  51.2 1.5 %collective-permute-start.14 = (f32[128,384]{1,0:T(8,128)S(1)}, f32[128,384]{1,0:T(8,128)S(1)}, u32[]{:S(2)}, u32[]{:S(2)}) collective-permute-start(f32[128,384]{1,0:T(8,128)S(1)} %get-tuple-element.58), channel_id=1, source_target_pairs={{0,8},{8,0},{16,24},{24,16},{1,9},{9,1},{17,25},{25,17},{2,10},{10... | collective-permute-start | bytes 589832 | tf_op jit(solution)/shard_map/ppermute | solution.py:16
  51.3 1.7 %collective-permute-start.17 = (f32[128,384]{1,0:T(8,128)S(1)}, f32[128,384]{1,0:T(8,128)S(1)}, u32[]{:S(2)}, u32[]{:S(2)}) collective-permute-start(f32[128,384]{1,0:T(8,128)S(1)} %get-tuple-element.59), channel_id=1, source_target_pairs={{0,8},{8,0},{16,24},{24,16},{1,9},{9,1},{17,25},{25,17},{2,10},{10... | collective-permute-start | bytes 589832 | tf_op jit(solution)/shard_map/ppermute | solution.py:16
  54.3 3.7 %collective-permute-start.18 = (f32[2,2,2,128]{3,2,1,0:T(2,128)S(1)}, f32[2,2,2,128]{3,2,1,0:T(2,128)S(1)}, u32[]{:S(2)}, u32[]{:S(2)}) collective-permute-start(f32[2,2,2,128]{3,2,1,0:T(2,128)S(1)} %pad_maximum_fusion.4), channel_id=1, source_target_pairs={{0,1},{1,0},{2,3},{3,2},{4,5},{5,4},{6,7},{7,6},{8,9},{9,8},{10,11... | collective-permute-start | bytes 12296 | tf_op jit(solution)/shard_map/ppermute | solution.py:16
  58.3 0.7 copy-start.4
  58.3 3.6 %collective-permute-start.19 = (f32[2,2,2,128]{3,2,1,0:T(2,128)S(1)}, f32[2,2,2,128]{3,2,1,0:T(2,128)S(1)}, u32[]{:S(2)}, u32[]{:S(2)}) collective-permute-start(f32[2,2,2,128]{3,2,1,0:T(2,128)S(1)} %log_add_fusion.2), channel_id=1, source_target_pairs={{0,2},{1,3},{2,0},{3,1},{4,6},{5,7},{6,4},{7,5},{8,10},{9,11},{10,... | collective-permute-start | bytes 12296 | tf_op jit(solution)/shard_map/ppermute | solution.py:16
  59.0 0.7 copy-start.3
  62.0 4.6 %collective-permute-start.20 = (f32[2,2,2,128]{3,2,1,0:T(2,128)S(1)}, f32[2,2,2,128]{3,2,1,0:T(2,128)S(1)}, u32[]{:S(2)}, u32[]{:S(2)}) collective-permute-start(f32[2,2,2,128]{3,2,1,0:T(2,128)S(1)} %log_add_fusion.1), channel_id=1, source_target_pairs={{0,4},{1,5},{2,6},{3,7},{4,0},{5,1},{6,2},{7,3},{8,12},{9,13},{10,... | collective-permute-start | bytes 12296 | tf_op jit(solution)/shard_map/ppermute | solution.py:16
  67.9 1.5 %collective-permute-start.21 = (f32[136,384]{1,0:T(8,128)S(1)}, f32[136,384]{1,0:T(8,128)S(1)}, u32[]{:S(2)}, u32[]{:S(2)}) collective-permute-start(f32[136,384]{1,0:T(8,128)S(1)} %select_maximum_fusion), channel_id=1, source_target_pairs={{0,8},{8,0},{16,24},{24,16},{1,9},{9,1},{17,25},{25,17},{2,10},{10... | collective-permute-start | bytes 626696 | tf_op jit(solution)/shard_map/ppermute | solution.py:16
  68.3 3.0 %collective-permute-start.24 = (f32[128,384]{1,0:T(8,128)S(1)}, f32[128,384]{1,0:T(8,128)S(1)}, u32[]{:S(2)}, u32[]{:S(2)}) collective-permute-start(f32[128,384]{1,0:T(8,128)S(1)} %slice_select_fusion.2), channel_id=1, source_target_pairs={{0,8},{8,0},{16,24},{24,16},{1,9},{9,1},{17,25},{25,17},{2,10},{10... | collective-permute-start | bytes 589832 | tf_op jit(solution)/shard_map/ppermute | solution.py:16
  69.7 5.8 %collective-permute-start.22 = (bf16[136,384]{1,0:T(8,128)(2,1)S(1)}, bf16[136,384]{1,0:T(8,128)(2,1)S(1)}, u32[]{:S(2)}, u32[]{:S(2)}) collective-permute-start(bf16[136,384]{1,0:T(8,128)(2,1)S(1)} %pad.45), channel_id=1, source_target_pairs={{0,16},{8,24},{16,0},{24,8},{1,17},{9,25},{17,1},{25,9},{2,18},{10... | collective-permute-start | bytes 313352 | tf_op jit(solution)/shard_map/ppermute | solution.py:16
  71.3 5.5 %collective-permute-start.25 = (bf16[128,384]{1,0:T(8,128)(2,1)S(1)}, bf16[128,384]{1,0:T(8,128)(2,1)S(1)}, u32[]{:S(2)}, u32[]{:S(2)}) collective-permute-start(bf16[128,384]{1,0:T(8,128)(2,1)S(1)} %add_convert_fusion), channel_id=1, source_target_pairs={{0,16},{8,24},{16,0},{24,8},{1,17},{9,25},{17,1},{25,9},{2,18},{10... | collective-permute-start | bytes 294920 | tf_op jit(solution)/shard_map/ppermute | solution.py:16
  77.0 1.5 %collective-permute-start.23 = (f32[128,384]{1,0:T(8,128)S(1)}, f32[128,384]{1,0:T(8,128)S(1)}, u32[]{:S(2)}, u32[]{:S(2)}) collective-permute-start(f32[128,384]{1,0:T(8,128)S(1)} %get-tuple-element.56), channel_id=1, source_target_pairs={{0,8},{8,0},{16,24},{24,16},{1,9},{9,1},{17,25},{25,17},{2,10},{10... | collective-permute-start | bytes 589832 | tf_op jit(solution)/shard_map/ppermute | solution.py:16
  77.0 1.7 %collective-permute-start.26 = (f32[128,384]{1,0:T(8,128)S(1)}, f32[128,384]{1,0:T(8,128)S(1)}, u32[]{:S(2)}, u32[]{:S(2)}) collective-permute-start(f32[128,384]{1,0:T(8,128)S(1)} %get-tuple-element.57), channel_id=1, source_target_pairs={{0,8},{8,0},{16,24},{24,16},{1,9},{9,1},{17,25},{25,17},{2,10},{10... | collective-permute-start | bytes 589832 | tf_op jit(solution)/shard_map/ppermute | solution.py:16

commit v4 on v3

--- a/solution.py
+++ b/solution.py
@@ -26,11 +26,15 @@
 
 def gathered_pieces(value, later, axis, size):
     far = size // 2
-    half = value.shape[0] // 2
+    half = 1 * value.shape[0] // 4
     pieces = {0: later}
     for mask in sorted(range(1, size), key=lambda m: (bin(m).count("1"), -m)):
         low = mask & -mask
         rest = mask ^ low
+        if rest == far and mask == far + far // 2 and far > 1:
+            later_far, pieces[far // 2] = lax.optimization_barrier((pieces[far], pieces[far // 2]))
+            pieces[mask] = swap(later_far, axis, low)
+            continue
         if rest & (rest - 1):
             second = rest & -rest
             pieces[mask] = jnp.concatenate(
@@ -166,8 +170,8 @@
                 sent = totals[part].astype(jnp.bfloat16)
                 packed = sent
                 if part == 0:
-                    parts = [jnp.pad(p[None, :], ((0, 0), (0, cut - p.shape[0]))) for p in in_three(line)]
-                    packed = jnp.concatenate([packed] + parts)
+                    parts = jnp.pad(jnp.stack(in_three(line)), ((0, 5), (0, cut - line.shape[0])))
+                    packed = jnp.concatenate([packed, parts])
                     if step == 0:
                         packed = jnp.concatenate([packed, asked[:, :cut], asked[:, cut:]])
                     packed = jnp.pad(packed, ((0, -packed.shape[0] % 8), (0, 0)))
@@ -177,7 +181,7 @@
                     three = other[kept : kept + 3, : line.shape[0]].astype(jnp.float32)
                     line = join_lines(line, (three[0] + three[1]) + three[2])
                     if step == 0:
-                        more = other[kept + 3 : kept + 3 + 2 * asked.shape[0]]
+                        more = other[kept + 8 : kept + 8 + 2 * asked.shape[0]]
                         more = jnp.concatenate([more[: asked.shape[0]], more[asked.shape[0] :]], axis=1)
                         asked = in_order(asked, more, dp & bit)
         if last:

time: 79.9 us -> 78.8 us (0.986)
  starting transfers between devices: 31.8 us -> 31 us
    unnamed x17 -> x15, local copies, waits for them, and re-layouts: 1.72 us -> 1.66 us
  transfers between devices with their start and end apart: 27 -> 27, of which waited for: 23 -> 23; matrix products, arithmetic and copies ran while one was open for 8% -> 7% of each run, Pallas kernels for 0% -> 0%
where the time goes in v4:
time: 78.8 us; the launch traced here: 78.7 us
  waiting for transfers between devices  34.5 us (44%)
  starting transfers between devices  31 us (39%)
  matrix products  4.88 us (6%)
  other arithmetic  4.29 us (5%)
  local copies, waits for them, and re-layouts  2.8 us (4%)
  between operations  1.11 us (1%)
    ppermute x27, waiting for transfers between devices, swap(): return lax.ppermute(value, axis, [(i, i ^ bit) for i in range(size)])  34.5 us
    ppermute x27, starting transfers between devices, swap(): return lax.ppermute(value, axis, [(i, i ^ bit) for i in range(size)])  31 us
    dot_general x8, matrix products, on_device(): jnp.dot(resps[index], held[index][:, part * cut:(part + 1) * cut], prefer...  2.33 us
    dot_general x4, matrix products, on_device(): lax.dot_general(centers_half, group, (((1,), (1,)), ((), ())), preferred_...  1.7 us
    unnamed x15, local copies, waits for them, and re-layouts  1.66 us
  transfers between devices with their start and end apart: 27, of which 23 were waited for; matrix products, arithmetic and copies ran while one was open for 7% of the time, Pallas kernels for 0%

profile of v4, /device:TPU:0, one launch (start us, length us, event | category | flops | bytes accessed | tf_op | source)
XLA Modules:
  0.0 78.7 jit_solution(15578292240920614881)
XLA Ops:
  0.6 4.1 %collective-permute-start.2 = (bf16[128,768]{1,0:T(8,128)(2,1)}, bf16[128,768]{1,0:T(8,128)(2,1)S(1)}, u32[]{:S(2)}, u32[]{:S(2)}) collective-permute-start(bf16[128,768]{1,0:T(8,128)(2,1)} %param.5), channel_id=1, source_target_pairs={{0,4},{1,5},{2,6},{3,7},{4,0},{5,1},{6,2},{7,3},{8,12},{9,13},{10,... | collective-permute-start | bytes 589832 | tf_op jit(solution)/shard_map/ppermute | solution.py:16
  4.7 1.4 %collective-permute-done = bf16[4,768]{1,0:T(4,128)(2,1)S(1)} collective-permute-done((bf16[4,768]{1,0:T(4,128)(2,1)}, bf16[4,768]{1,0:T(4,128)(2,1)S(1)}, u32[]{:S(2)}, u32[]{:S(2)}) %collective-permute-start) | collective-permute-done | bytes 6176 | tf_op jit(solution)/shard_map/ppermute | solution.py:16
  6.1 1.6 %collective-permute-start.3 = (bf16[128,768]{1,0:T(8,128)(2,1)}, bf16[128,768]{1,0:T(8,128)(2,1)S(1)}, u32[]{:S(2)}, u32[]{:S(2)}) collective-permute-start(bf16[128,768]{1,0:T(8,128)(2,1)} %param.5), channel_id=1, source_target_pairs={{0,2},{1,3},{2,0},{3,1},{4,6},{5,7},{6,4},{7,5},{8,10},{9,11},{10,... | collective-permute-start | bytes 589832 | tf_op jit(solution)/shard_map/ppermute | solution.py:16
  7.7 1.5 %collective-permute-start.1 = (bf16[128,768]{1,0:T(8,128)(2,1)}, bf16[128,768]{1,0:T(8,128)(2,1)S(1)}, u32[]{:S(2)}, u32[]{:S(2)}) collective-permute-start(bf16[128,768]{1,0:T(8,128)(2,1)} %param.5), channel_id=1, source_target_pairs={{0,1},{1,0},{2,3},{3,2},{4,5},{5,4},{6,7},{7,6},{8,9},{9,8},{10,11... | collective-permute-start | bytes 589832 | tf_op jit(solution)/shard_map/ppermute | solution.py:16
  9.2 1.0 %constant_dynamic-update-slice_fusion.3 = bf16[512,768]{1,0:T(8,128)(2,1)S(1)} fusion(bf16[128,768]{1,0:T(8,128)(2,1)} %param.5), kind=kLoop, calls=%fused_computation.99 | loop fusion | bytes 393216
  10.2 4.0 %collective-permute-done.2 = bf16[128,768]{1,0:T(8,128)(2,1)S(1)} collective-permute-done((bf16[128,768]{1,0:T(8,128)(2,1)}, bf16[128,768]{1,0:T(8,128)(2,1)S(1)}, u32[]{:S(2)}, u32[]{:S(2)}) %collective-permute-start.2) | collective-permute-done | bytes 196640 | tf_op jit(solution)/shard_map/ppermute | solution.py:16
  14.2 1.5 %collective-permute-start.5 = (bf16[128,768]{1,0:T(8,128)(2,1)S(1)}, bf16[128,768]{1,0:T(8,128)(2,1)S(1)}, u32[]{:S(2)}, u32[]{:S(2)}) collective-permute-start(bf16[128,768]{1,0:T(8,128)(2,1)S(1)} %collective-permute-done.2), channel_id=1, source_target_pairs={{0,1},{1,0},{2,3},{3,2},{4,5},{5,4},{6,7},{7,6},{8,9},{9,8},{10,11... | collective-permute-start | bytes 589832 | tf_op jit(solution)/shard_map/ppermute | solution.py:16
  16.7 1.2 %collective-permute-start.4 = (bf16[128,768]{1,0:T(8,128)(2,1)S(1)}, bf16[128,768]{1,0:T(8,128)(2,1)S(1)}, u32[]{:S(2)}, u32[]{:S(2)}) collective-permute-start(bf16[128,768]{1,0:T(8,128)(2,1)S(1)} %collective-permute-done.3), channel_id=1, source_target_pairs={{0,1},{1,0},{2,3},{3,2},{4,5},{5,4},{6,7},{7,6},{8,9},{9,8},{10,11... | collective-permute-start | bytes 589832 | tf_op jit(solution)/shard_map/ppermute | solution.py:16
  17.9 3.7 %collective-permute-done.5 = bf16[128,768]{1,0:T(8,128)(2,1)S(1)} collective-permute-done((bf16[128,768]{1,0:T(8,128)(2,1)S(1)}, bf16[128,768]{1,0:T(8,128)(2,1)S(1)}, u32[]{:S(2)}, u32[]{:S(2)}) %collective-permute-start.5) | collective-permute-done | bytes 196640 | tf_op jit(solution)/shard_map/ppermute | solution.py:16
  21.7 1.1 %collective-permute-start.8 = (bf16[96,768]{1,0:T(8,128)(2,1)S(1)}, bf16[96,768]{1,0:T(8,128)(2,1)S(1)}, u32[]{:S(2)}, u32[]{:S(2)}) collective-permute-start(bf16[96,768]{1,0:T(8,128)(2,1)S(1)} %slice.260), channel_id=1, source_target_pairs={{0,2},{1,3},{2,0},{3,1},{4,6},{5,7},{6,4},{7,5},{8,10},{9,11},{10,... | collective-permute-start | bytes 442376 | tf_op jit(solution)/shard_map/ppermute | solution.py:16
  23.1 1.6 %collective-permute-start.7 = (bf16[32,768]{1,0:T(8,128)(2,1)S(1)}, bf16[32,768]{1,0:T(8,128)(2,1)S(1)}, u32[]{:S(2)}, u32[]{:S(2)}) collective-permute-start(bf16[32,768]{1,0:T(8,128)(2,1)S(1)} %slice.259), channel_id=1, source_target_pairs={{0,1},{1,0},{2,3},{3,2},{4,5},{5,4},{6,7},{7,6},{8,9},{9,8},{10,11... | collective-permute-start | bytes 147464 | tf_op jit(solution)/shard_map/ppermute | solution.py:16
  25.5 1.6 %collective-permute-done.7 = bf16[32,768]{1,0:T(8,128)(2,1)S(1)} collective-permute-done((bf16[32,768]{1,0:T(8,128)(2,1)S(1)}, bf16[32,768]{1,0:T(8,128)(2,1)S(1)}, u32[]{:S(2)}, u32[]{:S(2)}) %collective-permute-start.7) | collective-permute-done | bytes 49184 | tf_op jit(solution)/shard_map/ppermute | solution.py:16
  27.8 1.7 %collective-permute-start.9 = (f32[2,2,2,128]{3,2,1,0:T(2,128)S(1)}, f32[2,2,2,128]{3,2,1,0:T(2,128)S(1)}, u32[]{:S(2)}, u32[]{:S(2)}) collective-permute-start(f32[2,2,2,128]{3,2,1,0:T(2,128)S(1)} %pad_maximum_fusion.5), channel_id=1, source_target_pairs={{0,1},{1,0},{2,3},{3,2},{4,5},{5,4},{6,7},{7,6},{8,9},{9,8},{10,11... | collective-permute-start | bytes 12296 | tf_op jit(solution)/shard_map/ppermute | solution.py:16
  29.4 2.0 %collective-permute-done.9 = f32[2,2,2,128]{3,2,1,0:T(2,128)S(1)} collective-permute-done((f32[2,2,2,128]{3,2,1,0:T(2,128)S(1)}, f32[2,2,2,128]{3,2,1,0:T(2,128)S(1)}, u32[]{:S(2)}, u32[]{:S(2)}) %collective-permute-start.9) | collective-permute-done | bytes 4128 | tf_op jit(solution)/shard_map/ppermute | solution.py:16
  31.5 0.9 %collective-permute-start.10 = (f32[2,2,2,128]{3,2,1,0:T(2,128)S(1)}, f32[2,2,2,128]{3,2,1,0:T(2,128)S(1)}, u32[]{:S(2)}, u32[]{:S(2)}) collective-permute-start(f32[2,2,2,128]{3,2,1,0:T(2,128)S(1)} %log_add_fusion.5), channel_id=1, source_target_pairs={{0,2},{1,3},{2,0},{3,1},{4,6},{5,7},{6,4},{7,5},{8,10},{9,11},{10,... | collective-permute-start | bytes 12296 | tf_op jit(solution)/shard_map/ppermute | solution.py:16
  32.4 2.8 %collective-permute-done.10 = f32[2,2,2,128]{3,2,1,0:T(2,128)S(1)} collective-permute-done((f32[2,2,2,128]{3,2,1,0:T(2,128)S(1)}, f32[2,2,2,128]{3,2,1,0:T(2,128)S(1)}, u32[]{:S(2)}, u32[]{:S(2)}) %collective-permute-start.10) | collective-permute-done | bytes 4128 | tf_op jit(solution)/shard_map/ppermute | solution.py:16
  35.2 3.3 %collective-permute-start.11 = (f32[2,2,2,128]{3,2,1,0:T(2,128)S(1)}, f32[2,2,2,128]{3,2,1,0:T(2,128)S(1)}, u32[]{:S(2)}, u32[]{:S(2)}) collective-permute-start(f32[2,2,2,128]{3,2,1,0:T(2,128)S(1)} %log_add_fusion.4), channel_id=1, source_target_pairs={{0,4},{1,5},{2,6},{3,7},{4,0},{5,1},{6,2},{7,3},{8,12},{9,13},{10,... | collective-permute-start | bytes 12296 | tf_op jit(solution)/shard_map/ppermute | solution.py:16
  38.5 1.5 %collective-permute-done.11 = f32[2,2,2,128]{3,2,1,0:T(2,128)S(1)} collective-permute-done((f32[2,2,2,128]{3,2,1,0:T(2,128)S(1)}, f32[2,2,2,128]{3,2,1,0:T(2,128)S(1)}, u32[]{:S(2)}, u32[]{:S(2)}) %collective-permute-start.11) | collective-permute-done | bytes 4128 | tf_op jit(solution)/shard_map/ppermute | solution.py:16
  42.6 1.6 %collective-permute-start.13 = (bf16[152,384]{1,0:T(8,128)(2,1)S(1)}, bf16[152,384]{1,0:T(8,128)(2,1)S(1)}, u32[]{:S(2)}, u32[]{:S(2)}) collective-permute-start(bf16[152,384]{1,0:T(8,128)(2,1)S(1)} %pad_maximum_fusion), channel_id=1, source_target_pairs={{0,16},{8,24},{16,0},{24,8},{1,17},{9,25},{17,1},{25,9},{2,18},{10... | collective-permute-start | bytes 350216 | tf_op jit(solution)/shard_map/ppermute | solution.py:16
  44.2 0.7 collective-permute-start.16
  45.0 3.7 %collective-permute-done.13 = bf16[152,384]{1,0:T(8,128)(2,1)S(1)} collective-permute-done((bf16[152,384]{1,0:T(8,128)(2,1)S(1)}, bf16[152,384]{1,0:T(8,128)(2,1)S(1)}, u32[]{:S(2)}, u32[]{:S(2)}) %collective-permute-start.13) | collective-permute-done | bytes 116768 | tf_op jit(solution)/shard_map/ppermute | solution.py:16
  48.7 1.3 %collective-permute-done.16 = bf16[128,384]{1,0:T(8,128)(2,1)S(1)} collective-permute-done((bf16[128,384]{1,0:T(8,128)(2,1)S(1)}, bf16[128,384]{1,0:T(8,128)(2,1)S(1)}, u32[]{:S(2)}, u32[]{:S(2)}) %collective-permute-start.16) | collective-permute-done | bytes 98336 | tf_op jit(solution)/shard_map/ppermute | solution.py:16
  50.7 0.9 %collective-permute-done.14 = f32[128,384]{1,0:T(8,128)S(1)} collective-permute-done((f32[128,384]{1,0:T(8,128)S(1)}, f32[128,384]{1,0:T(8,128)S(1)}, u32[]{:S(2)}, u32[]{:S(2)}) %collective-permute-start.14) | collective-permute-done | bytes 196640 | tf_op jit(solution)/shard_map/ppermute | solution.py:16
  53.2 1.6 %collective-permute-start.18 = (f32[2,2,2,128]{3,2,1,0:T(2,128)S(1)}, f32[2,2,2,128]{3,2,1,0:T(2,128)S(1)}, u32[]{:S(2)}, u32[]{:S(2)}) collective-permute-start(f32[2,2,2,128]{3,2,1,0:T(2,128)S(1)} %pad_maximum_fusion.6), channel_id=1, source_target_pairs={{0,1},{1,0},{2,3},{3,2},{4,5},{5,4},{6,7},{7,6},{8,9},{9,8},{10,11... | collective-permute-start | bytes 12296 | tf_op jit(solution)/shard_map/ppermute | solution.py:16
  54.8 2.1 %collective-permute-done.18 = f32[2,2,2,128]{3,2,1,0:T(2,128)S(1)} collective-permute-done((f32[2,2,2,128]{3,2,1,0:T(2,128)S(1)}, f32[2,2,2,128]{3,2,1,0:T(2,128)S(1)}, u32[]{:S(2)}, u32[]{:S(2)}) %collective-permute-start.18) | collective-permute-done | bytes 4128 | tf_op jit(solution)/shard_map/ppermute | solution.py:16
  57.3 0.9 %collective-permute-start.19 = (f32[2,2,2,128]{3,2,1,0:T(2,128)S(1)}, f32[2,2,2,128]{3,2,1,0:T(2,128)S(1)}, u32[]{:S(2)}, u32[]{:S(2)}) collective-permute-start(f32[2,2,2,128]{3,2,1,0:T(2,128)S(1)} %log_add_fusion.2), channel_id=1, source_target_pairs={{0,2},{1,3},{2,0},{3,1},{4,6},{5,7},{6,4},{7,5},{8,10},{9,11},{10,... | collective-permute-start | bytes 12296 | tf_op jit(solution)/shard_map/ppermute | solution.py:16
  60.9 3.0 %collective-permute-start.20 = (f32[2,2,2,128]{3,2,1,0:T(2,128)S(1)}, f32[2,2,2,128]{3,2,1,0:T(2,128)S(1)}, u32[]{:S(2)}, u32[]{:S(2)}) collective-permute-start(f32[2,2,2,128]{3,2,1,0:T(2,128)S(1)} %log_add_fusion.1), channel_id=1, source_target_pairs={{0,4},{1,5},{2,6},{3,7},{4,0},{5,1},{6,2},{7,3},{8,12},{9,13},{10,... | collective-permute-start | bytes 12296 | tf_op jit(solution)/shard_map/ppermute | solution.py:16
  63.9 1.6 %collective-permute-done.20 = f32[2,2,2,128]{3,2,1,0:T(2,128)S(1)} collective-permute-done((f32[2,2,2,128]{3,2,1,0:T(2,128)S(1)}, f32[2,2,2,128]{3,2,1,0:T(2,128)S(1)}, u32[]{:S(2)}, u32[]{:S(2)}) %collective-permute-start.20) | collective-permute-done | bytes 4128 | tf_op jit(solution)/shard_map/ppermute | solution.py:16
  68.6 1.6 %collective-permute-start.22 = (bf16[136,384]{1,0:T(8,128)(2,1)S(1)}, bf16[136,384]{1,0:T(8,128)(2,1)S(1)}, u32[]{:S(2)}, u32[]{:S(2)}) collective-permute-start(bf16[136,384]{1,0:T(8,128)(2,1)S(1)} %pad_maximum_fusion.1), channel_id=1, source_target_pairs={{0,16},{8,24},{16,0},{24,8},{1,17},{9,25},{17,1},{25,9},{2,18},{10... | collective-permute-start | bytes 313352 | tf_op jit(solution)/shard_map/ppermute | solution.py:16
  70.8 3.6 %collective-permute-done.22 = bf16[136,384]{1,0:T(8,128)(2,1)S(1)} collective-permute-done((bf16[136,384]{1,0:T(8,128)(2,1)S(1)}, bf16[136,384]{1,0:T(8,128)(2,1)S(1)}, u32[]{:S(2)}, u32[]{:S(2)}) %collective-permute-start.22) | collective-permute-done | bytes 104480 | tf_op jit(solution)/shard_map/ppermute | solution.py:16
  74.5 1.3 %collective-permute-done.25 = bf16[128,384]{1,0:T(8,128)(2,1)S(1)} collective-permute-done((bf16[128,384]{1,0:T(8,128)(2,1)S(1)}, bf16[128,384]{1,0:T(8,128)(2,1)S(1)}, u32[]{:S(2)}, u32[]{:S(2)}) %collective-permute-start.25) | collective-permute-done | bytes 98336 | tf_op jit(solution)/shard_map/ppermute | solution.py:16
  77.7 0.9 %maximum_maximum_fusion.1 = f32[256,768]{1,0:T(8,128)} fusion(f32[128,384]{1,0:T(8,128)S(1)} %get-tuple-element.67, f32[128,384]{1,0:T(8,128)S(1)} %get-tuple-element.66, f32[128,384]{1,0:T(8,128)S(1)} %get-tuple-element.65, f32[128,384]{1,0:T(8,128)S(1)} %get-tuple-element.64), kind=kLoop, calls=%fused_computation.19 | loop fusion | flops 589824 | bytes 1572864 | tf_op jit(solution)/shard_map/concatenate | solution.py:195
  (144 shorter events, 16.4 us)
Async XLA Ops:
  0.6 15.1 %copy-start = (f32[256,768]{1,0:T(8,128)S(1)}, f32[256,768]{1,0:T(8,128)}, u32[]{:S(2)}) copy-start(f32[256,768]{1,0:T(8,128)} %param.7) | copy-start | bytes 2359300
  0.6 13.5 %collective-permute-start.2 = (bf16[128,768]{1,0:T(8,128)(2,1)}, bf16[128,768]{1,0:T(8,128)(2,1)S(1)}, u32[]{:S(2)}, u32[]{:S(2)}) collective-permute-start(bf16[128,768]{1,0:T(8,128)(2,1)} %param.5), channel_id=1, source_target_pairs={{0,4},{1,5},{2,6},{3,7},{4,0},{5,1},{6,2},{7,3},{8,12},{9,13},{10,... | collective-permute-start | bytes 589832 | tf_op jit(solution)/shard_map/ppermute | solution.py:16
  4.7 1.4 %collective-permute-start = (bf16[4,768]{1,0:T(4,128)(2,1)}, bf16[4,768]{1,0:T(4,128)(2,1)S(1)}, u32[]{:S(2)}, u32[]{:S(2)}) collective-permute-start(bf16[4,768]{1,0:T(4,128)(2,1)} %param.6), channel_id=1, source_target_pairs={{0,8},{8,0},{16,24},{24,16},{1,9},{9,1},{17,25},{25,17},{2,10},{10... | collective-permute-start | bytes 18440 | tf_op jit(solution)/shard_map/ppermute | solution.py:16
  6.1 10.2 %collective-permute-start.3 = (bf16[128,768]{1,0:T(8,128)(2,1)}, bf16[128,768]{1,0:T(8,128)(2,1)S(1)}, u32[]{:S(2)}, u32[]{:S(2)}) collective-permute-start(bf16[128,768]{1,0:T(8,128)(2,1)} %param.5), channel_id=1, source_target_pairs={{0,2},{1,3},{2,0},{3,1},{4,6},{5,7},{6,4},{7,5},{8,10},{9,11},{10,... | collective-permute-start | bytes 589832 | tf_op jit(solution)/shard_map/ppermute | solution.py:16
  7.7 8.0 %collective-permute-start.1 = (bf16[128,768]{1,0:T(8,128)(2,1)}, bf16[128,768]{1,0:T(8,128)(2,1)S(1)}, u32[]{:S(2)}, u32[]{:S(2)}) collective-permute-start(bf16[128,768]{1,0:T(8,128)(2,1)} %param.5), channel_id=1, source_target_pairs={{0,1},{1,0},{2,3},{3,2},{4,5},{5,4},{6,7},{7,6},{8,9},{9,8},{10,11... | collective-permute-start | bytes 589832 | tf_op jit(solution)/shard_map/ppermute | solution.py:16
  14.2 7.5 %collective-permute-start.5 = (bf16[128,768]{1,0:T(8,128)(2,1)S(1)}, bf16[128,768]{1,0:T(8,128)(2,1)S(1)}, u32[]{:S(2)}, u32[]{:S(2)}) collective-permute-start(bf16[128,768]{1,0:T(8,128)(2,1)S(1)} %collective-permute-done.2), channel_id=1, source_target_pairs={{0,1},{1,0},{2,3},{3,2},{4,5},{5,4},{6,7},{7,6},{8,9},{9,8},{10,11... | collective-permute-start | bytes 589832 | tf_op jit(solution)/shard_map/ppermute | solution.py:16
  16.4 6.7 %collective-permute-start.6 = (bf16[128,768]{1,0:T(8,128)(2,1)S(1)}, bf16[128,768]{1,0:T(8,128)(2,1)S(1)}, u32[]{:S(2)}, u32[]{:S(2)}) collective-permute-start(bf16[128,768]{1,0:T(8,128)(2,1)S(1)} %collective-permute-done.2), channel_id=1, source_target_pairs={{0,2},{1,3},{2,0},{3,1},{4,6},{5,7},{6,4},{7,5},{8,10},{9,11},{10,... | collective-permute-start | bytes 589832 | tf_op jit(solution)/shard_map/ppermute | solution.py:16
  16.7 8.3 %collective-permute-start.4 = (bf16[128,768]{1,0:T(8,128)(2,1)S(1)}, bf16[128,768]{1,0:T(8,128)(2,1)S(1)}, u32[]{:S(2)}, u32[]{:S(2)}) collective-permute-start(bf16[128,768]{1,0:T(8,128)(2,1)S(1)} %collective-permute-done.3), channel_id=1, source_target_pairs={{0,1},{1,0},{2,3},{3,2},{4,5},{5,4},{6,7},{7,6},{8,9},{9,8},{10,11... | collective-permute-start | bytes 589832 | tf_op jit(solution)/shard_map/ppermute | solution.py:16
  21.7 5.5 %collective-permute-start.8 = (bf16[96,768]{1,0:T(8,128)(2,1)S(1)}, bf16[96,768]{1,0:T(8,128)(2,1)S(1)}, u32[]{:S(2)}, u32[]{:S(2)}) collective-permute-start(bf16[96,768]{1,0:T(8,128)(2,1)S(1)} %slice.260), channel_id=1, source_target_pairs={{0,2},{1,3},{2,0},{3,1},{4,6},{5,7},{6,4},{7,5},{8,10},{9,11},{10,... | collective-permute-start | bytes 442376 | tf_op jit(solution)/shard_map/ppermute | solution.py:16
  23.1 4.1 %collective-permute-start.7 = (bf16[32,768]{1,0:T(8,128)(2,1)S(1)}, bf16[32,768]{1,0:T(8,128)(2,1)S(1)}, u32[]{:S(2)}, u32[]{:S(2)}) collective-permute-start(bf16[32,768]{1,0:T(8,128)(2,1)S(1)} %slice.259), channel_id=1, source_target_pairs={{0,1},{1,0},{2,3},{3,2},{4,5},{5,4},{6,7},{7,6},{8,9},{9,8},{10,11... | collective-permute-start | bytes 147464 | tf_op jit(solution)/shard_map/ppermute | solution.py:16
  27.7 1.7 %copy-start.1 = (bf16[4,768]{1,0:T(4,128)(2,1)S(1)}, bf16[4,768]{1,0:T(4,128)(2,1)}, u32[]{:S(2)}) copy-start(bf16[4,768]{1,0:T(4,128)(2,1)} %param.6) | copy-start | bytes 18436
  27.8 3.7 %collective-permute-start.9 = (f32[2,2,2,128]{3,2,1,0:T(2,128)S(1)}, f32[2,2,2,128]{3,2,1,0:T(2,128)S(1)}, u32[]{:S(2)}, u32[]{:S(2)}) collective-permute-start(f32[2,2,2,128]{3,2,1,0:T(2,128)S(1)} %pad_maximum_fusion.5), channel_id=1, source_target_pairs={{0,1},{1,0},{2,3},{3,2},{4,5},{5,4},{6,7},{7,6},{8,9},{9,8},{10,11... | collective-permute-start | bytes 12296 | tf_op jit(solution)/shard_map/ppermute | solution.py:16
  31.5 3.7 %collective-permute-start.10 = (f32[2,2,2,128]{3,2,1,0:T(2,128)S(1)}, f32[2,2,2,128]{3,2,1,0:T(2,128)S(1)}, u32[]{:S(2)}, u32[]{:S(2)}) collective-permute-start(f32[2,2,2,128]{3,2,1,0:T(2,128)S(1)} %log_add_fusion.5), channel_id=1, source_target_pairs={{0,2},{1,3},{2,0},{3,1},{4,6},{5,7},{6,4},{7,5},{8,10},{9,11},{10,... | collective-permute-start | bytes 12296 | tf_op jit(solution)/shard_map/ppermute | solution.py:16
  35.2 4.9 %collective-permute-start.11 = (f32[2,2,2,128]{3,2,1,0:T(2,128)S(1)}, f32[2,2,2,128]{3,2,1,0:T(2,128)S(1)}, u32[]{:S(2)}, u32[]{:S(2)}) collective-permute-start(f32[2,2,2,128]{3,2,1,0:T(2,128)S(1)} %log_add_fusion.4), channel_id=1, source_target_pairs={{0,4},{1,5},{2,6},{3,7},{4,0},{5,1},{6,2},{7,3},{8,12},{9,13},{10,... | collective-permute-start | bytes 12296 | tf_op jit(solution)/shard_map/ppermute | solution.py:16
  41.0 1.5 %collective-permute-start.12 = (f32[136,384]{1,0:T(8,128)S(1)}, f32[136,384]{1,0:T(8,128)S(1)}, u32[]{:S(2)}, u32[]{:S(2)}) collective-permute-start(f32[136,384]{1,0:T(8,128)S(1)} %select_maximum_fusion.1), channel_id=1, source_target_pairs={{0,8},{8,0},{16,24},{24,16},{1,9},{9,1},{17,25},{25,17},{2,10},{10... | collective-permute-start | bytes 626696 | tf_op jit(solution)/shard_map/ppermute | solution.py:16
  41.7 2.5 %collective-permute-start.15 = (f32[128,384]{1,0:T(8,128)S(1)}, f32[128,384]{1,0:T(8,128)S(1)}, u32[]{:S(2)}, u32[]{:S(2)}) collective-permute-start(f32[128,384]{1,0:T(8,128)S(1)} %slice_select_fusion.3), channel_id=1, source_target_pairs={{0,8},{8,0},{16,24},{24,16},{1,9},{9,1},{17,25},{25,17},{2,10},{10... | collective-permute-start | bytes 589832 | tf_op jit(solution)/shard_map/ppermute | solution.py:16
  42.6 6.1 %collective-permute-start.13 = (bf16[152,384]{1,0:T(8,128)(2,1)S(1)}, bf16[152,384]{1,0:T(8,128)(2,1)S(1)}, u32[]{:S(2)}, u32[]{:S(2)}) collective-permute-start(bf16[152,384]{1,0:T(8,128)(2,1)S(1)} %pad_maximum_fusion), channel_id=1, source_target_pairs={{0,16},{8,24},{16,0},{24,8},{1,17},{9,25},{17,1},{25,9},{2,18},{10... | collective-permute-start | bytes 350216 | tf_op jit(solution)/shard_map/ppermute | solution.py:16
  44.2 5.8 %collective-permute-start.16 = (bf16[128,384]{1,0:T(8,128)(2,1)S(1)}, bf16[128,384]{1,0:T(8,128)(2,1)S(1)}, u32[]{:S(2)}, u32[]{:S(2)}) collective-permute-start(bf16[128,384]{1,0:T(8,128)(2,1)S(1)} %add_convert_fusion.1), channel_id=1, source_target_pairs={{0,16},{8,24},{16,0},{24,8},{1,17},{9,25},{17,1},{25,9},{2,18},{10... | collective-permute-start | bytes 294920 | tf_op jit(solution)/shard_map/ppermute | solution.py:16
  50.1 1.5 %collective-permute-start.14 = (f32[128,384]{1,0:T(8,128)S(1)}, f32[128,384]{1,0:T(8,128)S(1)}, u32[]{:S(2)}, u32[]{:S(2)}) collective-permute-start(f32[128,384]{1,0:T(8,128)S(1)} %get-tuple-element.62), channel_id=1, source_target_pairs={{0,8},{8,0},{16,24},{24,16},{1,9},{9,1},{17,25},{25,17},{2,10},{10... | collective-permute-start | bytes 589832 | tf_op jit(solution)/shard_map/ppermute | solution.py:16
  50.2 1.7 %collective-permute-start.17 = (f32[128,384]{1,0:T(8,128)S(1)}, f32[128,384]{1,0:T(8,128)S(1)}, u32[]{:S(2)}, u32[]{:S(2)}) collective-permute-start(f32[128,384]{1,0:T(8,128)S(1)} %get-tuple-element.63), channel_id=1, source_target_pairs={{0,8},{8,0},{16,24},{24,16},{1,9},{9,1},{17,25},{25,17},{2,10},{10... | collective-permute-start | bytes 589832 | tf_op jit(solution)/shard_map/ppermute | solution.py:16
  53.2 3.7 %collective-permute-start.18 = (f32[2,2,2,128]{3,2,1,0:T(2,128)S(1)}, f32[2,2,2,128]{3,2,1,0:T(2,128)S(1)}, u32[]{:S(2)}, u32[]{:S(2)}) collective-permute-start(f32[2,2,2,128]{3,2,1,0:T(2,128)S(1)} %pad_maximum_fusion.6), channel_id=1, source_target_pairs={{0,1},{1,0},{2,3},{3,2},{4,5},{5,4},{6,7},{7,6},{8,9},{9,8},{10,11... | collective-permute-start | bytes 12296 | tf_op jit(solution)/shard_map/ppermute | solution.py:16
  57.2 1.0 %copy-start.3 = (s32[128]{0:T(128)S(1)}, s32[128]{0:T(128)}, u32[]{:S(2)}) copy-start(s32[128]{0:T(128)} %param.9) | copy-start | bytes 1540
  57.3 3.6 %collective-permute-start.19 = (f32[2,2,2,128]{3,2,1,0:T(2,128)S(1)}, f32[2,2,2,128]{3,2,1,0:T(2,128)S(1)}, u32[]{:S(2)}, u32[]{:S(2)}) collective-permute-start(f32[2,2,2,128]{3,2,1,0:T(2,128)S(1)} %log_add_fusion.2), channel_id=1, source_target_pairs={{0,2},{1,3},{2,0},{3,1},{4,6},{5,7},{6,4},{7,5},{8,10},{9,11},{10,... | collective-permute-start | bytes 12296 | tf_op jit(solution)/shard_map/ppermute | solution.py:16
  58.3 0.7 copy-start.2
  60.9 4.6 %collective-permute-start.20 = (f32[2,2,2,128]{3,2,1,0:T(2,128)S(1)}, f32[2,2,2,128]{3,2,1,0:T(2,128)S(1)}, u32[]{:S(2)}, u32[]{:S(2)}) collective-permute-start(f32[2,2,2,128]{3,2,1,0:T(2,128)S(1)} %log_add_fusion.1), channel_id=1, source_target_pairs={{0,4},{1,5},{2,6},{3,7},{4,0},{5,1},{6,2},{7,3},{8,12},{9,13},{10,... | collective-permute-start | bytes 12296 | tf_op jit(solution)/shard_map/ppermute | solution.py:16
  66.9 1.5 %collective-permute-start.21 = (f32[136,384]{1,0:T(8,128)S(1)}, f32[136,384]{1,0:T(8,128)S(1)}, u32[]{:S(2)}, u32[]{:S(2)}) collective-permute-start(f32[136,384]{1,0:T(8,128)S(1)} %select_maximum_fusion), channel_id=1, source_target_pairs={{0,8},{8,0},{16,24},{24,16},{1,9},{9,1},{17,25},{25,17},{2,10},{10... | collective-permute-start | bytes 626696 | tf_op jit(solution)/shard_map/ppermute | solution.py:16
  67.3 3.0 %collective-permute-start.24 = (f32[128,384]{1,0:T(8,128)S(1)}, f32[128,384]{1,0:T(8,128)S(1)}, u32[]{:S(2)}, u32[]{:S(2)}) collective-permute-start(f32[128,384]{1,0:T(8,128)S(1)} %slice_select_fusion.2), channel_id=1, source_target_pairs={{0,8},{8,0},{16,24},{24,16},{1,9},{9,1},{17,25},{25,17},{2,10},{10... | collective-permute-start | bytes 589832 | tf_op jit(solution)/shard_map/ppermute | solution.py:16
  68.6 5.8 %collective-permute-start.22 = (bf16[136,384]{1,0:T(8,128)(2,1)S(1)}, bf16[136,384]{1,0:T(8,128)(2,1)S(1)}, u32[]{:S(2)}, u32[]{:S(2)}) collective-permute-start(bf16[136,384]{1,0:T(8,128)(2,1)S(1)} %pad_maximum_fusion.1), channel_id=1, source_target_pairs={{0,16},{8,24},{16,0},{24,8},{1,17},{9,25},{17,1},{25,9},{2,18},{10... | collective-permute-start | bytes 313352 | tf_op jit(solution)/shard_map/ppermute | solution.py:16
  70.3 5.5 %collective-permute-start.25 = (bf16[128,384]{1,0:T(8,128)(2,1)S(1)}, bf16[128,384]{1,0:T(8,128)(2,1)S(1)}, u32[]{:S(2)}, u32[]{:S(2)}) collective-permute-start(bf16[128,384]{1,0:T(8,128)(2,1)S(1)} %add_convert_fusion), channel_id=1, source_target_pairs={{0,16},{8,24},{16,0},{24,8},{1,17},{9,25},{17,1},{25,9},{2,18},{10... | collective-permute-start | bytes 294920 | tf_op jit(solution)/shard_map/ppermute | solution.py:16
  75.9 1.5 %collective-permute-start.23 = (f32[128,384]{1,0:T(8,128)S(1)}, f32[128,384]{1,0:T(8,128)S(1)}, u32[]{:S(2)}, u32[]{:S(2)}) collective-permute-start(f32[128,384]{1,0:T(8,128)S(1)} %get-tuple-element.60), channel_id=1, source_target_pairs={{0,8},{8,0},{16,24},{24,16},{1,9},{9,1},{17,25},{25,17},{2,10},{10... | collective-permute-start | bytes 589832 | tf_op jit(solution)/shard_map/ppermute | solution.py:16
  76.0 1.7 %collective-permute-start.26 = (f32[128,384]{1,0:T(8,128)S(1)}, f32[128,384]{1,0:T(8,128)S(1)}, u32[]{:S(2)}, u32[]{:S(2)}) collective-permute-start(f32[128,384]{1,0:T(8,128)S(1)} %get-tuple-element.61), channel_id=1, source_target_pairs={{0,8},{8,0},{16,24},{24,16},{1,9},{9,1},{17,25},{25,17},{2,10},{10... | collective-permute-start | bytes 589832 | tf_op jit(solution)/shard_map/ppermute | solution.py:16

commit v5 on v4

--- a/solution.py
+++ b/solution.py
@@ -167,7 +167,10 @@
                 line = join_lines(line, other[kept, : line.shape[0]])
         for bit in dp_bits[1:]:
             for part in range(2):
-                sent = totals[part].astype(jnp.bfloat16)
+                sent = totals[part]
+                if isinstance(sent, tuple):
+                    sent = sent[0].astype(jnp.float32) + sent[1].astype(jnp.float32)
+                sent = sent.astype(jnp.bfloat16)
                 packed = sent
                 if part == 0:
                     parts = jnp.pad(jnp.stack(in_three(line)), ((0, 5), (0, cut - line.shape[0])))
@@ -176,7 +179,7 @@
                         packed = jnp.concatenate([packed, asked[:, :cut], asked[:, cut:]])
                     packed = jnp.pad(packed, ((0, -packed.shape[0] % 8), (0, 0)))
                 other = swap(packed, "dp", bit)
-                totals[part] = sent.astype(jnp.float32) + other[:kept].astype(jnp.float32)
+                totals[part] = (sent, other[:kept])
                 if part == 0:
                     three = other[kept : kept + 3, : line.shape[0]].astype(jnp.float32)
                     line = join_lines(line, (three[0] + three[1]) + three[2])
@@ -190,7 +193,10 @@
         prior = jnp.where(first, means[:kept], means[kept:])
         fresh = []
         for part in range(2):
-            mine = (totals[part] + PRIOR * prior[:, part * cut : (part + 1) * cut]) / (line[:kept, None] + PRIOR)
+            mine = totals[part][0].astype(jnp.float32) + totals[part][1].astype(jnp.float32)
+            mine = (mine + PRIOR * prior[:, part * cut : (part + 1) * cut]) / (line[:kept, None] + PRIOR)
+            if part == 0:
+                totals[1], _ = lax.optimization_barrier((totals[1], mine))
             fresh.append(in_order(mine, swap(mine, "dp", dp_bits[0]), core))
         means = jnp.concatenate(fresh, axis=1)
     return means, loss

time: 78.8 us -> 78.3 us (level)
  starting transfers between devices: 31 us -> 30.2 us
    ppermute x27, starting transfers between devices: 31 us -> 30.2 us  [swap(): return lax.ppermute(value, axis, [(i, i ^ bit) for i in range(size)])]
  transfers between devices with their start and end apart: 27 -> 27, of which waited for: 23 -> 22; matrix products, arithmetic and copies ran while one was open for 7% -> 8% of each run, Pallas kernels for 0% -> 0%
where the time goes in v5:
time: 78.3 us; the launch traced here: 78.1 us
  waiting for transfers between devices  34.6 us (44%)
  starting transfers between devices  30.2 us (39%)
  matrix products  4.88 us (6%)
  other arithmetic  4.46 us (6%)
  local copies, waits for them, and re-layouts  2.8 us (4%)
  between operations  1.16 us (1%)
    ppermute x27, waiting for transfers between devices, swap(): return lax.ppermute(value, axis, [(i, i ^ bit) for i in range(size)])  34.6 us
    ppermute x27, starting transfers between devices, swap(): return lax.ppermute(value, axis, [(i, i ^ bit) for i in range(size)])  30.2 us
    dot_general x8, matrix products, on_device(): jnp.dot(resps[index], held[index][:, part * cut:(part + 1) * cut], prefer...  2.33 us
    dot_general x4, matrix products, on_device(): lax.dot_general(centers_half, group, (((1,), (1,)), ((), ())), preferred_...  1.69 us
    unnamed x15, local copies, waits for them, and re-layouts  1.66 us
  transfers between devices with their start and end apart: 27, of which 22 were waited for; matrix products, arithmetic and copies ran while one was open for 8% of the time, Pallas kernels for 0%

profile of v5, /device:TPU:0, one launch (start us, length us, event | category | flops | bytes accessed | tf_op | source)
XLA Modules:
  0.0 78.1 jit_solution(9965915406743922472)
XLA Ops:
  0.6 4.1 %collective-permute-start.2 = (bf16[128,768]{1,0:T(8,128)(2,1)}, bf16[128,768]{1,0:T(8,128)(2,1)S(1)}, u32[]{:S(2)}, u32[]{:S(2)}) collective-permute-start(bf16[128,768]{1,0:T(8,128)(2,1)} %param.5), channel_id=1, source_target_pairs={{0,4},{1,5},{2,6},{3,7},{4,0},{5,1},{6,2},{7,3},{8,12},{9,13},{10,... | collective-permute-start | bytes 589832 | tf_op jit(solution)/shard_map/ppermute | solution.py:16
  4.7 1.4 %collective-permute-done = bf16[4,768]{1,0:T(4,128)(2,1)S(1)} collective-permute-done((bf16[4,768]{1,0:T(4,128)(2,1)}, bf16[4,768]{1,0:T(4,128)(2,1)S(1)}, u32[]{:S(2)}, u32[]{:S(2)}) %collective-permute-start) | collective-permute-done | bytes 6176 | tf_op jit(solution)/shard_map/ppermute | solution.py:16
  6.1 1.6 %collective-permute-start.3 = (bf16[128,768]{1,0:T(8,128)(2,1)}, bf16[128,768]{1,0:T(8,128)(2,1)S(1)}, u32[]{:S(2)}, u32[]{:S(2)}) collective-permute-start(bf16[128,768]{1,0:T(8,128)(2,1)} %param.5), channel_id=1, source_target_pairs={{0,2},{1,3},{2,0},{3,1},{4,6},{5,7},{6,4},{7,5},{8,10},{9,11},{10,... | collective-permute-start | bytes 589832 | tf_op jit(solution)/shard_map/ppermute | solution.py:16
  7.7 1.5 %collective-permute-start.1 = (bf16[128,768]{1,0:T(8,128)(2,1)}, bf16[128,768]{1,0:T(8,128)(2,1)S(1)}, u32[]{:S(2)}, u32[]{:S(2)}) collective-permute-start(bf16[128,768]{1,0:T(8,128)(2,1)} %param.5), channel_id=1, source_target_pairs={{0,1},{1,0},{2,3},{3,2},{4,5},{5,4},{6,7},{7,6},{8,9},{9,8},{10,11... | collective-permute-start | bytes 589832 | tf_op jit(solution)/shard_map/ppermute | solution.py:16
  9.2 1.0 %constant_dynamic-update-slice_fusion.3 = bf16[512,768]{1,0:T(8,128)(2,1)S(1)} fusion(bf16[128,768]{1,0:T(8,128)(2,1)} %param.5), kind=kLoop, calls=%fused_computation.99 | loop fusion | bytes 393216
  10.2 4.0 %collective-permute-done.2 = bf16[128,768]{1,0:T(8,128)(2,1)S(1)} collective-permute-done((bf16[128,768]{1,0:T(8,128)(2,1)}, bf16[128,768]{1,0:T(8,128)(2,1)S(1)}, u32[]{:S(2)}, u32[]{:S(2)}) %collective-permute-start.2) | collective-permute-done | bytes 196640 | tf_op jit(solution)/shard_map/ppermute | solution.py:16
  14.2 1.5 %collective-permute-start.5 = (bf16[128,768]{1,0:T(8,128)(2,1)S(1)}, bf16[128,768]{1,0:T(8,128)(2,1)S(1)}, u32[]{:S(2)}, u32[]{:S(2)}) collective-permute-start(bf16[128,768]{1,0:T(8,128)(2,1)S(1)} %collective-permute-done.2), channel_id=1, source_target_pairs={{0,1},{1,0},{2,3},{3,2},{4,5},{5,4},{6,7},{7,6},{8,9},{9,8},{10,11... | collective-permute-start | bytes 589832 | tf_op jit(solution)/shard_map/ppermute | solution.py:16
  16.7 1.2 %collective-permute-start.4 = (bf16[128,768]{1,0:T(8,128)(2,1)S(1)}, bf16[128,768]{1,0:T(8,128)(2,1)S(1)}, u32[]{:S(2)}, u32[]{:S(2)}) collective-permute-start(bf16[128,768]{1,0:T(8,128)(2,1)S(1)} %collective-permute-done.3), channel_id=1, source_target_pairs={{0,1},{1,0},{2,3},{3,2},{4,5},{5,4},{6,7},{7,6},{8,9},{9,8},{10,11... | collective-permute-start | bytes 589832 | tf_op jit(solution)/shard_map/ppermute | solution.py:16
  17.9 3.7 %collective-permute-done.5 = bf16[128,768]{1,0:T(8,128)(2,1)S(1)} collective-permute-done((bf16[128,768]{1,0:T(8,128)(2,1)S(1)}, bf16[128,768]{1,0:T(8,128)(2,1)S(1)}, u32[]{:S(2)}, u32[]{:S(2)}) %collective-permute-start.5) | collective-permute-done | bytes 196640 | tf_op jit(solution)/shard_map/ppermute | solution.py:16
  21.7 1.1 %collective-permute-start.8 = (bf16[96,768]{1,0:T(8,128)(2,1)S(1)}, bf16[96,768]{1,0:T(8,128)(2,1)S(1)}, u32[]{:S(2)}, u32[]{:S(2)}) collective-permute-start(bf16[96,768]{1,0:T(8,128)(2,1)S(1)} %slice.260), channel_id=1, source_target_pairs={{0,2},{1,3},{2,0},{3,1},{4,6},{5,7},{6,4},{7,5},{8,10},{9,11},{10,... | collective-permute-start | bytes 442376 | tf_op jit(solution)/shard_map/ppermute | solution.py:16
  23.1 1.6 %collective-permute-start.7 = (bf16[32,768]{1,0:T(8,128)(2,1)S(1)}, bf16[32,768]{1,0:T(8,128)(2,1)S(1)}, u32[]{:S(2)}, u32[]{:S(2)}) collective-permute-start(bf16[32,768]{1,0:T(8,128)(2,1)S(1)} %slice.259), channel_id=1, source_target_pairs={{0,1},{1,0},{2,3},{3,2},{4,5},{5,4},{6,7},{7,6},{8,9},{9,8},{10,11... | collective-permute-start | bytes 147464 | tf_op jit(solution)/shard_map/ppermute | solution.py:16
  25.5 1.6 %collective-permute-done.7 = bf16[32,768]{1,0:T(8,128)(2,1)S(1)} collective-permute-done((bf16[32,768]{1,0:T(8,128)(2,1)S(1)}, bf16[32,768]{1,0:T(8,128)(2,1)S(1)}, u32[]{:S(2)}, u32[]{:S(2)}) %collective-permute-start.7) | collective-permute-done | bytes 49184 | tf_op jit(solution)/shard_map/ppermute | solution.py:16
  27.8 1.7 %collective-permute-start.9 = (f32[2,2,2,128]{3,2,1,0:T(2,128)S(1)}, f32[2,2,2,128]{3,2,1,0:T(2,128)S(1)}, u32[]{:S(2)}, u32[]{:S(2)}) collective-permute-start(f32[2,2,2,128]{3,2,1,0:T(2,128)S(1)} %pad_maximum_fusion.5), channel_id=1, source_target_pairs={{0,1},{1,0},{2,3},{3,2},{4,5},{5,4},{6,7},{7,6},{8,9},{9,8},{10,11... | collective-permute-start | bytes 12296 | tf_op jit(solution)/shard_map/ppermute | solution.py:16
  29.4 2.0 %collective-permute-done.9 = f32[2,2,2,128]{3,2,1,0:T(2,128)S(1)} collective-permute-done((f32[2,2,2,128]{3,2,1,0:T(2,128)S(1)}, f32[2,2,2,128]{3,2,1,0:T(2,128)S(1)}, u32[]{:S(2)}, u32[]{:S(2)}) %collective-permute-start.9) | collective-permute-done | bytes 4128 | tf_op jit(solution)/shard_map/ppermute | solution.py:16
  31.5 0.9 %collective-permute-start.10 = (f32[2,2,2,128]{3,2,1,0:T(2,128)S(1)}, f32[2,2,2,128]{3,2,1,0:T(2,128)S(1)}, u32[]{:S(2)}, u32[]{:S(2)}) collective-permute-start(f32[2,2,2,128]{3,2,1,0:T(2,128)S(1)} %log_add_fusion.5), channel_id=1, source_target_pairs={{0,2},{1,3},{2,0},{3,1},{4,6},{5,7},{6,4},{7,5},{8,10},{9,11},{10,... | collective-permute-start | bytes 12296 | tf_op jit(solution)/shard_map/ppermute | solution.py:16
  32.4 2.8 %collective-permute-done.10 = f32[2,2,2,128]{3,2,1,0:T(2,128)S(1)} collective-permute-done((f32[2,2,2,128]{3,2,1,0:T(2,128)S(1)}, f32[2,2,2,128]{3,2,1,0:T(2,128)S(1)}, u32[]{:S(2)}, u32[]{:S(2)}) %collective-permute-start.10) | collective-permute-done | bytes 4128 | tf_op jit(solution)/shard_map/ppermute | solution.py:16
  35.2 3.3 %collective-permute-start.11 = (f32[2,2,2,128]{3,2,1,0:T(2,128)S(1)}, f32[2,2,2,128]{3,2,1,0:T(2,128)S(1)}, u32[]{:S(2)}, u32[]{:S(2)}) collective-permute-start(f32[2,2,2,128]{3,2,1,0:T(2,128)S(1)} %log_add_fusion.4), channel_id=1, source_target_pairs={{0,4},{1,5},{2,6},{3,7},{4,0},{5,1},{6,2},{7,3},{8,12},{9,13},{10,... | collective-permute-start | bytes 12296 | tf_op jit(solution)/shard_map/ppermute | solution.py:16
  38.5 1.5 %collective-permute-done.11 = f32[2,2,2,128]{3,2,1,0:T(2,128)S(1)} collective-permute-done((f32[2,2,2,128]{3,2,1,0:T(2,128)S(1)}, f32[2,2,2,128]{3,2,1,0:T(2,128)S(1)}, u32[]{:S(2)}, u32[]{:S(2)}) %collective-permute-start.11) | collective-permute-done | bytes 4128 | tf_op jit(solution)/shard_map/ppermute | solution.py:16
  42.6 1.6 %collective-permute-start.13 = (bf16[152,384]{1,0:T(8,128)(2,1)S(1)}, bf16[152,384]{1,0:T(8,128)(2,1)S(1)}, u32[]{:S(2)}, u32[]{:S(2)}) collective-permute-start(bf16[152,384]{1,0:T(8,128)(2,1)S(1)} %pad_maximum_fusion), channel_id=1, source_target_pairs={{0,16},{8,24},{16,0},{24,8},{1,17},{9,25},{17,1},{25,9},{2,18},{10... | collective-permute-start | bytes 350216 | tf_op jit(solution)/shard_map/ppermute | solution.py:16
  45.0 3.7 %collective-permute-done.13 = bf16[152,384]{1,0:T(8,128)(2,1)S(1)} collective-permute-done((bf16[152,384]{1,0:T(8,128)(2,1)S(1)}, bf16[152,384]{1,0:T(8,128)(2,1)S(1)}, u32[]{:S(2)}, u32[]{:S(2)}) %collective-permute-start.13) | collective-permute-done | bytes 116768 | tf_op jit(solution)/shard_map/ppermute | solution.py:16
  48.9 1.1 %collective-permute-done.16 = bf16[128,384]{1,0:T(8,128)(2,1)S(1)} collective-permute-done((bf16[128,384]{1,0:T(8,128)(2,1)S(1)}, bf16[128,384]{1,0:T(8,128)(2,1)S(1)}, u32[]{:S(2)}, u32[]{:S(2)}) %collective-permute-start.16) | collective-permute-done | bytes 98336 | tf_op jit(solution)/shard_map/ppermute | solution.py:16
  50.4 1.3 %collective-permute-done.17 = f32[128,384]{1,0:T(8,128)S(1)} collective-permute-done((f32[128,384]{1,0:T(8,128)S(1)}, f32[128,384]{1,0:T(8,128)S(1)}, u32[]{:S(2)}, u32[]{:S(2)}) %collective-permute-start.17) | collective-permute-done | bytes 196640 | tf_op jit(solution)/shard_map/ppermute | solution.py:16
  52.9 1.6 %collective-permute-start.18 = (f32[2,2,2,128]{3,2,1,0:T(2,128)S(1)}, f32[2,2,2,128]{3,2,1,0:T(2,128)S(1)}, u32[]{:S(2)}, u32[]{:S(2)}) collective-permute-start(f32[2,2,2,128]{3,2,1,0:T(2,128)S(1)} %pad_maximum_fusion.6), channel_id=1, source_target_pairs={{0,1},{1,0},{2,3},{3,2},{4,5},{5,4},{6,7},{7,6},{8,9},{9,8},{10,11... | collective-permute-start | bytes 12296 | tf_op jit(solution)/shard_map/ppermute | solution.py:16
  54.5 2.1 %collective-permute-done.18 = f32[2,2,2,128]{3,2,1,0:T(2,128)S(1)} collective-permute-done((f32[2,2,2,128]{3,2,1,0:T(2,128)S(1)}, f32[2,2,2,128]{3,2,1,0:T(2,128)S(1)}, u32[]{:S(2)}, u32[]{:S(2)}) %collective-permute-start.18) | collective-permute-done | bytes 4128 | tf_op jit(solution)/shard_map/ppermute | solution.py:16
  57.0 0.9 %collective-permute-start.19 = (f32[2,2,2,128]{3,2,1,0:T(2,128)S(1)}, f32[2,2,2,128]{3,2,1,0:T(2,128)S(1)}, u32[]{:S(2)}, u32[]{:S(2)}) collective-permute-start(f32[2,2,2,128]{3,2,1,0:T(2,128)S(1)} %log_add_fusion.2), channel_id=1, source_target_pairs={{0,2},{1,3},{2,0},{3,1},{4,6},{5,7},{6,4},{7,5},{8,10},{9,11},{10,... | collective-permute-start | bytes 12296 | tf_op jit(solution)/shard_map/ppermute | solution.py:16
  60.6 3.0 %collective-permute-start.20 = (f32[2,2,2,128]{3,2,1,0:T(2,128)S(1)}, f32[2,2,2,128]{3,2,1,0:T(2,128)S(1)}, u32[]{:S(2)}, u32[]{:S(2)}) collective-permute-start(f32[2,2,2,128]{3,2,1,0:T(2,128)S(1)} %log_add_fusion.1), channel_id=1, source_target_pairs={{0,4},{1,5},{2,6},{3,7},{4,0},{5,1},{6,2},{7,3},{8,12},{9,13},{10,... | collective-permute-start | bytes 12296 | tf_op jit(solution)/shard_map/ppermute | solution.py:16
  63.6 1.6 %collective-permute-done.20 = f32[2,2,2,128]{3,2,1,0:T(2,128)S(1)} collective-permute-done((f32[2,2,2,128]{3,2,1,0:T(2,128)S(1)}, f32[2,2,2,128]{3,2,1,0:T(2,128)S(1)}, u32[]{:S(2)}, u32[]{:S(2)}) %collective-permute-start.20) | collective-permute-done | bytes 4128 | tf_op jit(solution)/shard_map/ppermute | solution.py:16
  68.4 1.6 %collective-permute-start.22 = (bf16[136,384]{1,0:T(8,128)(2,1)S(1)}, bf16[136,384]{1,0:T(8,128)(2,1)S(1)}, u32[]{:S(2)}, u32[]{:S(2)}) collective-permute-start(bf16[136,384]{1,0:T(8,128)(2,1)S(1)} %pad_maximum_fusion.1), channel_id=1, source_target_pairs={{0,16},{8,24},{16,0},{24,8},{1,17},{9,25},{17,1},{25,9},{2,18},{10... | collective-permute-start | bytes 313352 | tf_op jit(solution)/shard_map/ppermute | solution.py:16
  70.6 3.6 %collective-permute-done.22 = bf16[136,384]{1,0:T(8,128)(2,1)S(1)} collective-permute-done((bf16[136,384]{1,0:T(8,128)(2,1)S(1)}, bf16[136,384]{1,0:T(8,128)(2,1)S(1)}, u32[]{:S(2)}, u32[]{:S(2)}) %collective-permute-start.22) | collective-permute-done | bytes 104480 | tf_op jit(solution)/shard_map/ppermute | solution.py:16
  74.4 1.1 %collective-permute-done.25 = bf16[128,384]{1,0:T(8,128)(2,1)S(1)} collective-permute-done((bf16[128,384]{1,0:T(8,128)(2,1)S(1)}, bf16[128,384]{1,0:T(8,128)(2,1)S(1)}, u32[]{:S(2)}, u32[]{:S(2)}) %collective-permute-start.25) | collective-permute-done | bytes 98336 | tf_op jit(solution)/shard_map/ppermute | solution.py:16
  76.4 0.7 collective-permute-done.26
  77.2 0.9 %maximum_maximum_fusion.1 = f32[256,768]{1,0:T(8,128)} fusion(f32[128,384]{1,0:T(8,128)S(1)} %get-tuple-element.71, f32[128,384]{1,0:T(8,128)S(1)} %get-tuple-element.70, f32[128,384]{1,0:T(8,128)S(1)} %get-tuple-element.69, f32[128,384]{1,0:T(8,128)S(1)} %get-tuple-element.68), kind=kLoop, calls=%fused_computation.19 | loop fusion | flops 589824 | bytes 1572864 | tf_op jit(solution)/shard_map/concatenate | solution.py:201
  (146 shorter events, 15.8 us)
Async XLA Ops:
  0.6 15.1 %copy-start = (f32[256,768]{1,0:T(8,128)S(1)}, f32[256,768]{1,0:T(8,128)}, u32[]{:S(2)}) copy-start(f32[256,768]{1,0:T(8,128)} %param.7) | copy-start | bytes 2359300
  0.6 13.5 %collective-permute-start.2 = (bf16[128,768]{1,0:T(8,128)(2,1)}, bf16[128,768]{1,0:T(8,128)(2,1)S(1)}, u32[]{:S(2)}, u32[]{:S(2)}) collective-permute-start(bf16[128,768]{1,0:T(8,128)(2,1)} %param.5), channel_id=1, source_target_pairs={{0,4},{1,5},{2,6},{3,7},{4,0},{5,1},{6,2},{7,3},{8,12},{9,13},{10,... | collective-permute-start | bytes 589832 | tf_op jit(solution)/shard_map/ppermute | solution.py:16
  4.7 1.4 %collective-permute-start = (bf16[4,768]{1,0:T(4,128)(2,1)}, bf16[4,768]{1,0:T(4,128)(2,1)S(1)}, u32[]{:S(2)}, u32[]{:S(2)}) collective-permute-start(bf16[4,768]{1,0:T(4,128)(2,1)} %param.6), channel_id=1, source_target_pairs={{0,8},{8,0},{16,24},{24,16},{1,9},{9,1},{17,25},{25,17},{2,10},{10... | collective-permute-start | bytes 18440 | tf_op jit(solution)/shard_map/ppermute | solution.py:16
  6.1 10.2 %collective-permute-start.3 = (bf16[128,768]{1,0:T(8,128)(2,1)}, bf16[128,768]{1,0:T(8,128)(2,1)S(1)}, u32[]{:S(2)}, u32[]{:S(2)}) collective-permute-start(bf16[128,768]{1,0:T(8,128)(2,1)} %param.5), channel_id=1, source_target_pairs={{0,2},{1,3},{2,0},{3,1},{4,6},{5,7},{6,4},{7,5},{8,10},{9,11},{10,... | collective-permute-start | bytes 589832 | tf_op jit(solution)/shard_map/ppermute | solution.py:16
  7.7 8.0 %collective-permute-start.1 = (bf16[128,768]{1,0:T(8,128)(2,1)}, bf16[128,768]{1,0:T(8,128)(2,1)S(1)}, u32[]{:S(2)}, u32[]{:S(2)}) collective-permute-start(bf16[128,768]{1,0:T(8,128)(2,1)} %param.5), channel_id=1, source_target_pairs={{0,1},{1,0},{2,3},{3,2},{4,5},{5,4},{6,7},{7,6},{8,9},{9,8},{10,11... | collective-permute-start | bytes 589832 | tf_op jit(solution)/shard_map/ppermute | solution.py:16
  14.2 7.5 %collective-permute-start.5 = (bf16[128,768]{1,0:T(8,128)(2,1)S(1)}, bf16[128,768]{1,0:T(8,128)(2,1)S(1)}, u32[]{:S(2)}, u32[]{:S(2)}) collective-permute-start(bf16[128,768]{1,0:T(8,128)(2,1)S(1)} %collective-permute-done.2), channel_id=1, source_target_pairs={{0,1},{1,0},{2,3},{3,2},{4,5},{5,4},{6,7},{7,6},{8,9},{9,8},{10,11... | collective-permute-start | bytes 589832 | tf_op jit(solution)/shard_map/ppermute | solution.py:16
  16.4 6.7 %collective-permute-start.6 = (bf16[128,768]{1,0:T(8,128)(2,1)S(1)}, bf16[128,768]{1,0:T(8,128)(2,1)S(1)}, u32[]{:S(2)}, u32[]{:S(2)}) collective-permute-start(bf16[128,768]{1,0:T(8,128)(2,1)S(1)} %collective-permute-done.2), channel_id=1, source_target_pairs={{0,2},{1,3},{2,0},{3,1},{4,6},{5,7},{6,4},{7,5},{8,10},{9,11},{10,... | collective-permute-start | bytes 589832 | tf_op jit(solution)/shard_map/ppermute | solution.py:16
  16.7 8.3 %collective-permute-start.4 = (bf16[128,768]{1,0:T(8,128)(2,1)S(1)}, bf16[128,768]{1,0:T(8,128)(2,1)S(1)}, u32[]{:S(2)}, u32[]{:S(2)}) collective-permute-start(bf16[128,768]{1,0:T(8,128)(2,1)S(1)} %collective-permute-done.3), channel_id=1, source_target_pairs={{0,1},{1,0},{2,3},{3,2},{4,5},{5,4},{6,7},{7,6},{8,9},{9,8},{10,11... | collective-permute-start | bytes 589832 | tf_op jit(solution)/shard_map/ppermute | solution.py:16
  21.7 5.5 %collective-permute-start.8 = (bf16[96,768]{1,0:T(8,128)(2,1)S(1)}, bf16[96,768]{1,0:T(8,128)(2,1)S(1)}, u32[]{:S(2)}, u32[]{:S(2)}) collective-permute-start(bf16[96,768]{1,0:T(8,128)(2,1)S(1)} %slice.260), channel_id=1, source_target_pairs={{0,2},{1,3},{2,0},{3,1},{4,6},{5,7},{6,4},{7,5},{8,10},{9,11},{10,... | collective-permute-start | bytes 442376 | tf_op jit(solution)/shard_map/ppermute | solution.py:16
  23.1 4.1 %collective-permute-start.7 = (bf16[32,768]{1,0:T(8,128)(2,1)S(1)}, bf16[32,768]{1,0:T(8,128)(2,1)S(1)}, u32[]{:S(2)}, u32[]{:S(2)}) collective-permute-start(bf16[32,768]{1,0:T(8,128)(2,1)S(1)} %slice.259), channel_id=1, source_target_pairs={{0,1},{1,0},{2,3},{3,2},{4,5},{5,4},{6,7},{7,6},{8,9},{9,8},{10,11... | collective-permute-start | bytes 147464 | tf_op jit(solution)/shard_map/ppermute | solution.py:16
  27.7 1.7 %copy-start.1 = (bf16[4,768]{1,0:T(4,128)(2,1)S(1)}, bf16[4,768]{1,0:T(4,128)(2,1)}, u32[]{:S(2)}) copy-start(bf16[4,768]{1,0:T(4,128)(2,1)} %param.6) | copy-start | bytes 18436
  27.8 3.7 %collective-permute-start.9 = (f32[2,2,2,128]{3,2,1,0:T(2,128)S(1)}, f32[2,2,2,128]{3,2,1,0:T(2,128)S(1)}, u32[]{:S(2)}, u32[]{:S(2)}) collective-permute-start(f32[2,2,2,128]{3,2,1,0:T(2,128)S(1)} %pad_maximum_fusion.5), channel_id=1, source_target_pairs={{0,1},{1,0},{2,3},{3,2},{4,5},{5,4},{6,7},{7,6},{8,9},{9,8},{10,11... | collective-permute-start | bytes 12296 | tf_op jit(solution)/shard_map/ppermute | solution.py:16
  31.5 3.7 %collective-permute-start.10 = (f32[2,2,2,128]{3,2,1,0:T(2,128)S(1)}, f32[2,2,2,128]{3,2,1,0:T(2,128)S(1)}, u32[]{:S(2)}, u32[]{:S(2)}) collective-permute-start(f32[2,2,2,128]{3,2,1,0:T(2,128)S(1)} %log_add_fusion.5), channel_id=1, source_target_pairs={{0,2},{1,3},{2,0},{3,1},{4,6},{5,7},{6,4},{7,5},{8,10},{9,11},{10,... | collective-permute-start | bytes 12296 | tf_op jit(solution)/shard_map/ppermute | solution.py:16
  35.2 4.9 %collective-permute-start.11 = (f32[2,2,2,128]{3,2,1,0:T(2,128)S(1)}, f32[2,2,2,128]{3,2,1,0:T(2,128)S(1)}, u32[]{:S(2)}, u32[]{:S(2)}) collective-permute-start(f32[2,2,2,128]{3,2,1,0:T(2,128)S(1)} %log_add_fusion.4), channel_id=1, source_target_pairs={{0,4},{1,5},{2,6},{3,7},{4,0},{5,1},{6,2},{7,3},{8,12},{9,13},{10,... | collective-permute-start | bytes 12296 | tf_op jit(solution)/shard_map/ppermute | solution.py:16
  41.0 1.5 %collective-permute-start.12 = (f32[136,384]{1,0:T(8,128)S(1)}, f32[136,384]{1,0:T(8,128)S(1)}, u32[]{:S(2)}, u32[]{:S(2)}) collective-permute-start(f32[136,384]{1,0:T(8,128)S(1)} %select_maximum_fusion.1), channel_id=1, source_target_pairs={{0,8},{8,0},{16,24},{24,16},{1,9},{9,1},{17,25},{25,17},{2,10},{10... | collective-permute-start | bytes 626696 | tf_op jit(solution)/shard_map/ppermute | solution.py:16
  41.7 2.5 %collective-permute-start.15 = (f32[128,384]{1,0:T(8,128)S(1)}, f32[128,384]{1,0:T(8,128)S(1)}, u32[]{:S(2)}, u32[]{:S(2)}) collective-permute-start(f32[128,384]{1,0:T(8,128)S(1)} %slice_select_fusion.3), channel_id=1, source_target_pairs={{0,8},{8,0},{16,24},{24,16},{1,9},{9,1},{17,25},{25,17},{2,10},{10... | collective-permute-start | bytes 589832 | tf_op jit(solution)/shard_map/ppermute | solution.py:16
  42.6 6.1 %collective-permute-start.13 = (bf16[152,384]{1,0:T(8,128)(2,1)S(1)}, bf16[152,384]{1,0:T(8,128)(2,1)S(1)}, u32[]{:S(2)}, u32[]{:S(2)}) collective-permute-start(bf16[152,384]{1,0:T(8,128)(2,1)S(1)} %pad_maximum_fusion), channel_id=1, source_target_pairs={{0,16},{8,24},{16,0},{24,8},{1,17},{9,25},{17,1},{25,9},{2,18},{10... | collective-permute-start | bytes 350216 | tf_op jit(solution)/shard_map/ppermute | solution.py:16
  44.2 5.8 %collective-permute-start.16 = (bf16[128,384]{1,0:T(8,128)(2,1)S(1)}, bf16[128,384]{1,0:T(8,128)(2,1)S(1)}, u32[]{:S(2)}, u32[]{:S(2)}) collective-permute-start(bf16[128,384]{1,0:T(8,128)(2,1)S(1)} %add_convert_fusion.1), channel_id=1, source_target_pairs={{0,16},{8,24},{16,0},{24,8},{1,17},{9,25},{17,1},{25,9},{2,18},{10... | collective-permute-start | bytes 294920 | tf_op jit(solution)/shard_map/ppermute | solution.py:16
  48.8 1.5 %collective-permute-start.14 = (f32[128,384]{1,0:T(8,128)S(1)}, f32[128,384]{1,0:T(8,128)S(1)}, u32[]{:S(2)}, u32[]{:S(2)}) collective-permute-start(f32[128,384]{1,0:T(8,128)S(1)} %fusion.32), channel_id=1, source_target_pairs={{0,8},{8,0},{16,24},{24,16},{1,9},{9,1},{17,25},{25,17},{2,10},{10... | collective-permute-start | bytes 589832 | tf_op jit(solution)/shard_map/ppermute | solution.py:16
  50.1 1.5 %collective-permute-start.17 = (f32[128,384]{1,0:T(8,128)S(1)}, f32[128,384]{1,0:T(8,128)S(1)}, u32[]{:S(2)}, u32[]{:S(2)}) collective-permute-start(f32[128,384]{1,0:T(8,128)S(1)} %fusion.31), channel_id=1, source_target_pairs={{0,8},{8,0},{16,24},{24,16},{1,9},{9,1},{17,25},{25,17},{2,10},{10... | collective-permute-start | bytes 589832 | tf_op jit(solution)/shard_map/ppermute | solution.py:16
  52.9 3.7 %collective-permute-start.18 = (f32[2,2,2,128]{3,2,1,0:T(2,128)S(1)}, f32[2,2,2,128]{3,2,1,0:T(2,128)S(1)}, u32[]{:S(2)}, u32[]{:S(2)}) collective-permute-start(f32[2,2,2,128]{3,2,1,0:T(2,128)S(1)} %pad_maximum_fusion.6), channel_id=1, source_target_pairs={{0,1},{1,0},{2,3},{3,2},{4,5},{5,4},{6,7},{7,6},{8,9},{9,8},{10,11... | collective-permute-start | bytes 12296 | tf_op jit(solution)/shard_map/ppermute | solution.py:16
  56.9 1.0 %copy-start.3 = (s32[128]{0:T(128)S(1)}, s32[128]{0:T(128)}, u32[]{:S(2)}) copy-start(s32[128]{0:T(128)} %param.9) | copy-start | bytes 1540
  57.0 3.6 %collective-permute-start.19 = (f32[2,2,2,128]{3,2,1,0:T(2,128)S(1)}, f32[2,2,2,128]{3,2,1,0:T(2,128)S(1)}, u32[]{:S(2)}, u32[]{:S(2)}) collective-permute-start(f32[2,2,2,128]{3,2,1,0:T(2,128)S(1)} %log_add_fusion.2), channel_id=1, source_target_pairs={{0,2},{1,3},{2,0},{3,1},{4,6},{5,7},{6,4},{7,5},{8,10},{9,11},{10,... | collective-permute-start | bytes 12296 | tf_op jit(solution)/shard_map/ppermute | solution.py:16
  58.0 0.7 copy-start.2
  60.6 4.6 %collective-permute-start.20 = (f32[2,2,2,128]{3,2,1,0:T(2,128)S(1)}, f32[2,2,2,128]{3,2,1,0:T(2,128)S(1)}, u32[]{:S(2)}, u32[]{:S(2)}) collective-permute-start(f32[2,2,2,128]{3,2,1,0:T(2,128)S(1)} %log_add_fusion.1), channel_id=1, source_target_pairs={{0,4},{1,5},{2,6},{3,7},{4,0},{5,1},{6,2},{7,3},{8,12},{9,13},{10,... | collective-permute-start | bytes 12296 | tf_op jit(solution)/shard_map/ppermute | solution.py:16
  66.6 1.5 %collective-permute-start.21 = (f32[136,384]{1,0:T(8,128)S(1)}, f32[136,384]{1,0:T(8,128)S(1)}, u32[]{:S(2)}, u32[]{:S(2)}) collective-permute-start(f32[136,384]{1,0:T(8,128)S(1)} %select_maximum_fusion), channel_id=1, source_target_pairs={{0,8},{8,0},{16,24},{24,16},{1,9},{9,1},{17,25},{25,17},{2,10},{10... | collective-permute-start | bytes 626696 | tf_op jit(solution)/shard_map/ppermute | solution.py:16
  67.0 3.0 %collective-permute-start.24 = (f32[128,384]{1,0:T(8,128)S(1)}, f32[128,384]{1,0:T(8,128)S(1)}, u32[]{:S(2)}, u32[]{:S(2)}) collective-permute-start(f32[128,384]{1,0:T(8,128)S(1)} %slice_select_fusion.2), channel_id=1, source_target_pairs={{0,8},{8,0},{16,24},{24,16},{1,9},{9,1},{17,25},{25,17},{2,10},{10... | collective-permute-start | bytes 589832 | tf_op jit(solution)/shard_map/ppermute | solution.py:16
  68.4 5.8 %collective-permute-start.22 = (bf16[136,384]{1,0:T(8,128)(2,1)S(1)}, bf16[136,384]{1,0:T(8,128)(2,1)S(1)}, u32[]{:S(2)}, u32[]{:S(2)}) collective-permute-start(bf16[136,384]{1,0:T(8,128)(2,1)S(1)} %pad_maximum_fusion.1), channel_id=1, source_target_pairs={{0,16},{8,24},{16,0},{24,8},{1,17},{9,25},{17,1},{25,9},{2,18},{10... | collective-permute-start | bytes 313352 | tf_op jit(solution)/shard_map/ppermute | solution.py:16
  70.0 5.5 %collective-permute-start.25 = (bf16[128,384]{1,0:T(8,128)(2,1)S(1)}, bf16[128,384]{1,0:T(8,128)(2,1)S(1)}, u32[]{:S(2)}, u32[]{:S(2)}) collective-permute-start(bf16[128,384]{1,0:T(8,128)(2,1)S(1)} %add_convert_fusion), channel_id=1, source_target_pairs={{0,16},{8,24},{16,0},{24,8},{1,17},{9,25},{17,1},{25,9},{2,18},{10... | collective-permute-start | bytes 294920 | tf_op jit(solution)/shard_map/ppermute | solution.py:16
  74.3 2.8 %collective-permute-start.23 = (f32[128,384]{1,0:T(8,128)S(1)}, f32[128,384]{1,0:T(8,128)S(1)}, u32[]{:S(2)}, u32[]{:S(2)}) collective-permute-start(f32[128,384]{1,0:T(8,128)S(1)} %fusion.29), channel_id=1, source_target_pairs={{0,8},{8,0},{16,24},{24,16},{1,9},{9,1},{17,25},{25,17},{2,10},{10... | collective-permute-start | bytes 589832 | tf_op jit(solution)/shard_map/ppermute | solution.py:16
  75.6 1.5 %collective-permute-start.26 = (f32[128,384]{1,0:T(8,128)S(1)}, f32[128,384]{1,0:T(8,128)S(1)}, u32[]{:S(2)}, u32[]{:S(2)}) collective-permute-start(f32[128,384]{1,0:T(8,128)S(1)} %fusion.28), channel_id=1, source_target_pairs={{0,8},{8,0},{16,24},{24,16},{1,9},{9,1},{17,25},{25,17},{2,10},{10... | collective-permute-start | bytes 589832 | tf_op jit(solution)/shard_map/ppermute | solution.py:16

commit v6 on v5

--- a/solution.py
+++ b/solution.py
@@ -24,24 +24,12 @@
     return jnp.concatenate([jnp.where(flag == 0, mine, other), jnp.where(flag == 0, other, mine)])
 
 
-def gathered_pieces(value, later, axis, size):
+def column_pieces(value, later, axis, size):
     far = size // 2
-    half = 1 * value.shape[0] // 4
     pieces = {0: later}
-    for mask in sorted(range(1, size), key=lambda m: (bin(m).count("1"), -m)):
+    for mask in sorted(range(2, size, 2), key=lambda m: (bin(m).count("1"), -m)):
         low = mask & -mask
-        rest = mask ^ low
-        if rest == far and mask == far + far // 2 and far > 1:
-            later_far, pieces[far // 2] = lax.optimization_barrier((pieces[far], pieces[far // 2]))
-            pieces[mask] = swap(later_far, axis, low)
-            continue
-        if rest & (rest - 1):
-            second = rest & -rest
-            pieces[mask] = jnp.concatenate(
-                [swap(pieces[rest][:half], axis, low), swap(pieces[mask ^ second][half:], axis, second)]
-            )
-        else:
-            pieces[mask] = swap(value if mask == far else pieces[rest], axis, low)
+        pieces[mask] = swap(value if mask == far else pieces[mask ^ low], axis, low)
     return pieces
 
 
@@ -69,13 +57,27 @@
     half = n_cent // 2
 
     asked = swap(queries, "dp", dp_bits[0])
-    asked, later = lax.optimization_barrier((asked, passages))
-
-    pieces = gathered_pieces(passages, later, "cent", n_cent)
-    pieces[1], means = lax.optimization_barrier((pieces[1], init_centroids))
-    near = jnp.concatenate([pieces[mask] for mask in range(half)])
-    far = jnp.concatenate([pieces[mask] for mask in range(half, n_cent)])
-    held = [near, far]
+    asked, later, means = lax.optimization_barrier((asked, passages, init_centroids))
+
+    evens = list(range(0, n_cent, 2))
+    pieces = column_pieces(passages, later, "cent", n_cent)
+    across = {mask: swap(pieces[mask], "cent", 1) for mask in evens[:-1]}
+    pieces[2], pieces[0] = lax.optimization_barrier((pieces[2], passages))
+    held = [jnp.concatenate([pieces[mask] for mask in evens])]
+
+    centers = means.shape[0]
+    kept = centers // 2
+    first = core == 0
+    norms = jnp.sum(means * means, axis=1)
+    centers_half = means.astype(jnp.bfloat16)
+    packed = jnp.where(first, centers_half[:kept], centers_half[kept:])
+    line = jnp.where(first, norms[:kept], norms[kept:])
+    packed = jnp.concatenate([packed, jnp.pad(jnp.stack(in_three(line)), ((0, 5), (0, width - kept)))])
+    mine = swap(packed, "cent", 1)
+    other = swap(mine, "dp", dp_bits[0])
+    partner_half = in_order(mine[:kept], other[:kept], core)
+    lines = [part[kept : kept + 3, :kept].astype(jnp.float32) for part in (mine, other)]
+    partner_norms = in_order(*[(three[0] + three[1]) + three[2] for three in lines], core)
 
     def loss_partials(asked, pattern, positive_offset, dp, cent):
         mine = (n_dp, n_cent, own_queries)
@@ -85,7 +87,7 @@
         target = picks[:, 0] * BLOCK + offset
         partials, positive = [], 0.0
         for index, group in enumerate(held):
-            masks = jnp.arange(index * half, (index + 1) * half, dtype=jnp.int32)
+            masks = jnp.array(evens, jnp.int32) | index
             owner = (dp * n_cent + (cent ^ masks)) * rows
             column = (owner[:, None] + jnp.arange(rows, dtype=jnp.int32)[None, :]).reshape(-1)
             scores = SCALE * lax.dot_general(
@@ -98,34 +100,51 @@
             positive = positive + jnp.sum(jnp.where(column[None, :] == target[:, None], scores, 0.0), axis=1)
         return positive, join_lse(*partials)
 
-    centers = means.shape[0]
-    kept = centers // 2
-    first = core == 0
+    def logits_of(centers_half, norms, group):
+        products = lax.dot_general(centers_half, group, (((1,), (1,)), ((), ())), preferred_element_type=jnp.float32)
+        return SHARPNESS * (2.0 * products - norms[:, None])
+
+    def stats_of(*logits):
+        top = jnp.max(logits[0], axis=0)
+        for more in logits[1:]:
+            top = jnp.maximum(top, jnp.max(more, axis=0))
+        return top + jnp.log(sum(jnp.sum(jnp.exp(part - top[None, :]), axis=0) for part in logits))
+
+    def over_column(bit, lse):
+        axis = 0 if bit == 1 else len(cent_bits) - cent_bits.index(bit)
+        return join_lse(lse, jnp.flip(swap(lse, "cent", bit), axis=axis))
+
     asks = n_dp * own_queries
     for step in range(ITERS):
         last = step == ITERS - 1
-        centers_half = means.astype(jnp.bfloat16)
-        norms = jnp.sum(means * means, axis=1)
-        odds, stats = [], []
-        for group in held:
-            logits = SHARPNESS * (
-                2.0
-                * lax.dot_general(
-                    centers_half, group, (((1,), (1,)), ((), ())), preferred_element_type=jnp.float32
-                )
-                - norms[:, None]
-            )
-            top = jnp.max(logits, axis=0)
-            odds.append(logits)
-            stats.append(top + jnp.log(jnp.sum(jnp.exp(logits - top[None, :]), axis=0)))
-        lse = jnp.concatenate(stats).reshape((2,) * len(cent_bits) + (rows,))
-        for bit in cent_bits:
-            position = len(cent_bits) - 1 - cent_bits.index(bit)
-            lse = join_lse(lse, jnp.flip(swap(lse, "cent", bit), axis=position))
-            if last and bit == cent_bits[0]:
-                inputs = (lse, asked, pattern, positive_offset, dp, cent)
-                lse, *inputs = lax.optimization_barrier(inputs)
-                positive, found = loss_partials(*inputs)
+        shape = (-1,) + (2,) * (len(cent_bits) - 1) + (rows,)
+        if step == 0:
+            odds = [logits_of(centers_half, norms, held[0])]
+            lse = stats_of(odds[0], logits_of(partner_half, partner_norms, held[0])).reshape(shape)
+            lse, tail = lax.optimization_barrier((lse, pieces[evens[-1]]))
+            across[evens[-1]] = swap(tail, "cent", 1)
+            stops = [0, half // 4, half - half // 4, half]
+            for index, bit in enumerate(cent_bits[1:] + [None]):
+                ties = evens[stops[index] : stops[index + 1]] if index < 3 else []
+                lse, *parts = lax.optimization_barrier([lse] + [across[mask] for mask in ties])
+                across.update(zip(ties, parts))
+                if bit is not None:
+                    lse = over_column(bit, lse)
+            held.append(jnp.concatenate([across[mask] for mask in evens]))
+            lse = jnp.concatenate([lse, swap(lse, "cent", 1)])
+            odds.append(logits_of(centers_half, norms, held[-1]))
+            lse, odds[-1] = lax.optimization_barrier((lse, odds[-1]))
+        else:
+            norms = jnp.sum(means * means, axis=1)
+            centers_half = means.astype(jnp.bfloat16)
+            odds = [logits_of(centers_half, norms, group) for group in held]
+            lse = jnp.concatenate([stats_of(part) for part in odds]).reshape(shape)
+            for bit in cent_bits:
+                lse = over_column(bit, lse)
+                if last and bit == cent_bits[0]:
+                    inputs = (lse, asked, pattern, positive_offset, dp, cent)
+                    lse, *inputs = lax.optimization_barrier(inputs)
+                    positive, found = loss_partials(*inputs)
         lse = lse.reshape(2, half * rows)
         resps, counts = [], 0.0
         for index in range(2):
@@ -155,12 +174,12 @@
                 numer = numer + jnp.dot(
                     resps[index], held[index][:, part * cut : (part + 1) * cut], preferred_element_type=jnp.float32
                 )
-            if part == 0:
-                numer, resps = lax.optimization_barrier((numer, resps))
             total = jnp.where(first, numer[:kept], numer[kept:])
             sent = jnp.where(first, numer[kept:], numer[:kept])
             if part == 0:
                 sent = jnp.concatenate([sent, jnp.pad(rest[None, :], ((0, 7), (0, cut - rest.shape[0])))])
+            if part == 0:
+                resps, _ = lax.optimization_barrier((resps, sent))
             other = swap(sent, "dp", dp_bits[0])
             totals.append(total + other[:kept])
             if part == 0:

time: 78.3 us -> 74.3 us (0.949)
  waiting for transfers between devices: 34.6 us -> 27.5 us
  local copies, waits for them, and re-layouts: 2.8 us -> 5.06 us
  other arithmetic: 4.46 us -> 5.82 us
  starting transfers between devices: 30.2 us -> 29.1 us
    ppermute x27 -> x28, waiting for transfers between devices: 34.6 us -> 27.5 us  [swap(): return lax.ppermute(value, axis, [(i, i ^ bit) for i in range(size)])]
    reduce_sum x2, other arithmetic: 0.28 us -> 1.65 us  [on_device(): norms = jnp.sum(means * means, axis=1)]
    unnamed x15 -> x16, local copies, waits for them, and re-layouts: 1.66 us -> 3 us
    ppermute x27 -> x28, starting transfers between devices: 30.2 us -> 29.1 us  [swap(): return lax.ppermute(value, axis, [(i, i ^ bit) for i in range(size)])]
    concatenate x2, local copies, waits for them, and re-layouts: 0.03 us -> 0.95 us  [the longest x1 0.94 us: on_device(): held.append(jnp.concatenate([across[mask] for mask in evens]))]
    dot_general x4 -> x5, matrix products: 1.69 us -> 2.08 us  [logits_of(): lax.dot_general(centers_half, group, (((1,), (1,)), ((), ())), preferred_...]
  transfers between devices with their start and end apart: 27 -> 28, of which waited for: 22 -> 17; matrix products, arithmetic and copies ran while one was open for 8% -> 14% of each run, Pallas kernels for 0% -> 0%
where the time goes in v6:
time: 74.3 us; the launch traced here: 74.1 us
  starting transfers between devices  29.1 us (39%)
  waiting for transfers between devices  27.5 us (37%)
  other arithmetic  5.82 us (8%)
  matrix products  5.27 us (7%)
  local copies, waits for them, and re-layouts  5.06 us (7%)
  between operations  1.26 us (2%)
    ppermute x28, starting transfers between devices, swap(): return lax.ppermute(value, axis, [(i, i ^ bit) for i in range(size)])  29.1 us
    ppermute x28, waiting for transfers between devices, swap(): return lax.ppermute(value, axis, [(i, i ^ bit) for i in range(size)])  27.5 us
    unnamed x16, local copies, waits for them, and re-layouts  3 us
    dot_general x8, matrix products, on_device(): jnp.dot(resps[index], held[index][:, part * cut:(part + 1) * cut], prefer...  2.34 us
    dot_general x5, matrix products, logits_of(): lax.dot_general(centers_half, group, (((1,), (1,)), ((), ())), preferred_...  2.08 us
    reduce_sum x2, other arithmetic, on_device(): norms = jnp.sum(means * means, axis=1)  1.65 us
  transfers between devices with their start and end apart: 28, of which 17 were waited for; matrix products, arithmetic and copies ran while one was open for 14% of the time, Pallas kernels for 0%

profile of v6, /device:TPU:0, one launch (start us, length us, event | category | flops | bytes accessed | tf_op | source)
XLA Modules:
  0.0 74.1 jit_solution(7006112700277323573)
XLA Ops:
  1.1 3.7 %collective-permute-start.2 = (bf16[128,768]{1,0:T(8,128)(2,1)}, bf16[128,768]{1,0:T(8,128)(2,1)S(1)}, u32[]{:S(2)}, u32[]{:S(2)}) collective-permute-start(bf16[128,768]{1,0:T(8,128)(2,1)} %param.7), channel_id=1, source_target_pairs={{0,4},{1,5},{2,6},{3,7},{4,0},{5,1},{6,2},{7,3},{8,12},{9,13},{10,... | collective-permute-start | bytes 589832 | tf_op jit(solution)/shard_map/ppermute | solution.py:16
  4.8 1.6 %collective-permute-start.1 = (bf16[128,768]{1,0:T(8,128)(2,1)}, bf16[128,768]{1,0:T(8,128)(2,1)S(1)}, u32[]{:S(2)}, u32[]{:S(2)}) collective-permute-start(bf16[128,768]{1,0:T(8,128)(2,1)} %param.7), channel_id=1, source_target_pairs={{0,2},{1,3},{2,0},{3,1},{4,6},{5,7},{6,4},{7,5},{8,10},{9,11},{10,... | collective-permute-start | bytes 589832 | tf_op jit(solution)/shard_map/ppermute | solution.py:16
  6.4 1.5 %collective-permute-start.6 = (bf16[128,768]{1,0:T(8,128)(2,1)}, bf16[128,768]{1,0:T(8,128)(2,1)S(1)}, u32[]{:S(2)}, u32[]{:S(2)}) collective-permute-start(bf16[128,768]{1,0:T(8,128)(2,1)} %param.7), channel_id=1, source_target_pairs={{0,1},{1,0},{2,3},{3,2},{4,5},{5,4},{6,7},{7,6},{8,9},{9,8},{10,11... | collective-permute-start | bytes 589832 | tf_op jit(solution)/shard_map/ppermute | solution.py:16
  7.9 1.5 %multiply_reduce_fusion.1 = (f32[256]{0:T(256)S(1)}, bf16[256,768]{1,0:T(8,128)(2,1)S(1)}) fusion(f32[256,768]{1,0:T(8,128)} %param.9), kind=kLoop, calls=%fused_computation.24 | loop fusion | flops 589568 | bytes 1180672 | tf_op jit(solution)/shard_map/reduce_sum | solution.py:71
  10.6 4.2 %collective-permute-done.2 = bf16[128,768]{1,0:T(8,128)(2,1)S(1)} collective-permute-done((bf16[128,768]{1,0:T(8,128)(2,1)}, bf16[128,768]{1,0:T(8,128)(2,1)S(1)}, u32[]{:S(2)}, u32[]{:S(2)}) %collective-permute-start.2) | collective-permute-done | bytes 196640 | tf_op jit(solution)/shard_map/ppermute | solution.py:16
  14.8 0.8 %collective-permute-start.3 = (bf16[128,768]{1,0:T(8,128)(2,1)S(1)}, bf16[128,768]{1,0:T(8,128)(2,1)S(1)}, u32[]{:S(2)}, u32[]{:S(2)}) collective-permute-start(bf16[128,768]{1,0:T(8,128)(2,1)S(1)} %collective-permute-done.2), channel_id=1, source_target_pairs={{0,2},{1,3},{2,0},{3,1},{4,6},{5,7},{6,4},{7,5},{8,10},{9,11},{10,... | collective-permute-start | bytes 589832 | tf_op jit(solution)/shard_map/ppermute | solution.py:16
  15.6 1.5 %collective-permute-start.9 = (bf16[128,768]{1,0:T(8,128)(2,1)S(1)}, bf16[128,768]{1,0:T(8,128)(2,1)}, u32[]{:S(2)}, u32[]{:S(2)}) collective-permute-start(bf16[128,768]{1,0:T(8,128)(2,1)S(1)} %collective-permute-done.2), channel_id=1, source_target_pairs={{0,1},{1,0},{2,3},{3,2},{4,5},{5,4},{6,7},{7,6},{8,9},{9,8},{10,11... | collective-permute-start | bytes 589832 | tf_op jit(solution)/shard_map/ppermute | solution.py:16
  17.9 3.6 %collective-permute-done.3 = bf16[128,768]{1,0:T(8,128)(2,1)S(1)} collective-permute-done((bf16[128,768]{1,0:T(8,128)(2,1)S(1)}, bf16[128,768]{1,0:T(8,128)(2,1)S(1)}, u32[]{:S(2)}, u32[]{:S(2)}) %collective-permute-start.3) | collective-permute-done | bytes 196640 | tf_op jit(solution)/shard_map/ppermute | solution.py:16
  22.6 1.1 %collective-permute-start.7 = (f32[1,2,2,128]{3,2,1,0:T(2,128)S(1)}, f32[1,2,2,128]{3,2,1,0:T(2,128)S(1)}, u32[]{:S(2)}, u32[]{:S(2)}) collective-permute-start(f32[1,2,2,128]{3,2,1,0:T(2,128)S(1)} %bitcast.143), channel_id=1, source_target_pairs={{0,2},{1,3},{2,0},{3,1},{4,6},{5,7},{6,4},{7,5},{8,10},{9,11},{10,... | collective-permute-start | bytes 6152 | tf_op jit(solution)/shard_map/ppermute | solution.py:16
  23.7 1.6 %collective-permute-start.11 = (bf16[128,768]{1,0:T(8,128)(2,1)S(1)}, bf16[128,768]{1,0:T(8,128)(2,1)}, u32[]{:S(2)}, u32[]{:S(2)}) collective-permute-start(bf16[128,768]{1,0:T(8,128)(2,1)S(1)} %collective-permute-done.3), channel_id=1, source_target_pairs={{0,1},{1,0},{2,3},{3,2},{4,5},{5,4},{6,7},{7,6},{8,9},{9,8},{10,11... | collective-permute-start | bytes 589832 | tf_op jit(solution)/shard_map/ppermute | solution.py:16
  25.3 0.9 %collective-permute-done.7 = f32[1,2,2,128]{3,2,1,0:T(2,128)S(1)} collective-permute-done((f32[1,2,2,128]{3,2,1,0:T(2,128)S(1)}, f32[1,2,2,128]{3,2,1,0:T(2,128)S(1)}, u32[]{:S(2)}, u32[]{:S(2)}) %collective-permute-start.7) | collective-permute-done | bytes 2080 | tf_op jit(solution)/shard_map/ppermute | solution.py:16
  26.3 1.2 %collective-permute-done.8 = bf16[128,768]{1,0:T(8,128)(2,1)} collective-permute-done((bf16[128,768]{1,0:T(8,128)(2,1)S(1)}, bf16[128,768]{1,0:T(8,128)(2,1)}, u32[]{:S(2)}, u32[]{:S(2)}) %collective-permute-start.8) | collective-permute-done | bytes 196640 | tf_op jit(solution)/shard_map/ppermute | solution.py:16
  27.4 3.3 %collective-permute-start.10 = (f32[1,2,2,128]{3,2,1,0:T(2,128)S(1)}, f32[1,2,2,128]{3,2,1,0:T(2,128)S(1)}, u32[]{:S(2)}, u32[]{:S(2)}) collective-permute-start(f32[1,2,2,128]{3,2,1,0:T(2,128)S(1)} %log_add_fusion.6), channel_id=1, source_target_pairs={{0,4},{1,5},{2,6},{3,7},{4,0},{5,1},{6,2},{7,3},{8,12},{9,13},{10,... | collective-permute-start | bytes 6152 | tf_op jit(solution)/shard_map/ppermute | solution.py:16
  30.8 0.9 %constant_dynamic-update-slice_fusion.6 = bf16[512,768]{1,0:T(8,128)(2,1)S(1)} fusion(bf16[512,768]{1,0:T(8,128)(2,1)S(1)} %constant_dynamic-update-slice_fusion.7, bf16[128,768]{1,0:T(8,128)(2,1)} %collective-permute-done.8), kind=kLoop, calls=%fused_computation.116 | loop fusion | bytes 393216
  31.7 0.9 %constant_dynamic-update-slice_fusion.5 = bf16[512,768]{1,0:T(8,128)(2,1)S(1)} fusion(bf16[512,768]{1,0:T(8,128)(2,1)S(1)} %constant_dynamic-update-slice_fusion.6, bf16[128,768]{1,0:T(8,128)(2,1)} %collective-permute-done.9), kind=kLoop, calls=%fused_computation.115 | loop fusion | bytes 393216
  32.7 1.6 %collective-permute-start.12 = (f32[1,2,2,128]{3,2,1,0:T(2,128)S(1)}, f32[1,2,2,128]{3,2,1,0:T(2,128)S(1)}, u32[]{:S(2)}, u32[]{:S(2)}) collective-permute-start(f32[1,2,2,128]{3,2,1,0:T(2,128)S(1)} %log_add_fusion.5), channel_id=1, source_target_pairs={{0,1},{1,0},{2,3},{3,2},{4,5},{5,4},{6,7},{7,6},{8,9},{9,8},{10,11... | collective-permute-start | bytes 6152 | tf_op jit(solution)/shard_map/ppermute | solution.py:16
  34.3 0.9 %constant_dynamic-update-slice_fusion.4 = bf16[512,768]{1,0:T(8,128)(2,1)S(1)} fusion(bf16[512,768]{1,0:T(8,128)(2,1)S(1)} %constant_dynamic-update-slice_fusion.5, bf16[128,768]{1,0:T(8,128)(2,1)} %collective-permute-done.11), kind=kLoop, calls=%fused_computation.114 | loop fusion | bytes 393216 | tf_op jit(solution)/shard_map/concatenate | solution.py:133
  35.6 0.7 collective-permute-done.12
  38.9 1.6 %collective-permute-start.14 = (bf16[152,384]{1,0:T(8,128)(2,1)S(1)}, bf16[152,384]{1,0:T(8,128)(2,1)S(1)}, u32[]{:S(2)}, u32[]{:S(2)}) collective-permute-start(bf16[152,384]{1,0:T(8,128)(2,1)S(1)} %pad_maximum_fusion.1), channel_id=1, source_target_pairs={{0,16},{8,24},{16,0},{24,8},{1,17},{9,25},{17,1},{25,9},{2,18},{10... | collective-permute-start | bytes 350216 | tf_op jit(solution)/shard_map/ppermute | solution.py:16
  40.5 0.7 collective-permute-start.17
  41.3 3.7 %collective-permute-done.14 = bf16[152,384]{1,0:T(8,128)(2,1)S(1)} collective-permute-done((bf16[152,384]{1,0:T(8,128)(2,1)S(1)}, bf16[152,384]{1,0:T(8,128)(2,1)S(1)}, u32[]{:S(2)}, u32[]{:S(2)}) %collective-permute-start.14) | collective-permute-done | bytes 116768 | tf_op jit(solution)/shard_map/ppermute | solution.py:16
  45.2 1.1 %collective-permute-done.17 = bf16[128,384]{1,0:T(8,128)(2,1)S(1)} collective-permute-done((bf16[128,384]{1,0:T(8,128)(2,1)S(1)}, bf16[128,384]{1,0:T(8,128)(2,1)S(1)}, u32[]{:S(2)}, u32[]{:S(2)}) %collective-permute-start.17) | collective-permute-done | bytes 98336 | tf_op jit(solution)/shard_map/ppermute | solution.py:16
  46.7 1.3 %collective-permute-done.18 = f32[128,384]{1,0:T(8,128)S(1)} collective-permute-done((f32[128,384]{1,0:T(8,128)S(1)}, f32[128,384]{1,0:T(8,128)S(1)}, u32[]{:S(2)}, u32[]{:S(2)}) %collective-permute-start.18) | collective-permute-done | bytes 196640 | tf_op jit(solution)/shard_map/ppermute | solution.py:16
  49.2 1.6 %collective-permute-start.19 = (f32[2,2,2,128]{3,2,1,0:T(2,128)S(1)}, f32[2,2,2,128]{3,2,1,0:T(2,128)S(1)}, u32[]{:S(2)}, u32[]{:S(2)}) collective-permute-start(f32[2,2,2,128]{3,2,1,0:T(2,128)S(1)} %pad_maximum_fusion.7), channel_id=1, source_target_pairs={{0,1},{1,0},{2,3},{3,2},{4,5},{5,4},{6,7},{7,6},{8,9},{9,8},{10,11... | collective-permute-start | bytes 12296 | tf_op jit(solution)/shard_map/ppermute | solution.py:16
  50.8 2.1 %collective-permute-done.19 = f32[2,2,2,128]{3,2,1,0:T(2,128)S(1)} collective-permute-done((f32[2,2,2,128]{3,2,1,0:T(2,128)S(1)}, f32[2,2,2,128]{3,2,1,0:T(2,128)S(1)}, u32[]{:S(2)}, u32[]{:S(2)}) %collective-permute-start.19) | collective-permute-done | bytes 4128 | tf_op jit(solution)/shard_map/ppermute | solution.py:16
  56.1 0.8 %collective-permute-done.20 = f32[2,2,2,128]{3,2,1,0:T(2,128)S(1)} collective-permute-done((f32[2,2,2,128]{3,2,1,0:T(2,128)S(1)}, f32[2,2,2,128]{3,2,1,0:T(2,128)S(1)}, u32[]{:S(2)}, u32[]{:S(2)}) %collective-permute-start.20) | collective-permute-done | bytes 4128 | tf_op jit(solution)/shard_map/ppermute | solution.py:16
  56.9 2.6 %collective-permute-start.21 = (f32[2,2,2,128]{3,2,1,0:T(2,128)S(1)}, f32[2,2,2,128]{3,2,1,0:T(2,128)S(1)}, u32[]{:S(2)}, u32[]{:S(2)}) collective-permute-start(f32[2,2,2,128]{3,2,1,0:T(2,128)S(1)} %log_add_fusion.1), channel_id=1, source_target_pairs={{0,4},{1,5},{2,6},{3,7},{4,0},{5,1},{6,2},{7,3},{8,12},{9,13},{10,... | collective-permute-start | bytes 12296 | tf_op jit(solution)/shard_map/ppermute | solution.py:16
  59.6 1.9 %collective-permute-done.21 = f32[2,2,2,128]{3,2,1,0:T(2,128)S(1)} collective-permute-done((f32[2,2,2,128]{3,2,1,0:T(2,128)S(1)}, f32[2,2,2,128]{3,2,1,0:T(2,128)S(1)}, u32[]{:S(2)}, u32[]{:S(2)}) %collective-permute-start.21) | collective-permute-done | bytes 4128 | tf_op jit(solution)/shard_map/ppermute | solution.py:16
  64.4 1.6 %collective-permute-start.23 = (bf16[136,384]{1,0:T(8,128)(2,1)S(1)}, bf16[136,384]{1,0:T(8,128)(2,1)S(1)}, u32[]{:S(2)}, u32[]{:S(2)}) collective-permute-start(bf16[136,384]{1,0:T(8,128)(2,1)S(1)} %pad_maximum_fusion.2), channel_id=1, source_target_pairs={{0,16},{8,24},{16,0},{24,8},{1,17},{9,25},{17,1},{25,9},{2,18},{10... | collective-permute-start | bytes 313352 | tf_op jit(solution)/shard_map/ppermute | solution.py:16
  66.6 3.6 %collective-permute-done.23 = bf16[136,384]{1,0:T(8,128)(2,1)S(1)} collective-permute-done((bf16[136,384]{1,0:T(8,128)(2,1)S(1)}, bf16[136,384]{1,0:T(8,128)(2,1)S(1)}, u32[]{:S(2)}, u32[]{:S(2)}) %collective-permute-start.23) | collective-permute-done | bytes 104480 | tf_op jit(solution)/shard_map/ppermute | solution.py:16
  70.4 1.1 %collective-permute-done.26 = bf16[128,384]{1,0:T(8,128)(2,1)S(1)} collective-permute-done((bf16[128,384]{1,0:T(8,128)(2,1)S(1)}, bf16[128,384]{1,0:T(8,128)(2,1)S(1)}, u32[]{:S(2)}, u32[]{:S(2)}) %collective-permute-start.26) | collective-permute-done | bytes 98336 | tf_op jit(solution)/shard_map/ppermute | solution.py:16
  73.1 0.9 %maximum_maximum_fusion.1 = f32[256,768]{1,0:T(8,128)} fusion(f32[128,384]{1,0:T(8,128)S(1)} %get-tuple-element.95, f32[128,384]{1,0:T(8,128)S(1)} %get-tuple-element.94, f32[128,384]{1,0:T(8,128)S(1)} %get-tuple-element.93, f32[128,384]{1,0:T(8,128)S(1)} %get-tuple-element.92), kind=kLoop, calls=%fused_computation.22 | loop fusion | flops 589824 | bytes 1572864 | tf_op jit(solution)/shard_map/concatenate | solution.py:220
  (156 shorter events, 16.7 us)
Async XLA Ops:
  0.6 4.2 %collective-permute-start = (bf16[4,768]{1,0:T(4,128)(2,1)}, bf16[4,768]{1,0:T(4,128)(2,1)S(1)}, u32[]{:S(2)}, u32[]{:S(2)}) collective-permute-start(bf16[4,768]{1,0:T(4,128)(2,1)} %param.8), channel_id=1, source_target_pairs={{0,8},{8,0},{16,24},{24,16},{1,9},{9,1},{17,25},{25,17},{2,10},{10... | collective-permute-start | bytes 18440 | tf_op jit(solution)/shard_map/ppermute | solution.py:16
  1.1 13.7 %collective-permute-start.2 = (bf16[128,768]{1,0:T(8,128)(2,1)}, bf16[128,768]{1,0:T(8,128)(2,1)S(1)}, u32[]{:S(2)}, u32[]{:S(2)}) collective-permute-start(bf16[128,768]{1,0:T(8,128)(2,1)} %param.7), channel_id=1, source_target_pairs={{0,4},{1,5},{2,6},{3,7},{4,0},{5,1},{6,2},{7,3},{8,12},{9,13},{10,... | collective-permute-start | bytes 589832 | tf_op jit(solution)/shard_map/ppermute | solution.py:16
  4.8 12.3 %collective-permute-start.1 = (bf16[128,768]{1,0:T(8,128)(2,1)}, bf16[128,768]{1,0:T(8,128)(2,1)S(1)}, u32[]{:S(2)}, u32[]{:S(2)}) collective-permute-start(bf16[128,768]{1,0:T(8,128)(2,1)} %param.7), channel_id=1, source_target_pairs={{0,2},{1,3},{2,0},{3,1},{4,6},{5,7},{6,4},{7,5},{8,10},{9,11},{10,... | collective-permute-start | bytes 589832 | tf_op jit(solution)/shard_map/ppermute | solution.py:16
  6.4 16.2 %collective-permute-start.6 = (bf16[128,768]{1,0:T(8,128)(2,1)}, bf16[128,768]{1,0:T(8,128)(2,1)S(1)}, u32[]{:S(2)}, u32[]{:S(2)}) collective-permute-start(bf16[128,768]{1,0:T(8,128)(2,1)} %param.7), channel_id=1, source_target_pairs={{0,1},{1,0},{2,3},{3,2},{4,5},{5,4},{6,7},{7,6},{8,9},{9,8},{10,11... | collective-permute-start | bytes 589832 | tf_op jit(solution)/shard_map/ppermute | solution.py:16
  9.4 1.2 %copy-start = (f32[256,768]{1,0:T(8,128)S(1)}, f32[256,768]{1,0:T(8,128)}, u32[]{:S(2)}) copy-start(f32[256,768]{1,0:T(8,128)} %param.9) | copy-start | bytes 2359300
  9.5 0.8 %copy-start.2 = (bf16[4,768]{1,0:T(4,128)(2,1)S(1)}, bf16[4,768]{1,0:T(4,128)(2,1)}, u32[]{:S(2)}) copy-start(bf16[4,768]{1,0:T(4,128)(2,1)} %param.8) | copy-start | bytes 18436
  9.5 8.3 %collective-permute-start.4 = (bf16[136,768]{1,0:T(8,128)(2,1)S(1)}, bf16[136,768]{1,0:T(8,128)(2,1)S(1)}, u32[]{:S(2)}, u32[]{:S(2)}) collective-permute-start(bf16[136,768]{1,0:T(8,128)(2,1)S(1)} %pad_maximum_fusion), channel_id=1, source_target_pairs={{0,1},{1,0},{2,3},{3,2},{4,5},{5,4},{6,7},{7,6},{8,9},{9,8},{10,11... | collective-permute-start | bytes 626696 | tf_op jit(solution)/shard_map/ppermute | solution.py:16
  10.5 6.6 %copy-start.1 = (bf16[128,768]{1,0:T(8,128)(2,1)S(1)}, bf16[128,768]{1,0:T(8,128)(2,1)}, u32[]{:S(2)}) copy-start(bf16[128,768]{1,0:T(8,128)(2,1)} %param.7) | copy-start | bytes 589828
  14.8 6.6 %collective-permute-start.3 = (bf16[128,768]{1,0:T(8,128)(2,1)S(1)}, bf16[128,768]{1,0:T(8,128)(2,1)S(1)}, u32[]{:S(2)}, u32[]{:S(2)}) collective-permute-start(bf16[128,768]{1,0:T(8,128)(2,1)S(1)} %collective-permute-done.2), channel_id=1, source_target_pairs={{0,2},{1,3},{2,0},{3,1},{4,6},{5,7},{6,4},{7,5},{8,10},{9,11},{10,... | collective-permute-start | bytes 589832 | tf_op jit(solution)/shard_map/ppermute | solution.py:16
  15.6 10.7 %collective-permute-start.9 = (bf16[128,768]{1,0:T(8,128)(2,1)S(1)}, bf16[128,768]{1,0:T(8,128)(2,1)}, u32[]{:S(2)}, u32[]{:S(2)}) collective-permute-start(bf16[128,768]{1,0:T(8,128)(2,1)S(1)} %collective-permute-done.2), channel_id=1, source_target_pairs={{0,1},{1,0},{2,3},{3,2},{4,5},{5,4},{6,7},{7,6},{8,9},{9,8},{10,11... | collective-permute-start | bytes 589832 | tf_op jit(solution)/shard_map/ppermute | solution.py:16
  17.1 10.3 %collective-permute-start.8 = (bf16[128,768]{1,0:T(8,128)(2,1)S(1)}, bf16[128,768]{1,0:T(8,128)(2,1)}, u32[]{:S(2)}, u32[]{:S(2)}) collective-permute-start(bf16[128,768]{1,0:T(8,128)(2,1)S(1)} %collective-permute-done.1), channel_id=1, source_target_pairs={{0,1},{1,0},{2,3},{3,2},{4,5},{5,4},{6,7},{7,6},{8,9},{9,8},{10,11... | collective-permute-start | bytes 589832 | tf_op jit(solution)/shard_map/ppermute | solution.py:16
  17.8 4.1 %collective-permute-start.5 = (bf16[136,768]{1,0:T(8,128)(2,1)S(1)}, bf16[136,768]{1,0:T(8,128)(2,1)S(1)}, u32[]{:S(2)}, u32[]{:S(2)}) collective-permute-start(bf16[136,768]{1,0:T(8,128)(2,1)S(1)} %collective-permute-done.4), channel_id=1, source_target_pairs={{0,8},{8,0},{16,24},{24,16},{1,9},{9,1},{17,25},{25,17},{2,10},{10... | collective-permute-start | bytes 626696 | tf_op jit(solution)/shard_map/ppermute | solution.py:16
  22.6 3.7 %collective-permute-start.7 = (f32[1,2,2,128]{3,2,1,0:T(2,128)S(1)}, f32[1,2,2,128]{3,2,1,0:T(2,128)S(1)}, u32[]{:S(2)}, u32[]{:S(2)}) collective-permute-start(f32[1,2,2,128]{3,2,1,0:T(2,128)S(1)} %bitcast.143), channel_id=1, source_target_pairs={{0,2},{1,3},{2,0},{3,1},{4,6},{5,7},{6,4},{7,5},{8,10},{9,11},{10,... | collective-permute-start | bytes 6152 | tf_op jit(solution)/shard_map/ppermute | solution.py:16
  23.7 9.0 %collective-permute-start.11 = (bf16[128,768]{1,0:T(8,128)(2,1)S(1)}, bf16[128,768]{1,0:T(8,128)(2,1)}, u32[]{:S(2)}, u32[]{:S(2)}) collective-permute-start(bf16[128,768]{1,0:T(8,128)(2,1)S(1)} %collective-permute-done.3), channel_id=1, source_target_pairs={{0,1},{1,0},{2,3},{3,2},{4,5},{5,4},{6,7},{7,6},{8,9},{9,8},{10,11... | collective-permute-start | bytes 589832 | tf_op jit(solution)/shard_map/ppermute | solution.py:16
  27.4 5.2 %collective-permute-start.10 = (f32[1,2,2,128]{3,2,1,0:T(2,128)S(1)}, f32[1,2,2,128]{3,2,1,0:T(2,128)S(1)}, u32[]{:S(2)}, u32[]{:S(2)}) collective-permute-start(f32[1,2,2,128]{3,2,1,0:T(2,128)S(1)} %log_add_fusion.6), channel_id=1, source_target_pairs={{0,4},{1,5},{2,6},{3,7},{4,0},{5,1},{6,2},{7,3},{8,12},{9,13},{10,... | collective-permute-start | bytes 6152 | tf_op jit(solution)/shard_map/ppermute | solution.py:16
  32.7 3.7 %collective-permute-start.12 = (f32[1,2,2,128]{3,2,1,0:T(2,128)S(1)}, f32[1,2,2,128]{3,2,1,0:T(2,128)S(1)}, u32[]{:S(2)}, u32[]{:S(2)}) collective-permute-start(f32[1,2,2,128]{3,2,1,0:T(2,128)S(1)} %log_add_fusion.5), channel_id=1, source_target_pairs={{0,1},{1,0},{2,3},{3,2},{4,5},{5,4},{6,7},{7,6},{8,9},{9,8},{10,11... | collective-permute-start | bytes 6152 | tf_op jit(solution)/shard_map/ppermute | solution.py:16
  37.3 1.5 %collective-permute-start.13 = (f32[136,384]{1,0:T(8,128)S(1)}, f32[136,384]{1,0:T(8,128)S(1)}, u32[]{:S(2)}, u32[]{:S(2)}) collective-permute-start(f32[136,384]{1,0:T(8,128)S(1)} %select_maximum_fusion.1), channel_id=1, source_target_pairs={{0,8},{8,0},{16,24},{24,16},{1,9},{9,1},{17,25},{25,17},{2,10},{10... | collective-permute-start | bytes 626696 | tf_op jit(solution)/shard_map/ppermute | solution.py:16
  38.0 2.5 %collective-permute-start.16 = (f32[128,384]{1,0:T(8,128)S(1)}, f32[128,384]{1,0:T(8,128)S(1)}, u32[]{:S(2)}, u32[]{:S(2)}) collective-permute-start(f32[128,384]{1,0:T(8,128)S(1)} %slice_select_fusion.5), channel_id=1, source_target_pairs={{0,8},{8,0},{16,24},{24,16},{1,9},{9,1},{17,25},{25,17},{2,10},{10... | collective-permute-start | bytes 589832 | tf_op jit(solution)/shard_map/ppermute | solution.py:16
  38.9 6.1 %collective-permute-start.14 = (bf16[152,384]{1,0:T(8,128)(2,1)S(1)}, bf16[152,384]{1,0:T(8,128)(2,1)S(1)}, u32[]{:S(2)}, u32[]{:S(2)}) collective-permute-start(bf16[152,384]{1,0:T(8,128)(2,1)S(1)} %pad_maximum_fusion.1), channel_id=1, source_target_pairs={{0,16},{8,24},{16,0},{24,8},{1,17},{9,25},{17,1},{25,9},{2,18},{10... | collective-permute-start | bytes 350216 | tf_op jit(solution)/shard_map/ppermute | solution.py:16
  40.5 5.8 %collective-permute-start.17 = (bf16[128,384]{1,0:T(8,128)(2,1)S(1)}, bf16[128,384]{1,0:T(8,128)(2,1)S(1)}, u32[]{:S(2)}, u32[]{:S(2)}) collective-permute-start(bf16[128,384]{1,0:T(8,128)(2,1)S(1)} %add_convert_fusion.1), channel_id=1, source_target_pairs={{0,16},{8,24},{16,0},{24,8},{1,17},{9,25},{17,1},{25,9},{2,18},{10... | collective-permute-start | bytes 294920 | tf_op jit(solution)/shard_map/ppermute | solution.py:16
  45.1 1.5 %collective-permute-start.15 = (f32[128,384]{1,0:T(8,128)S(1)}, f32[128,384]{1,0:T(8,128)S(1)}, u32[]{:S(2)}, u32[]{:S(2)}) collective-permute-start(f32[128,384]{1,0:T(8,128)S(1)} %fusion.37), channel_id=1, source_target_pairs={{0,8},{8,0},{16,24},{24,16},{1,9},{9,1},{17,25},{25,17},{2,10},{10... | collective-permute-start | bytes 589832 | tf_op jit(solution)/shard_map/ppermute | solution.py:16
  46.4 1.5 %collective-permute-start.18 = (f32[128,384]{1,0:T(8,128)S(1)}, f32[128,384]{1,0:T(8,128)S(1)}, u32[]{:S(2)}, u32[]{:S(2)}) collective-permute-start(f32[128,384]{1,0:T(8,128)S(1)} %fusion.36), channel_id=1, source_target_pairs={{0,8},{8,0},{16,24},{24,16},{1,9},{9,1},{17,25},{25,17},{2,10},{10... | collective-permute-start | bytes 589832 | tf_op jit(solution)/shard_map/ppermute | solution.py:16
  49.2 3.7 %collective-permute-start.19 = (f32[2,2,2,128]{3,2,1,0:T(2,128)S(1)}, f32[2,2,2,128]{3,2,1,0:T(2,128)S(1)}, u32[]{:S(2)}, u32[]{:S(2)}) collective-permute-start(f32[2,2,2,128]{3,2,1,0:T(2,128)S(1)} %pad_maximum_fusion.7), channel_id=1, source_target_pairs={{0,1},{1,0},{2,3},{3,2},{4,5},{5,4},{6,7},{7,6},{8,9},{9,8},{10,11... | collective-permute-start | bytes 12296 | tf_op jit(solution)/shard_map/ppermute | solution.py:16
  53.2 3.6 %collective-permute-start.20 = (f32[2,2,2,128]{3,2,1,0:T(2,128)S(1)}, f32[2,2,2,128]{3,2,1,0:T(2,128)S(1)}, u32[]{:S(2)}, u32[]{:S(2)}) collective-permute-start(f32[2,2,2,128]{3,2,1,0:T(2,128)S(1)} %log_add_fusion.2), channel_id=1, source_target_pairs={{0,2},{1,3},{2,0},{3,1},{4,6},{5,7},{6,4},{7,5},{8,10},{9,11},{10,... | collective-permute-start | bytes 12296 | tf_op jit(solution)/shard_map/ppermute | solution.py:16
  53.9 0.7 copy-start.3
  56.9 4.6 %collective-permute-start.21 = (f32[2,2,2,128]{3,2,1,0:T(2,128)S(1)}, f32[2,2,2,128]{3,2,1,0:T(2,128)S(1)}, u32[]{:S(2)}, u32[]{:S(2)}) collective-permute-start(f32[2,2,2,128]{3,2,1,0:T(2,128)S(1)} %log_add_fusion.1), channel_id=1, source_target_pairs={{0,4},{1,5},{2,6},{3,7},{4,0},{5,1},{6,2},{7,3},{8,12},{9,13},{10,... | collective-permute-start | bytes 12296 | tf_op jit(solution)/shard_map/ppermute | solution.py:16
  62.6 1.5 %collective-permute-start.22 = (f32[136,384]{1,0:T(8,128)S(1)}, f32[136,384]{1,0:T(8,128)S(1)}, u32[]{:S(2)}, u32[]{:S(2)}) collective-permute-start(f32[136,384]{1,0:T(8,128)S(1)} %select_maximum_fusion), channel_id=1, source_target_pairs={{0,8},{8,0},{16,24},{24,16},{1,9},{9,1},{17,25},{25,17},{2,10},{10... | collective-permute-start | bytes 626696 | tf_op jit(solution)/shard_map/ppermute | solution.py:16
  63.3 2.7 %collective-permute-start.25 = (f32[128,384]{1,0:T(8,128)S(1)}, f32[128,384]{1,0:T(8,128)S(1)}, u32[]{:S(2)}, u32[]{:S(2)}) collective-permute-start(f32[128,384]{1,0:T(8,128)S(1)} %slice_select_fusion.3), channel_id=1, source_target_pairs={{0,8},{8,0},{16,24},{24,16},{1,9},{9,1},{17,25},{25,17},{2,10},{10... | collective-permute-start | bytes 589832 | tf_op jit(solution)/shard_map/ppermute | solution.py:16
  64.4 5.8 %collective-permute-start.23 = (bf16[136,384]{1,0:T(8,128)(2,1)S(1)}, bf16[136,384]{1,0:T(8,128)(2,1)S(1)}, u32[]{:S(2)}, u32[]{:S(2)}) collective-permute-start(bf16[136,384]{1,0:T(8,128)(2,1)S(1)} %pad_maximum_fusion.2), channel_id=1, source_target_pairs={{0,16},{8,24},{16,0},{24,8},{1,17},{9,25},{17,1},{25,9},{2,18},{10... | collective-permute-start | bytes 313352 | tf_op jit(solution)/shard_map/ppermute | solution.py:16
  66.0 5.5 %collective-permute-start.26 = (bf16[128,384]{1,0:T(8,128)(2,1)S(1)}, bf16[128,384]{1,0:T(8,128)(2,1)S(1)}, u32[]{:S(2)}, u32[]{:S(2)}) collective-permute-start(bf16[128,384]{1,0:T(8,128)(2,1)S(1)} %add_convert_fusion), channel_id=1, source_target_pairs={{0,16},{8,24},{16,0},{24,8},{1,17},{9,25},{17,1},{25,9},{2,18},{10... | collective-permute-start | bytes 294920 | tf_op jit(solution)/shard_map/ppermute | solution.py:16
  70.3 2.0 %collective-permute-start.24 = (f32[128,384]{1,0:T(8,128)S(1)}, f32[128,384]{1,0:T(8,128)S(1)}, u32[]{:S(2)}, u32[]{:S(2)}) collective-permute-start(f32[128,384]{1,0:T(8,128)S(1)} %fusion.34), channel_id=1, source_target_pairs={{0,8},{8,0},{16,24},{24,16},{1,9},{9,1},{17,25},{25,17},{2,10},{10... | collective-permute-start | bytes 589832 | tf_op jit(solution)/shard_map/ppermute | solution.py:16
  71.6 1.5 %collective-permute-start.27 = (f32[128,384]{1,0:T(8,128)S(1)}, f32[128,384]{1,0:T(8,128)S(1)}, u32[]{:S(2)}, u32[]{:S(2)}) collective-permute-start(f32[128,384]{1,0:T(8,128)S(1)} %fusion.33), channel_id=1, source_target_pairs={{0,8},{8,0},{16,24},{24,16},{1,9},{9,1},{17,25},{25,17},{2,10},{10... | collective-permute-start | bytes 589832 | tf_op jit(solution)/shard_map/ppermute | solution.py:16
  (1 other events, 0.7 us)

commit v7 on v6

--- a/solution.py
+++ b/solution.py
@@ -121,11 +121,12 @@
         if step == 0:
             odds = [logits_of(centers_half, norms, held[0])]
             lse = stats_of(odds[0], logits_of(partner_half, partner_norms, held[0])).reshape(shape)
-            lse, tail = lax.optimization_barrier((lse, pieces[evens[-1]]))
-            across[evens[-1]] = swap(tail, "cent", 1)
-            stops = [0, half // 4, half - half // 4, half]
+            lse, held[0] = lax.optimization_barrier((lse, held[0]))
+            across[evens[-1]] = swap(held[0][-rows:], "cent", 1)
+            stops = [0, half // 4, half // 2, half]
+            turn = evens
             for index, bit in enumerate(cent_bits[1:] + [None]):
-                ties = evens[stops[index] : stops[index + 1]] if index < 3 else []
+                ties = turn[stops[index] : stops[index + 1]] if index < 3 else []
                 lse, *parts = lax.optimization_barrier([lse] + [across[mask] for mask in ties])
                 across.update(zip(ties, parts))
                 if bit is not None:

time: 74.3 us -> 73.3 us (0.987)
  waiting for transfers between devices: 27.5 us -> 26.2 us
    ppermute x28, waiting for transfers between devices: 27.5 us -> 26.2 us  [swap(): return lax.ppermute(value, axis, [(i, i ^ bit) for i in range(size)])]
    unnamed x16, local copies, waits for them, and re-layouts: 3 us -> 2.01 us
  transfers between devices with their start and end apart: 28 -> 28, of which waited for: 17 -> 18; matrix products, arithmetic and copies ran while one was open for 14% -> 14% of each run, Pallas kernels for 0% -> 0%
where the time goes in v7:
time: 73.3 us; the launch traced here: 73 us
  starting transfers between devices  29.7 us (41%)
  waiting for transfers between devices  26.2 us (36%)
  other arithmetic  5.82 us (8%)
  matrix products  5.27 us (7%)
  local copies, waits for them, and re-layouts  4.76 us (6%)
  between operations  1.26 us (2%)
    ppermute x28, starting transfers between devices, swap(): return lax.ppermute(value, axis, [(i, i ^ bit) for i in range(size)])  29.7 us
    ppermute x28, waiting for transfers between devices, swap(): return lax.ppermute(value, axis, [(i, i ^ bit) for i in range(size)])  26.2 us
    dot_general x8, matrix products, on_device(): jnp.dot(resps[index], held[index][:, part * cut:(part + 1) * cut], prefer...  2.34 us
    dot_general x5, matrix products, logits_of(): lax.dot_general(centers_half, group, (((1,), (1,)), ((), ())), preferred_...  2.08 us
    unnamed x16, local copies, waits for them, and re-layouts  2.01 us
    reduce_sum x2, other arithmetic, on_device(): norms = jnp.sum(means * means, axis=1)  1.65 us
  transfers between devices with their start and end apart: 28, of which 18 were waited for; matrix products, arithmetic and copies ran while one was open for 14% of the time, Pallas kernels for 0%

profile of v7, /device:TPU:0, one launch (start us, length us, event | category | flops | bytes accessed | tf_op | source)
XLA Modules:
  0.0 73.0 jit_solution(9262984214112870505)
XLA Ops:
  1.1 3.7 %collective-permute-start.2 = (bf16[128,768]{1,0:T(8,128)(2,1)}, bf16[128,768]{1,0:T(8,128)(2,1)S(1)}, u32[]{:S(2)}, u32[]{:S(2)}) collective-permute-start(bf16[128,768]{1,0:T(8,128)(2,1)} %param.7), channel_id=1, source_target_pairs={{0,4},{1,5},{2,6},{3,7},{4,0},{5,1},{6,2},{7,3},{8,12},{9,13},{10,... | collective-permute-start | bytes 589832 | tf_op jit(solution)/shard_map/ppermute | solution.py:16
  4.8 1.6 %collective-permute-start.1 = (bf16[128,768]{1,0:T(8,128)(2,1)}, bf16[128,768]{1,0:T(8,128)(2,1)S(1)}, u32[]{:S(2)}, u32[]{:S(2)}) collective-permute-start(bf16[128,768]{1,0:T(8,128)(2,1)} %param.7), channel_id=1, source_target_pairs={{0,2},{1,3},{2,0},{3,1},{4,6},{5,7},{6,4},{7,5},{8,10},{9,11},{10,... | collective-permute-start | bytes 589832 | tf_op jit(solution)/shard_map/ppermute | solution.py:16
  6.4 1.5 %collective-permute-start.6 = (bf16[128,768]{1,0:T(8,128)(2,1)}, bf16[128,768]{1,0:T(8,128)(2,1)S(1)}, u32[]{:S(2)}, u32[]{:S(2)}) collective-permute-start(bf16[128,768]{1,0:T(8,128)(2,1)} %param.7), channel_id=1, source_target_pairs={{0,1},{1,0},{2,3},{3,2},{4,5},{5,4},{6,7},{7,6},{8,9},{9,8},{10,11... | collective-permute-start | bytes 589832 | tf_op jit(solution)/shard_map/ppermute | solution.py:16
  7.9 1.5 %multiply_reduce_fusion.1 = (f32[256]{0:T(256)S(1)}, bf16[256,768]{1,0:T(8,128)(2,1)S(1)}) fusion(f32[256,768]{1,0:T(8,128)} %param.9), kind=kLoop, calls=%fused_computation.24 | loop fusion | flops 589568 | bytes 1180672 | tf_op jit(solution)/shard_map/reduce_sum | solution.py:71
  10.6 4.2 %collective-permute-done.2 = bf16[128,768]{1,0:T(8,128)(2,1)S(1)} collective-permute-done((bf16[128,768]{1,0:T(8,128)(2,1)}, bf16[128,768]{1,0:T(8,128)(2,1)S(1)}, u32[]{:S(2)}, u32[]{:S(2)}) %collective-permute-start.2) | collective-permute-done | bytes 196640 | tf_op jit(solution)/shard_map/ppermute | solution.py:16
  14.8 0.8 %collective-permute-start.3 = (bf16[128,768]{1,0:T(8,128)(2,1)S(1)}, bf16[128,768]{1,0:T(8,128)(2,1)S(1)}, u32[]{:S(2)}, u32[]{:S(2)}) collective-permute-start(bf16[128,768]{1,0:T(8,128)(2,1)S(1)} %collective-permute-done.2), channel_id=1, source_target_pairs={{0,2},{1,3},{2,0},{3,1},{4,6},{5,7},{6,4},{7,5},{8,10},{9,11},{10,... | collective-permute-start | bytes 589832 | tf_op jit(solution)/shard_map/ppermute | solution.py:16
  15.6 1.5 %collective-permute-start.10 = (bf16[128,768]{1,0:T(8,128)(2,1)S(1)}, bf16[128,768]{1,0:T(8,128)(2,1)S(1)}, u32[]{:S(2)}, u32[]{:S(2)}) collective-permute-start(bf16[128,768]{1,0:T(8,128)(2,1)S(1)} %collective-permute-done.2), channel_id=1, source_target_pairs={{0,1},{1,0},{2,3},{3,2},{4,5},{5,4},{6,7},{7,6},{8,9},{9,8},{10,11... | collective-permute-start | bytes 589832 | tf_op jit(solution)/shard_map/ppermute | solution.py:16
  17.9 3.6 %collective-permute-done.3 = bf16[128,768]{1,0:T(8,128)(2,1)S(1)} collective-permute-done((bf16[128,768]{1,0:T(8,128)(2,1)S(1)}, bf16[128,768]{1,0:T(8,128)(2,1)S(1)}, u32[]{:S(2)}, u32[]{:S(2)}) %collective-permute-start.3) | collective-permute-done | bytes 196640 | tf_op jit(solution)/shard_map/ppermute | solution.py:16
  22.6 1.1 %collective-permute-start.7 = (f32[1,2,2,128]{3,2,1,0:T(2,128)S(1)}, f32[1,2,2,128]{3,2,1,0:T(2,128)S(1)}, u32[]{:S(2)}, u32[]{:S(2)}) collective-permute-start(f32[1,2,2,128]{3,2,1,0:T(2,128)S(1)} %bitcast.143), channel_id=1, source_target_pairs={{0,2},{1,3},{2,0},{3,1},{4,6},{5,7},{6,4},{7,5},{8,10},{9,11},{10,... | collective-permute-start | bytes 6152 | tf_op jit(solution)/shard_map/ppermute | solution.py:16
  23.7 0.7 slice.254
  24.4 1.5 %collective-permute-start.11 = (bf16[128,768]{1,0:T(8,128)(2,1)}, bf16[128,768]{1,0:T(8,128)(2,1)}, u32[]{:S(2)}, u32[]{:S(2)}) collective-permute-start(bf16[128,768]{1,0:T(8,128)(2,1)} %slice.254), channel_id=1, source_target_pairs={{0,1},{1,0},{2,3},{3,2},{4,5},{5,4},{6,7},{7,6},{8,9},{9,8},{10,11... | collective-permute-start | bytes 589832 | tf_op jit(solution)/shard_map/ppermute | solution.py:16
  26.7 3.3 %collective-permute-start.9 = (f32[1,2,2,128]{3,2,1,0:T(2,128)S(1)}, f32[1,2,2,128]{3,2,1,0:T(2,128)S(1)}, u32[]{:S(2)}, u32[]{:S(2)}) collective-permute-start(f32[1,2,2,128]{3,2,1,0:T(2,128)S(1)} %log_add_fusion.6), channel_id=1, source_target_pairs={{0,4},{1,5},{2,6},{3,7},{4,0},{5,1},{6,2},{7,3},{8,12},{9,13},{10,... | collective-permute-start | bytes 6152 | tf_op jit(solution)/shard_map/ppermute | solution.py:16
  30.1 0.9 %constant_dynamic-update-slice_fusion.6 = bf16[512,768]{1,0:T(8,128)(2,1)S(1)} fusion(bf16[512,768]{1,0:T(8,128)(2,1)S(1)} %constant_dynamic-update-slice_fusion.7, bf16[128,768]{1,0:T(8,128)(2,1)} %collective-permute-done.8), kind=kLoop, calls=%fused_computation.116 | loop fusion | bytes 393216
  31.0 0.6 collective-permute-done.9
  31.7 1.6 %collective-permute-start.12 = (f32[1,2,2,128]{3,2,1,0:T(2,128)S(1)}, f32[1,2,2,128]{3,2,1,0:T(2,128)S(1)}, u32[]{:S(2)}, u32[]{:S(2)}) collective-permute-start(f32[1,2,2,128]{3,2,1,0:T(2,128)S(1)} %log_add_fusion.5), channel_id=1, source_target_pairs={{0,1},{1,0},{2,3},{3,2},{4,5},{5,4},{6,7},{7,6},{8,9},{9,8},{10,11... | collective-permute-start | bytes 6152 | tf_op jit(solution)/shard_map/ppermute | solution.py:16
  33.2 0.9 %constant_dynamic-update-slice_fusion.4 = bf16[512,768]{1,0:T(8,128)(2,1)S(1)} fusion(bf16[512,768]{1,0:T(8,128)(2,1)S(1)} %constant_dynamic-update-slice_fusion.5, bf16[128,768]{1,0:T(8,128)(2,1)} %collective-permute-done.11), kind=kLoop, calls=%fused_computation.114 | loop fusion | bytes 393216 | tf_op jit(solution)/shard_map/concatenate | solution.py:134
  34.6 0.7 collective-permute-done.12
  37.9 1.6 %collective-permute-start.14 = (bf16[152,384]{1,0:T(8,128)(2,1)S(1)}, bf16[152,384]{1,0:T(8,128)(2,1)S(1)}, u32[]{:S(2)}, u32[]{:S(2)}) collective-permute-start(bf16[152,384]{1,0:T(8,128)(2,1)S(1)} %pad_maximum_fusion.1), channel_id=1, source_target_pairs={{0,16},{8,24},{16,0},{24,8},{1,17},{9,25},{17,1},{25,9},{2,18},{10... | collective-permute-start | bytes 350216 | tf_op jit(solution)/shard_map/ppermute | solution.py:16
  39.5 0.7 collective-permute-start.17
  40.2 3.7 %collective-permute-done.14 = bf16[152,384]{1,0:T(8,128)(2,1)S(1)} collective-permute-done((bf16[152,384]{1,0:T(8,128)(2,1)S(1)}, bf16[152,384]{1,0:T(8,128)(2,1)S(1)}, u32[]{:S(2)}, u32[]{:S(2)}) %collective-permute-start.14) | collective-permute-done | bytes 116768 | tf_op jit(solution)/shard_map/ppermute | solution.py:16
  44.1 1.1 %collective-permute-done.17 = bf16[128,384]{1,0:T(8,128)(2,1)S(1)} collective-permute-done((bf16[128,384]{1,0:T(8,128)(2,1)S(1)}, bf16[128,384]{1,0:T(8,128)(2,1)S(1)}, u32[]{:S(2)}, u32[]{:S(2)}) %collective-permute-start.17) | collective-permute-done | bytes 98336 | tf_op jit(solution)/shard_map/ppermute | solution.py:16
  45.6 1.3 %collective-permute-done.18 = f32[128,384]{1,0:T(8,128)S(1)} collective-permute-done((f32[128,384]{1,0:T(8,128)S(1)}, f32[128,384]{1,0:T(8,128)S(1)}, u32[]{:S(2)}, u32[]{:S(2)}) %collective-permute-start.18) | collective-permute-done | bytes 196640 | tf_op jit(solution)/shard_map/ppermute | solution.py:16
  48.1 1.6 %collective-permute-start.19 = (f32[2,2,2,128]{3,2,1,0:T(2,128)S(1)}, f32[2,2,2,128]{3,2,1,0:T(2,128)S(1)}, u32[]{:S(2)}, u32[]{:S(2)}) collective-permute-start(f32[2,2,2,128]{3,2,1,0:T(2,128)S(1)} %pad_maximum_fusion.7), channel_id=1, source_target_pairs={{0,1},{1,0},{2,3},{3,2},{4,5},{5,4},{6,7},{7,6},{8,9},{9,8},{10,11... | collective-permute-start | bytes 12296 | tf_op jit(solution)/shard_map/ppermute | solution.py:16
  49.8 2.1 %collective-permute-done.19 = f32[2,2,2,128]{3,2,1,0:T(2,128)S(1)} collective-permute-done((f32[2,2,2,128]{3,2,1,0:T(2,128)S(1)}, f32[2,2,2,128]{3,2,1,0:T(2,128)S(1)}, u32[]{:S(2)}, u32[]{:S(2)}) %collective-permute-start.19) | collective-permute-done | bytes 4128 | tf_op jit(solution)/shard_map/ppermute | solution.py:16
  52.2 0.9 %collective-permute-start.20 = (f32[2,2,2,128]{3,2,1,0:T(2,128)S(1)}, f32[2,2,2,128]{3,2,1,0:T(2,128)S(1)}, u32[]{:S(2)}, u32[]{:S(2)}) collective-permute-start(f32[2,2,2,128]{3,2,1,0:T(2,128)S(1)} %log_add_fusion.2), channel_id=1, source_target_pairs={{0,2},{1,3},{2,0},{3,1},{4,6},{5,7},{6,4},{7,5},{8,10},{9,11},{10,... | collective-permute-start | bytes 12296 | tf_op jit(solution)/shard_map/ppermute | solution.py:16
  55.8 3.0 %collective-permute-start.21 = (f32[2,2,2,128]{3,2,1,0:T(2,128)S(1)}, f32[2,2,2,128]{3,2,1,0:T(2,128)S(1)}, u32[]{:S(2)}, u32[]{:S(2)}) collective-permute-start(f32[2,2,2,128]{3,2,1,0:T(2,128)S(1)} %log_add_fusion.1), channel_id=1, source_target_pairs={{0,4},{1,5},{2,6},{3,7},{4,0},{5,1},{6,2},{7,3},{8,12},{9,13},{10,... | collective-permute-start | bytes 12296 | tf_op jit(solution)/shard_map/ppermute | solution.py:16
  58.8 1.6 %collective-permute-done.21 = f32[2,2,2,128]{3,2,1,0:T(2,128)S(1)} collective-permute-done((f32[2,2,2,128]{3,2,1,0:T(2,128)S(1)}, f32[2,2,2,128]{3,2,1,0:T(2,128)S(1)}, u32[]{:S(2)}, u32[]{:S(2)}) %collective-permute-start.21) | collective-permute-done | bytes 4128 | tf_op jit(solution)/shard_map/ppermute | solution.py:16
  63.3 1.6 %collective-permute-start.23 = (bf16[136,384]{1,0:T(8,128)(2,1)S(1)}, bf16[136,384]{1,0:T(8,128)(2,1)S(1)}, u32[]{:S(2)}, u32[]{:S(2)}) collective-permute-start(bf16[136,384]{1,0:T(8,128)(2,1)S(1)} %pad_maximum_fusion.2), channel_id=1, source_target_pairs={{0,16},{8,24},{16,0},{24,8},{1,17},{9,25},{17,1},{25,9},{2,18},{10... | collective-permute-start | bytes 313352 | tf_op jit(solution)/shard_map/ppermute | solution.py:16
  65.5 3.6 %collective-permute-done.23 = bf16[136,384]{1,0:T(8,128)(2,1)S(1)} collective-permute-done((bf16[136,384]{1,0:T(8,128)(2,1)S(1)}, bf16[136,384]{1,0:T(8,128)(2,1)S(1)}, u32[]{:S(2)}, u32[]{:S(2)}) %collective-permute-start.23) | collective-permute-done | bytes 104480 | tf_op jit(solution)/shard_map/ppermute | solution.py:16
  69.4 1.1 %collective-permute-done.26 = bf16[128,384]{1,0:T(8,128)(2,1)S(1)} collective-permute-done((bf16[128,384]{1,0:T(8,128)(2,1)S(1)}, bf16[128,384]{1,0:T(8,128)(2,1)S(1)}, u32[]{:S(2)}, u32[]{:S(2)}) %collective-permute-start.26) | collective-permute-done | bytes 98336 | tf_op jit(solution)/shard_map/ppermute | solution.py:16
  71.4 0.7 collective-permute-done.27
  72.1 0.9 %maximum_maximum_fusion.1 = f32[256,768]{1,0:T(8,128)} fusion(f32[128,384]{1,0:T(8,128)S(1)} %get-tuple-element.95, f32[128,384]{1,0:T(8,128)S(1)} %get-tuple-element.94, f32[128,384]{1,0:T(8,128)S(1)} %get-tuple-element.93, f32[128,384]{1,0:T(8,128)S(1)} %get-tuple-element.92), kind=kLoop, calls=%fused_computation.22 | loop fusion | flops 589824 | bytes 1572864 | tf_op jit(solution)/shard_map/concatenate | solution.py:221
  (157 shorter events, 16.6 us)
Async XLA Ops:
  0.6 4.2 %collective-permute-start = (bf16[4,768]{1,0:T(4,128)(2,1)}, bf16[4,768]{1,0:T(4,128)(2,1)S(1)}, u32[]{:S(2)}, u32[]{:S(2)}) collective-permute-start(bf16[4,768]{1,0:T(4,128)(2,1)} %param.8), channel_id=1, source_target_pairs={{0,8},{8,0},{16,24},{24,16},{1,9},{9,1},{17,25},{25,17},{2,10},{10... | collective-permute-start | bytes 18440 | tf_op jit(solution)/shard_map/ppermute | solution.py:16
  1.1 13.7 %collective-permute-start.2 = (bf16[128,768]{1,0:T(8,128)(2,1)}, bf16[128,768]{1,0:T(8,128)(2,1)S(1)}, u32[]{:S(2)}, u32[]{:S(2)}) collective-permute-start(bf16[128,768]{1,0:T(8,128)(2,1)} %param.7), channel_id=1, source_target_pairs={{0,4},{1,5},{2,6},{3,7},{4,0},{5,1},{6,2},{7,3},{8,12},{9,13},{10,... | collective-permute-start | bytes 589832 | tf_op jit(solution)/shard_map/ppermute | solution.py:16
  4.8 12.3 %collective-permute-start.1 = (bf16[128,768]{1,0:T(8,128)(2,1)}, bf16[128,768]{1,0:T(8,128)(2,1)S(1)}, u32[]{:S(2)}, u32[]{:S(2)}) collective-permute-start(bf16[128,768]{1,0:T(8,128)(2,1)} %param.7), channel_id=1, source_target_pairs={{0,2},{1,3},{2,0},{3,1},{4,6},{5,7},{6,4},{7,5},{8,10},{9,11},{10,... | collective-permute-start | bytes 589832 | tf_op jit(solution)/shard_map/ppermute | solution.py:16
  6.4 16.2 %collective-permute-start.6 = (bf16[128,768]{1,0:T(8,128)(2,1)}, bf16[128,768]{1,0:T(8,128)(2,1)S(1)}, u32[]{:S(2)}, u32[]{:S(2)}) collective-permute-start(bf16[128,768]{1,0:T(8,128)(2,1)} %param.7), channel_id=1, source_target_pairs={{0,1},{1,0},{2,3},{3,2},{4,5},{5,4},{6,7},{7,6},{8,9},{9,8},{10,11... | collective-permute-start | bytes 589832 | tf_op jit(solution)/shard_map/ppermute | solution.py:16
  9.4 1.2 %copy-start = (f32[256,768]{1,0:T(8,128)S(1)}, f32[256,768]{1,0:T(8,128)}, u32[]{:S(2)}) copy-start(f32[256,768]{1,0:T(8,128)} %param.9) | copy-start | bytes 2359300
  9.5 0.8 %copy-start.2 = (bf16[4,768]{1,0:T(4,128)(2,1)S(1)}, bf16[4,768]{1,0:T(4,128)(2,1)}, u32[]{:S(2)}) copy-start(bf16[4,768]{1,0:T(4,128)(2,1)} %param.8) | copy-start | bytes 18436
  9.5 8.3 %collective-permute-start.4 = (bf16[136,768]{1,0:T(8,128)(2,1)S(1)}, bf16[136,768]{1,0:T(8,128)(2,1)S(1)}, u32[]{:S(2)}, u32[]{:S(2)}) collective-permute-start(bf16[136,768]{1,0:T(8,128)(2,1)S(1)} %pad_maximum_fusion), channel_id=1, source_target_pairs={{0,1},{1,0},{2,3},{3,2},{4,5},{5,4},{6,7},{7,6},{8,9},{9,8},{10,11... | collective-permute-start | bytes 626696 | tf_op jit(solution)/shard_map/ppermute | solution.py:16
  10.5 6.6 %copy-start.1 = (bf16[128,768]{1,0:T(8,128)(2,1)S(1)}, bf16[128,768]{1,0:T(8,128)(2,1)}, u32[]{:S(2)}) copy-start(bf16[128,768]{1,0:T(8,128)(2,1)} %param.7) | copy-start | bytes 589828
  14.8 6.6 %collective-permute-start.3 = (bf16[128,768]{1,0:T(8,128)(2,1)S(1)}, bf16[128,768]{1,0:T(8,128)(2,1)S(1)}, u32[]{:S(2)}, u32[]{:S(2)}) collective-permute-start(bf16[128,768]{1,0:T(8,128)(2,1)S(1)} %collective-permute-done.2), channel_id=1, source_target_pairs={{0,2},{1,3},{2,0},{3,1},{4,6},{5,7},{6,4},{7,5},{8,10},{9,11},{10,... | collective-permute-start | bytes 589832 | tf_op jit(solution)/shard_map/ppermute | solution.py:16
  15.6 16.0 %collective-permute-start.10 = (bf16[128,768]{1,0:T(8,128)(2,1)S(1)}, bf16[128,768]{1,0:T(8,128)(2,1)S(1)}, u32[]{:S(2)}, u32[]{:S(2)}) collective-permute-start(bf16[128,768]{1,0:T(8,128)(2,1)S(1)} %collective-permute-done.2), channel_id=1, source_target_pairs={{0,1},{1,0},{2,3},{3,2},{4,5},{5,4},{6,7},{7,6},{8,9},{9,8},{10,11... | collective-permute-start | bytes 589832 | tf_op jit(solution)/shard_map/ppermute | solution.py:16
  17.1 9.6 %collective-permute-start.8 = (bf16[128,768]{1,0:T(8,128)(2,1)S(1)}, bf16[128,768]{1,0:T(8,128)(2,1)}, u32[]{:S(2)}, u32[]{:S(2)}) collective-permute-start(bf16[128,768]{1,0:T(8,128)(2,1)S(1)} %collective-permute-done.1), channel_id=1, source_target_pairs={{0,1},{1,0},{2,3},{3,2},{4,5},{5,4},{6,7},{7,6},{8,9},{9,8},{10,11... | collective-permute-start | bytes 589832 | tf_op jit(solution)/shard_map/ppermute | solution.py:16
  17.8 4.1 %collective-permute-start.5 = (bf16[136,768]{1,0:T(8,128)(2,1)S(1)}, bf16[136,768]{1,0:T(8,128)(2,1)S(1)}, u32[]{:S(2)}, u32[]{:S(2)}) collective-permute-start(bf16[136,768]{1,0:T(8,128)(2,1)S(1)} %collective-permute-done.4), channel_id=1, source_target_pairs={{0,8},{8,0},{16,24},{24,16},{1,9},{9,1},{17,25},{25,17},{2,10},{10... | collective-permute-start | bytes 626696 | tf_op jit(solution)/shard_map/ppermute | solution.py:16
  22.6 3.7 %collective-permute-start.7 = (f32[1,2,2,128]{3,2,1,0:T(2,128)S(1)}, f32[1,2,2,128]{3,2,1,0:T(2,128)S(1)}, u32[]{:S(2)}, u32[]{:S(2)}) collective-permute-start(f32[1,2,2,128]{3,2,1,0:T(2,128)S(1)} %bitcast.143), channel_id=1, source_target_pairs={{0,2},{1,3},{2,0},{3,1},{4,6},{5,7},{6,4},{7,5},{8,10},{9,11},{10,... | collective-permute-start | bytes 6152 | tf_op jit(solution)/shard_map/ppermute | solution.py:16
  24.4 7.2 %collective-permute-start.11 = (bf16[128,768]{1,0:T(8,128)(2,1)}, bf16[128,768]{1,0:T(8,128)(2,1)}, u32[]{:S(2)}, u32[]{:S(2)}) collective-permute-start(bf16[128,768]{1,0:T(8,128)(2,1)} %slice.254), channel_id=1, source_target_pairs={{0,1},{1,0},{2,3},{3,2},{4,5},{5,4},{6,7},{7,6},{8,9},{9,8},{10,11... | collective-permute-start | bytes 589832 | tf_op jit(solution)/shard_map/ppermute | solution.py:16
  26.7 4.9 %collective-permute-start.9 = (f32[1,2,2,128]{3,2,1,0:T(2,128)S(1)}, f32[1,2,2,128]{3,2,1,0:T(2,128)S(1)}, u32[]{:S(2)}, u32[]{:S(2)}) collective-permute-start(f32[1,2,2,128]{3,2,1,0:T(2,128)S(1)} %log_add_fusion.6), channel_id=1, source_target_pairs={{0,4},{1,5},{2,6},{3,7},{4,0},{5,1},{6,2},{7,3},{8,12},{9,13},{10,... | collective-permute-start | bytes 6152 | tf_op jit(solution)/shard_map/ppermute | solution.py:16
  31.7 3.7 %collective-permute-start.12 = (f32[1,2,2,128]{3,2,1,0:T(2,128)S(1)}, f32[1,2,2,128]{3,2,1,0:T(2,128)S(1)}, u32[]{:S(2)}, u32[]{:S(2)}) collective-permute-start(f32[1,2,2,128]{3,2,1,0:T(2,128)S(1)} %log_add_fusion.5), channel_id=1, source_target_pairs={{0,1},{1,0},{2,3},{3,2},{4,5},{5,4},{6,7},{7,6},{8,9},{9,8},{10,11... | collective-permute-start | bytes 6152 | tf_op jit(solution)/shard_map/ppermute | solution.py:16
  36.2 1.5 %collective-permute-start.13 = (f32[136,384]{1,0:T(8,128)S(1)}, f32[136,384]{1,0:T(8,128)S(1)}, u32[]{:S(2)}, u32[]{:S(2)}) collective-permute-start(f32[136,384]{1,0:T(8,128)S(1)} %select_maximum_fusion.1), channel_id=1, source_target_pairs={{0,8},{8,0},{16,24},{24,16},{1,9},{9,1},{17,25},{25,17},{2,10},{10... | collective-permute-start | bytes 626696 | tf_op jit(solution)/shard_map/ppermute | solution.py:16
  36.9 2.5 %collective-permute-start.16 = (f32[128,384]{1,0:T(8,128)S(1)}, f32[128,384]{1,0:T(8,128)S(1)}, u32[]{:S(2)}, u32[]{:S(2)}) collective-permute-start(f32[128,384]{1,0:T(8,128)S(1)} %slice_select_fusion.5), channel_id=1, source_target_pairs={{0,8},{8,0},{16,24},{24,16},{1,9},{9,1},{17,25},{25,17},{2,10},{10... | collective-permute-start | bytes 589832 | tf_op jit(solution)/shard_map/ppermute | solution.py:16
  37.9 6.1 %collective-permute-start.14 = (bf16[152,384]{1,0:T(8,128)(2,1)S(1)}, bf16[152,384]{1,0:T(8,128)(2,1)S(1)}, u32[]{:S(2)}, u32[]{:S(2)}) collective-permute-start(bf16[152,384]{1,0:T(8,128)(2,1)S(1)} %pad_maximum_fusion.1), channel_id=1, source_target_pairs={{0,16},{8,24},{16,0},{24,8},{1,17},{9,25},{17,1},{25,9},{2,18},{10... | collective-permute-start | bytes 350216 | tf_op jit(solution)/shard_map/ppermute | solution.py:16
  39.5 5.8 %collective-permute-start.17 = (bf16[128,384]{1,0:T(8,128)(2,1)S(1)}, bf16[128,384]{1,0:T(8,128)(2,1)S(1)}, u32[]{:S(2)}, u32[]{:S(2)}) collective-permute-start(bf16[128,384]{1,0:T(8,128)(2,1)S(1)} %add_convert_fusion.1), channel_id=1, source_target_pairs={{0,16},{8,24},{16,0},{24,8},{1,17},{9,25},{17,1},{25,9},{2,18},{10... | collective-permute-start | bytes 294920 | tf_op jit(solution)/shard_map/ppermute | solution.py:16
  44.1 1.5 %collective-permute-start.15 = (f32[128,384]{1,0:T(8,128)S(1)}, f32[128,384]{1,0:T(8,128)S(1)}, u32[]{:S(2)}, u32[]{:S(2)}) collective-permute-start(f32[128,384]{1,0:T(8,128)S(1)} %fusion.37), channel_id=1, source_target_pairs={{0,8},{8,0},{16,24},{24,16},{1,9},{9,1},{17,25},{25,17},{2,10},{10... | collective-permute-start | bytes 589832 | tf_op jit(solution)/shard_map/ppermute | solution.py:16
  45.4 1.5 %collective-permute-start.18 = (f32[128,384]{1,0:T(8,128)S(1)}, f32[128,384]{1,0:T(8,128)S(1)}, u32[]{:S(2)}, u32[]{:S(2)}) collective-permute-start(f32[128,384]{1,0:T(8,128)S(1)} %fusion.36), channel_id=1, source_target_pairs={{0,8},{8,0},{16,24},{24,16},{1,9},{9,1},{17,25},{25,17},{2,10},{10... | collective-permute-start | bytes 589832 | tf_op jit(solution)/shard_map/ppermute | solution.py:16
  48.1 3.7 %collective-permute-start.19 = (f32[2,2,2,128]{3,2,1,0:T(2,128)S(1)}, f32[2,2,2,128]{3,2,1,0:T(2,128)S(1)}, u32[]{:S(2)}, u32[]{:S(2)}) collective-permute-start(f32[2,2,2,128]{3,2,1,0:T(2,128)S(1)} %pad_maximum_fusion.7), channel_id=1, source_target_pairs={{0,1},{1,0},{2,3},{3,2},{4,5},{5,4},{6,7},{7,6},{8,9},{9,8},{10,11... | collective-permute-start | bytes 12296 | tf_op jit(solution)/shard_map/ppermute | solution.py:16
  52.1 0.9 %copy-start.4 = (s32[128]{0:T(128)S(1)}, s32[128]{0:T(128)}, u32[]{:S(2)}) copy-start(s32[128]{0:T(128)} %param.11) | copy-start | bytes 1540
  52.2 3.6 %collective-permute-start.20 = (f32[2,2,2,128]{3,2,1,0:T(2,128)S(1)}, f32[2,2,2,128]{3,2,1,0:T(2,128)S(1)}, u32[]{:S(2)}, u32[]{:S(2)}) collective-permute-start(f32[2,2,2,128]{3,2,1,0:T(2,128)S(1)} %log_add_fusion.2), channel_id=1, source_target_pairs={{0,2},{1,3},{2,0},{3,1},{4,6},{5,7},{6,4},{7,5},{8,10},{9,11},{10,... | collective-permute-start | bytes 12296 | tf_op jit(solution)/shard_map/ppermute | solution.py:16
  55.8 4.6 %collective-permute-start.21 = (f32[2,2,2,128]{3,2,1,0:T(2,128)S(1)}, f32[2,2,2,128]{3,2,1,0:T(2,128)S(1)}, u32[]{:S(2)}, u32[]{:S(2)}) collective-permute-start(f32[2,2,2,128]{3,2,1,0:T(2,128)S(1)} %log_add_fusion.1), channel_id=1, source_target_pairs={{0,4},{1,5},{2,6},{3,7},{4,0},{5,1},{6,2},{7,3},{8,12},{9,13},{10,... | collective-permute-start | bytes 12296 | tf_op jit(solution)/shard_map/ppermute | solution.py:16
  61.5 1.5 %collective-permute-start.22 = (f32[136,384]{1,0:T(8,128)S(1)}, f32[136,384]{1,0:T(8,128)S(1)}, u32[]{:S(2)}, u32[]{:S(2)}) collective-permute-start(f32[136,384]{1,0:T(8,128)S(1)} %select_maximum_fusion), channel_id=1, source_target_pairs={{0,8},{8,0},{16,24},{24,16},{1,9},{9,1},{17,25},{25,17},{2,10},{10... | collective-permute-start | bytes 626696 | tf_op jit(solution)/shard_map/ppermute | solution.py:16
  62.2 2.7 %collective-permute-start.25 = (f32[128,384]{1,0:T(8,128)S(1)}, f32[128,384]{1,0:T(8,128)S(1)}, u32[]{:S(2)}, u32[]{:S(2)}) collective-permute-start(f32[128,384]{1,0:T(8,128)S(1)} %slice_select_fusion.3), channel_id=1, source_target_pairs={{0,8},{8,0},{16,24},{24,16},{1,9},{9,1},{17,25},{25,17},{2,10},{10... | collective-permute-start | bytes 589832 | tf_op jit(solution)/shard_map/ppermute | solution.py:16
  63.3 5.8 %collective-permute-start.23 = (bf16[136,384]{1,0:T(8,128)(2,1)S(1)}, bf16[136,384]{1,0:T(8,128)(2,1)S(1)}, u32[]{:S(2)}, u32[]{:S(2)}) collective-permute-start(bf16[136,384]{1,0:T(8,128)(2,1)S(1)} %pad_maximum_fusion.2), channel_id=1, source_target_pairs={{0,16},{8,24},{16,0},{24,8},{1,17},{9,25},{17,1},{25,9},{2,18},{10... | collective-permute-start | bytes 313352 | tf_op jit(solution)/shard_map/ppermute | solution.py:16
  64.9 5.5 %collective-permute-start.26 = (bf16[128,384]{1,0:T(8,128)(2,1)S(1)}, bf16[128,384]{1,0:T(8,128)(2,1)S(1)}, u32[]{:S(2)}, u32[]{:S(2)}) collective-permute-start(bf16[128,384]{1,0:T(8,128)(2,1)S(1)} %add_convert_fusion), channel_id=1, source_target_pairs={{0,16},{8,24},{16,0},{24,8},{1,17},{9,25},{17,1},{25,9},{2,18},{10... | collective-permute-start | bytes 294920 | tf_op jit(solution)/shard_map/ppermute | solution.py:16
  69.3 2.0 %collective-permute-start.24 = (f32[128,384]{1,0:T(8,128)S(1)}, f32[128,384]{1,0:T(8,128)S(1)}, u32[]{:S(2)}, u32[]{:S(2)}) collective-permute-start(f32[128,384]{1,0:T(8,128)S(1)} %fusion.34), channel_id=1, source_target_pairs={{0,8},{8,0},{16,24},{24,16},{1,9},{9,1},{17,25},{25,17},{2,10},{10... | collective-permute-start | bytes 589832 | tf_op jit(solution)/shard_map/ppermute | solution.py:16
  70.5 1.5 %collective-permute-start.27 = (f32[128,384]{1,0:T(8,128)S(1)}, f32[128,384]{1,0:T(8,128)S(1)}, u32[]{:S(2)}, u32[]{:S(2)}) collective-permute-start(f32[128,384]{1,0:T(8,128)S(1)} %fusion.33), channel_id=1, source_target_pairs={{0,8},{8,0},{16,24},{24,16},{1,9},{9,1},{17,25},{25,17},{2,10},{10... | collective-permute-start | bytes 589832 | tf_op jit(solution)/shard_map/ppermute | solution.py:16
  (1 other events, 0.7 us)

commit v8 on v7

--- a/solution.py
+++ b/solution.py
@@ -62,7 +62,11 @@
     evens = list(range(0, n_cent, 2))
     pieces = column_pieces(passages, later, "cent", n_cent)
     across = {mask: swap(pieces[mask], "cent", 1) for mask in evens[:-1]}
+    asked = in_order(queries, asked, core)
+    for bit in dp_bits[1:]:
+        asked = in_order(asked, swap(asked, "dp", bit), dp & bit)
     pieces[2], pieces[0] = lax.optimization_barrier((pieces[2], passages))
+    pieces[evens[-1]], asked = lax.optimization_barrier((pieces[evens[-1]], asked))
     held = [jnp.concatenate([pieces[mask] for mask in evens])]
 
     centers = means.shape[0]
@@ -153,8 +157,6 @@
             counts = counts + jnp.sum(resp, axis=1)
             resps.append(resp.astype(jnp.bfloat16))
 
-        if step == 0:
-            asked = in_order(queries, asked, core)
         line = jnp.where(first, counts[:kept], counts[kept:])
         rest = jnp.where(first, counts[kept:], counts[:kept])
         if last:
@@ -195,18 +197,12 @@
                 if part == 0:
                     parts = jnp.pad(jnp.stack(in_three(line)), ((0, 5), (0, cut - line.shape[0])))
                     packed = jnp.concatenate([packed, parts])
-                    if step == 0:
-                        packed = jnp.concatenate([packed, asked[:, :cut], asked[:, cut:]])
                     packed = jnp.pad(packed, ((0, -packed.shape[0] % 8), (0, 0)))
                 other = swap(packed, "dp", bit)
                 totals[part] = (sent, other[:kept])
                 if part == 0:
                     three = other[kept : kept + 3, : line.shape[0]].astype(jnp.float32)
                     line = join_lines(line, (three[0] + three[1]) + three[2])
-                    if step == 0:
-                        more = other[kept + 8 : kept + 8 + 2 * asked.shape[0]]
-                        more = jnp.concatenate([more[: asked.shape[0]], more[asked.shape[0] :]], axis=1)
-                        asked = in_order(asked, more, dp & bit)
         if last:
             whole = line[kept + asks :] - line[kept : kept + asks]
             loss = lax.dynamic_slice_in_dim(whole, dp * own_queries, own_queries, 0)

time: 73.3 us -> 73.2 us (level)
  waiting for transfers between devices: 26.2 us -> 24.2 us
  local copies, waits for them, and re-layouts: 4.76 us -> 5.94 us
    ppermute x28 -> x29, waiting for transfers between devices: 26.2 us -> 24.2 us  [swap(): return lax.ppermute(value, axis, [(i, i ^ bit) for i in range(size)])]
    unnamed x16, local copies, waits for them, and re-layouts: 2.01 us -> 3.2 us
    ppermute x28 -> x29, starting transfers between devices: 29.7 us -> 30.4 us  [swap(): return lax.ppermute(value, axis, [(i, i ^ bit) for i in range(size)])]
  transfers between devices with their start and end apart: 28 -> 29, of which waited for: 18 -> 19; matrix products, arithmetic and copies ran while one was open for 14% -> 15% of each run, Pallas kernels for 0% -> 0%
where the time goes in v8:
time: 73.2 us; the launch traced here: 72.9 us
  starting transfers between devices  30.4 us (42%)
  waiting for transfers between devices  24.2 us (33%)
  local copies, waits for them, and re-layouts  5.94 us (8%)
  other arithmetic  5.81 us (8%)
  matrix products  5.27 us (7%)
  between operations  1.26 us (2%)
    ppermute x29, starting transfers between devices, swap(): return lax.ppermute(value, axis, [(i, i ^ bit) for i in range(size)])  30.4 us
    ppermute x29, waiting for transfers between devices, swap(): return lax.ppermute(value, axis, [(i, i ^ bit) for i in range(size)])  24.2 us
    unnamed x16, local copies, waits for them, and re-layouts  3.2 us
    dot_general x8, matrix products, on_device(): jnp.dot(resps[index], held[index][:, part * cut:(part + 1) * cut], prefer...  2.34 us
    dot_general x5, matrix products, logits_of(): lax.dot_general(centers_half, group, (((1,), (1,)), ((), ())), preferred_...  2.08 us
    reduce_sum x2, other arithmetic, on_device(): norms = jnp.sum(means * means, axis=1)  1.65 us
  transfers between devices with their start and end apart: 29, of which 19 were waited for; matrix products, arithmetic and copies ran while one was open for 15% of the time, Pallas kernels for 0%

profile of v8, /device:TPU:0, one launch (start us, length us, event | category | flops | bytes accessed | tf_op | source)
XLA Modules:
  0.0 72.9 jit_solution(2721879643590328696)
XLA Ops:
  1.2 3.7 %collective-permute-start.2 = (bf16[128,768]{1,0:T(8,128)(2,1)}, bf16[128,768]{1,0:T(8,128)(2,1)S(1)}, u32[]{:S(2)}, u32[]{:S(2)}) collective-permute-start(bf16[128,768]{1,0:T(8,128)(2,1)} %param.7), channel_id=1, source_target_pairs={{0,4},{1,5},{2,6},{3,7},{4,0},{5,1},{6,2},{7,3},{8,12},{9,13},{10,... | collective-permute-start | bytes 589832 | tf_op jit(solution)/shard_map/ppermute | solution.py:16
  4.8 1.6 %collective-permute-start.1 = (bf16[128,768]{1,0:T(8,128)(2,1)}, bf16[128,768]{1,0:T(8,128)(2,1)S(1)}, u32[]{:S(2)}, u32[]{:S(2)}) collective-permute-start(bf16[128,768]{1,0:T(8,128)(2,1)} %param.7), channel_id=1, source_target_pairs={{0,2},{1,3},{2,0},{3,1},{4,6},{5,7},{6,4},{7,5},{8,10},{9,11},{10,... | collective-permute-start | bytes 589832 | tf_op jit(solution)/shard_map/ppermute | solution.py:16
  6.4 1.5 %collective-permute-start.7 = (bf16[128,768]{1,0:T(8,128)(2,1)}, bf16[128,768]{1,0:T(8,128)(2,1)S(1)}, u32[]{:S(2)}, u32[]{:S(2)}) collective-permute-start(bf16[128,768]{1,0:T(8,128)(2,1)} %param.7), channel_id=1, source_target_pairs={{0,1},{1,0},{2,3},{3,2},{4,5},{5,4},{6,7},{7,6},{8,9},{9,8},{10,11... | collective-permute-start | bytes 589832 | tf_op jit(solution)/shard_map/ppermute | solution.py:16
  7.9 1.5 %multiply_reduce_fusion.1 = (f32[256]{0:T(256)S(1)}, bf16[256,768]{1,0:T(8,128)(2,1)S(1)}) fusion(f32[256,768]{1,0:T(8,128)} %param.9), kind=kLoop, calls=%fused_computation.24 | loop fusion | flops 589568 | bytes 1180672 | tf_op jit(solution)/shard_map/reduce_sum | solution.py:75
  10.2 1.6 %collective-permute-start.4 = (bf16[8,768]{1,0:T(8,128)(2,1)S(1)}, bf16[8,768]{1,0:T(8,128)(2,1)S(1)}, u32[]{:S(2)}, u32[]{:S(2)}) collective-permute-start(bf16[8,768]{1,0:T(8,128)(2,1)S(1)} %pad_maximum_fusion.4), channel_id=1, source_target_pairs={{0,16},{8,24},{16,0},{24,8},{1,17},{9,25},{17,1},{25,9},{2,18},{10... | collective-permute-start | bytes 36872 | tf_op jit(solution)/shard_map/ppermute | solution.py:16
  12.4 1.5 %collective-permute-done.4 = bf16[8,768]{1,0:T(8,128)(2,1)S(1)} collective-permute-done((bf16[8,768]{1,0:T(8,128)(2,1)S(1)}, bf16[8,768]{1,0:T(8,128)(2,1)S(1)}, u32[]{:S(2)}, u32[]{:S(2)}) %collective-permute-start.4) | collective-permute-done | bytes 12320 | tf_op jit(solution)/shard_map/ppermute | solution.py:16
  14.0 0.8 %collective-permute-done.2 = bf16[128,768]{1,0:T(8,128)(2,1)S(1)} collective-permute-done((bf16[128,768]{1,0:T(8,128)(2,1)}, bf16[128,768]{1,0:T(8,128)(2,1)S(1)}, u32[]{:S(2)}, u32[]{:S(2)}) %collective-permute-start.2) | collective-permute-done | bytes 196640 | tf_op jit(solution)/shard_map/ppermute | solution.py:16
  14.8 0.8 %collective-permute-start.3 = (bf16[128,768]{1,0:T(8,128)(2,1)S(1)}, bf16[128,768]{1,0:T(8,128)(2,1)S(1)}, u32[]{:S(2)}, u32[]{:S(2)}) collective-permute-start(bf16[128,768]{1,0:T(8,128)(2,1)S(1)} %collective-permute-done.2), channel_id=1, source_target_pairs={{0,2},{1,3},{2,0},{3,1},{4,6},{5,7},{6,4},{7,5},{8,10},{9,11},{10,... | collective-permute-start | bytes 589832 | tf_op jit(solution)/shard_map/ppermute | solution.py:16
  15.6 1.5 %collective-permute-start.11 = (bf16[128,768]{1,0:T(8,128)(2,1)S(1)}, bf16[128,768]{1,0:T(8,128)(2,1)}, u32[]{:S(2)}, u32[]{:S(2)}) collective-permute-start(bf16[128,768]{1,0:T(8,128)(2,1)S(1)} %collective-permute-done.2), channel_id=1, source_target_pairs={{0,1},{1,0},{2,3},{3,2},{4,5},{5,4},{6,7},{7,6},{8,9},{9,8},{10,11... | collective-permute-start | bytes 589832 | tf_op jit(solution)/shard_map/ppermute | solution.py:16
  18.5 2.9 %collective-permute-done.3 = bf16[128,768]{1,0:T(8,128)(2,1)S(1)} collective-permute-done((bf16[128,768]{1,0:T(8,128)(2,1)S(1)}, bf16[128,768]{1,0:T(8,128)(2,1)S(1)}, u32[]{:S(2)}, u32[]{:S(2)}) %collective-permute-start.3) | collective-permute-done | bytes 196640 | tf_op jit(solution)/shard_map/ppermute | solution.py:16
  22.6 1.1 %collective-permute-start.8 = (f32[1,2,2,128]{3,2,1,0:T(2,128)S(1)}, f32[1,2,2,128]{3,2,1,0:T(2,128)S(1)}, u32[]{:S(2)}, u32[]{:S(2)}) collective-permute-start(f32[1,2,2,128]{3,2,1,0:T(2,128)S(1)} %bitcast.143), channel_id=1, source_target_pairs={{0,2},{1,3},{2,0},{3,1},{4,6},{5,7},{6,4},{7,5},{8,10},{9,11},{10,... | collective-permute-start | bytes 6152 | tf_op jit(solution)/shard_map/ppermute | solution.py:16
  24.4 1.5 %collective-permute-start.12 = (bf16[128,768]{1,0:T(8,128)(2,1)}, bf16[128,768]{1,0:T(8,128)(2,1)}, u32[]{:S(2)}, u32[]{:S(2)}) collective-permute-start(bf16[128,768]{1,0:T(8,128)(2,1)} %slice.239), channel_id=1, source_target_pairs={{0,1},{1,0},{2,3},{3,2},{4,5},{5,4},{6,7},{7,6},{8,9},{9,8},{10,11... | collective-permute-start | bytes 589832 | tf_op jit(solution)/shard_map/ppermute | solution.py:16
  26.3 0.9 %collective-permute-done.9 = bf16[128,768]{1,0:T(8,128)(2,1)} collective-permute-done((bf16[128,768]{1,0:T(8,128)(2,1)S(1)}, bf16[128,768]{1,0:T(8,128)(2,1)}, u32[]{:S(2)}, u32[]{:S(2)}) %collective-permute-start.9) | collective-permute-done | bytes 196640 | tf_op jit(solution)/shard_map/ppermute | solution.py:16
  27.2 2.8 %collective-permute-start.10 = (f32[1,2,2,128]{3,2,1,0:T(2,128)S(1)}, f32[1,2,2,128]{3,2,1,0:T(2,128)S(1)}, u32[]{:S(2)}, u32[]{:S(2)}) collective-permute-start(f32[1,2,2,128]{3,2,1,0:T(2,128)S(1)} %log_add_fusion.6), channel_id=1, source_target_pairs={{0,4},{1,5},{2,6},{3,7},{4,0},{5,1},{6,2},{7,3},{8,12},{9,13},{10,... | collective-permute-start | bytes 6152 | tf_op jit(solution)/shard_map/ppermute | solution.py:16
  30.0 0.9 %constant_dynamic-update-slice_fusion.6 = bf16[512,768]{1,0:T(8,128)(2,1)S(1)} fusion(bf16[512,768]{1,0:T(8,128)(2,1)S(1)} %constant_dynamic-update-slice_fusion.7, bf16[128,768]{1,0:T(8,128)(2,1)} %collective-permute-done.9), kind=kLoop, calls=%fused_computation.116 | loop fusion | bytes 393216
  30.9 0.8 %collective-permute-done.10 = f32[1,2,2,128]{3,2,1,0:T(2,128)S(1)} collective-permute-done((f32[1,2,2,128]{3,2,1,0:T(2,128)S(1)}, f32[1,2,2,128]{3,2,1,0:T(2,128)S(1)}, u32[]{:S(2)}, u32[]{:S(2)}) %collective-permute-start.10) | collective-permute-done | bytes 2080 | tf_op jit(solution)/shard_map/ppermute | solution.py:16
  31.7 1.4 %collective-permute-start.13 = (f32[1,2,2,128]{3,2,1,0:T(2,128)S(1)}, f32[1,2,2,128]{3,2,1,0:T(2,128)S(1)}, u32[]{:S(2)}, u32[]{:S(2)}) collective-permute-start(f32[1,2,2,128]{3,2,1,0:T(2,128)S(1)} %log_add_fusion.5), channel_id=1, source_target_pairs={{0,1},{1,0},{2,3},{3,2},{4,5},{5,4},{6,7},{7,6},{8,9},{9,8},{10,11... | collective-permute-start | bytes 6152 | tf_op jit(solution)/shard_map/ppermute | solution.py:16
  33.1 0.9 %constant_dynamic-update-slice_fusion.5 = bf16[512,768]{1,0:T(8,128)(2,1)S(1)} fusion(bf16[512,768]{1,0:T(8,128)(2,1)S(1)} %constant_dynamic-update-slice_fusion.6, bf16[128,768]{1,0:T(8,128)(2,1)} %collective-permute-done.11), kind=kLoop, calls=%fused_computation.115 | loop fusion | bytes 393216
  34.1 0.9 %constant_dynamic-update-slice_fusion.4 = bf16[512,768]{1,0:T(8,128)(2,1)S(1)} fusion(bf16[512,768]{1,0:T(8,128)(2,1)S(1)} %constant_dynamic-update-slice_fusion.5, bf16[128,768]{1,0:T(8,128)(2,1)} %collective-permute-done.12), kind=kLoop, calls=%fused_computation.114 | loop fusion | bytes 393216 | tf_op jit(solution)/shard_map/concatenate | solution.py:138
  38.0 1.6 %collective-permute-start.15 = (bf16[136,384]{1,0:T(8,128)(2,1)S(1)}, bf16[136,384]{1,0:T(8,128)(2,1)S(1)}, u32[]{:S(2)}, u32[]{:S(2)}) collective-permute-start(bf16[136,384]{1,0:T(8,128)(2,1)S(1)} %pad_maximum_fusion.1), channel_id=1, source_target_pairs={{0,16},{8,24},{16,0},{24,8},{1,17},{9,25},{17,1},{25,9},{2,18},{10... | collective-permute-start | bytes 313352 | tf_op jit(solution)/shard_map/ppermute | solution.py:16
  40.3 3.5 %collective-permute-done.15 = bf16[136,384]{1,0:T(8,128)(2,1)S(1)} collective-permute-done((bf16[136,384]{1,0:T(8,128)(2,1)S(1)}, bf16[136,384]{1,0:T(8,128)(2,1)S(1)}, u32[]{:S(2)}, u32[]{:S(2)}) %collective-permute-start.15) | collective-permute-done | bytes 104480 | tf_op jit(solution)/shard_map/ppermute | solution.py:16
  44.0 1.1 %collective-permute-done.18 = bf16[128,384]{1,0:T(8,128)(2,1)S(1)} collective-permute-done((bf16[128,384]{1,0:T(8,128)(2,1)S(1)}, bf16[128,384]{1,0:T(8,128)(2,1)S(1)}, u32[]{:S(2)}, u32[]{:S(2)}) %collective-permute-start.18) | collective-permute-done | bytes 98336 | tf_op jit(solution)/shard_map/ppermute | solution.py:16
  45.5 1.3 %collective-permute-done.19 = f32[128,384]{1,0:T(8,128)S(1)} collective-permute-done((f32[128,384]{1,0:T(8,128)S(1)}, f32[128,384]{1,0:T(8,128)S(1)}, u32[]{:S(2)}, u32[]{:S(2)}) %collective-permute-start.19) | collective-permute-done | bytes 196640 | tf_op jit(solution)/shard_map/ppermute | solution.py:16
  48.0 1.3 %collective-permute-start.20 = (f32[2,2,2,128]{3,2,1,0:T(2,128)S(1)}, f32[2,2,2,128]{3,2,1,0:T(2,128)S(1)}, u32[]{:S(2)}, u32[]{:S(2)}) collective-permute-start(f32[2,2,2,128]{3,2,1,0:T(2,128)S(1)} %pad_maximum_fusion.6), channel_id=1, source_target_pairs={{0,1},{1,0},{2,3},{3,2},{4,5},{5,4},{6,7},{7,6},{8,9},{9,8},{10,11... | collective-permute-start | bytes 12296 | tf_op jit(solution)/shard_map/ppermute | solution.py:16
  49.4 2.3 %collective-permute-done.20 = f32[2,2,2,128]{3,2,1,0:T(2,128)S(1)} collective-permute-done((f32[2,2,2,128]{3,2,1,0:T(2,128)S(1)}, f32[2,2,2,128]{3,2,1,0:T(2,128)S(1)}, u32[]{:S(2)}, u32[]{:S(2)}) %collective-permute-start.20) | collective-permute-done | bytes 4128 | tf_op jit(solution)/shard_map/ppermute | solution.py:16
  52.0 1.0 %collective-permute-start.21 = (f32[2,2,2,128]{3,2,1,0:T(2,128)S(1)}, f32[2,2,2,128]{3,2,1,0:T(2,128)S(1)}, u32[]{:S(2)}, u32[]{:S(2)}) collective-permute-start(f32[2,2,2,128]{3,2,1,0:T(2,128)S(1)} %log_add_fusion.2), channel_id=1, source_target_pairs={{0,2},{1,3},{2,0},{3,1},{4,6},{5,7},{6,4},{7,5},{8,10},{9,11},{10,... | collective-permute-start | bytes 12296 | tf_op jit(solution)/shard_map/ppermute | solution.py:16
  55.7 3.0 %collective-permute-start.22 = (f32[2,2,2,128]{3,2,1,0:T(2,128)S(1)}, f32[2,2,2,128]{3,2,1,0:T(2,128)S(1)}, u32[]{:S(2)}, u32[]{:S(2)}) collective-permute-start(f32[2,2,2,128]{3,2,1,0:T(2,128)S(1)} %log_add_fusion.1), channel_id=1, source_target_pairs={{0,4},{1,5},{2,6},{3,7},{4,0},{5,1},{6,2},{7,3},{8,12},{9,13},{10,... | collective-permute-start | bytes 12296 | tf_op jit(solution)/shard_map/ppermute | solution.py:16
  58.7 1.6 %collective-permute-done.22 = f32[2,2,2,128]{3,2,1,0:T(2,128)S(1)} collective-permute-done((f32[2,2,2,128]{3,2,1,0:T(2,128)S(1)}, f32[2,2,2,128]{3,2,1,0:T(2,128)S(1)}, u32[]{:S(2)}, u32[]{:S(2)}) %collective-permute-start.22) | collective-permute-done | bytes 4128 | tf_op jit(solution)/shard_map/ppermute | solution.py:16
  63.2 1.6 %collective-permute-start.24 = (bf16[136,384]{1,0:T(8,128)(2,1)S(1)}, bf16[136,384]{1,0:T(8,128)(2,1)S(1)}, u32[]{:S(2)}, u32[]{:S(2)}) collective-permute-start(bf16[136,384]{1,0:T(8,128)(2,1)S(1)} %pad_maximum_fusion.2), channel_id=1, source_target_pairs={{0,16},{8,24},{16,0},{24,8},{1,17},{9,25},{17,1},{25,9},{2,18},{10... | collective-permute-start | bytes 313352 | tf_op jit(solution)/shard_map/ppermute | solution.py:16
  65.4 3.6 %collective-permute-done.24 = bf16[136,384]{1,0:T(8,128)(2,1)S(1)} collective-permute-done((bf16[136,384]{1,0:T(8,128)(2,1)S(1)}, bf16[136,384]{1,0:T(8,128)(2,1)S(1)}, u32[]{:S(2)}, u32[]{:S(2)}) %collective-permute-start.24) | collective-permute-done | bytes 104480 | tf_op jit(solution)/shard_map/ppermute | solution.py:16
  69.2 1.1 %collective-permute-done.27 = bf16[128,384]{1,0:T(8,128)(2,1)S(1)} collective-permute-done((bf16[128,384]{1,0:T(8,128)(2,1)S(1)}, bf16[128,384]{1,0:T(8,128)(2,1)S(1)}, u32[]{:S(2)}, u32[]{:S(2)}) %collective-permute-start.27) | collective-permute-done | bytes 98336 | tf_op jit(solution)/shard_map/ppermute | solution.py:16
  71.9 0.9 %maximum_maximum_fusion.1 = f32[256,768]{1,0:T(8,128)} fusion(f32[128,384]{1,0:T(8,128)S(1)} %get-tuple-element.99, f32[128,384]{1,0:T(8,128)S(1)} %get-tuple-element.98, f32[128,384]{1,0:T(8,128)S(1)} %get-tuple-element.97, f32[128,384]{1,0:T(8,128)S(1)} %get-tuple-element.96), kind=kLoop, calls=%fused_computation.22 | loop fusion | flops 589824 | bytes 1572864 | tf_op jit(solution)/shard_map/concatenate | solution.py:217
  (158 shorter events, 19.2 us)
Async XLA Ops:
  0.6 8.8 %copy-start = (f32[256,768]{1,0:T(8,128)S(1)}, f32[256,768]{1,0:T(8,128)}, u32[]{:S(2)}) copy-start(f32[256,768]{1,0:T(8,128)} %param.9) | copy-start | bytes 2359300
  0.6 4.2 %collective-permute-start = (bf16[4,768]{1,0:T(4,128)(2,1)}, bf16[4,768]{1,0:T(4,128)(2,1)S(1)}, u32[]{:S(2)}, u32[]{:S(2)}) collective-permute-start(bf16[4,768]{1,0:T(4,128)(2,1)} %param.8), channel_id=1, source_target_pairs={{0,8},{8,0},{16,24},{24,16},{1,9},{9,1},{17,25},{25,17},{2,10},{10... | collective-permute-start | bytes 18440 | tf_op jit(solution)/shard_map/ppermute | solution.py:16
  1.2 13.7 %collective-permute-start.2 = (bf16[128,768]{1,0:T(8,128)(2,1)}, bf16[128,768]{1,0:T(8,128)(2,1)S(1)}, u32[]{:S(2)}, u32[]{:S(2)}) collective-permute-start(bf16[128,768]{1,0:T(8,128)(2,1)} %param.7), channel_id=1, source_target_pairs={{0,4},{1,5},{2,6},{3,7},{4,0},{5,1},{6,2},{7,3},{8,12},{9,13},{10,... | collective-permute-start | bytes 589832 | tf_op jit(solution)/shard_map/ppermute | solution.py:16
  4.8 12.3 %collective-permute-start.1 = (bf16[128,768]{1,0:T(8,128)(2,1)}, bf16[128,768]{1,0:T(8,128)(2,1)S(1)}, u32[]{:S(2)}, u32[]{:S(2)}) collective-permute-start(bf16[128,768]{1,0:T(8,128)(2,1)} %param.7), channel_id=1, source_target_pairs={{0,2},{1,3},{2,0},{3,1},{4,6},{5,7},{6,4},{7,5},{8,10},{9,11},{10,... | collective-permute-start | bytes 589832 | tf_op jit(solution)/shard_map/ppermute | solution.py:16
  6.4 16.2 %collective-permute-start.7 = (bf16[128,768]{1,0:T(8,128)(2,1)}, bf16[128,768]{1,0:T(8,128)(2,1)S(1)}, u32[]{:S(2)}, u32[]{:S(2)}) collective-permute-start(bf16[128,768]{1,0:T(8,128)(2,1)} %param.7), channel_id=1, source_target_pairs={{0,1},{1,0},{2,3},{3,2},{4,5},{5,4},{6,7},{7,6},{8,9},{9,8},{10,11... | collective-permute-start | bytes 589832 | tf_op jit(solution)/shard_map/ppermute | solution.py:16
  10.2 3.8 %collective-permute-start.4 = (bf16[8,768]{1,0:T(8,128)(2,1)S(1)}, bf16[8,768]{1,0:T(8,128)(2,1)S(1)}, u32[]{:S(2)}, u32[]{:S(2)}) collective-permute-start(bf16[8,768]{1,0:T(8,128)(2,1)S(1)} %pad_maximum_fusion.4), channel_id=1, source_target_pairs={{0,16},{8,24},{16,0},{24,8},{1,17},{9,25},{17,1},{25,9},{2,18},{10... | collective-permute-start | bytes 36872 | tf_op jit(solution)/shard_map/ppermute | solution.py:16
  11.8 5.3 %copy-start.1 = (bf16[128,768]{1,0:T(8,128)(2,1)S(1)}, bf16[128,768]{1,0:T(8,128)(2,1)}, u32[]{:S(2)}) copy-start(bf16[128,768]{1,0:T(8,128)(2,1)} %param.7) | copy-start | bytes 589828
  11.8 6.7 %collective-permute-start.5 = (bf16[136,768]{1,0:T(8,128)(2,1)S(1)}, bf16[136,768]{1,0:T(8,128)(2,1)S(1)}, u32[]{:S(2)}, u32[]{:S(2)}) collective-permute-start(bf16[136,768]{1,0:T(8,128)(2,1)S(1)} %pad_maximum_fusion), channel_id=1, source_target_pairs={{0,1},{1,0},{2,3},{3,2},{4,5},{5,4},{6,7},{7,6},{8,9},{9,8},{10,11... | collective-permute-start | bytes 626696 | tf_op jit(solution)/shard_map/ppermute | solution.py:16
  14.8 6.6 %collective-permute-start.3 = (bf16[128,768]{1,0:T(8,128)(2,1)S(1)}, bf16[128,768]{1,0:T(8,128)(2,1)S(1)}, u32[]{:S(2)}, u32[]{:S(2)}) collective-permute-start(bf16[128,768]{1,0:T(8,128)(2,1)S(1)} %collective-permute-done.2), channel_id=1, source_target_pairs={{0,2},{1,3},{2,0},{3,1},{4,6},{5,7},{6,4},{7,5},{8,10},{9,11},{10,... | collective-permute-start | bytes 589832 | tf_op jit(solution)/shard_map/ppermute | solution.py:16
  15.6 16.1 %collective-permute-start.11 = (bf16[128,768]{1,0:T(8,128)(2,1)S(1)}, bf16[128,768]{1,0:T(8,128)(2,1)}, u32[]{:S(2)}, u32[]{:S(2)}) collective-permute-start(bf16[128,768]{1,0:T(8,128)(2,1)S(1)} %collective-permute-done.2), channel_id=1, source_target_pairs={{0,1},{1,0},{2,3},{3,2},{4,5},{5,4},{6,7},{7,6},{8,9},{9,8},{10,11... | collective-permute-start | bytes 589832 | tf_op jit(solution)/shard_map/ppermute | solution.py:16
  17.1 10.1 %collective-permute-start.9 = (bf16[128,768]{1,0:T(8,128)(2,1)S(1)}, bf16[128,768]{1,0:T(8,128)(2,1)}, u32[]{:S(2)}, u32[]{:S(2)}) collective-permute-start(bf16[128,768]{1,0:T(8,128)(2,1)S(1)} %collective-permute-done.1), channel_id=1, source_target_pairs={{0,1},{1,0},{2,3},{3,2},{4,5},{5,4},{6,7},{7,6},{8,9},{9,8},{10,11... | collective-permute-start | bytes 589832 | tf_op jit(solution)/shard_map/ppermute | solution.py:16
  18.5 3.3 %collective-permute-start.6 = (bf16[136,768]{1,0:T(8,128)(2,1)S(1)}, bf16[136,768]{1,0:T(8,128)(2,1)S(1)}, u32[]{:S(2)}, u32[]{:S(2)}) collective-permute-start(bf16[136,768]{1,0:T(8,128)(2,1)S(1)} %collective-permute-done.5), channel_id=1, source_target_pairs={{0,8},{8,0},{16,24},{24,16},{1,9},{9,1},{17,25},{25,17},{2,10},{10... | collective-permute-start | bytes 626696 | tf_op jit(solution)/shard_map/ppermute | solution.py:16
  22.6 3.7 %collective-permute-start.8 = (f32[1,2,2,128]{3,2,1,0:T(2,128)S(1)}, f32[1,2,2,128]{3,2,1,0:T(2,128)S(1)}, u32[]{:S(2)}, u32[]{:S(2)}) collective-permute-start(f32[1,2,2,128]{3,2,1,0:T(2,128)S(1)} %bitcast.143), channel_id=1, source_target_pairs={{0,2},{1,3},{2,0},{3,1},{4,6},{5,7},{6,4},{7,5},{8,10},{9,11},{10,... | collective-permute-start | bytes 6152 | tf_op jit(solution)/shard_map/ppermute | solution.py:16
  24.4 7.3 %collective-permute-start.12 = (bf16[128,768]{1,0:T(8,128)(2,1)}, bf16[128,768]{1,0:T(8,128)(2,1)}, u32[]{:S(2)}, u32[]{:S(2)}) collective-permute-start(bf16[128,768]{1,0:T(8,128)(2,1)} %slice.239), channel_id=1, source_target_pairs={{0,1},{1,0},{2,3},{3,2},{4,5},{5,4},{6,7},{7,6},{8,9},{9,8},{10,11... | collective-permute-start | bytes 589832 | tf_op jit(solution)/shard_map/ppermute | solution.py:16
  27.2 4.5 %collective-permute-start.10 = (f32[1,2,2,128]{3,2,1,0:T(2,128)S(1)}, f32[1,2,2,128]{3,2,1,0:T(2,128)S(1)}, u32[]{:S(2)}, u32[]{:S(2)}) collective-permute-start(f32[1,2,2,128]{3,2,1,0:T(2,128)S(1)} %log_add_fusion.6), channel_id=1, source_target_pairs={{0,4},{1,5},{2,6},{3,7},{4,0},{5,1},{6,2},{7,3},{8,12},{9,13},{10,... | collective-permute-start | bytes 6152 | tf_op jit(solution)/shard_map/ppermute | solution.py:16
  31.7 3.7 %collective-permute-start.13 = (f32[1,2,2,128]{3,2,1,0:T(2,128)S(1)}, f32[1,2,2,128]{3,2,1,0:T(2,128)S(1)}, u32[]{:S(2)}, u32[]{:S(2)}) collective-permute-start(f32[1,2,2,128]{3,2,1,0:T(2,128)S(1)} %log_add_fusion.5), channel_id=1, source_target_pairs={{0,1},{1,0},{2,3},{3,2},{4,5},{5,4},{6,7},{7,6},{8,9},{9,8},{10,11... | collective-permute-start | bytes 6152 | tf_op jit(solution)/shard_map/ppermute | solution.py:16
  36.4 1.5 %collective-permute-start.14 = (f32[136,384]{1,0:T(8,128)S(1)}, f32[136,384]{1,0:T(8,128)S(1)}, u32[]{:S(2)}, u32[]{:S(2)}) collective-permute-start(f32[136,384]{1,0:T(8,128)S(1)} %select_maximum_fusion.1), channel_id=1, source_target_pairs={{0,8},{8,0},{16,24},{24,16},{1,9},{9,1},{17,25},{25,17},{2,10},{10... | collective-permute-start | bytes 626696 | tf_op jit(solution)/shard_map/ppermute | solution.py:16
  37.1 2.5 %collective-permute-start.17 = (f32[128,384]{1,0:T(8,128)S(1)}, f32[128,384]{1,0:T(8,128)S(1)}, u32[]{:S(2)}, u32[]{:S(2)}) collective-permute-start(f32[128,384]{1,0:T(8,128)S(1)} %slice_select_fusion.5), channel_id=1, source_target_pairs={{0,8},{8,0},{16,24},{24,16},{1,9},{9,1},{17,25},{25,17},{2,10},{10... | collective-permute-start | bytes 589832 | tf_op jit(solution)/shard_map/ppermute | solution.py:16
  38.0 5.8 %collective-permute-start.15 = (bf16[136,384]{1,0:T(8,128)(2,1)S(1)}, bf16[136,384]{1,0:T(8,128)(2,1)S(1)}, u32[]{:S(2)}, u32[]{:S(2)}) collective-permute-start(bf16[136,384]{1,0:T(8,128)(2,1)S(1)} %pad_maximum_fusion.1), channel_id=1, source_target_pairs={{0,16},{8,24},{16,0},{24,8},{1,17},{9,25},{17,1},{25,9},{2,18},{10... | collective-permute-start | bytes 313352 | tf_op jit(solution)/shard_map/ppermute | solution.py:16
  39.6 5.5 %collective-permute-start.18 = (bf16[128,384]{1,0:T(8,128)(2,1)S(1)}, bf16[128,384]{1,0:T(8,128)(2,1)S(1)}, u32[]{:S(2)}, u32[]{:S(2)}) collective-permute-start(bf16[128,384]{1,0:T(8,128)(2,1)S(1)} %add_convert_fusion.1), channel_id=1, source_target_pairs={{0,16},{8,24},{16,0},{24,8},{1,17},{9,25},{17,1},{25,9},{2,18},{10... | collective-permute-start | bytes 294920 | tf_op jit(solution)/shard_map/ppermute | solution.py:16
  43.9 1.5 %collective-permute-start.16 = (f32[128,384]{1,0:T(8,128)S(1)}, f32[128,384]{1,0:T(8,128)S(1)}, u32[]{:S(2)}, u32[]{:S(2)}) collective-permute-start(f32[128,384]{1,0:T(8,128)S(1)} %fusion.37), channel_id=1, source_target_pairs={{0,8},{8,0},{16,24},{24,16},{1,9},{9,1},{17,25},{25,17},{2,10},{10... | collective-permute-start | bytes 589832 | tf_op jit(solution)/shard_map/ppermute | solution.py:16
  45.2 1.5 %collective-permute-start.19 = (f32[128,384]{1,0:T(8,128)S(1)}, f32[128,384]{1,0:T(8,128)S(1)}, u32[]{:S(2)}, u32[]{:S(2)}) collective-permute-start(f32[128,384]{1,0:T(8,128)S(1)} %fusion.36), channel_id=1, source_target_pairs={{0,8},{8,0},{16,24},{24,16},{1,9},{9,1},{17,25},{25,17},{2,10},{10... | collective-permute-start | bytes 589832 | tf_op jit(solution)/shard_map/ppermute | solution.py:16
  48.0 3.7 %collective-permute-start.20 = (f32[2,2,2,128]{3,2,1,0:T(2,128)S(1)}, f32[2,2,2,128]{3,2,1,0:T(2,128)S(1)}, u32[]{:S(2)}, u32[]{:S(2)}) collective-permute-start(f32[2,2,2,128]{3,2,1,0:T(2,128)S(1)} %pad_maximum_fusion.6), channel_id=1, source_target_pairs={{0,1},{1,0},{2,3},{3,2},{4,5},{5,4},{6,7},{7,6},{8,9},{9,8},{10,11... | collective-permute-start | bytes 12296 | tf_op jit(solution)/shard_map/ppermute | solution.py:16
  52.0 1.0 %copy-start.4 = (s32[128]{0:T(128)S(1)}, s32[128]{0:T(128)}, u32[]{:S(2)}) copy-start(s32[128]{0:T(128)} %param.11) | copy-start | bytes 1540
  52.0 3.6 %collective-permute-start.21 = (f32[2,2,2,128]{3,2,1,0:T(2,128)S(1)}, f32[2,2,2,128]{3,2,1,0:T(2,128)S(1)}, u32[]{:S(2)}, u32[]{:S(2)}) collective-permute-start(f32[2,2,2,128]{3,2,1,0:T(2,128)S(1)} %log_add_fusion.2), channel_id=1, source_target_pairs={{0,2},{1,3},{2,0},{3,1},{4,6},{5,7},{6,4},{7,5},{8,10},{9,11},{10,... | collective-permute-start | bytes 12296 | tf_op jit(solution)/shard_map/ppermute | solution.py:16
  55.7 4.6 %collective-permute-start.22 = (f32[2,2,2,128]{3,2,1,0:T(2,128)S(1)}, f32[2,2,2,128]{3,2,1,0:T(2,128)S(1)}, u32[]{:S(2)}, u32[]{:S(2)}) collective-permute-start(f32[2,2,2,128]{3,2,1,0:T(2,128)S(1)} %log_add_fusion.1), channel_id=1, source_target_pairs={{0,4},{1,5},{2,6},{3,7},{4,0},{5,1},{6,2},{7,3},{8,12},{9,13},{10,... | collective-permute-start | bytes 12296 | tf_op jit(solution)/shard_map/ppermute | solution.py:16
  61.4 1.5 %collective-permute-start.23 = (f32[136,384]{1,0:T(8,128)S(1)}, f32[136,384]{1,0:T(8,128)S(1)}, u32[]{:S(2)}, u32[]{:S(2)}) collective-permute-start(f32[136,384]{1,0:T(8,128)S(1)} %select_maximum_fusion), channel_id=1, source_target_pairs={{0,8},{8,0},{16,24},{24,16},{1,9},{9,1},{17,25},{25,17},{2,10},{10... | collective-permute-start | bytes 626696 | tf_op jit(solution)/shard_map/ppermute | solution.py:16
  62.1 2.7 %collective-permute-start.26 = (f32[128,384]{1,0:T(8,128)S(1)}, f32[128,384]{1,0:T(8,128)S(1)}, u32[]{:S(2)}, u32[]{:S(2)}) collective-permute-start(f32[128,384]{1,0:T(8,128)S(1)} %slice_select_fusion.3), channel_id=1, source_target_pairs={{0,8},{8,0},{16,24},{24,16},{1,9},{9,1},{17,25},{25,17},{2,10},{10... | collective-permute-start | bytes 589832 | tf_op jit(solution)/shard_map/ppermute | solution.py:16
  63.2 5.8 %collective-permute-start.24 = (bf16[136,384]{1,0:T(8,128)(2,1)S(1)}, bf16[136,384]{1,0:T(8,128)(2,1)S(1)}, u32[]{:S(2)}, u32[]{:S(2)}) collective-permute-start(bf16[136,384]{1,0:T(8,128)(2,1)S(1)} %pad_maximum_fusion.2), channel_id=1, source_target_pairs={{0,16},{8,24},{16,0},{24,8},{1,17},{9,25},{17,1},{25,9},{2,18},{10... | collective-permute-start | bytes 313352 | tf_op jit(solution)/shard_map/ppermute | solution.py:16
  64.8 5.5 %collective-permute-start.27 = (bf16[128,384]{1,0:T(8,128)(2,1)S(1)}, bf16[128,384]{1,0:T(8,128)(2,1)S(1)}, u32[]{:S(2)}, u32[]{:S(2)}) collective-permute-start(bf16[128,384]{1,0:T(8,128)(2,1)S(1)} %add_convert_fusion), channel_id=1, source_target_pairs={{0,16},{8,24},{16,0},{24,8},{1,17},{9,25},{17,1},{25,9},{2,18},{10... | collective-permute-start | bytes 294920 | tf_op jit(solution)/shard_map/ppermute | solution.py:16
  69.1 2.0 %collective-permute-start.25 = (f32[128,384]{1,0:T(8,128)S(1)}, f32[128,384]{1,0:T(8,128)S(1)}, u32[]{:S(2)}, u32[]{:S(2)}) collective-permute-start(f32[128,384]{1,0:T(8,128)S(1)} %fusion.34), channel_id=1, source_target_pairs={{0,8},{8,0},{16,24},{24,16},{1,9},{9,1},{17,25},{25,17},{2,10},{10... | collective-permute-start | bytes 589832 | tf_op jit(solution)/shard_map/ppermute | solution.py:16
  70.4 1.5 %collective-permute-start.28 = (f32[128,384]{1,0:T(8,128)S(1)}, f32[128,384]{1,0:T(8,128)S(1)}, u32[]{:S(2)}, u32[]{:S(2)}) collective-permute-start(f32[128,384]{1,0:T(8,128)S(1)} %fusion.33), channel_id=1, source_target_pairs={{0,8},{8,0},{16,24},{24,16},{1,9},{9,1},{17,25},{25,17},{2,10},{10... | collective-permute-start | bytes 589832 | tf_op jit(solution)/shard_map/ppermute | solution.py:16
  (2 other events, 1.4 us)

commit v9 on v8

--- a/solution.py
+++ b/solution.py
@@ -61,7 +61,9 @@
 
     evens = list(range(0, n_cent, 2))
     pieces = column_pieces(passages, later, "cent", n_cent)
-    across = {mask: swap(pieces[mask], "cent", 1) for mask in evens[:-1]}
+    far = evens[half // 2]
+    late, pieces[2] = lax.optimization_barrier((pieces[far], pieces[2]))
+    across = {mask: swap(late if mask == far else pieces[mask], "cent", 1) for mask in evens[:-1]}
     asked = in_order(queries, asked, core)
     for bit in dp_bits[1:]:
         asked = in_order(asked, swap(asked, "dp", bit), dp & bit)

time: 73.2 us -> 72.6 us (level)
  waiting for transfers between devices: 24.2 us -> 22.9 us
  starting transfers between devices: 30.4 us -> 31.2 us
    ppermute x29, waiting for transfers between devices: 24.2 us -> 22.9 us  [swap(): return lax.ppermute(value, axis, [(i, i ^ bit) for i in range(size)])]
    ppermute x29, starting transfers between devices: 30.4 us -> 31.2 us  [swap(): return lax.ppermute(value, axis, [(i, i ^ bit) for i in range(size)])]
  transfers between devices with their start and end apart: 29 -> 29, of which waited for: 19 -> 18; matrix products, arithmetic and copies ran while one was open for 15% -> 15% of each run, Pallas kernels for 0% -> 0%
where the time goes in v9:
time: 72.6 us; the launch traced here: 72.4 us
  starting transfers between devices  31.2 us (43%)
  waiting for transfers between devices  22.9 us (32%)
  local copies, waits for them, and re-layouts  5.94 us (8%)
  other arithmetic  5.81 us (8%)
  matrix products  5.27 us (7%)
  between operations  1.25 us (2%)
    ppermute x29, starting transfers between devices, swap(): return lax.ppermute(value, axis, [(i, i ^ bit) for i in range(size)])  31.2 us
    ppermute x29, waiting for transfers between devices, swap(): return lax.ppermute(value, axis, [(i, i ^ bit) for i in range(size)])  22.9 us
    unnamed x16, local copies, waits for them, and re-layouts  3.2 us
    dot_general x8, matrix products, on_device(): jnp.dot(resps[index], held[index][:, part * cut:(part + 1) * cut], prefer...  2.34 us
    dot_general x5, matrix products, logits_of(): lax.dot_general(centers_half, group, (((1,), (1,)), ((), ())), preferred_...  2.08 us
    reduce_sum x2, other arithmetic, on_device(): norms = jnp.sum(means * means, axis=1)  1.65 us
  transfers between devices with their start and end apart: 29, of which 18 were waited for; matrix products, arithmetic and copies ran while one was open for 15% of the time, Pallas kernels for 0%

profile of v9, /device:TPU:0, one launch (start us, length us, event | category | flops | bytes accessed | tf_op | source)
XLA Modules:
  0.0 72.4 jit_solution(2493066814255820576)
XLA Ops:
  1.2 3.7 %collective-permute-start.1 = (bf16[128,768]{1,0:T(8,128)(2,1)}, bf16[128,768]{1,0:T(8,128)(2,1)S(1)}, u32[]{:S(2)}, u32[]{:S(2)}) collective-permute-start(bf16[128,768]{1,0:T(8,128)(2,1)} %param.7), channel_id=1, source_target_pairs={{0,4},{1,5},{2,6},{3,7},{4,0},{5,1},{6,2},{7,3},{8,12},{9,13},{10,... | collective-permute-start | bytes 589832 | tf_op jit(solution)/shard_map/ppermute | solution.py:16
  4.8 1.6 %collective-permute-start.2 = (bf16[128,768]{1,0:T(8,128)(2,1)}, bf16[128,768]{1,0:T(8,128)(2,1)S(1)}, u32[]{:S(2)}, u32[]{:S(2)}) collective-permute-start(bf16[128,768]{1,0:T(8,128)(2,1)} %param.7), channel_id=1, source_target_pairs={{0,2},{1,3},{2,0},{3,1},{4,6},{5,7},{6,4},{7,5},{8,10},{9,11},{10,... | collective-permute-start | bytes 589832 | tf_op jit(solution)/shard_map/ppermute | solution.py:16
  6.4 1.5 %collective-permute-start.7 = (bf16[128,768]{1,0:T(8,128)(2,1)}, bf16[128,768]{1,0:T(8,128)(2,1)S(1)}, u32[]{:S(2)}, u32[]{:S(2)}) collective-permute-start(bf16[128,768]{1,0:T(8,128)(2,1)} %param.7), channel_id=1, source_target_pairs={{0,1},{1,0},{2,3},{3,2},{4,5},{5,4},{6,7},{7,6},{8,9},{9,8},{10,11... | collective-permute-start | bytes 589832 | tf_op jit(solution)/shard_map/ppermute | solution.py:16
  7.9 1.5 %multiply_reduce_fusion.1 = (f32[256]{0:T(256)S(1)}, bf16[256,768]{1,0:T(8,128)(2,1)S(1)}) fusion(f32[256,768]{1,0:T(8,128)} %param.9), kind=kLoop, calls=%fused_computation.24 | loop fusion | flops 589568 | bytes 1180672 | tf_op jit(solution)/shard_map/reduce_sum | solution.py:77
  10.2 1.6 %collective-permute-start.4 = (bf16[8,768]{1,0:T(8,128)(2,1)S(1)}, bf16[8,768]{1,0:T(8,128)(2,1)S(1)}, u32[]{:S(2)}, u32[]{:S(2)}) collective-permute-start(bf16[8,768]{1,0:T(8,128)(2,1)S(1)} %pad_maximum_fusion.4), channel_id=1, source_target_pairs={{0,16},{8,24},{16,0},{24,8},{1,17},{9,25},{17,1},{25,9},{2,18},{10... | collective-permute-start | bytes 36872 | tf_op jit(solution)/shard_map/ppermute | solution.py:16
  12.4 1.5 %collective-permute-done.4 = bf16[8,768]{1,0:T(8,128)(2,1)S(1)} collective-permute-done((bf16[8,768]{1,0:T(8,128)(2,1)S(1)}, bf16[8,768]{1,0:T(8,128)(2,1)S(1)}, u32[]{:S(2)}, u32[]{:S(2)}) %collective-permute-start.4) | collective-permute-done | bytes 12320 | tf_op jit(solution)/shard_map/ppermute | solution.py:16
  14.0 0.8 %collective-permute-done.1 = bf16[128,768]{1,0:T(8,128)(2,1)S(1)} collective-permute-done((bf16[128,768]{1,0:T(8,128)(2,1)}, bf16[128,768]{1,0:T(8,128)(2,1)S(1)}, u32[]{:S(2)}, u32[]{:S(2)}) %collective-permute-start.1) | collective-permute-done | bytes 196640 | tf_op jit(solution)/shard_map/ppermute | solution.py:16
  14.8 0.8 %collective-permute-start.3 = (bf16[128,768]{1,0:T(8,128)(2,1)S(1)}, bf16[128,768]{1,0:T(8,128)(2,1)S(1)}, u32[]{:S(2)}, u32[]{:S(2)}) collective-permute-start(bf16[128,768]{1,0:T(8,128)(2,1)S(1)} %collective-permute-done.1), channel_id=1, source_target_pairs={{0,2},{1,3},{2,0},{3,1},{4,6},{5,7},{6,4},{7,5},{8,10},{9,11},{10,... | collective-permute-start | bytes 589832 | tf_op jit(solution)/shard_map/ppermute | solution.py:16
  15.6 1.5 %collective-permute-start.9 = (bf16[128,768]{1,0:T(8,128)(2,1)S(1)}, bf16[128,768]{1,0:T(8,128)(2,1)}, u32[]{:S(2)}, u32[]{:S(2)}) collective-permute-start(bf16[128,768]{1,0:T(8,128)(2,1)S(1)} %collective-permute-done.2), channel_id=1, source_target_pairs={{0,1},{1,0},{2,3},{3,2},{4,5},{5,4},{6,7},{7,6},{8,9},{9,8},{10,11... | collective-permute-start | bytes 589832 | tf_op jit(solution)/shard_map/ppermute | solution.py:16
  17.8 0.7 %collective-permute-done.5 = bf16[136,768]{1,0:T(8,128)(2,1)S(1)} collective-permute-done((bf16[136,768]{1,0:T(8,128)(2,1)S(1)}, bf16[136,768]{1,0:T(8,128)(2,1)S(1)}, u32[]{:S(2)}, u32[]{:S(2)}) %collective-permute-start.5) | collective-permute-done | bytes 208928 | tf_op jit(solution)/shard_map/ppermute | solution.py:16
  18.5 2.9 %collective-permute-done.3 = bf16[128,768]{1,0:T(8,128)(2,1)S(1)} collective-permute-done((bf16[128,768]{1,0:T(8,128)(2,1)S(1)}, bf16[128,768]{1,0:T(8,128)(2,1)S(1)}, u32[]{:S(2)}, u32[]{:S(2)}) %collective-permute-start.3) | collective-permute-done | bytes 196640 | tf_op jit(solution)/shard_map/ppermute | solution.py:16
  22.6 1.1 %collective-permute-start.8 = (f32[1,2,2,128]{3,2,1,0:T(2,128)S(1)}, f32[1,2,2,128]{3,2,1,0:T(2,128)S(1)}, u32[]{:S(2)}, u32[]{:S(2)}) collective-permute-start(f32[1,2,2,128]{3,2,1,0:T(2,128)S(1)} %bitcast.143), channel_id=1, source_target_pairs={{0,2},{1,3},{2,0},{3,1},{4,6},{5,7},{6,4},{7,5},{8,10},{9,11},{10,... | collective-permute-start | bytes 6152 | tf_op jit(solution)/shard_map/ppermute | solution.py:16
  24.4 1.5 %collective-permute-start.12 = (bf16[128,768]{1,0:T(8,128)(2,1)}, bf16[128,768]{1,0:T(8,128)(2,1)}, u32[]{:S(2)}, u32[]{:S(2)}) collective-permute-start(bf16[128,768]{1,0:T(8,128)(2,1)} %slice.239), channel_id=1, source_target_pairs={{0,1},{1,0},{2,3},{3,2},{4,5},{5,4},{6,7},{7,6},{8,9},{9,8},{10,11... | collective-permute-start | bytes 589832 | tf_op jit(solution)/shard_map/ppermute | solution.py:16
  26.3 3.0 %collective-permute-start.10 = (f32[1,2,2,128]{3,2,1,0:T(2,128)S(1)}, f32[1,2,2,128]{3,2,1,0:T(2,128)S(1)}, u32[]{:S(2)}, u32[]{:S(2)}) collective-permute-start(f32[1,2,2,128]{3,2,1,0:T(2,128)S(1)} %log_add_fusion.6), channel_id=1, source_target_pairs={{0,4},{1,5},{2,6},{3,7},{4,0},{5,1},{6,2},{7,3},{8,12},{9,13},{10,... | collective-permute-start | bytes 6152 | tf_op jit(solution)/shard_map/ppermute | solution.py:16
  29.3 0.9 %constant_dynamic-update-slice_fusion.6 = bf16[512,768]{1,0:T(8,128)(2,1)S(1)} fusion(bf16[512,768]{1,0:T(8,128)(2,1)S(1)} %constant_dynamic-update-slice_fusion.7, bf16[128,768]{1,0:T(8,128)(2,1)} %collective-permute-done.9), kind=kLoop, calls=%fused_computation.116 | loop fusion | bytes 393216
  31.0 1.3 %collective-permute-start.13 = (f32[1,2,2,128]{3,2,1,0:T(2,128)S(1)}, f32[1,2,2,128]{3,2,1,0:T(2,128)S(1)}, u32[]{:S(2)}, u32[]{:S(2)}) collective-permute-start(f32[1,2,2,128]{3,2,1,0:T(2,128)S(1)} %log_add_fusion.5), channel_id=1, source_target_pairs={{0,1},{1,0},{2,3},{3,2},{4,5},{5,4},{6,7},{7,6},{8,9},{9,8},{10,11... | collective-permute-start | bytes 6152 | tf_op jit(solution)/shard_map/ppermute | solution.py:16
  32.3 0.9 %constant_dynamic-update-slice_fusion.5 = bf16[512,768]{1,0:T(8,128)(2,1)S(1)} fusion(bf16[512,768]{1,0:T(8,128)(2,1)S(1)} %constant_dynamic-update-slice_fusion.6, bf16[128,768]{1,0:T(8,128)(2,1)} %collective-permute-done.11), kind=kLoop, calls=%fused_computation.115 | loop fusion | bytes 393216
  33.3 0.9 %constant_dynamic-update-slice_fusion.4 = bf16[512,768]{1,0:T(8,128)(2,1)S(1)} fusion(bf16[512,768]{1,0:T(8,128)(2,1)S(1)} %constant_dynamic-update-slice_fusion.5, bf16[128,768]{1,0:T(8,128)(2,1)} %collective-permute-done.12), kind=kLoop, calls=%fused_computation.114 | loop fusion | bytes 393216 | tf_op jit(solution)/shard_map/concatenate | solution.py:140
  37.2 1.6 %collective-permute-start.15 = (bf16[136,384]{1,0:T(8,128)(2,1)S(1)}, bf16[136,384]{1,0:T(8,128)(2,1)S(1)}, u32[]{:S(2)}, u32[]{:S(2)}) collective-permute-start(bf16[136,384]{1,0:T(8,128)(2,1)S(1)} %pad_maximum_fusion.1), channel_id=1, source_target_pairs={{0,16},{8,24},{16,0},{24,8},{1,17},{9,25},{17,1},{25,9},{2,18},{10... | collective-permute-start | bytes 313352 | tf_op jit(solution)/shard_map/ppermute | solution.py:16
  38.8 0.7 %collective-permute-start.18 = (bf16[128,384]{1,0:T(8,128)(2,1)S(1)}, bf16[128,384]{1,0:T(8,128)(2,1)S(1)}, u32[]{:S(2)}, u32[]{:S(2)}) collective-permute-start(bf16[128,384]{1,0:T(8,128)(2,1)S(1)} %add_convert_fusion.1), channel_id=1, source_target_pairs={{0,16},{8,24},{16,0},{24,8},{1,17},{9,25},{17,1},{25,9},{2,18},{10... | collective-permute-start | bytes 294920 | tf_op jit(solution)/shard_map/ppermute | solution.py:16
  39.5 3.5 %collective-permute-done.15 = bf16[136,384]{1,0:T(8,128)(2,1)S(1)} collective-permute-done((bf16[136,384]{1,0:T(8,128)(2,1)S(1)}, bf16[136,384]{1,0:T(8,128)(2,1)S(1)}, u32[]{:S(2)}, u32[]{:S(2)}) %collective-permute-start.15) | collective-permute-done | bytes 104480 | tf_op jit(solution)/shard_map/ppermute | solution.py:16
  43.2 1.1 %collective-permute-done.18 = bf16[128,384]{1,0:T(8,128)(2,1)S(1)} collective-permute-done((bf16[128,384]{1,0:T(8,128)(2,1)S(1)}, bf16[128,384]{1,0:T(8,128)(2,1)S(1)}, u32[]{:S(2)}, u32[]{:S(2)}) %collective-permute-start.18) | collective-permute-done | bytes 98336 | tf_op jit(solution)/shard_map/ppermute | solution.py:16
  44.7 1.3 %collective-permute-done.19 = f32[128,384]{1,0:T(8,128)S(1)} collective-permute-done((f32[128,384]{1,0:T(8,128)S(1)}, f32[128,384]{1,0:T(8,128)S(1)}, u32[]{:S(2)}, u32[]{:S(2)}) %collective-permute-start.19) | collective-permute-done | bytes 196640 | tf_op jit(solution)/shard_map/ppermute | solution.py:16
  47.2 1.3 %collective-permute-start.20 = (f32[2,2,2,128]{3,2,1,0:T(2,128)S(1)}, f32[2,2,2,128]{3,2,1,0:T(2,128)S(1)}, u32[]{:S(2)}, u32[]{:S(2)}) collective-permute-start(f32[2,2,2,128]{3,2,1,0:T(2,128)S(1)} %pad_maximum_fusion.6), channel_id=1, source_target_pairs={{0,1},{1,0},{2,3},{3,2},{4,5},{5,4},{6,7},{7,6},{8,9},{9,8},{10,11... | collective-permute-start | bytes 12296 | tf_op jit(solution)/shard_map/ppermute | solution.py:16
  48.6 2.3 %collective-permute-done.20 = f32[2,2,2,128]{3,2,1,0:T(2,128)S(1)} collective-permute-done((f32[2,2,2,128]{3,2,1,0:T(2,128)S(1)}, f32[2,2,2,128]{3,2,1,0:T(2,128)S(1)}, u32[]{:S(2)}, u32[]{:S(2)}) %collective-permute-start.20) | collective-permute-done | bytes 4128 | tf_op jit(solution)/shard_map/ppermute | solution.py:16
  51.2 1.5 %collective-permute-start.21 = (f32[2,2,2,128]{3,2,1,0:T(2,128)S(1)}, f32[2,2,2,128]{3,2,1,0:T(2,128)S(1)}, u32[]{:S(2)}, u32[]{:S(2)}) collective-permute-start(f32[2,2,2,128]{3,2,1,0:T(2,128)S(1)} %log_add_fusion.2), channel_id=1, source_target_pairs={{0,2},{1,3},{2,0},{3,1},{4,6},{5,7},{6,4},{7,5},{8,10},{9,11},{10,... | collective-permute-start | bytes 12296 | tf_op jit(solution)/shard_map/ppermute | solution.py:16
  55.1 3.1 %collective-permute-start.22 = (f32[2,2,2,128]{3,2,1,0:T(2,128)S(1)}, f32[2,2,2,128]{3,2,1,0:T(2,128)S(1)}, u32[]{:S(2)}, u32[]{:S(2)}) collective-permute-start(f32[2,2,2,128]{3,2,1,0:T(2,128)S(1)} %log_add_fusion.1), channel_id=1, source_target_pairs={{0,4},{1,5},{2,6},{3,7},{4,0},{5,1},{6,2},{7,3},{8,12},{9,13},{10,... | collective-permute-start | bytes 12296 | tf_op jit(solution)/shard_map/ppermute | solution.py:16
  58.2 1.6 %collective-permute-done.22 = f32[2,2,2,128]{3,2,1,0:T(2,128)S(1)} collective-permute-done((f32[2,2,2,128]{3,2,1,0:T(2,128)S(1)}, f32[2,2,2,128]{3,2,1,0:T(2,128)S(1)}, u32[]{:S(2)}, u32[]{:S(2)}) %collective-permute-start.22) | collective-permute-done | bytes 4128 | tf_op jit(solution)/shard_map/ppermute | solution.py:16
  62.6 1.6 %collective-permute-start.24 = (bf16[136,384]{1,0:T(8,128)(2,1)S(1)}, bf16[136,384]{1,0:T(8,128)(2,1)S(1)}, u32[]{:S(2)}, u32[]{:S(2)}) collective-permute-start(bf16[136,384]{1,0:T(8,128)(2,1)S(1)} %pad_maximum_fusion.2), channel_id=1, source_target_pairs={{0,16},{8,24},{16,0},{24,8},{1,17},{9,25},{17,1},{25,9},{2,18},{10... | collective-permute-start | bytes 313352 | tf_op jit(solution)/shard_map/ppermute | solution.py:16
  64.8 3.6 %collective-permute-done.24 = bf16[136,384]{1,0:T(8,128)(2,1)S(1)} collective-permute-done((bf16[136,384]{1,0:T(8,128)(2,1)S(1)}, bf16[136,384]{1,0:T(8,128)(2,1)S(1)}, u32[]{:S(2)}, u32[]{:S(2)}) %collective-permute-start.24) | collective-permute-done | bytes 104480 | tf_op jit(solution)/shard_map/ppermute | solution.py:16
  68.7 1.1 %collective-permute-done.27 = bf16[128,384]{1,0:T(8,128)(2,1)S(1)} collective-permute-done((bf16[128,384]{1,0:T(8,128)(2,1)S(1)}, bf16[128,384]{1,0:T(8,128)(2,1)S(1)}, u32[]{:S(2)}, u32[]{:S(2)}) %collective-permute-start.27) | collective-permute-done | bytes 98336 | tf_op jit(solution)/shard_map/ppermute | solution.py:16
  71.4 0.9 %maximum_maximum_fusion.1 = f32[256,768]{1,0:T(8,128)} fusion(f32[128,384]{1,0:T(8,128)S(1)} %get-tuple-element.103, f32[128,384]{1,0:T(8,128)S(1)} %get-tuple-element.102, f32[128,384]{1,0:T(8,128)S(1)} %get-tuple-element.101, f32[128,384]{1,0:T(8,128)S(1)} %get-tuple-element.100), kind=kLoop, calls=%fused_computation.22 | loop fusion | flops 589824 | bytes 1572864 | tf_op jit(solution)/shard_map/concatenate | solution.py:219
  (158 shorter events, 18.1 us)
Async XLA Ops:
  0.6 8.8 %copy-start = (f32[256,768]{1,0:T(8,128)S(1)}, f32[256,768]{1,0:T(8,128)}, u32[]{:S(2)}) copy-start(f32[256,768]{1,0:T(8,128)} %param.9) | copy-start | bytes 2359300
  0.6 4.2 %collective-permute-start = (bf16[4,768]{1,0:T(4,128)(2,1)}, bf16[4,768]{1,0:T(4,128)(2,1)S(1)}, u32[]{:S(2)}, u32[]{:S(2)}) collective-permute-start(bf16[4,768]{1,0:T(4,128)(2,1)} %param.8), channel_id=1, source_target_pairs={{0,8},{8,0},{16,24},{24,16},{1,9},{9,1},{17,25},{25,17},{2,10},{10... | collective-permute-start | bytes 18440 | tf_op jit(solution)/shard_map/ppermute | solution.py:16
  1.2 13.7 %collective-permute-start.1 = (bf16[128,768]{1,0:T(8,128)(2,1)}, bf16[128,768]{1,0:T(8,128)(2,1)S(1)}, u32[]{:S(2)}, u32[]{:S(2)}) collective-permute-start(bf16[128,768]{1,0:T(8,128)(2,1)} %param.7), channel_id=1, source_target_pairs={{0,4},{1,5},{2,6},{3,7},{4,0},{5,1},{6,2},{7,3},{8,12},{9,13},{10,... | collective-permute-start | bytes 589832 | tf_op jit(solution)/shard_map/ppermute | solution.py:16
  4.8 10.8 %collective-permute-start.2 = (bf16[128,768]{1,0:T(8,128)(2,1)}, bf16[128,768]{1,0:T(8,128)(2,1)S(1)}, u32[]{:S(2)}, u32[]{:S(2)}) collective-permute-start(bf16[128,768]{1,0:T(8,128)(2,1)} %param.7), channel_id=1, source_target_pairs={{0,2},{1,3},{2,0},{3,1},{4,6},{5,7},{6,4},{7,5},{8,10},{9,11},{10,... | collective-permute-start | bytes 589832 | tf_op jit(solution)/shard_map/ppermute | solution.py:16
  6.4 16.2 %collective-permute-start.7 = (bf16[128,768]{1,0:T(8,128)(2,1)}, bf16[128,768]{1,0:T(8,128)(2,1)S(1)}, u32[]{:S(2)}, u32[]{:S(2)}) collective-permute-start(bf16[128,768]{1,0:T(8,128)(2,1)} %param.7), channel_id=1, source_target_pairs={{0,1},{1,0},{2,3},{3,2},{4,5},{5,4},{6,7},{7,6},{8,9},{9,8},{10,11... | collective-permute-start | bytes 589832 | tf_op jit(solution)/shard_map/ppermute | solution.py:16
  10.2 3.8 %collective-permute-start.4 = (bf16[8,768]{1,0:T(8,128)(2,1)S(1)}, bf16[8,768]{1,0:T(8,128)(2,1)S(1)}, u32[]{:S(2)}, u32[]{:S(2)}) collective-permute-start(bf16[8,768]{1,0:T(8,128)(2,1)S(1)} %pad_maximum_fusion.4), channel_id=1, source_target_pairs={{0,16},{8,24},{16,0},{24,8},{1,17},{9,25},{17,1},{25,9},{2,18},{10... | collective-permute-start | bytes 36872 | tf_op jit(solution)/shard_map/ppermute | solution.py:16
  11.8 5.3 %copy-start.1 = (bf16[128,768]{1,0:T(8,128)(2,1)S(1)}, bf16[128,768]{1,0:T(8,128)(2,1)}, u32[]{:S(2)}) copy-start(bf16[128,768]{1,0:T(8,128)(2,1)} %param.7) | copy-start | bytes 589828
  11.8 6.7 %collective-permute-start.5 = (bf16[136,768]{1,0:T(8,128)(2,1)S(1)}, bf16[136,768]{1,0:T(8,128)(2,1)S(1)}, u32[]{:S(2)}, u32[]{:S(2)}) collective-permute-start(bf16[136,768]{1,0:T(8,128)(2,1)S(1)} %pad_maximum_fusion), channel_id=1, source_target_pairs={{0,1},{1,0},{2,3},{3,2},{4,5},{5,4},{6,7},{7,6},{8,9},{9,8},{10,11... | collective-permute-start | bytes 626696 | tf_op jit(solution)/shard_map/ppermute | solution.py:16
  14.8 6.6 %collective-permute-start.3 = (bf16[128,768]{1,0:T(8,128)(2,1)S(1)}, bf16[128,768]{1,0:T(8,128)(2,1)S(1)}, u32[]{:S(2)}, u32[]{:S(2)}) collective-permute-start(bf16[128,768]{1,0:T(8,128)(2,1)S(1)} %collective-permute-done.1), channel_id=1, source_target_pairs={{0,2},{1,3},{2,0},{3,1},{4,6},{5,7},{6,4},{7,5},{8,10},{9,11},{10,... | collective-permute-start | bytes 589832 | tf_op jit(solution)/shard_map/ppermute | solution.py:16
  15.6 10.7 %collective-permute-start.9 = (bf16[128,768]{1,0:T(8,128)(2,1)S(1)}, bf16[128,768]{1,0:T(8,128)(2,1)}, u32[]{:S(2)}, u32[]{:S(2)}) collective-permute-start(bf16[128,768]{1,0:T(8,128)(2,1)S(1)} %collective-permute-done.2), channel_id=1, source_target_pairs={{0,1},{1,0},{2,3},{3,2},{4,5},{5,4},{6,7},{7,6},{8,9},{9,8},{10,11... | collective-permute-start | bytes 589832 | tf_op jit(solution)/shard_map/ppermute | solution.py:16
  17.1 13.8 %collective-permute-start.11 = (bf16[128,768]{1,0:T(8,128)(2,1)S(1)}, bf16[128,768]{1,0:T(8,128)(2,1)}, u32[]{:S(2)}, u32[]{:S(2)}) collective-permute-start(bf16[128,768]{1,0:T(8,128)(2,1)S(1)} %collective-permute-done.1), channel_id=1, source_target_pairs={{0,1},{1,0},{2,3},{3,2},{4,5},{5,4},{6,7},{7,6},{8,9},{9,8},{10,11... | collective-permute-start | bytes 589832 | tf_op jit(solution)/shard_map/ppermute | solution.py:16
  18.5 3.4 %collective-permute-start.6 = (bf16[136,768]{1,0:T(8,128)(2,1)S(1)}, bf16[136,768]{1,0:T(8,128)(2,1)S(1)}, u32[]{:S(2)}, u32[]{:S(2)}) collective-permute-start(bf16[136,768]{1,0:T(8,128)(2,1)S(1)} %collective-permute-done.5), channel_id=1, source_target_pairs={{0,8},{8,0},{16,24},{24,16},{1,9},{9,1},{17,25},{25,17},{2,10},{10... | collective-permute-start | bytes 626696 | tf_op jit(solution)/shard_map/ppermute | solution.py:16
  22.6 3.7 %collective-permute-start.8 = (f32[1,2,2,128]{3,2,1,0:T(2,128)S(1)}, f32[1,2,2,128]{3,2,1,0:T(2,128)S(1)}, u32[]{:S(2)}, u32[]{:S(2)}) collective-permute-start(f32[1,2,2,128]{3,2,1,0:T(2,128)S(1)} %bitcast.143), channel_id=1, source_target_pairs={{0,2},{1,3},{2,0},{3,1},{4,6},{5,7},{6,4},{7,5},{8,10},{9,11},{10,... | collective-permute-start | bytes 6152 | tf_op jit(solution)/shard_map/ppermute | solution.py:16
  24.4 6.6 %collective-permute-start.12 = (bf16[128,768]{1,0:T(8,128)(2,1)}, bf16[128,768]{1,0:T(8,128)(2,1)}, u32[]{:S(2)}, u32[]{:S(2)}) collective-permute-start(bf16[128,768]{1,0:T(8,128)(2,1)} %slice.239), channel_id=1, source_target_pairs={{0,1},{1,0},{2,3},{3,2},{4,5},{5,4},{6,7},{7,6},{8,9},{9,8},{10,11... | collective-permute-start | bytes 589832 | tf_op jit(solution)/shard_map/ppermute | solution.py:16
  26.3 4.6 %collective-permute-start.10 = (f32[1,2,2,128]{3,2,1,0:T(2,128)S(1)}, f32[1,2,2,128]{3,2,1,0:T(2,128)S(1)}, u32[]{:S(2)}, u32[]{:S(2)}) collective-permute-start(f32[1,2,2,128]{3,2,1,0:T(2,128)S(1)} %log_add_fusion.6), channel_id=1, source_target_pairs={{0,4},{1,5},{2,6},{3,7},{4,0},{5,1},{6,2},{7,3},{8,12},{9,13},{10,... | collective-permute-start | bytes 6152 | tf_op jit(solution)/shard_map/ppermute | solution.py:16
  31.0 3.6 %collective-permute-start.13 = (f32[1,2,2,128]{3,2,1,0:T(2,128)S(1)}, f32[1,2,2,128]{3,2,1,0:T(2,128)S(1)}, u32[]{:S(2)}, u32[]{:S(2)}) collective-permute-start(f32[1,2,2,128]{3,2,1,0:T(2,128)S(1)} %log_add_fusion.5), channel_id=1, source_target_pairs={{0,1},{1,0},{2,3},{3,2},{4,5},{5,4},{6,7},{7,6},{8,9},{9,8},{10,11... | collective-permute-start | bytes 6152 | tf_op jit(solution)/shard_map/ppermute | solution.py:16
  35.6 1.5 %collective-permute-start.14 = (f32[136,384]{1,0:T(8,128)S(1)}, f32[136,384]{1,0:T(8,128)S(1)}, u32[]{:S(2)}, u32[]{:S(2)}) collective-permute-start(f32[136,384]{1,0:T(8,128)S(1)} %select_maximum_fusion.1), channel_id=1, source_target_pairs={{0,8},{8,0},{16,24},{24,16},{1,9},{9,1},{17,25},{25,17},{2,10},{10... | collective-permute-start | bytes 626696 | tf_op jit(solution)/shard_map/ppermute | solution.py:16
  36.3 2.5 %collective-permute-start.17 = (f32[128,384]{1,0:T(8,128)S(1)}, f32[128,384]{1,0:T(8,128)S(1)}, u32[]{:S(2)}, u32[]{:S(2)}) collective-permute-start(f32[128,384]{1,0:T(8,128)S(1)} %slice_select_fusion.5), channel_id=1, source_target_pairs={{0,8},{8,0},{16,24},{24,16},{1,9},{9,1},{17,25},{25,17},{2,10},{10... | collective-permute-start | bytes 589832 | tf_op jit(solution)/shard_map/ppermute | solution.py:16
  37.2 5.8 %collective-permute-start.15 = (bf16[136,384]{1,0:T(8,128)(2,1)S(1)}, bf16[136,384]{1,0:T(8,128)(2,1)S(1)}, u32[]{:S(2)}, u32[]{:S(2)}) collective-permute-start(bf16[136,384]{1,0:T(8,128)(2,1)S(1)} %pad_maximum_fusion.1), channel_id=1, source_target_pairs={{0,16},{8,24},{16,0},{24,8},{1,17},{9,25},{17,1},{25,9},{2,18},{10... | collective-permute-start | bytes 313352 | tf_op jit(solution)/shard_map/ppermute | solution.py:16
  38.8 5.5 %collective-permute-start.18 = (bf16[128,384]{1,0:T(8,128)(2,1)S(1)}, bf16[128,384]{1,0:T(8,128)(2,1)S(1)}, u32[]{:S(2)}, u32[]{:S(2)}) collective-permute-start(bf16[128,384]{1,0:T(8,128)(2,1)S(1)} %add_convert_fusion.1), channel_id=1, source_target_pairs={{0,16},{8,24},{16,0},{24,8},{1,17},{9,25},{17,1},{25,9},{2,18},{10... | collective-permute-start | bytes 294920 | tf_op jit(solution)/shard_map/ppermute | solution.py:16
  43.1 1.5 %collective-permute-start.16 = (f32[128,384]{1,0:T(8,128)S(1)}, f32[128,384]{1,0:T(8,128)S(1)}, u32[]{:S(2)}, u32[]{:S(2)}) collective-permute-start(f32[128,384]{1,0:T(8,128)S(1)} %fusion.37), channel_id=1, source_target_pairs={{0,8},{8,0},{16,24},{24,16},{1,9},{9,1},{17,25},{25,17},{2,10},{10... | collective-permute-start | bytes 589832 | tf_op jit(solution)/shard_map/ppermute | solution.py:16
  44.4 1.5 %collective-permute-start.19 = (f32[128,384]{1,0:T(8,128)S(1)}, f32[128,384]{1,0:T(8,128)S(1)}, u32[]{:S(2)}, u32[]{:S(2)}) collective-permute-start(f32[128,384]{1,0:T(8,128)S(1)} %fusion.36), channel_id=1, source_target_pairs={{0,8},{8,0},{16,24},{24,16},{1,9},{9,1},{17,25},{25,17},{2,10},{10... | collective-permute-start | bytes 589832 | tf_op jit(solution)/shard_map/ppermute | solution.py:16
  47.2 3.7 %collective-permute-start.20 = (f32[2,2,2,128]{3,2,1,0:T(2,128)S(1)}, f32[2,2,2,128]{3,2,1,0:T(2,128)S(1)}, u32[]{:S(2)}, u32[]{:S(2)}) collective-permute-start(f32[2,2,2,128]{3,2,1,0:T(2,128)S(1)} %pad_maximum_fusion.6), channel_id=1, source_target_pairs={{0,1},{1,0},{2,3},{3,2},{4,5},{5,4},{6,7},{7,6},{8,9},{9,8},{10,11... | collective-permute-start | bytes 12296 | tf_op jit(solution)/shard_map/ppermute | solution.py:16
  51.2 1.6 %copy-start.4 = (s32[128]{0:T(128)S(1)}, s32[128]{0:T(128)}, u32[]{:S(2)}) copy-start(s32[128]{0:T(128)} %param.11) | copy-start | bytes 1540
  51.2 3.8 %collective-permute-start.21 = (f32[2,2,2,128]{3,2,1,0:T(2,128)S(1)}, f32[2,2,2,128]{3,2,1,0:T(2,128)S(1)}, u32[]{:S(2)}, u32[]{:S(2)}) collective-permute-start(f32[2,2,2,128]{3,2,1,0:T(2,128)S(1)} %log_add_fusion.2), channel_id=1, source_target_pairs={{0,2},{1,3},{2,0},{3,1},{4,6},{5,7},{6,4},{7,5},{8,10},{9,11},{10,... | collective-permute-start | bytes 12296 | tf_op jit(solution)/shard_map/ppermute | solution.py:16
  55.1 4.6 %collective-permute-start.22 = (f32[2,2,2,128]{3,2,1,0:T(2,128)S(1)}, f32[2,2,2,128]{3,2,1,0:T(2,128)S(1)}, u32[]{:S(2)}, u32[]{:S(2)}) collective-permute-start(f32[2,2,2,128]{3,2,1,0:T(2,128)S(1)} %log_add_fusion.1), channel_id=1, source_target_pairs={{0,4},{1,5},{2,6},{3,7},{4,0},{5,1},{6,2},{7,3},{8,12},{9,13},{10,... | collective-permute-start | bytes 12296 | tf_op jit(solution)/shard_map/ppermute | solution.py:16
  60.8 1.5 %collective-permute-start.23 = (f32[136,384]{1,0:T(8,128)S(1)}, f32[136,384]{1,0:T(8,128)S(1)}, u32[]{:S(2)}, u32[]{:S(2)}) collective-permute-start(f32[136,384]{1,0:T(8,128)S(1)} %select_maximum_fusion), channel_id=1, source_target_pairs={{0,8},{8,0},{16,24},{24,16},{1,9},{9,1},{17,25},{25,17},{2,10},{10... | collective-permute-start | bytes 626696 | tf_op jit(solution)/shard_map/ppermute | solution.py:16
  61.6 2.7 %collective-permute-start.26 = (f32[128,384]{1,0:T(8,128)S(1)}, f32[128,384]{1,0:T(8,128)S(1)}, u32[]{:S(2)}, u32[]{:S(2)}) collective-permute-start(f32[128,384]{1,0:T(8,128)S(1)} %slice_select_fusion.3), channel_id=1, source_target_pairs={{0,8},{8,0},{16,24},{24,16},{1,9},{9,1},{17,25},{25,17},{2,10},{10... | collective-permute-start | bytes 589832 | tf_op jit(solution)/shard_map/ppermute | solution.py:16
  62.6 5.8 %collective-permute-start.24 = (bf16[136,384]{1,0:T(8,128)(2,1)S(1)}, bf16[136,384]{1,0:T(8,128)(2,1)S(1)}, u32[]{:S(2)}, u32[]{:S(2)}) collective-permute-start(bf16[136,384]{1,0:T(8,128)(2,1)S(1)} %pad_maximum_fusion.2), channel_id=1, source_target_pairs={{0,16},{8,24},{16,0},{24,8},{1,17},{9,25},{17,1},{25,9},{2,18},{10... | collective-permute-start | bytes 313352 | tf_op jit(solution)/shard_map/ppermute | solution.py:16
  64.3 5.5 %collective-permute-start.27 = (bf16[128,384]{1,0:T(8,128)(2,1)S(1)}, bf16[128,384]{1,0:T(8,128)(2,1)S(1)}, u32[]{:S(2)}, u32[]{:S(2)}) collective-permute-start(bf16[128,384]{1,0:T(8,128)(2,1)S(1)} %add_convert_fusion), channel_id=1, source_target_pairs={{0,16},{8,24},{16,0},{24,8},{1,17},{9,25},{17,1},{25,9},{2,18},{10... | collective-permute-start | bytes 294920 | tf_op jit(solution)/shard_map/ppermute | solution.py:16
  68.6 2.0 %collective-permute-start.25 = (f32[128,384]{1,0:T(8,128)S(1)}, f32[128,384]{1,0:T(8,128)S(1)}, u32[]{:S(2)}, u32[]{:S(2)}) collective-permute-start(f32[128,384]{1,0:T(8,128)S(1)} %fusion.34), channel_id=1, source_target_pairs={{0,8},{8,0},{16,24},{24,16},{1,9},{9,1},{17,25},{25,17},{2,10},{10... | collective-permute-start | bytes 589832 | tf_op jit(solution)/shard_map/ppermute | solution.py:16
  69.9 1.5 %collective-permute-start.28 = (f32[128,384]{1,0:T(8,128)S(1)}, f32[128,384]{1,0:T(8,128)S(1)}, u32[]{:S(2)}, u32[]{:S(2)}) collective-permute-start(f32[128,384]{1,0:T(8,128)S(1)} %fusion.33), channel_id=1, source_target_pairs={{0,8},{8,0},{16,24},{24,16},{1,9},{9,1},{17,25},{25,17},{2,10},{10... | collective-permute-start | bytes 589832 | tf_op jit(solution)/shard_map/ppermute | solution.py:16
  (2 other events, 1.4 us)

commit v10 on v9

--- a/solution.py
+++ b/solution.py
@@ -125,22 +125,28 @@
         last = step == ITERS - 1
         shape = (-1,) + (2,) * (len(cent_bits) - 1) + (rows,)
         if step == 0:
-            odds = [logits_of(centers_half, norms, held[0])]
-            lse = stats_of(odds[0], logits_of(partner_half, partner_norms, held[0])).reshape(shape)
+            early = jnp.concatenate([pieces[mask] for mask in evens[:-1]])
+            lse = [
+                stats_of(logits_of(centers_half, norms, group), logits_of(partner_half, partner_norms, group))
+                for group in (early, pieces[evens[-1]])
+            ]
+            lse = jnp.concatenate(lse).reshape(shape)
             lse, held[0] = lax.optimization_barrier((lse, held[0]))
             across[evens[-1]] = swap(held[0][-rows:], "cent", 1)
             stops = [0, half // 4, half // 2, half]
-            turn = evens
             for index, bit in enumerate(cent_bits[1:] + [None]):
-                ties = turn[stops[index] : stops[index + 1]] if index < 3 else []
+                ties = evens[stops[index] : stops[index + 1]] if index < 3 else []
                 lse, *parts = lax.optimization_barrier([lse] + [across[mask] for mask in ties])
                 across.update(zip(ties, parts))
                 if bit is not None:
                     lse = over_column(bit, lse)
+                if index == 0:
+                    lse, held[0] = lax.optimization_barrier((lse, held[0]))
+                    odds = [logits_of(centers_half, norms, held[0])]
             held.append(jnp.concatenate([across[mask] for mask in evens]))
             lse = jnp.concatenate([lse, swap(lse, "cent", 1)])
             odds.append(logits_of(centers_half, norms, held[-1]))
-            lse, odds[-1] = lax.optimization_barrier((lse, odds[-1]))
+            lse, odds = lax.optimization_barrier((lse, odds))
         else:
             norms = jnp.sum(means * means, axis=1)
             centers_half = means.astype(jnp.bfloat16)

time: 72.6 us -> 72.5 us (level)
  local copies, waits for them, and re-layouts: 5.94 us -> 2.48 us
  waiting for transfers between devices: 22.9 us -> 25.2 us
  matrix products: 5.27 us -> 6.21 us
    unnamed x16 -> x15, local copies, waits for them, and re-layouts: 3.2 us -> 0.66 us
    ppermute x29, waiting for transfers between devices: 22.9 us -> 25.2 us  [swap(): return lax.ppermute(value, axis, [(i, i ^ bit) for i in range(size)])]
    dot_general x5 -> x8, matrix products: 2.08 us -> 3.03 us  [logits_of(): lax.dot_general(centers_half, group, (((1,), (1,)), ((), ())), preferred_...]
    concatenate x1, local copies, waits for them, and re-layouts: 0.94 us -> 0.02 us  [on_device(): held.append(jnp.concatenate([across[mask] for mask in evens]))]
  transfers between devices with their start and end apart: 29 -> 29, of which waited for: 18 -> 19; matrix products, arithmetic and copies ran while one was open for 15% -> 13% of each run, Pallas kernels for 0% -> 0%
where the time goes in v10:
time: 72.5 us; the launch traced here: 72.3 us
  starting transfers between devices  31.1 us (43%)
  waiting for transfers between devices  25.2 us (35%)
  matrix products  6.21 us (9%)
  other arithmetic  5.92 us (8%)
  local copies, waits for them, and re-layouts  2.48 us (3%)
  between operations  1.28 us (2%)
    ppermute x29, starting transfers between devices, swap(): return lax.ppermute(value, axis, [(i, i ^ bit) for i in range(size)])  31.1 us
    ppermute x29, waiting for transfers between devices, swap(): return lax.ppermute(value, axis, [(i, i ^ bit) for i in range(size)])  25.2 us
    dot_general x8, matrix products, logits_of(): lax.dot_general(centers_half, group, (((1,), (1,)), ((), ())), preferred_...  3.03 us
    dot_general x8, matrix products, on_device(): jnp.dot(resps[index], held[index][:, part * cut:(part + 1) * cut], prefer...  2.33 us
    reduce_sum x2, other arithmetic, on_device(): norms = jnp.sum(means * means, axis=1)  1.64 us
  transfers between devices with their start and end apart: 29, of which 19 were waited for; matrix products, arithmetic and copies ran while one was open for 13% of the time, Pallas kernels for 0%

profile of v10, /device:TPU:0, one launch (start us, length us, event | category | flops | bytes accessed | tf_op | source)
XLA Modules:
  0.0 72.3 jit_solution(15188115111396283421)
XLA Ops:
  1.2 3.7 %collective-permute-start.1 = (bf16[128,768]{1,0:T(8,128)(2,1)}, bf16[128,768]{1,0:T(8,128)(2,1)S(1)}, u32[]{:S(2)}, u32[]{:S(2)}) collective-permute-start(bf16[128,768]{1,0:T(8,128)(2,1)} %param.7), channel_id=1, source_target_pairs={{0,4},{1,5},{2,6},{3,7},{4,0},{5,1},{6,2},{7,3},{8,12},{9,13},{10,... | collective-permute-start | bytes 589832 | tf_op jit(solution)/shard_map/ppermute | solution.py:16
  4.8 1.6 %collective-permute-start.2 = (bf16[128,768]{1,0:T(8,128)(2,1)}, bf16[128,768]{1,0:T(8,128)(2,1)S(1)}, u32[]{:S(2)}, u32[]{:S(2)}) collective-permute-start(bf16[128,768]{1,0:T(8,128)(2,1)} %param.7), channel_id=1, source_target_pairs={{0,2},{1,3},{2,0},{3,1},{4,6},{5,7},{6,4},{7,5},{8,10},{9,11},{10,... | collective-permute-start | bytes 589832 | tf_op jit(solution)/shard_map/ppermute | solution.py:16
  6.4 1.5 %collective-permute-start.7 = (bf16[128,768]{1,0:T(8,128)(2,1)}, bf16[128,768]{1,0:T(8,128)(2,1)S(1)}, u32[]{:S(2)}, u32[]{:S(2)}) collective-permute-start(bf16[128,768]{1,0:T(8,128)(2,1)} %param.7), channel_id=1, source_target_pairs={{0,1},{1,0},{2,3},{3,2},{4,5},{5,4},{6,7},{7,6},{8,9},{9,8},{10,11... | collective-permute-start | bytes 589832 | tf_op jit(solution)/shard_map/ppermute | solution.py:16
  7.9 1.5 %multiply_reduce_fusion.1 = (f32[256]{0:T(256)S(1)}, bf16[256,768]{1,0:T(8,128)(2,1)S(1)}) fusion(f32[256,768]{1,0:T(8,128)} %param.9), kind=kLoop, calls=%fused_computation.34 | loop fusion | flops 589568 | bytes 1180672 | tf_op jit(solution)/shard_map/reduce_sum | solution.py:77
  10.1 1.6 %collective-permute-start.6 = (bf16[8,768]{1,0:T(8,128)(2,1)S(1)}, bf16[8,768]{1,0:T(8,128)(2,1)S(1)}, u32[]{:S(2)}, u32[]{:S(2)}) collective-permute-start(bf16[8,768]{1,0:T(8,128)(2,1)S(1)} %pad_maximum_fusion.8), channel_id=1, source_target_pairs={{0,16},{8,24},{16,0},{24,8},{1,17},{9,25},{17,1},{25,9},{2,18},{10... | collective-permute-start | bytes 36872 | tf_op jit(solution)/shard_map/ppermute | solution.py:16
  12.4 1.5 %collective-permute-done.6 = bf16[8,768]{1,0:T(8,128)(2,1)S(1)} collective-permute-done((bf16[8,768]{1,0:T(8,128)(2,1)S(1)}, bf16[8,768]{1,0:T(8,128)(2,1)S(1)}, u32[]{:S(2)}, u32[]{:S(2)}) %collective-permute-start.6) | collective-permute-done | bytes 12320 | tf_op jit(solution)/shard_map/ppermute | solution.py:16
  13.9 0.9 %collective-permute-done.1 = bf16[128,768]{1,0:T(8,128)(2,1)S(1)} collective-permute-done((bf16[128,768]{1,0:T(8,128)(2,1)}, bf16[128,768]{1,0:T(8,128)(2,1)S(1)}, u32[]{:S(2)}, u32[]{:S(2)}) %collective-permute-start.1) | collective-permute-done | bytes 196640 | tf_op jit(solution)/shard_map/ppermute | solution.py:16
  14.8 0.8 %collective-permute-start.5 = (bf16[128,768]{1,0:T(8,128)(2,1)S(1)}, bf16[128,768]{1,0:T(8,128)(2,1)S(1)}, u32[]{:S(2)}, u32[]{:S(2)}) collective-permute-start(bf16[128,768]{1,0:T(8,128)(2,1)S(1)} %collective-permute-done.1), channel_id=1, source_target_pairs={{0,2},{1,3},{2,0},{3,1},{4,6},{5,7},{6,4},{7,5},{8,10},{9,11},{10,... | collective-permute-start | bytes 589832 | tf_op jit(solution)/shard_map/ppermute | solution.py:16
  15.6 1.5 %collective-permute-start.9 = (bf16[128,768]{1,0:T(8,128)(2,1)S(1)}, bf16[128,768]{1,0:T(8,128)(2,1)S(1)}, u32[]{:S(2)}, u32[]{:S(2)}) collective-permute-start(bf16[128,768]{1,0:T(8,128)(2,1)S(1)} %collective-permute-done.2), channel_id=1, source_target_pairs={{0,1},{1,0},{2,3},{3,2},{4,5},{5,4},{6,7},{7,6},{8,9},{9,8},{10,11... | collective-permute-start | bytes 589832 | tf_op jit(solution)/shard_map/ppermute | solution.py:16
  18.3 3.1 %collective-permute-done.5 = bf16[128,768]{1,0:T(8,128)(2,1)S(1)} collective-permute-done((bf16[128,768]{1,0:T(8,128)(2,1)S(1)}, bf16[128,768]{1,0:T(8,128)(2,1)S(1)}, u32[]{:S(2)}, u32[]{:S(2)}) %collective-permute-start.5) | collective-permute-done | bytes 196640 | tf_op jit(solution)/shard_map/ppermute | solution.py:16
  22.8 1.1 %collective-permute-start.8 = (f32[1,2,2,128]{3,2,1,0:T(2,128)S(1)}, f32[1,2,2,128]{3,2,1,0:T(2,128)S(1)}, u32[]{:S(2)}, u32[]{:S(2)}) collective-permute-start(f32[1,2,2,128]{3,2,1,0:T(2,128)S(1)} %bitcast.148), channel_id=1, source_target_pairs={{0,2},{1,3},{2,0},{3,1},{4,6},{5,7},{6,4},{7,5},{8,10},{9,11},{10,... | collective-permute-start | bytes 6152 | tf_op jit(solution)/shard_map/ppermute | solution.py:16
  24.0 0.7 slice.239
  24.7 1.5 %collective-permute-start.12 = (bf16[128,768]{1,0:T(8,128)(2,1)}, bf16[128,768]{1,0:T(8,128)(2,1)S(1)}, u32[]{:S(2)}, u32[]{:S(2)}) collective-permute-start(bf16[128,768]{1,0:T(8,128)(2,1)} %slice.239), channel_id=1, source_target_pairs={{0,1},{1,0},{2,3},{3,2},{4,5},{5,4},{6,7},{7,6},{8,9},{9,8},{10,11... | collective-permute-start | bytes 589832 | tf_op jit(solution)/shard_map/ppermute | solution.py:16
  26.5 3.0 %collective-permute-start.10 = (f32[1,2,2,128]{3,2,1,0:T(2,128)S(1)}, f32[1,2,2,128]{3,2,1,0:T(2,128)S(1)}, u32[]{:S(2)}, u32[]{:S(2)}) collective-permute-start(f32[1,2,2,128]{3,2,1,0:T(2,128)S(1)} %log_add_fusion.6), channel_id=1, source_target_pairs={{0,4},{1,5},{2,6},{3,7},{4,0},{5,1},{6,2},{7,3},{8,12},{9,13},{10,... | collective-permute-start | bytes 6152 | tf_op jit(solution)/shard_map/ppermute | solution.py:16
  30.0 1.1 %collective-permute-done.10 = f32[1,2,2,128]{3,2,1,0:T(2,128)S(1)} collective-permute-done((f32[1,2,2,128]{3,2,1,0:T(2,128)S(1)}, f32[1,2,2,128]{3,2,1,0:T(2,128)S(1)}, u32[]{:S(2)}, u32[]{:S(2)}) %collective-permute-start.10) | collective-permute-done | bytes 2080 | tf_op jit(solution)/shard_map/ppermute | solution.py:16
  31.1 1.4 %collective-permute-start.13 = (f32[1,2,2,128]{3,2,1,0:T(2,128)S(1)}, f32[1,2,2,128]{3,2,1,0:T(2,128)S(1)}, u32[]{:S(2)}, u32[]{:S(2)}) collective-permute-start(f32[1,2,2,128]{3,2,1,0:T(2,128)S(1)} %log_add_fusion.5), channel_id=1, source_target_pairs={{0,1},{1,0},{2,3},{3,2},{4,5},{5,4},{6,7},{7,6},{8,9},{9,8},{10,11... | collective-permute-start | bytes 6152 | tf_op jit(solution)/shard_map/ppermute | solution.py:16
  33.0 1.8 %collective-permute-done.13 = f32[1,2,2,128]{3,2,1,0:T(2,128)S(1)} collective-permute-done((f32[1,2,2,128]{3,2,1,0:T(2,128)S(1)}, f32[1,2,2,128]{3,2,1,0:T(2,128)S(1)}, u32[]{:S(2)}, u32[]{:S(2)}) %collective-permute-start.13) | collective-permute-done | bytes 2080 | tf_op jit(solution)/shard_map/ppermute | solution.py:16
  37.3 1.6 %collective-permute-start.15 = (bf16[136,384]{1,0:T(8,128)(2,1)S(1)}, bf16[136,384]{1,0:T(8,128)(2,1)S(1)}, u32[]{:S(2)}, u32[]{:S(2)}) collective-permute-start(bf16[136,384]{1,0:T(8,128)(2,1)S(1)} %pad_maximum_fusion.5), channel_id=1, source_target_pairs={{0,16},{8,24},{16,0},{24,8},{1,17},{9,25},{17,1},{25,9},{2,18},{10... | collective-permute-start | bytes 313352 | tf_op jit(solution)/shard_map/ppermute | solution.py:16
  39.0 0.7 %collective-permute-start.18 = (bf16[128,384]{1,0:T(8,128)(2,1)S(1)}, bf16[128,384]{1,0:T(8,128)(2,1)S(1)}, u32[]{:S(2)}, u32[]{:S(2)}) collective-permute-start(bf16[128,384]{1,0:T(8,128)(2,1)S(1)} %add_convert_fusion.1), channel_id=1, source_target_pairs={{0,16},{8,24},{16,0},{24,8},{1,17},{9,25},{17,1},{25,9},{2,18},{10... | collective-permute-start | bytes 294920 | tf_op jit(solution)/shard_map/ppermute | solution.py:16
  39.7 3.5 %collective-permute-done.15 = bf16[136,384]{1,0:T(8,128)(2,1)S(1)} collective-permute-done((bf16[136,384]{1,0:T(8,128)(2,1)S(1)}, bf16[136,384]{1,0:T(8,128)(2,1)S(1)}, u32[]{:S(2)}, u32[]{:S(2)}) %collective-permute-start.15) | collective-permute-done | bytes 104480 | tf_op jit(solution)/shard_map/ppermute | solution.py:16
  43.4 1.1 %collective-permute-done.18 = bf16[128,384]{1,0:T(8,128)(2,1)S(1)} collective-permute-done((bf16[128,384]{1,0:T(8,128)(2,1)S(1)}, bf16[128,384]{1,0:T(8,128)(2,1)S(1)}, u32[]{:S(2)}, u32[]{:S(2)}) %collective-permute-start.18) | collective-permute-done | bytes 98336 | tf_op jit(solution)/shard_map/ppermute | solution.py:16
  44.8 1.3 %collective-permute-done.19 = f32[128,384]{1,0:T(8,128)S(1)} collective-permute-done((f32[128,384]{1,0:T(8,128)S(1)}, f32[128,384]{1,0:T(8,128)S(1)}, u32[]{:S(2)}, u32[]{:S(2)}) %collective-permute-start.19) | collective-permute-done | bytes 196640 | tf_op jit(solution)/shard_map/ppermute | solution.py:16
  47.4 1.4 %collective-permute-start.20 = (f32[2,2,2,128]{3,2,1,0:T(2,128)S(1)}, f32[2,2,2,128]{3,2,1,0:T(2,128)S(1)}, u32[]{:S(2)}, u32[]{:S(2)}) collective-permute-start(f32[2,2,2,128]{3,2,1,0:T(2,128)S(1)} %pad_maximum_fusion.10), channel_id=1, source_target_pairs={{0,1},{1,0},{2,3},{3,2},{4,5},{5,4},{6,7},{7,6},{8,9},{9,8},{10,11... | collective-permute-start | bytes 12296 | tf_op jit(solution)/shard_map/ppermute | solution.py:16
  48.9 2.2 %collective-permute-done.20 = f32[2,2,2,128]{3,2,1,0:T(2,128)S(1)} collective-permute-done((f32[2,2,2,128]{3,2,1,0:T(2,128)S(1)}, f32[2,2,2,128]{3,2,1,0:T(2,128)S(1)}, u32[]{:S(2)}, u32[]{:S(2)}) %collective-permute-start.20) | collective-permute-done | bytes 4128 | tf_op jit(solution)/shard_map/ppermute | solution.py:16
  51.4 1.4 %collective-permute-start.21 = (f32[2,2,2,128]{3,2,1,0:T(2,128)S(1)}, f32[2,2,2,128]{3,2,1,0:T(2,128)S(1)}, u32[]{:S(2)}, u32[]{:S(2)}) collective-permute-start(f32[2,2,2,128]{3,2,1,0:T(2,128)S(1)} %log_add_fusion.2), channel_id=1, source_target_pairs={{0,2},{1,3},{2,0},{3,1},{4,6},{5,7},{6,4},{7,5},{8,10},{9,11},{10,... | collective-permute-start | bytes 12296 | tf_op jit(solution)/shard_map/ppermute | solution.py:16
  55.1 3.0 %collective-permute-start.22 = (f32[2,2,2,128]{3,2,1,0:T(2,128)S(1)}, f32[2,2,2,128]{3,2,1,0:T(2,128)S(1)}, u32[]{:S(2)}, u32[]{:S(2)}) collective-permute-start(f32[2,2,2,128]{3,2,1,0:T(2,128)S(1)} %log_add_fusion.1), channel_id=1, source_target_pairs={{0,4},{1,5},{2,6},{3,7},{4,0},{5,1},{6,2},{7,3},{8,12},{9,13},{10,... | collective-permute-start | bytes 12296 | tf_op jit(solution)/shard_map/ppermute | solution.py:16
  58.1 1.6 %collective-permute-done.22 = f32[2,2,2,128]{3,2,1,0:T(2,128)S(1)} collective-permute-done((f32[2,2,2,128]{3,2,1,0:T(2,128)S(1)}, f32[2,2,2,128]{3,2,1,0:T(2,128)S(1)}, u32[]{:S(2)}, u32[]{:S(2)}) %collective-permute-start.22) | collective-permute-done | bytes 4128 | tf_op jit(solution)/shard_map/ppermute | solution.py:16
  62.5 1.6 %collective-permute-start.24 = (bf16[136,384]{1,0:T(8,128)(2,1)S(1)}, bf16[136,384]{1,0:T(8,128)(2,1)S(1)}, u32[]{:S(2)}, u32[]{:S(2)}) collective-permute-start(bf16[136,384]{1,0:T(8,128)(2,1)S(1)} %pad_maximum_fusion.6), channel_id=1, source_target_pairs={{0,16},{8,24},{16,0},{24,8},{1,17},{9,25},{17,1},{25,9},{2,18},{10... | collective-permute-start | bytes 313352 | tf_op jit(solution)/shard_map/ppermute | solution.py:16
  64.7 3.6 %collective-permute-done.24 = bf16[136,384]{1,0:T(8,128)(2,1)S(1)} collective-permute-done((bf16[136,384]{1,0:T(8,128)(2,1)S(1)}, bf16[136,384]{1,0:T(8,128)(2,1)S(1)}, u32[]{:S(2)}, u32[]{:S(2)}) %collective-permute-start.24) | collective-permute-done | bytes 104480 | tf_op jit(solution)/shard_map/ppermute | solution.py:16
  68.6 1.1 %collective-permute-done.27 = bf16[128,384]{1,0:T(8,128)(2,1)S(1)} collective-permute-done((bf16[128,384]{1,0:T(8,128)(2,1)S(1)}, bf16[128,384]{1,0:T(8,128)(2,1)S(1)}, u32[]{:S(2)}, u32[]{:S(2)}) %collective-permute-start.27) | collective-permute-done | bytes 98336 | tf_op jit(solution)/shard_map/ppermute | solution.py:16
  70.6 0.7 collective-permute-done.28
  71.3 0.9 %maximum_maximum_fusion.1 = f32[256,768]{1,0:T(8,128)} fusion(f32[128,384]{1,0:T(8,128)S(1)} %get-tuple-element.111, f32[128,384]{1,0:T(8,128)S(1)} %get-tuple-element.110, f32[128,384]{1,0:T(8,128)S(1)} %get-tuple-element.109, f32[128,384]{1,0:T(8,128)S(1)} %get-tuple-element.108), kind=kLoop, calls=%fused_computation.32 | loop fusion | flops 589824 | bytes 1572864 | tf_op jit(solution)/shard_map/concatenate | solution.py:225
  (165 shorter events, 17.0 us)
Async XLA Ops:
  0.6 8.8 %copy-start = (f32[256,768]{1,0:T(8,128)S(1)}, f32[256,768]{1,0:T(8,128)}, u32[]{:S(2)}) copy-start(f32[256,768]{1,0:T(8,128)} %param.9) | copy-start | bytes 2359300
  0.6 4.2 %collective-permute-start = (bf16[4,768]{1,0:T(4,128)(2,1)}, bf16[4,768]{1,0:T(4,128)(2,1)S(1)}, u32[]{:S(2)}, u32[]{:S(2)}) collective-permute-start(bf16[4,768]{1,0:T(4,128)(2,1)} %param.8), channel_id=1, source_target_pairs={{0,8},{8,0},{16,24},{24,16},{1,9},{9,1},{17,25},{25,17},{2,10},{10... | collective-permute-start | bytes 18440 | tf_op jit(solution)/shard_map/ppermute | solution.py:16
  1.2 13.7 %collective-permute-start.1 = (bf16[128,768]{1,0:T(8,128)(2,1)}, bf16[128,768]{1,0:T(8,128)(2,1)S(1)}, u32[]{:S(2)}, u32[]{:S(2)}) collective-permute-start(bf16[128,768]{1,0:T(8,128)(2,1)} %param.7), channel_id=1, source_target_pairs={{0,4},{1,5},{2,6},{3,7},{4,0},{5,1},{6,2},{7,3},{8,12},{9,13},{10,... | collective-permute-start | bytes 589832 | tf_op jit(solution)/shard_map/ppermute | solution.py:16
  4.8 10.8 %collective-permute-start.2 = (bf16[128,768]{1,0:T(8,128)(2,1)}, bf16[128,768]{1,0:T(8,128)(2,1)S(1)}, u32[]{:S(2)}, u32[]{:S(2)}) collective-permute-start(bf16[128,768]{1,0:T(8,128)(2,1)} %param.7), channel_id=1, source_target_pairs={{0,2},{1,3},{2,0},{3,1},{4,6},{5,7},{6,4},{7,5},{8,10},{9,11},{10,... | collective-permute-start | bytes 589832 | tf_op jit(solution)/shard_map/ppermute | solution.py:16
  6.4 16.4 %collective-permute-start.7 = (bf16[128,768]{1,0:T(8,128)(2,1)}, bf16[128,768]{1,0:T(8,128)(2,1)S(1)}, u32[]{:S(2)}, u32[]{:S(2)}) collective-permute-start(bf16[128,768]{1,0:T(8,128)(2,1)} %param.7), channel_id=1, source_target_pairs={{0,1},{1,0},{2,3},{3,2},{4,5},{5,4},{6,7},{7,6},{8,9},{9,8},{10,11... | collective-permute-start | bytes 589832 | tf_op jit(solution)/shard_map/ppermute | solution.py:16
  9.5 7.7 %copy-start.1 = (bf16[128,768]{1,0:T(8,128)(2,1)S(1)}, bf16[128,768]{1,0:T(8,128)(2,1)}, u32[]{:S(2)}) copy-start(bf16[128,768]{1,0:T(8,128)(2,1)} %param.7) | copy-start | bytes 589828
  10.1 3.8 %collective-permute-start.6 = (bf16[8,768]{1,0:T(8,128)(2,1)S(1)}, bf16[8,768]{1,0:T(8,128)(2,1)S(1)}, u32[]{:S(2)}, u32[]{:S(2)}) collective-permute-start(bf16[8,768]{1,0:T(8,128)(2,1)S(1)} %pad_maximum_fusion.8), channel_id=1, source_target_pairs={{0,16},{8,24},{16,0},{24,8},{1,17},{9,25},{17,1},{25,9},{2,18},{10... | collective-permute-start | bytes 36872 | tf_op jit(solution)/shard_map/ppermute | solution.py:16
  11.8 6.6 %collective-permute-start.3 = (bf16[136,768]{1,0:T(8,128)(2,1)S(1)}, bf16[136,768]{1,0:T(8,128)(2,1)S(1)}, u32[]{:S(2)}, u32[]{:S(2)}) collective-permute-start(bf16[136,768]{1,0:T(8,128)(2,1)S(1)} %pad_maximum_fusion.4), channel_id=1, source_target_pairs={{0,1},{1,0},{2,3},{3,2},{4,5},{5,4},{6,7},{7,6},{8,9},{9,8},{10,11... | collective-permute-start | bytes 626696 | tf_op jit(solution)/shard_map/ppermute | solution.py:16
  14.8 6.6 %collective-permute-start.5 = (bf16[128,768]{1,0:T(8,128)(2,1)S(1)}, bf16[128,768]{1,0:T(8,128)(2,1)S(1)}, u32[]{:S(2)}, u32[]{:S(2)}) collective-permute-start(bf16[128,768]{1,0:T(8,128)(2,1)S(1)} %collective-permute-done.1), channel_id=1, source_target_pairs={{0,2},{1,3},{2,0},{3,1},{4,6},{5,7},{6,4},{7,5},{8,10},{9,11},{10,... | collective-permute-start | bytes 589832 | tf_op jit(solution)/shard_map/ppermute | solution.py:16
  15.6 10.9 %collective-permute-start.9 = (bf16[128,768]{1,0:T(8,128)(2,1)S(1)}, bf16[128,768]{1,0:T(8,128)(2,1)S(1)}, u32[]{:S(2)}, u32[]{:S(2)}) collective-permute-start(bf16[128,768]{1,0:T(8,128)(2,1)S(1)} %collective-permute-done.2), channel_id=1, source_target_pairs={{0,1},{1,0},{2,3},{3,2},{4,5},{5,4},{6,7},{7,6},{8,9},{9,8},{10,11... | collective-permute-start | bytes 589832 | tf_op jit(solution)/shard_map/ppermute | solution.py:16
  17.1 14.0 %collective-permute-start.11 = (bf16[128,768]{1,0:T(8,128)(2,1)S(1)}, bf16[128,768]{1,0:T(8,128)(2,1)S(1)}, u32[]{:S(2)}, u32[]{:S(2)}) collective-permute-start(bf16[128,768]{1,0:T(8,128)(2,1)S(1)} %collective-permute-done.1), channel_id=1, source_target_pairs={{0,1},{1,0},{2,3},{3,2},{4,5},{5,4},{6,7},{7,6},{8,9},{9,8},{10,11... | collective-permute-start | bytes 589832 | tf_op jit(solution)/shard_map/ppermute | solution.py:16
  18.3 3.4 %collective-permute-start.4 = (bf16[136,768]{1,0:T(8,128)(2,1)S(1)}, bf16[136,768]{1,0:T(8,128)(2,1)S(1)}, u32[]{:S(2)}, u32[]{:S(2)}) collective-permute-start(bf16[136,768]{1,0:T(8,128)(2,1)S(1)} %collective-permute-done.3), channel_id=1, source_target_pairs={{0,8},{8,0},{16,24},{24,16},{1,9},{9,1},{17,25},{25,17},{2,10},{10... | collective-permute-start | bytes 626696 | tf_op jit(solution)/shard_map/ppermute | solution.py:16
  22.8 3.7 %collective-permute-start.8 = (f32[1,2,2,128]{3,2,1,0:T(2,128)S(1)}, f32[1,2,2,128]{3,2,1,0:T(2,128)S(1)}, u32[]{:S(2)}, u32[]{:S(2)}) collective-permute-start(f32[1,2,2,128]{3,2,1,0:T(2,128)S(1)} %bitcast.148), channel_id=1, source_target_pairs={{0,2},{1,3},{2,0},{3,1},{4,6},{5,7},{6,4},{7,5},{8,10},{9,11},{10,... | collective-permute-start | bytes 6152 | tf_op jit(solution)/shard_map/ppermute | solution.py:16
  24.7 6.5 %collective-permute-start.12 = (bf16[128,768]{1,0:T(8,128)(2,1)}, bf16[128,768]{1,0:T(8,128)(2,1)S(1)}, u32[]{:S(2)}, u32[]{:S(2)}) collective-permute-start(bf16[128,768]{1,0:T(8,128)(2,1)} %slice.239), channel_id=1, source_target_pairs={{0,1},{1,0},{2,3},{3,2},{4,5},{5,4},{6,7},{7,6},{8,9},{9,8},{10,11... | collective-permute-start | bytes 589832 | tf_op jit(solution)/shard_map/ppermute | solution.py:16
  26.5 4.6 %collective-permute-start.10 = (f32[1,2,2,128]{3,2,1,0:T(2,128)S(1)}, f32[1,2,2,128]{3,2,1,0:T(2,128)S(1)}, u32[]{:S(2)}, u32[]{:S(2)}) collective-permute-start(f32[1,2,2,128]{3,2,1,0:T(2,128)S(1)} %log_add_fusion.6), channel_id=1, source_target_pairs={{0,4},{1,5},{2,6},{3,7},{4,0},{5,1},{6,2},{7,3},{8,12},{9,13},{10,... | collective-permute-start | bytes 6152 | tf_op jit(solution)/shard_map/ppermute | solution.py:16
  31.1 3.7 %collective-permute-start.13 = (f32[1,2,2,128]{3,2,1,0:T(2,128)S(1)}, f32[1,2,2,128]{3,2,1,0:T(2,128)S(1)}, u32[]{:S(2)}, u32[]{:S(2)}) collective-permute-start(f32[1,2,2,128]{3,2,1,0:T(2,128)S(1)} %log_add_fusion.5), channel_id=1, source_target_pairs={{0,1},{1,0},{2,3},{3,2},{4,5},{5,4},{6,7},{7,6},{8,9},{9,8},{10,11... | collective-permute-start | bytes 6152 | tf_op jit(solution)/shard_map/ppermute | solution.py:16
  35.7 1.5 %collective-permute-start.14 = (f32[136,384]{1,0:T(8,128)S(1)}, f32[136,384]{1,0:T(8,128)S(1)}, u32[]{:S(2)}, u32[]{:S(2)}) collective-permute-start(f32[136,384]{1,0:T(8,128)S(1)} %select_maximum_fusion.1), channel_id=1, source_target_pairs={{0,8},{8,0},{16,24},{24,16},{1,9},{9,1},{17,25},{25,17},{2,10},{10... | collective-permute-start | bytes 626696 | tf_op jit(solution)/shard_map/ppermute | solution.py:16
  36.4 2.5 %collective-permute-start.17 = (f32[128,384]{1,0:T(8,128)S(1)}, f32[128,384]{1,0:T(8,128)S(1)}, u32[]{:S(2)}, u32[]{:S(2)}) collective-permute-start(f32[128,384]{1,0:T(8,128)S(1)} %slice_select_fusion.5), channel_id=1, source_target_pairs={{0,8},{8,0},{16,24},{24,16},{1,9},{9,1},{17,25},{25,17},{2,10},{10... | collective-permute-start | bytes 589832 | tf_op jit(solution)/shard_map/ppermute | solution.py:16
  37.3 5.8 %collective-permute-start.15 = (bf16[136,384]{1,0:T(8,128)(2,1)S(1)}, bf16[136,384]{1,0:T(8,128)(2,1)S(1)}, u32[]{:S(2)}, u32[]{:S(2)}) collective-permute-start(bf16[136,384]{1,0:T(8,128)(2,1)S(1)} %pad_maximum_fusion.5), channel_id=1, source_target_pairs={{0,16},{8,24},{16,0},{24,8},{1,17},{9,25},{17,1},{25,9},{2,18},{10... | collective-permute-start | bytes 313352 | tf_op jit(solution)/shard_map/ppermute | solution.py:16
  39.0 5.5 %collective-permute-start.18 = (bf16[128,384]{1,0:T(8,128)(2,1)S(1)}, bf16[128,384]{1,0:T(8,128)(2,1)S(1)}, u32[]{:S(2)}, u32[]{:S(2)}) collective-permute-start(bf16[128,384]{1,0:T(8,128)(2,1)S(1)} %add_convert_fusion.1), channel_id=1, source_target_pairs={{0,16},{8,24},{16,0},{24,8},{1,17},{9,25},{17,1},{25,9},{2,18},{10... | collective-permute-start | bytes 294920 | tf_op jit(solution)/shard_map/ppermute | solution.py:16
  43.3 1.5 %collective-permute-start.16 = (f32[128,384]{1,0:T(8,128)S(1)}, f32[128,384]{1,0:T(8,128)S(1)}, u32[]{:S(2)}, u32[]{:S(2)}) collective-permute-start(f32[128,384]{1,0:T(8,128)S(1)} %fusion.40), channel_id=1, source_target_pairs={{0,8},{8,0},{16,24},{24,16},{1,9},{9,1},{17,25},{25,17},{2,10},{10... | collective-permute-start | bytes 589832 | tf_op jit(solution)/shard_map/ppermute | solution.py:16
  44.6 1.5 %collective-permute-start.19 = (f32[128,384]{1,0:T(8,128)S(1)}, f32[128,384]{1,0:T(8,128)S(1)}, u32[]{:S(2)}, u32[]{:S(2)}) collective-permute-start(f32[128,384]{1,0:T(8,128)S(1)} %fusion.39), channel_id=1, source_target_pairs={{0,8},{8,0},{16,24},{24,16},{1,9},{9,1},{17,25},{25,17},{2,10},{10... | collective-permute-start | bytes 589832 | tf_op jit(solution)/shard_map/ppermute | solution.py:16
  47.3 5.8 %copy-start.3 = (s32[128,4]{0,1:T(4,128)S(1)}, s32[128,4]{0,1:T(4,128)}, u32[]{:S(2)}) copy-start(s32[128,4]{0,1:T(4,128)} %param.10) | copy-start | bytes 6148
  47.4 3.7 %collective-permute-start.20 = (f32[2,2,2,128]{3,2,1,0:T(2,128)S(1)}, f32[2,2,2,128]{3,2,1,0:T(2,128)S(1)}, u32[]{:S(2)}, u32[]{:S(2)}) collective-permute-start(f32[2,2,2,128]{3,2,1,0:T(2,128)S(1)} %pad_maximum_fusion.10), channel_id=1, source_target_pairs={{0,1},{1,0},{2,3},{3,2},{4,5},{5,4},{6,7},{7,6},{8,9},{9,8},{10,11... | collective-permute-start | bytes 12296 | tf_op jit(solution)/shard_map/ppermute | solution.py:16
  51.4 3.6 %collective-permute-start.21 = (f32[2,2,2,128]{3,2,1,0:T(2,128)S(1)}, f32[2,2,2,128]{3,2,1,0:T(2,128)S(1)}, u32[]{:S(2)}, u32[]{:S(2)}) collective-permute-start(f32[2,2,2,128]{3,2,1,0:T(2,128)S(1)} %log_add_fusion.2), channel_id=1, source_target_pairs={{0,2},{1,3},{2,0},{3,1},{4,6},{5,7},{6,4},{7,5},{8,10},{9,11},{10,... | collective-permute-start | bytes 12296 | tf_op jit(solution)/shard_map/ppermute | solution.py:16
  55.1 4.6 %collective-permute-start.22 = (f32[2,2,2,128]{3,2,1,0:T(2,128)S(1)}, f32[2,2,2,128]{3,2,1,0:T(2,128)S(1)}, u32[]{:S(2)}, u32[]{:S(2)}) collective-permute-start(f32[2,2,2,128]{3,2,1,0:T(2,128)S(1)} %log_add_fusion.1), channel_id=1, source_target_pairs={{0,4},{1,5},{2,6},{3,7},{4,0},{5,1},{6,2},{7,3},{8,12},{9,13},{10,... | collective-permute-start | bytes 12296 | tf_op jit(solution)/shard_map/ppermute | solution.py:16
  60.8 1.5 %collective-permute-start.23 = (f32[136,384]{1,0:T(8,128)S(1)}, f32[136,384]{1,0:T(8,128)S(1)}, u32[]{:S(2)}, u32[]{:S(2)}) collective-permute-start(f32[136,384]{1,0:T(8,128)S(1)} %select_maximum_fusion), channel_id=1, source_target_pairs={{0,8},{8,0},{16,24},{24,16},{1,9},{9,1},{17,25},{25,17},{2,10},{10... | collective-permute-start | bytes 626696 | tf_op jit(solution)/shard_map/ppermute | solution.py:16
  61.5 2.7 %collective-permute-start.26 = (f32[128,384]{1,0:T(8,128)S(1)}, f32[128,384]{1,0:T(8,128)S(1)}, u32[]{:S(2)}, u32[]{:S(2)}) collective-permute-start(f32[128,384]{1,0:T(8,128)S(1)} %slice_select_fusion.3), channel_id=1, source_target_pairs={{0,8},{8,0},{16,24},{24,16},{1,9},{9,1},{17,25},{25,17},{2,10},{10... | collective-permute-start | bytes 589832 | tf_op jit(solution)/shard_map/ppermute | solution.py:16
  62.5 5.8 %collective-permute-start.24 = (bf16[136,384]{1,0:T(8,128)(2,1)S(1)}, bf16[136,384]{1,0:T(8,128)(2,1)S(1)}, u32[]{:S(2)}, u32[]{:S(2)}) collective-permute-start(bf16[136,384]{1,0:T(8,128)(2,1)S(1)} %pad_maximum_fusion.6), channel_id=1, source_target_pairs={{0,16},{8,24},{16,0},{24,8},{1,17},{9,25},{17,1},{25,9},{2,18},{10... | collective-permute-start | bytes 313352 | tf_op jit(solution)/shard_map/ppermute | solution.py:16
  64.2 5.5 %collective-permute-start.27 = (bf16[128,384]{1,0:T(8,128)(2,1)S(1)}, bf16[128,384]{1,0:T(8,128)(2,1)S(1)}, u32[]{:S(2)}, u32[]{:S(2)}) collective-permute-start(bf16[128,384]{1,0:T(8,128)(2,1)S(1)} %add_convert_fusion), channel_id=1, source_target_pairs={{0,16},{8,24},{16,0},{24,8},{1,17},{9,25},{17,1},{25,9},{2,18},{10... | collective-permute-start | bytes 294920 | tf_op jit(solution)/shard_map/ppermute | solution.py:16
  68.5 2.0 %collective-permute-start.25 = (f32[128,384]{1,0:T(8,128)S(1)}, f32[128,384]{1,0:T(8,128)S(1)}, u32[]{:S(2)}, u32[]{:S(2)}) collective-permute-start(f32[128,384]{1,0:T(8,128)S(1)} %fusion.37), channel_id=1, source_target_pairs={{0,8},{8,0},{16,24},{24,16},{1,9},{9,1},{17,25},{25,17},{2,10},{10... | collective-permute-start | bytes 589832 | tf_op jit(solution)/shard_map/ppermute | solution.py:16
  69.8 1.5 %collective-permute-start.28 = (f32[128,384]{1,0:T(8,128)S(1)}, f32[128,384]{1,0:T(8,128)S(1)}, u32[]{:S(2)}, u32[]{:S(2)}) collective-permute-start(f32[128,384]{1,0:T(8,128)S(1)} %fusion.36), channel_id=1, source_target_pairs={{0,8},{8,0},{16,24},{24,16},{1,9},{9,1},{17,25},{25,17},{2,10},{10... | collective-permute-start | bytes 589832 | tf_op jit(solution)/shard_map/ppermute | solution.py:16
  (2 other events, 6.3 us)

commit v11 on v10

--- a/solution.py
+++ b/solution.py
@@ -178,6 +178,14 @@
             return jnp.concatenate([line[:cut] + other[:cut], join_lse(line[cut:], other[cut:])])
 
         cut = width // 2
+
+        def lines_of(line):
+            return jnp.pad(jnp.stack(in_three(line)), ((0, 5), (0, cut - line.shape[0])))
+
+        def line_of(packed, count):
+            three = packed[kept : kept + 3, :count].astype(jnp.float32)
+            return (three[0] + three[1]) + three[2]
+
         totals = []
         for part in range(2):
             numer = 0.0
@@ -187,14 +195,14 @@
                 )
             total = jnp.where(first, numer[:kept], numer[kept:])
             sent = jnp.where(first, numer[kept:], numer[:kept])
+            sent = sent.astype(jnp.bfloat16)
             if part == 0:
-                sent = jnp.concatenate([sent, jnp.pad(rest[None, :], ((0, 7), (0, cut - rest.shape[0])))])
-            if part == 0:
+                sent = jnp.concatenate([sent, lines_of(rest)])
                 resps, _ = lax.optimization_barrier((resps, sent))
             other = swap(sent, "dp", dp_bits[0])
-            totals.append(total + other[:kept])
+            totals.append(total + other[:kept].astype(jnp.float32))
             if part == 0:
-                line = join_lines(line, other[kept, : line.shape[0]])
+                line = join_lines(line, line_of(other, line.shape[0]))
         for bit in dp_bits[1:]:
             for part in range(2):
                 sent = totals[part]
@@ -203,14 +211,11 @@
                 sent = sent.astype(jnp.bfloat16)
                 packed = sent
                 if part == 0:
-                    parts = jnp.pad(jnp.stack(in_three(line)), ((0, 5), (0, cut - line.shape[0])))
-                    packed = jnp.concatenate([packed, parts])
-                    packed = jnp.pad(packed, ((0, -packed.shape[0] % 8), (0, 0)))
+                    packed = jnp.concatenate([packed, lines_of(line)])
                 other = swap(packed, "dp", bit)
                 totals[part] = (sent, other[:kept])
                 if part == 0:
-                    three = other[kept : kept + 3, : line.shape[0]].astype(jnp.float32)
-                    line = join_lines(line, (three[0] + three[1]) + three[2])
+                    line = join_lines(line, line_of(other, line.shape[0]))
         if last:
             whole = line[kept + asks :] - line[kept : kept + asks]
             loss = lax.dynamic_slice_in_dim(whole, dp * own_queries, own_queries, 0)

time: 72.5 us -> 72.3 us (level)
  no operation moved by 1% of the time
where the time goes in v11:
time: 72.3 us; the launch traced here: 72.1 us
  starting transfers between devices  31.2 us (43%)
  waiting for transfers between devices  25 us (35%)
  matrix products  6.22 us (9%)
  other arithmetic  5.98 us (8%)
  local copies, waits for them, and re-layouts  2.47 us (3%)
  between operations  1.31 us (2%)
    ppermute x29, starting transfers between devices, swap(): return lax.ppermute(value, axis, [(i, i ^ bit) for i in range(size)])  31.2 us
    ppermute x29, waiting for transfers between devices, swap(): return lax.ppermute(value, axis, [(i, i ^ bit) for i in range(size)])  25 us
    dot_general x8, matrix products, logits_of(): lax.dot_general(centers_half, group, (((1,), (1,)), ((), ())), preferred_...  3.03 us
    dot_general x8, matrix products, on_device(): jnp.dot(resps[index], held[index][:, part * cut:(part + 1) * cut], prefer...  2.34 us
    reduce_sum x2, other arithmetic, on_device(): norms = jnp.sum(means * means, axis=1)  1.64 us
  transfers between devices with their start and end apart: 29, of which 19 were waited for; matrix products, arithmetic and copies ran while one was open for 13% of the time, Pallas kernels for 0%

profile of v11, /device:TPU:0, one launch (start us, length us, event | category | flops | bytes accessed | tf_op | source)
XLA Modules:
  0.0 72.1 jit_solution(14026845704958228097)
XLA Ops:
  1.2 3.7 %collective-permute-start.1 = (bf16[128,768]{1,0:T(8,128)(2,1)}, bf16[128,768]{1,0:T(8,128)(2,1)S(1)}, u32[]{:S(2)}, u32[]{:S(2)}) collective-permute-start(bf16[128,768]{1,0:T(8,128)(2,1)} %param.7), channel_id=1, source_target_pairs={{0,4},{1,5},{2,6},{3,7},{4,0},{5,1},{6,2},{7,3},{8,12},{9,13},{10,... | collective-permute-start | bytes 589832 | tf_op jit(solution)/shard_map/ppermute | solution.py:16
  4.8 1.6 %collective-permute-start.2 = (bf16[128,768]{1,0:T(8,128)(2,1)}, bf16[128,768]{1,0:T(8,128)(2,1)S(1)}, u32[]{:S(2)}, u32[]{:S(2)}) collective-permute-start(bf16[128,768]{1,0:T(8,128)(2,1)} %param.7), channel_id=1, source_target_pairs={{0,2},{1,3},{2,0},{3,1},{4,6},{5,7},{6,4},{7,5},{8,10},{9,11},{10,... | collective-permute-start | bytes 589832 | tf_op jit(solution)/shard_map/ppermute | solution.py:16
  6.4 1.5 %collective-permute-start.7 = (bf16[128,768]{1,0:T(8,128)(2,1)}, bf16[128,768]{1,0:T(8,128)(2,1)S(1)}, u32[]{:S(2)}, u32[]{:S(2)}) collective-permute-start(bf16[128,768]{1,0:T(8,128)(2,1)} %param.7), channel_id=1, source_target_pairs={{0,1},{1,0},{2,3},{3,2},{4,5},{5,4},{6,7},{7,6},{8,9},{9,8},{10,11... | collective-permute-start | bytes 589832 | tf_op jit(solution)/shard_map/ppermute | solution.py:16
  7.9 1.5 %multiply_reduce_fusion.1 = (f32[256]{0:T(256)S(1)}, bf16[256,768]{1,0:T(8,128)(2,1)S(1)}) fusion(f32[256,768]{1,0:T(8,128)} %param.9), kind=kLoop, calls=%fused_computation.34 | loop fusion | flops 589568 | bytes 1180672 | tf_op jit(solution)/shard_map/reduce_sum | solution.py:77
  10.1 1.6 %collective-permute-start.6 = (bf16[8,768]{1,0:T(8,128)(2,1)S(1)}, bf16[8,768]{1,0:T(8,128)(2,1)S(1)}, u32[]{:S(2)}, u32[]{:S(2)}) collective-permute-start(bf16[8,768]{1,0:T(8,128)(2,1)S(1)} %pad_maximum_fusion.10), channel_id=1, source_target_pairs={{0,16},{8,24},{16,0},{24,8},{1,17},{9,25},{17,1},{25,9},{2,18},{10... | collective-permute-start | bytes 36872 | tf_op jit(solution)/shard_map/ppermute | solution.py:16
  12.4 1.5 %collective-permute-done.6 = bf16[8,768]{1,0:T(8,128)(2,1)S(1)} collective-permute-done((bf16[8,768]{1,0:T(8,128)(2,1)S(1)}, bf16[8,768]{1,0:T(8,128)(2,1)S(1)}, u32[]{:S(2)}, u32[]{:S(2)}) %collective-permute-start.6) | collective-permute-done | bytes 12320 | tf_op jit(solution)/shard_map/ppermute | solution.py:16
  13.9 0.9 %collective-permute-done.1 = bf16[128,768]{1,0:T(8,128)(2,1)S(1)} collective-permute-done((bf16[128,768]{1,0:T(8,128)(2,1)}, bf16[128,768]{1,0:T(8,128)(2,1)S(1)}, u32[]{:S(2)}, u32[]{:S(2)}) %collective-permute-start.1) | collective-permute-done | bytes 196640 | tf_op jit(solution)/shard_map/ppermute | solution.py:16
  14.8 0.8 %collective-permute-start.5 = (bf16[128,768]{1,0:T(8,128)(2,1)S(1)}, bf16[128,768]{1,0:T(8,128)(2,1)S(1)}, u32[]{:S(2)}, u32[]{:S(2)}) collective-permute-start(bf16[128,768]{1,0:T(8,128)(2,1)S(1)} %collective-permute-done.1), channel_id=1, source_target_pairs={{0,2},{1,3},{2,0},{3,1},{4,6},{5,7},{6,4},{7,5},{8,10},{9,11},{10,... | collective-permute-start | bytes 589832 | tf_op jit(solution)/shard_map/ppermute | solution.py:16
  15.6 1.5 %collective-permute-start.9 = (bf16[128,768]{1,0:T(8,128)(2,1)S(1)}, bf16[128,768]{1,0:T(8,128)(2,1)S(1)}, u32[]{:S(2)}, u32[]{:S(2)}) collective-permute-start(bf16[128,768]{1,0:T(8,128)(2,1)S(1)} %collective-permute-done.2), channel_id=1, source_target_pairs={{0,1},{1,0},{2,3},{3,2},{4,5},{5,4},{6,7},{7,6},{8,9},{9,8},{10,11... | collective-permute-start | bytes 589832 | tf_op jit(solution)/shard_map/ppermute | solution.py:16
  18.3 3.1 %collective-permute-done.5 = bf16[128,768]{1,0:T(8,128)(2,1)S(1)} collective-permute-done((bf16[128,768]{1,0:T(8,128)(2,1)S(1)}, bf16[128,768]{1,0:T(8,128)(2,1)S(1)}, u32[]{:S(2)}, u32[]{:S(2)}) %collective-permute-start.5) | collective-permute-done | bytes 196640 | tf_op jit(solution)/shard_map/ppermute | solution.py:16
  22.8 1.1 %collective-permute-start.8 = (f32[1,2,2,128]{3,2,1,0:T(2,128)S(1)}, f32[1,2,2,128]{3,2,1,0:T(2,128)S(1)}, u32[]{:S(2)}, u32[]{:S(2)}) collective-permute-start(f32[1,2,2,128]{3,2,1,0:T(2,128)S(1)} %bitcast.133), channel_id=1, source_target_pairs={{0,2},{1,3},{2,0},{3,1},{4,6},{5,7},{6,4},{7,5},{8,10},{9,11},{10,... | collective-permute-start | bytes 6152 | tf_op jit(solution)/shard_map/ppermute | solution.py:16
  24.0 0.7 slice.257
  24.7 1.5 %collective-permute-start.12 = (bf16[128,768]{1,0:T(8,128)(2,1)}, bf16[128,768]{1,0:T(8,128)(2,1)S(1)}, u32[]{:S(2)}, u32[]{:S(2)}) collective-permute-start(bf16[128,768]{1,0:T(8,128)(2,1)} %slice.257), channel_id=1, source_target_pairs={{0,1},{1,0},{2,3},{3,2},{4,5},{5,4},{6,7},{7,6},{8,9},{9,8},{10,11... | collective-permute-start | bytes 589832 | tf_op jit(solution)/shard_map/ppermute | solution.py:16
  26.5 3.0 %collective-permute-start.10 = (f32[1,2,2,128]{3,2,1,0:T(2,128)S(1)}, f32[1,2,2,128]{3,2,1,0:T(2,128)S(1)}, u32[]{:S(2)}, u32[]{:S(2)}) collective-permute-start(f32[1,2,2,128]{3,2,1,0:T(2,128)S(1)} %log_add_fusion.6), channel_id=1, source_target_pairs={{0,4},{1,5},{2,6},{3,7},{4,0},{5,1},{6,2},{7,3},{8,12},{9,13},{10,... | collective-permute-start | bytes 6152 | tf_op jit(solution)/shard_map/ppermute | solution.py:16
  30.0 1.1 %collective-permute-done.10 = f32[1,2,2,128]{3,2,1,0:T(2,128)S(1)} collective-permute-done((f32[1,2,2,128]{3,2,1,0:T(2,128)S(1)}, f32[1,2,2,128]{3,2,1,0:T(2,128)S(1)}, u32[]{:S(2)}, u32[]{:S(2)}) %collective-permute-start.10) | collective-permute-done | bytes 2080 | tf_op jit(solution)/shard_map/ppermute | solution.py:16
  31.1 1.4 %collective-permute-start.13 = (f32[1,2,2,128]{3,2,1,0:T(2,128)S(1)}, f32[1,2,2,128]{3,2,1,0:T(2,128)S(1)}, u32[]{:S(2)}, u32[]{:S(2)}) collective-permute-start(f32[1,2,2,128]{3,2,1,0:T(2,128)S(1)} %log_add_fusion.5), channel_id=1, source_target_pairs={{0,1},{1,0},{2,3},{3,2},{4,5},{5,4},{6,7},{7,6},{8,9},{9,8},{10,11... | collective-permute-start | bytes 6152 | tf_op jit(solution)/shard_map/ppermute | solution.py:16
  33.0 1.8 %collective-permute-done.13 = f32[1,2,2,128]{3,2,1,0:T(2,128)S(1)} collective-permute-done((f32[1,2,2,128]{3,2,1,0:T(2,128)S(1)}, f32[1,2,2,128]{3,2,1,0:T(2,128)S(1)}, u32[]{:S(2)}, u32[]{:S(2)}) %collective-permute-start.13) | collective-permute-done | bytes 2080 | tf_op jit(solution)/shard_map/ppermute | solution.py:16
  37.2 1.6 %collective-permute-start.15 = (bf16[136,384]{1,0:T(8,128)(2,1)S(1)}, bf16[136,384]{1,0:T(8,128)(2,1)S(1)}, u32[]{:S(2)}, u32[]{:S(2)}) collective-permute-start(bf16[136,384]{1,0:T(8,128)(2,1)S(1)} %pad_maximum_fusion.6), channel_id=1, source_target_pairs={{0,16},{8,24},{16,0},{24,8},{1,17},{9,25},{17,1},{25,9},{2,18},{10... | collective-permute-start | bytes 313352 | tf_op jit(solution)/shard_map/ppermute | solution.py:16
  38.9 0.7 %collective-permute-start.18 = (bf16[128,384]{1,0:T(8,128)(2,1)S(1)}, bf16[128,384]{1,0:T(8,128)(2,1)S(1)}, u32[]{:S(2)}, u32[]{:S(2)}) collective-permute-start(bf16[128,384]{1,0:T(8,128)(2,1)S(1)} %add_convert_fusion.2), channel_id=1, source_target_pairs={{0,16},{8,24},{16,0},{24,8},{1,17},{9,25},{17,1},{25,9},{2,18},{10... | collective-permute-start | bytes 294920 | tf_op jit(solution)/shard_map/ppermute | solution.py:16
  39.6 3.5 %collective-permute-done.15 = bf16[136,384]{1,0:T(8,128)(2,1)S(1)} collective-permute-done((bf16[136,384]{1,0:T(8,128)(2,1)S(1)}, bf16[136,384]{1,0:T(8,128)(2,1)S(1)}, u32[]{:S(2)}, u32[]{:S(2)}) %collective-permute-start.15) | collective-permute-done | bytes 104480 | tf_op jit(solution)/shard_map/ppermute | solution.py:16
  43.3 1.1 %collective-permute-done.18 = bf16[128,384]{1,0:T(8,128)(2,1)S(1)} collective-permute-done((bf16[128,384]{1,0:T(8,128)(2,1)S(1)}, bf16[128,384]{1,0:T(8,128)(2,1)S(1)}, u32[]{:S(2)}, u32[]{:S(2)}) %collective-permute-start.18) | collective-permute-done | bytes 98336 | tf_op jit(solution)/shard_map/ppermute | solution.py:16
  44.7 1.3 %collective-permute-done.19 = f32[128,384]{1,0:T(8,128)S(1)} collective-permute-done((f32[128,384]{1,0:T(8,128)S(1)}, f32[128,384]{1,0:T(8,128)S(1)}, u32[]{:S(2)}, u32[]{:S(2)}) %collective-permute-start.19) | collective-permute-done | bytes 196640 | tf_op jit(solution)/shard_map/ppermute | solution.py:16
  47.3 1.4 %collective-permute-start.20 = (f32[2,2,2,128]{3,2,1,0:T(2,128)S(1)}, f32[2,2,2,128]{3,2,1,0:T(2,128)S(1)}, u32[]{:S(2)}, u32[]{:S(2)}) collective-permute-start(f32[2,2,2,128]{3,2,1,0:T(2,128)S(1)} %pad_maximum_fusion.12), channel_id=1, source_target_pairs={{0,1},{1,0},{2,3},{3,2},{4,5},{5,4},{6,7},{7,6},{8,9},{9,8},{10,11... | collective-permute-start | bytes 12296 | tf_op jit(solution)/shard_map/ppermute | solution.py:16
  48.8 2.2 %collective-permute-done.20 = f32[2,2,2,128]{3,2,1,0:T(2,128)S(1)} collective-permute-done((f32[2,2,2,128]{3,2,1,0:T(2,128)S(1)}, f32[2,2,2,128]{3,2,1,0:T(2,128)S(1)}, u32[]{:S(2)}, u32[]{:S(2)}) %collective-permute-start.20) | collective-permute-done | bytes 4128 | tf_op jit(solution)/shard_map/ppermute | solution.py:16
  51.3 1.4 %collective-permute-start.21 = (f32[2,2,2,128]{3,2,1,0:T(2,128)S(1)}, f32[2,2,2,128]{3,2,1,0:T(2,128)S(1)}, u32[]{:S(2)}, u32[]{:S(2)}) collective-permute-start(f32[2,2,2,128]{3,2,1,0:T(2,128)S(1)} %log_add_fusion.2), channel_id=1, source_target_pairs={{0,2},{1,3},{2,0},{3,1},{4,6},{5,7},{6,4},{7,5},{8,10},{9,11},{10,... | collective-permute-start | bytes 12296 | tf_op jit(solution)/shard_map/ppermute | solution.py:16
  55.0 3.0 %collective-permute-start.22 = (f32[2,2,2,128]{3,2,1,0:T(2,128)S(1)}, f32[2,2,2,128]{3,2,1,0:T(2,128)S(1)}, u32[]{:S(2)}, u32[]{:S(2)}) collective-permute-start(f32[2,2,2,128]{3,2,1,0:T(2,128)S(1)} %log_add_fusion.1), channel_id=1, source_target_pairs={{0,4},{1,5},{2,6},{3,7},{4,0},{5,1},{6,2},{7,3},{8,12},{9,13},{10,... | collective-permute-start | bytes 12296 | tf_op jit(solution)/shard_map/ppermute | solution.py:16
  58.0 1.6 %collective-permute-done.22 = f32[2,2,2,128]{3,2,1,0:T(2,128)S(1)} collective-permute-done((f32[2,2,2,128]{3,2,1,0:T(2,128)S(1)}, f32[2,2,2,128]{3,2,1,0:T(2,128)S(1)}, u32[]{:S(2)}, u32[]{:S(2)}) %collective-permute-start.22) | collective-permute-done | bytes 4128 | tf_op jit(solution)/shard_map/ppermute | solution.py:16
  62.4 1.6 %collective-permute-start.24 = (bf16[136,384]{1,0:T(8,128)(2,1)S(1)}, bf16[136,384]{1,0:T(8,128)(2,1)S(1)}, u32[]{:S(2)}, u32[]{:S(2)}) collective-permute-start(bf16[136,384]{1,0:T(8,128)(2,1)S(1)} %pad_maximum_fusion.8), channel_id=1, source_target_pairs={{0,16},{8,24},{16,0},{24,8},{1,17},{9,25},{17,1},{25,9},{2,18},{10... | collective-permute-start | bytes 313352 | tf_op jit(solution)/shard_map/ppermute | solution.py:16
  64.6 3.6 %collective-permute-done.24 = bf16[136,384]{1,0:T(8,128)(2,1)S(1)} collective-permute-done((bf16[136,384]{1,0:T(8,128)(2,1)S(1)}, bf16[136,384]{1,0:T(8,128)(2,1)S(1)}, u32[]{:S(2)}, u32[]{:S(2)}) %collective-permute-start.24) | collective-permute-done | bytes 104480 | tf_op jit(solution)/shard_map/ppermute | solution.py:16
  68.4 1.1 %collective-permute-done.27 = bf16[128,384]{1,0:T(8,128)(2,1)S(1)} collective-permute-done((bf16[128,384]{1,0:T(8,128)(2,1)S(1)}, bf16[128,384]{1,0:T(8,128)(2,1)S(1)}, u32[]{:S(2)}, u32[]{:S(2)}) %collective-permute-start.27) | collective-permute-done | bytes 98336 | tf_op jit(solution)/shard_map/ppermute | solution.py:16
  70.4 0.7 collective-permute-done.28
  71.2 0.9 %maximum_maximum_fusion.1 = f32[256,768]{1,0:T(8,128)} fusion(f32[128,384]{1,0:T(8,128)S(1)} %get-tuple-element.115, f32[128,384]{1,0:T(8,128)S(1)} %get-tuple-element.114, f32[128,384]{1,0:T(8,128)S(1)} %get-tuple-element.113, f32[128,384]{1,0:T(8,128)S(1)} %get-tuple-element.112), kind=kLoop, calls=%fused_computation.32 | loop fusion | flops 589824 | bytes 1572864 | tf_op jit(solution)/shard_map/concatenate | solution.py:230
  (172 shorter events, 16.8 us)
Async XLA Ops:
  0.6 8.8 %copy-start = (f32[256,768]{1,0:T(8,128)S(1)}, f32[256,768]{1,0:T(8,128)}, u32[]{:S(2)}) copy-start(f32[256,768]{1,0:T(8,128)} %param.9) | copy-start | bytes 2359300
  0.6 4.2 %collective-permute-start = (bf16[4,768]{1,0:T(4,128)(2,1)}, bf16[4,768]{1,0:T(4,128)(2,1)S(1)}, u32[]{:S(2)}, u32[]{:S(2)}) collective-permute-start(bf16[4,768]{1,0:T(4,128)(2,1)} %param.8), channel_id=1, source_target_pairs={{0,8},{8,0},{16,24},{24,16},{1,9},{9,1},{17,25},{25,17},{2,10},{10... | collective-permute-start | bytes 18440 | tf_op jit(solution)/shard_map/ppermute | solution.py:16
  1.2 13.7 %collective-permute-start.1 = (bf16[128,768]{1,0:T(8,128)(2,1)}, bf16[128,768]{1,0:T(8,128)(2,1)S(1)}, u32[]{:S(2)}, u32[]{:S(2)}) collective-permute-start(bf16[128,768]{1,0:T(8,128)(2,1)} %param.7), channel_id=1, source_target_pairs={{0,4},{1,5},{2,6},{3,7},{4,0},{5,1},{6,2},{7,3},{8,12},{9,13},{10,... | collective-permute-start | bytes 589832 | tf_op jit(solution)/shard_map/ppermute | solution.py:16
  4.8 10.8 %collective-permute-start.2 = (bf16[128,768]{1,0:T(8,128)(2,1)}, bf16[128,768]{1,0:T(8,128)(2,1)S(1)}, u32[]{:S(2)}, u32[]{:S(2)}) collective-permute-start(bf16[128,768]{1,0:T(8,128)(2,1)} %param.7), channel_id=1, source_target_pairs={{0,2},{1,3},{2,0},{3,1},{4,6},{5,7},{6,4},{7,5},{8,10},{9,11},{10,... | collective-permute-start | bytes 589832 | tf_op jit(solution)/shard_map/ppermute | solution.py:16
  6.4 16.4 %collective-permute-start.7 = (bf16[128,768]{1,0:T(8,128)(2,1)}, bf16[128,768]{1,0:T(8,128)(2,1)S(1)}, u32[]{:S(2)}, u32[]{:S(2)}) collective-permute-start(bf16[128,768]{1,0:T(8,128)(2,1)} %param.7), channel_id=1, source_target_pairs={{0,1},{1,0},{2,3},{3,2},{4,5},{5,4},{6,7},{7,6},{8,9},{9,8},{10,11... | collective-permute-start | bytes 589832 | tf_op jit(solution)/shard_map/ppermute | solution.py:16
  9.5 7.7 %copy-start.1 = (bf16[128,768]{1,0:T(8,128)(2,1)S(1)}, bf16[128,768]{1,0:T(8,128)(2,1)}, u32[]{:S(2)}) copy-start(bf16[128,768]{1,0:T(8,128)(2,1)} %param.7) | copy-start | bytes 589828
  10.1 3.8 %collective-permute-start.6 = (bf16[8,768]{1,0:T(8,128)(2,1)S(1)}, bf16[8,768]{1,0:T(8,128)(2,1)S(1)}, u32[]{:S(2)}, u32[]{:S(2)}) collective-permute-start(bf16[8,768]{1,0:T(8,128)(2,1)S(1)} %pad_maximum_fusion.10), channel_id=1, source_target_pairs={{0,16},{8,24},{16,0},{24,8},{1,17},{9,25},{17,1},{25,9},{2,18},{10... | collective-permute-start | bytes 36872 | tf_op jit(solution)/shard_map/ppermute | solution.py:16
  11.8 6.6 %collective-permute-start.3 = (bf16[136,768]{1,0:T(8,128)(2,1)S(1)}, bf16[136,768]{1,0:T(8,128)(2,1)S(1)}, u32[]{:S(2)}, u32[]{:S(2)}) collective-permute-start(bf16[136,768]{1,0:T(8,128)(2,1)S(1)} %pad_maximum_fusion.4), channel_id=1, source_target_pairs={{0,1},{1,0},{2,3},{3,2},{4,5},{5,4},{6,7},{7,6},{8,9},{9,8},{10,11... | collective-permute-start | bytes 626696 | tf_op jit(solution)/shard_map/ppermute | solution.py:16
  14.8 6.6 %collective-permute-start.5 = (bf16[128,768]{1,0:T(8,128)(2,1)S(1)}, bf16[128,768]{1,0:T(8,128)(2,1)S(1)}, u32[]{:S(2)}, u32[]{:S(2)}) collective-permute-start(bf16[128,768]{1,0:T(8,128)(2,1)S(1)} %collective-permute-done.1), channel_id=1, source_target_pairs={{0,2},{1,3},{2,0},{3,1},{4,6},{5,7},{6,4},{7,5},{8,10},{9,11},{10,... | collective-permute-start | bytes 589832 | tf_op jit(solution)/shard_map/ppermute | solution.py:16
  15.6 10.9 %collective-permute-start.9 = (bf16[128,768]{1,0:T(8,128)(2,1)S(1)}, bf16[128,768]{1,0:T(8,128)(2,1)S(1)}, u32[]{:S(2)}, u32[]{:S(2)}) collective-permute-start(bf16[128,768]{1,0:T(8,128)(2,1)S(1)} %collective-permute-done.2), channel_id=1, source_target_pairs={{0,1},{1,0},{2,3},{3,2},{4,5},{5,4},{6,7},{7,6},{8,9},{9,8},{10,11... | collective-permute-start | bytes 589832 | tf_op jit(solution)/shard_map/ppermute | solution.py:16
  17.1 14.0 %collective-permute-start.11 = (bf16[128,768]{1,0:T(8,128)(2,1)S(1)}, bf16[128,768]{1,0:T(8,128)(2,1)S(1)}, u32[]{:S(2)}, u32[]{:S(2)}) collective-permute-start(bf16[128,768]{1,0:T(8,128)(2,1)S(1)} %collective-permute-done.1), channel_id=1, source_target_pairs={{0,1},{1,0},{2,3},{3,2},{4,5},{5,4},{6,7},{7,6},{8,9},{9,8},{10,11... | collective-permute-start | bytes 589832 | tf_op jit(solution)/shard_map/ppermute | solution.py:16
  18.3 3.4 %collective-permute-start.4 = (bf16[136,768]{1,0:T(8,128)(2,1)S(1)}, bf16[136,768]{1,0:T(8,128)(2,1)S(1)}, u32[]{:S(2)}, u32[]{:S(2)}) collective-permute-start(bf16[136,768]{1,0:T(8,128)(2,1)S(1)} %collective-permute-done.3), channel_id=1, source_target_pairs={{0,8},{8,0},{16,24},{24,16},{1,9},{9,1},{17,25},{25,17},{2,10},{10... | collective-permute-start | bytes 626696 | tf_op jit(solution)/shard_map/ppermute | solution.py:16
  22.8 3.7 %collective-permute-start.8 = (f32[1,2,2,128]{3,2,1,0:T(2,128)S(1)}, f32[1,2,2,128]{3,2,1,0:T(2,128)S(1)}, u32[]{:S(2)}, u32[]{:S(2)}) collective-permute-start(f32[1,2,2,128]{3,2,1,0:T(2,128)S(1)} %bitcast.133), channel_id=1, source_target_pairs={{0,2},{1,3},{2,0},{3,1},{4,6},{5,7},{6,4},{7,5},{8,10},{9,11},{10,... | collective-permute-start | bytes 6152 | tf_op jit(solution)/shard_map/ppermute | solution.py:16
  24.7 6.5 %collective-permute-start.12 = (bf16[128,768]{1,0:T(8,128)(2,1)}, bf16[128,768]{1,0:T(8,128)(2,1)S(1)}, u32[]{:S(2)}, u32[]{:S(2)}) collective-permute-start(bf16[128,768]{1,0:T(8,128)(2,1)} %slice.257), channel_id=1, source_target_pairs={{0,1},{1,0},{2,3},{3,2},{4,5},{5,4},{6,7},{7,6},{8,9},{9,8},{10,11... | collective-permute-start | bytes 589832 | tf_op jit(solution)/shard_map/ppermute | solution.py:16
  26.5 4.6 %collective-permute-start.10 = (f32[1,2,2,128]{3,2,1,0:T(2,128)S(1)}, f32[1,2,2,128]{3,2,1,0:T(2,128)S(1)}, u32[]{:S(2)}, u32[]{:S(2)}) collective-permute-start(f32[1,2,2,128]{3,2,1,0:T(2,128)S(1)} %log_add_fusion.6), channel_id=1, source_target_pairs={{0,4},{1,5},{2,6},{3,7},{4,0},{5,1},{6,2},{7,3},{8,12},{9,13},{10,... | collective-permute-start | bytes 6152 | tf_op jit(solution)/shard_map/ppermute | solution.py:16
  31.1 3.7 %collective-permute-start.13 = (f32[1,2,2,128]{3,2,1,0:T(2,128)S(1)}, f32[1,2,2,128]{3,2,1,0:T(2,128)S(1)}, u32[]{:S(2)}, u32[]{:S(2)}) collective-permute-start(f32[1,2,2,128]{3,2,1,0:T(2,128)S(1)} %log_add_fusion.5), channel_id=1, source_target_pairs={{0,1},{1,0},{2,3},{3,2},{4,5},{5,4},{6,7},{7,6},{8,9},{9,8},{10,11... | collective-permute-start | bytes 6152 | tf_op jit(solution)/shard_map/ppermute | solution.py:16
  35.8 1.4 %collective-permute-start.14 = (bf16[136,384]{1,0:T(8,128)(2,1)S(1)}, bf16[136,384]{1,0:T(8,128)(2,1)S(1)}, u32[]{:S(2)}, u32[]{:S(2)}) collective-permute-start(bf16[136,384]{1,0:T(8,128)(2,1)S(1)} %pad_maximum_fusion.5), channel_id=1, source_target_pairs={{0,8},{8,0},{16,24},{24,16},{1,9},{9,1},{17,25},{25,17},{2,10},{10... | collective-permute-start | bytes 313352 | tf_op jit(solution)/shard_map/ppermute | solution.py:16
  36.5 2.4 %collective-permute-start.17 = (bf16[128,384]{1,0:T(8,128)(2,1)S(1)}, bf16[128,384]{1,0:T(8,128)(2,1)S(1)}, u32[]{:S(2)}, u32[]{:S(2)}) collective-permute-start(bf16[128,384]{1,0:T(8,128)(2,1)S(1)} %select_convert_fusion.2), channel_id=1, source_target_pairs={{0,8},{8,0},{16,24},{24,16},{1,9},{9,1},{17,25},{25,17},{2,10},{10... | collective-permute-start | bytes 294920 | tf_op jit(solution)/shard_map/ppermute | solution.py:16
  37.2 5.8 %collective-permute-start.15 = (bf16[136,384]{1,0:T(8,128)(2,1)S(1)}, bf16[136,384]{1,0:T(8,128)(2,1)S(1)}, u32[]{:S(2)}, u32[]{:S(2)}) collective-permute-start(bf16[136,384]{1,0:T(8,128)(2,1)S(1)} %pad_maximum_fusion.6), channel_id=1, source_target_pairs={{0,16},{8,24},{16,0},{24,8},{1,17},{9,25},{17,1},{25,9},{2,18},{10... | collective-permute-start | bytes 313352 | tf_op jit(solution)/shard_map/ppermute | solution.py:16
  38.9 5.5 %collective-permute-start.18 = (bf16[128,384]{1,0:T(8,128)(2,1)S(1)}, bf16[128,384]{1,0:T(8,128)(2,1)S(1)}, u32[]{:S(2)}, u32[]{:S(2)}) collective-permute-start(bf16[128,384]{1,0:T(8,128)(2,1)S(1)} %add_convert_fusion.2), channel_id=1, source_target_pairs={{0,16},{8,24},{16,0},{24,8},{1,17},{9,25},{17,1},{25,9},{2,18},{10... | collective-permute-start | bytes 294920 | tf_op jit(solution)/shard_map/ppermute | solution.py:16
  43.2 1.5 %collective-permute-start.16 = (f32[128,384]{1,0:T(8,128)S(1)}, f32[128,384]{1,0:T(8,128)S(1)}, u32[]{:S(2)}, u32[]{:S(2)}) collective-permute-start(f32[128,384]{1,0:T(8,128)S(1)} %fusion.39), channel_id=1, source_target_pairs={{0,8},{8,0},{16,24},{24,16},{1,9},{9,1},{17,25},{25,17},{2,10},{10... | collective-permute-start | bytes 589832 | tf_op jit(solution)/shard_map/ppermute | solution.py:16
  44.5 1.5 %collective-permute-start.19 = (f32[128,384]{1,0:T(8,128)S(1)}, f32[128,384]{1,0:T(8,128)S(1)}, u32[]{:S(2)}, u32[]{:S(2)}) collective-permute-start(f32[128,384]{1,0:T(8,128)S(1)} %fusion.38), channel_id=1, source_target_pairs={{0,8},{8,0},{16,24},{24,16},{1,9},{9,1},{17,25},{25,17},{2,10},{10... | collective-permute-start | bytes 589832 | tf_op jit(solution)/shard_map/ppermute | solution.py:16
  47.3 5.7 %copy-start.4 = (s32[128]{0:T(128)S(1)}, s32[128]{0:T(128)}, u32[]{:S(2)}) copy-start(s32[128]{0:T(128)} %param.11) | copy-start | bytes 1540
  47.3 3.7 %collective-permute-start.20 = (f32[2,2,2,128]{3,2,1,0:T(2,128)S(1)}, f32[2,2,2,128]{3,2,1,0:T(2,128)S(1)}, u32[]{:S(2)}, u32[]{:S(2)}) collective-permute-start(f32[2,2,2,128]{3,2,1,0:T(2,128)S(1)} %pad_maximum_fusion.12), channel_id=1, source_target_pairs={{0,1},{1,0},{2,3},{3,2},{4,5},{5,4},{6,7},{7,6},{8,9},{9,8},{10,11... | collective-permute-start | bytes 12296 | tf_op jit(solution)/shard_map/ppermute | solution.py:16
  51.3 3.6 %collective-permute-start.21 = (f32[2,2,2,128]{3,2,1,0:T(2,128)S(1)}, f32[2,2,2,128]{3,2,1,0:T(2,128)S(1)}, u32[]{:S(2)}, u32[]{:S(2)}) collective-permute-start(f32[2,2,2,128]{3,2,1,0:T(2,128)S(1)} %log_add_fusion.2), channel_id=1, source_target_pairs={{0,2},{1,3},{2,0},{3,1},{4,6},{5,7},{6,4},{7,5},{8,10},{9,11},{10,... | collective-permute-start | bytes 12296 | tf_op jit(solution)/shard_map/ppermute | solution.py:16
  55.0 4.6 %collective-permute-start.22 = (f32[2,2,2,128]{3,2,1,0:T(2,128)S(1)}, f32[2,2,2,128]{3,2,1,0:T(2,128)S(1)}, u32[]{:S(2)}, u32[]{:S(2)}) collective-permute-start(f32[2,2,2,128]{3,2,1,0:T(2,128)S(1)} %log_add_fusion.1), channel_id=1, source_target_pairs={{0,4},{1,5},{2,6},{3,7},{4,0},{5,1},{6,2},{7,3},{8,12},{9,13},{10,... | collective-permute-start | bytes 12296 | tf_op jit(solution)/shard_map/ppermute | solution.py:16
  60.7 1.4 %collective-permute-start.23 = (bf16[136,384]{1,0:T(8,128)(2,1)S(1)}, bf16[136,384]{1,0:T(8,128)(2,1)S(1)}, u32[]{:S(2)}, u32[]{:S(2)}) collective-permute-start(bf16[136,384]{1,0:T(8,128)(2,1)S(1)} %pad_maximum_fusion.7), channel_id=1, source_target_pairs={{0,8},{8,0},{16,24},{24,16},{1,9},{9,1},{17,25},{25,17},{2,10},{10... | collective-permute-start | bytes 313352 | tf_op jit(solution)/shard_map/ppermute | solution.py:16
  61.4 2.5 %collective-permute-start.26 = (bf16[128,384]{1,0:T(8,128)(2,1)S(1)}, bf16[128,384]{1,0:T(8,128)(2,1)S(1)}, u32[]{:S(2)}, u32[]{:S(2)}) collective-permute-start(bf16[128,384]{1,0:T(8,128)(2,1)S(1)} %select_convert_fusion), channel_id=1, source_target_pairs={{0,8},{8,0},{16,24},{24,16},{1,9},{9,1},{17,25},{25,17},{2,10},{10... | collective-permute-start | bytes 294920 | tf_op jit(solution)/shard_map/ppermute | solution.py:16
  62.4 5.8 %collective-permute-start.24 = (bf16[136,384]{1,0:T(8,128)(2,1)S(1)}, bf16[136,384]{1,0:T(8,128)(2,1)S(1)}, u32[]{:S(2)}, u32[]{:S(2)}) collective-permute-start(bf16[136,384]{1,0:T(8,128)(2,1)S(1)} %pad_maximum_fusion.8), channel_id=1, source_target_pairs={{0,16},{8,24},{16,0},{24,8},{1,17},{9,25},{17,1},{25,9},{2,18},{10... | collective-permute-start | bytes 313352 | tf_op jit(solution)/shard_map/ppermute | solution.py:16
  64.0 5.5 %collective-permute-start.27 = (bf16[128,384]{1,0:T(8,128)(2,1)S(1)}, bf16[128,384]{1,0:T(8,128)(2,1)S(1)}, u32[]{:S(2)}, u32[]{:S(2)}) collective-permute-start(bf16[128,384]{1,0:T(8,128)(2,1)S(1)} %add_convert_fusion), channel_id=1, source_target_pairs={{0,16},{8,24},{16,0},{24,8},{1,17},{9,25},{17,1},{25,9},{2,18},{10... | collective-permute-start | bytes 294920 | tf_op jit(solution)/shard_map/ppermute | solution.py:16
  68.3 2.0 %collective-permute-start.25 = (f32[128,384]{1,0:T(8,128)S(1)}, f32[128,384]{1,0:T(8,128)S(1)}, u32[]{:S(2)}, u32[]{:S(2)}) collective-permute-start(f32[128,384]{1,0:T(8,128)S(1)} %fusion.37), channel_id=1, source_target_pairs={{0,8},{8,0},{16,24},{24,16},{1,9},{9,1},{17,25},{25,17},{2,10},{10... | collective-permute-start | bytes 589832 | tf_op jit(solution)/shard_map/ppermute | solution.py:16
  69.6 1.5 %collective-permute-start.28 = (f32[128,384]{1,0:T(8,128)S(1)}, f32[128,384]{1,0:T(8,128)S(1)}, u32[]{:S(2)}, u32[]{:S(2)}) collective-permute-start(f32[128,384]{1,0:T(8,128)S(1)} %fusion.36), channel_id=1, source_target_pairs={{0,8},{8,0},{16,24},{24,16},{1,9},{9,1},{17,25},{25,17},{2,10},{10... | collective-permute-start | bytes 589832 | tf_op jit(solution)/shard_map/ppermute | solution.py:16
  (2 other events, 6.3 us)

commit v12 on v11

--- a/solution.py
+++ b/solution.py
@@ -152,9 +152,10 @@
             centers_half = means.astype(jnp.bfloat16)
             odds = [logits_of(centers_half, norms, group) for group in held]
             lse = jnp.concatenate([stats_of(part) for part in odds]).reshape(shape)
-            for bit in cent_bits:
+            hops = cent_bits[::-1]
+            for bit in hops:
                 lse = over_column(bit, lse)
-                if last and bit == cent_bits[0]:
+                if last and bit == hops[0]:
                     inputs = (lse, asked, pattern, positive_offset, dp, cent)
                     lse, *inputs = lax.optimization_barrier(inputs)
                     positive, found = loss_partials(*inputs)

time: 72.3 us -> 72.3 us (level)
  no operation moved by 1% of the time
where the time goes in v12:
time: 72.3 us; the launch traced here: 72.1 us
  starting transfers between devices  31.1 us (43%)
  waiting for transfers between devices  25 us (35%)
  matrix products  6.22 us (9%)
  other arithmetic  5.98 us (8%)
  local copies, waits for them, and re-layouts  2.47 us (3%)
  between operations  1.31 us (2%)
    ppermute x29, starting transfers between devices, swap(): return lax.ppermute(value, axis, [(i, i ^ bit) for i in range(size)])  31.1 us
    ppermute x29, waiting for transfers between devices, swap(): return lax.ppermute(value, axis, [(i, i ^ bit) for i in range(size)])  25 us
    dot_general x8, matrix products, logits_of(): lax.dot_general(centers_half, group, (((1,), (1,)), ((), ())), preferred_...  3.03 us
    dot_general x8, matrix products, on_device(): jnp.dot(resps[index], held[index][:, part * cut:(part + 1) * cut], prefer...  2.34 us
    reduce_sum x2, other arithmetic, on_device(): norms = jnp.sum(means * means, axis=1)  1.64 us
  transfers between devices with their start and end apart: 29, of which 19 were waited for; matrix products, arithmetic and copies ran while one was open for 13% of the time, Pallas kernels for 0%

profile of v12, /device:TPU:0, one launch (start us, length us, event | category | flops | bytes accessed | tf_op | source)
XLA Modules:
  0.0 72.1 jit_solution(3123667462109580822)
XLA Ops:
  1.2 3.7 %collective-permute-start.1 = (bf16[128,768]{1,0:T(8,128)(2,1)}, bf16[128,768]{1,0:T(8,128)(2,1)S(1)}, u32[]{:S(2)}, u32[]{:S(2)}) collective-permute-start(bf16[128,768]{1,0:T(8,128)(2,1)} %param.7), channel_id=1, source_target_pairs={{0,4},{1,5},{2,6},{3,7},{4,0},{5,1},{6,2},{7,3},{8,12},{9,13},{10,... | collective-permute-start | bytes 589832 | tf_op jit(solution)/shard_map/ppermute | solution.py:16
  4.8 1.6 %collective-permute-start.2 = (bf16[128,768]{1,0:T(8,128)(2,1)}, bf16[128,768]{1,0:T(8,128)(2,1)S(1)}, u32[]{:S(2)}, u32[]{:S(2)}) collective-permute-start(bf16[128,768]{1,0:T(8,128)(2,1)} %param.7), channel_id=1, source_target_pairs={{0,2},{1,3},{2,0},{3,1},{4,6},{5,7},{6,4},{7,5},{8,10},{9,11},{10,... | collective-permute-start | bytes 589832 | tf_op jit(solution)/shard_map/ppermute | solution.py:16
  6.4 1.5 %collective-permute-start.7 = (bf16[128,768]{1,0:T(8,128)(2,1)}, bf16[128,768]{1,0:T(8,128)(2,1)S(1)}, u32[]{:S(2)}, u32[]{:S(2)}) collective-permute-start(bf16[128,768]{1,0:T(8,128)(2,1)} %param.7), channel_id=1, source_target_pairs={{0,1},{1,0},{2,3},{3,2},{4,5},{5,4},{6,7},{7,6},{8,9},{9,8},{10,11... | collective-permute-start | bytes 589832 | tf_op jit(solution)/shard_map/ppermute | solution.py:16
  7.9 1.5 %multiply_reduce_fusion.1 = (f32[256]{0:T(256)S(1)}, bf16[256,768]{1,0:T(8,128)(2,1)S(1)}) fusion(f32[256,768]{1,0:T(8,128)} %param.9), kind=kLoop, calls=%fused_computation.34 | loop fusion | flops 589568 | bytes 1180672 | tf_op jit(solution)/shard_map/reduce_sum | solution.py:77
  10.1 1.6 %collective-permute-start.6 = (bf16[8,768]{1,0:T(8,128)(2,1)S(1)}, bf16[8,768]{1,0:T(8,128)(2,1)S(1)}, u32[]{:S(2)}, u32[]{:S(2)}) collective-permute-start(bf16[8,768]{1,0:T(8,128)(2,1)S(1)} %pad_maximum_fusion.10), channel_id=1, source_target_pairs={{0,16},{8,24},{16,0},{24,8},{1,17},{9,25},{17,1},{25,9},{2,18},{10... | collective-permute-start | bytes 36872 | tf_op jit(solution)/shard_map/ppermute | solution.py:16
  12.4 1.5 %collective-permute-done.6 = bf16[8,768]{1,0:T(8,128)(2,1)S(1)} collective-permute-done((bf16[8,768]{1,0:T(8,128)(2,1)S(1)}, bf16[8,768]{1,0:T(8,128)(2,1)S(1)}, u32[]{:S(2)}, u32[]{:S(2)}) %collective-permute-start.6) | collective-permute-done | bytes 12320 | tf_op jit(solution)/shard_map/ppermute | solution.py:16
  13.9 0.9 %collective-permute-done.1 = bf16[128,768]{1,0:T(8,128)(2,1)S(1)} collective-permute-done((bf16[128,768]{1,0:T(8,128)(2,1)}, bf16[128,768]{1,0:T(8,128)(2,1)S(1)}, u32[]{:S(2)}, u32[]{:S(2)}) %collective-permute-start.1) | collective-permute-done | bytes 196640 | tf_op jit(solution)/shard_map/ppermute | solution.py:16
  14.8 0.8 %collective-permute-start.5 = (bf16[128,768]{1,0:T(8,128)(2,1)S(1)}, bf16[128,768]{1,0:T(8,128)(2,1)S(1)}, u32[]{:S(2)}, u32[]{:S(2)}) collective-permute-start(bf16[128,768]{1,0:T(8,128)(2,1)S(1)} %collective-permute-done.1), channel_id=1, source_target_pairs={{0,2},{1,3},{2,0},{3,1},{4,6},{5,7},{6,4},{7,5},{8,10},{9,11},{10,... | collective-permute-start | bytes 589832 | tf_op jit(solution)/shard_map/ppermute | solution.py:16
  15.6 1.5 %collective-permute-start.9 = (bf16[128,768]{1,0:T(8,128)(2,1)S(1)}, bf16[128,768]{1,0:T(8,128)(2,1)S(1)}, u32[]{:S(2)}, u32[]{:S(2)}) collective-permute-start(bf16[128,768]{1,0:T(8,128)(2,1)S(1)} %collective-permute-done.2), channel_id=1, source_target_pairs={{0,1},{1,0},{2,3},{3,2},{4,5},{5,4},{6,7},{7,6},{8,9},{9,8},{10,11... | collective-permute-start | bytes 589832 | tf_op jit(solution)/shard_map/ppermute | solution.py:16
  18.3 3.1 %collective-permute-done.5 = bf16[128,768]{1,0:T(8,128)(2,1)S(1)} collective-permute-done((bf16[128,768]{1,0:T(8,128)(2,1)S(1)}, bf16[128,768]{1,0:T(8,128)(2,1)S(1)}, u32[]{:S(2)}, u32[]{:S(2)}) %collective-permute-start.5) | collective-permute-done | bytes 196640 | tf_op jit(solution)/shard_map/ppermute | solution.py:16
  22.8 1.1 %collective-permute-start.8 = (f32[1,2,2,128]{3,2,1,0:T(2,128)S(1)}, f32[1,2,2,128]{3,2,1,0:T(2,128)S(1)}, u32[]{:S(2)}, u32[]{:S(2)}) collective-permute-start(f32[1,2,2,128]{3,2,1,0:T(2,128)S(1)} %bitcast.133), channel_id=1, source_target_pairs={{0,2},{1,3},{2,0},{3,1},{4,6},{5,7},{6,4},{7,5},{8,10},{9,11},{10,... | collective-permute-start | bytes 6152 | tf_op jit(solution)/shard_map/ppermute | solution.py:16
  24.0 0.7 slice.257
  24.7 1.5 %collective-permute-start.12 = (bf16[128,768]{1,0:T(8,128)(2,1)}, bf16[128,768]{1,0:T(8,128)(2,1)S(1)}, u32[]{:S(2)}, u32[]{:S(2)}) collective-permute-start(bf16[128,768]{1,0:T(8,128)(2,1)} %slice.257), channel_id=1, source_target_pairs={{0,1},{1,0},{2,3},{3,2},{4,5},{5,4},{6,7},{7,6},{8,9},{9,8},{10,11... | collective-permute-start | bytes 589832 | tf_op jit(solution)/shard_map/ppermute | solution.py:16
  26.5 3.0 %collective-permute-start.10 = (f32[1,2,2,128]{3,2,1,0:T(2,128)S(1)}, f32[1,2,2,128]{3,2,1,0:T(2,128)S(1)}, u32[]{:S(2)}, u32[]{:S(2)}) collective-permute-start(f32[1,2,2,128]{3,2,1,0:T(2,128)S(1)} %log_add_fusion.6), channel_id=1, source_target_pairs={{0,4},{1,5},{2,6},{3,7},{4,0},{5,1},{6,2},{7,3},{8,12},{9,13},{10,... | collective-permute-start | bytes 6152 | tf_op jit(solution)/shard_map/ppermute | solution.py:16
  30.0 1.1 %collective-permute-done.10 = f32[1,2,2,128]{3,2,1,0:T(2,128)S(1)} collective-permute-done((f32[1,2,2,128]{3,2,1,0:T(2,128)S(1)}, f32[1,2,2,128]{3,2,1,0:T(2,128)S(1)}, u32[]{:S(2)}, u32[]{:S(2)}) %collective-permute-start.10) | collective-permute-done | bytes 2080 | tf_op jit(solution)/shard_map/ppermute | solution.py:16
  31.1 1.4 %collective-permute-start.13 = (f32[1,2,2,128]{3,2,1,0:T(2,128)S(1)}, f32[1,2,2,128]{3,2,1,0:T(2,128)S(1)}, u32[]{:S(2)}, u32[]{:S(2)}) collective-permute-start(f32[1,2,2,128]{3,2,1,0:T(2,128)S(1)} %log_add_fusion.5), channel_id=1, source_target_pairs={{0,1},{1,0},{2,3},{3,2},{4,5},{5,4},{6,7},{7,6},{8,9},{9,8},{10,11... | collective-permute-start | bytes 6152 | tf_op jit(solution)/shard_map/ppermute | solution.py:16
  33.0 1.8 %collective-permute-done.13 = f32[1,2,2,128]{3,2,1,0:T(2,128)S(1)} collective-permute-done((f32[1,2,2,128]{3,2,1,0:T(2,128)S(1)}, f32[1,2,2,128]{3,2,1,0:T(2,128)S(1)}, u32[]{:S(2)}, u32[]{:S(2)}) %collective-permute-start.13) | collective-permute-done | bytes 2080 | tf_op jit(solution)/shard_map/ppermute | solution.py:16
  37.2 1.6 %collective-permute-start.15 = (bf16[136,384]{1,0:T(8,128)(2,1)S(1)}, bf16[136,384]{1,0:T(8,128)(2,1)S(1)}, u32[]{:S(2)}, u32[]{:S(2)}) collective-permute-start(bf16[136,384]{1,0:T(8,128)(2,1)S(1)} %pad_maximum_fusion.6), channel_id=1, source_target_pairs={{0,16},{8,24},{16,0},{24,8},{1,17},{9,25},{17,1},{25,9},{2,18},{10... | collective-permute-start | bytes 313352 | tf_op jit(solution)/shard_map/ppermute | solution.py:16
  38.9 0.7 %collective-permute-start.18 = (bf16[128,384]{1,0:T(8,128)(2,1)S(1)}, bf16[128,384]{1,0:T(8,128)(2,1)S(1)}, u32[]{:S(2)}, u32[]{:S(2)}) collective-permute-start(bf16[128,384]{1,0:T(8,128)(2,1)S(1)} %add_convert_fusion.2), channel_id=1, source_target_pairs={{0,16},{8,24},{16,0},{24,8},{1,17},{9,25},{17,1},{25,9},{2,18},{10... | collective-permute-start | bytes 294920 | tf_op jit(solution)/shard_map/ppermute | solution.py:16
  39.6 3.5 %collective-permute-done.15 = bf16[136,384]{1,0:T(8,128)(2,1)S(1)} collective-permute-done((bf16[136,384]{1,0:T(8,128)(2,1)S(1)}, bf16[136,384]{1,0:T(8,128)(2,1)S(1)}, u32[]{:S(2)}, u32[]{:S(2)}) %collective-permute-start.15) | collective-permute-done | bytes 104480 | tf_op jit(solution)/shard_map/ppermute | solution.py:16
  43.3 1.1 %collective-permute-done.18 = bf16[128,384]{1,0:T(8,128)(2,1)S(1)} collective-permute-done((bf16[128,384]{1,0:T(8,128)(2,1)S(1)}, bf16[128,384]{1,0:T(8,128)(2,1)S(1)}, u32[]{:S(2)}, u32[]{:S(2)}) %collective-permute-start.18) | collective-permute-done | bytes 98336 | tf_op jit(solution)/shard_map/ppermute | solution.py:16
  44.7 1.3 %collective-permute-done.19 = f32[128,384]{1,0:T(8,128)S(1)} collective-permute-done((f32[128,384]{1,0:T(8,128)S(1)}, f32[128,384]{1,0:T(8,128)S(1)}, u32[]{:S(2)}, u32[]{:S(2)}) %collective-permute-start.19) | collective-permute-done | bytes 196640 | tf_op jit(solution)/shard_map/ppermute | solution.py:16
  47.3 3.0 %collective-permute-start.20 = (f32[2,2,2,128]{3,2,1,0:T(2,128)S(1)}, f32[2,2,2,128]{3,2,1,0:T(2,128)S(1)}, u32[]{:S(2)}, u32[]{:S(2)}) collective-permute-start(f32[2,2,2,128]{3,2,1,0:T(2,128)S(1)} %pad_maximum_fusion.12), channel_id=1, source_target_pairs={{0,4},{1,5},{2,6},{3,7},{4,0},{5,1},{6,2},{7,3},{8,12},{9,13},{10,... | collective-permute-start | bytes 12296 | tf_op jit(solution)/shard_map/ppermute | solution.py:16
  50.3 1.5 %collective-permute-done.20 = f32[2,2,2,128]{3,2,1,0:T(2,128)S(1)} collective-permute-done((f32[2,2,2,128]{3,2,1,0:T(2,128)S(1)}, f32[2,2,2,128]{3,2,1,0:T(2,128)S(1)}, u32[]{:S(2)}, u32[]{:S(2)}) %collective-permute-start.20) | collective-permute-done | bytes 4128 | tf_op jit(solution)/shard_map/ppermute | solution.py:16
  52.2 1.4 %collective-permute-start.21 = (f32[2,2,2,128]{3,2,1,0:T(2,128)S(1)}, f32[2,2,2,128]{3,2,1,0:T(2,128)S(1)}, u32[]{:S(2)}, u32[]{:S(2)}) collective-permute-start(f32[2,2,2,128]{3,2,1,0:T(2,128)S(1)} %log_add_fusion.2), channel_id=1, source_target_pairs={{0,2},{1,3},{2,0},{3,1},{4,6},{5,7},{6,4},{7,5},{8,10},{9,11},{10,... | collective-permute-start | bytes 12296 | tf_op jit(solution)/shard_map/ppermute | solution.py:16
  55.9 1.4 %collective-permute-start.22 = (f32[2,2,2,128]{3,2,1,0:T(2,128)S(1)}, f32[2,2,2,128]{3,2,1,0:T(2,128)S(1)}, u32[]{:S(2)}, u32[]{:S(2)}) collective-permute-start(f32[2,2,2,128]{3,2,1,0:T(2,128)S(1)} %log_add_fusion.1), channel_id=1, source_target_pairs={{0,1},{1,0},{2,3},{3,2},{4,5},{5,4},{6,7},{7,6},{8,9},{9,8},{10,11... | collective-permute-start | bytes 12296 | tf_op jit(solution)/shard_map/ppermute | solution.py:16
  57.3 2.2 %collective-permute-done.22 = f32[2,2,2,128]{3,2,1,0:T(2,128)S(1)} collective-permute-done((f32[2,2,2,128]{3,2,1,0:T(2,128)S(1)}, f32[2,2,2,128]{3,2,1,0:T(2,128)S(1)}, u32[]{:S(2)}, u32[]{:S(2)}) %collective-permute-start.22) | collective-permute-done | bytes 4128 | tf_op jit(solution)/shard_map/ppermute | solution.py:16
  62.4 1.6 %collective-permute-start.24 = (bf16[136,384]{1,0:T(8,128)(2,1)S(1)}, bf16[136,384]{1,0:T(8,128)(2,1)S(1)}, u32[]{:S(2)}, u32[]{:S(2)}) collective-permute-start(bf16[136,384]{1,0:T(8,128)(2,1)S(1)} %pad_maximum_fusion.8), channel_id=1, source_target_pairs={{0,16},{8,24},{16,0},{24,8},{1,17},{9,25},{17,1},{25,9},{2,18},{10... | collective-permute-start | bytes 313352 | tf_op jit(solution)/shard_map/ppermute | solution.py:16
  64.6 3.6 %collective-permute-done.24 = bf16[136,384]{1,0:T(8,128)(2,1)S(1)} collective-permute-done((bf16[136,384]{1,0:T(8,128)(2,1)S(1)}, bf16[136,384]{1,0:T(8,128)(2,1)S(1)}, u32[]{:S(2)}, u32[]{:S(2)}) %collective-permute-start.24) | collective-permute-done | bytes 104480 | tf_op jit(solution)/shard_map/ppermute | solution.py:16
  68.4 1.1 %collective-permute-done.27 = bf16[128,384]{1,0:T(8,128)(2,1)S(1)} collective-permute-done((bf16[128,384]{1,0:T(8,128)(2,1)S(1)}, bf16[128,384]{1,0:T(8,128)(2,1)S(1)}, u32[]{:S(2)}, u32[]{:S(2)}) %collective-permute-start.27) | collective-permute-done | bytes 98336 | tf_op jit(solution)/shard_map/ppermute | solution.py:16
  70.4 0.7 collective-permute-done.28
  71.2 0.9 %maximum_maximum_fusion.1 = f32[256,768]{1,0:T(8,128)} fusion(f32[128,384]{1,0:T(8,128)S(1)} %get-tuple-element.115, f32[128,384]{1,0:T(8,128)S(1)} %get-tuple-element.114, f32[128,384]{1,0:T(8,128)S(1)} %get-tuple-element.113, f32[128,384]{1,0:T(8,128)S(1)} %get-tuple-element.112), kind=kLoop, calls=%fused_computation.32 | loop fusion | flops 589824 | bytes 1572864 | tf_op jit(solution)/shard_map/concatenate | solution.py:231
  (172 shorter events, 16.8 us)
Async XLA Ops:
  0.6 8.8 %copy-start = (f32[256,768]{1,0:T(8,128)S(1)}, f32[256,768]{1,0:T(8,128)}, u32[]{:S(2)}) copy-start(f32[256,768]{1,0:T(8,128)} %param.9) | copy-start | bytes 2359300
  0.6 4.2 %collective-permute-start = (bf16[4,768]{1,0:T(4,128)(2,1)}, bf16[4,768]{1,0:T(4,128)(2,1)S(1)}, u32[]{:S(2)}, u32[]{:S(2)}) collective-permute-start(bf16[4,768]{1,0:T(4,128)(2,1)} %param.8), channel_id=1, source_target_pairs={{0,8},{8,0},{16,24},{24,16},{1,9},{9,1},{17,25},{25,17},{2,10},{10... | collective-permute-start | bytes 18440 | tf_op jit(solution)/shard_map/ppermute | solution.py:16
  1.2 13.7 %collective-permute-start.1 = (bf16[128,768]{1,0:T(8,128)(2,1)}, bf16[128,768]{1,0:T(8,128)(2,1)S(1)}, u32[]{:S(2)}, u32[]{:S(2)}) collective-permute-start(bf16[128,768]{1,0:T(8,128)(2,1)} %param.7), channel_id=1, source_target_pairs={{0,4},{1,5},{2,6},{3,7},{4,0},{5,1},{6,2},{7,3},{8,12},{9,13},{10,... | collective-permute-start | bytes 589832 | tf_op jit(solution)/shard_map/ppermute | solution.py:16
  4.8 10.8 %collective-permute-start.2 = (bf16[128,768]{1,0:T(8,128)(2,1)}, bf16[128,768]{1,0:T(8,128)(2,1)S(1)}, u32[]{:S(2)}, u32[]{:S(2)}) collective-permute-start(bf16[128,768]{1,0:T(8,128)(2,1)} %param.7), channel_id=1, source_target_pairs={{0,2},{1,3},{2,0},{3,1},{4,6},{5,7},{6,4},{7,5},{8,10},{9,11},{10,... | collective-permute-start | bytes 589832 | tf_op jit(solution)/shard_map/ppermute | solution.py:16
  6.4 16.4 %collective-permute-start.7 = (bf16[128,768]{1,0:T(8,128)(2,1)}, bf16[128,768]{1,0:T(8,128)(2,1)S(1)}, u32[]{:S(2)}, u32[]{:S(2)}) collective-permute-start(bf16[128,768]{1,0:T(8,128)(2,1)} %param.7), channel_id=1, source_target_pairs={{0,1},{1,0},{2,3},{3,2},{4,5},{5,4},{6,7},{7,6},{8,9},{9,8},{10,11... | collective-permute-start | bytes 589832 | tf_op jit(solution)/shard_map/ppermute | solution.py:16
  9.5 7.7 %copy-start.1 = (bf16[128,768]{1,0:T(8,128)(2,1)S(1)}, bf16[128,768]{1,0:T(8,128)(2,1)}, u32[]{:S(2)}) copy-start(bf16[128,768]{1,0:T(8,128)(2,1)} %param.7) | copy-start | bytes 589828
  10.1 3.8 %collective-permute-start.6 = (bf16[8,768]{1,0:T(8,128)(2,1)S(1)}, bf16[8,768]{1,0:T(8,128)(2,1)S(1)}, u32[]{:S(2)}, u32[]{:S(2)}) collective-permute-start(bf16[8,768]{1,0:T(8,128)(2,1)S(1)} %pad_maximum_fusion.10), channel_id=1, source_target_pairs={{0,16},{8,24},{16,0},{24,8},{1,17},{9,25},{17,1},{25,9},{2,18},{10... | collective-permute-start | bytes 36872 | tf_op jit(solution)/shard_map/ppermute | solution.py:16
  11.8 6.6 %collective-permute-start.3 = (bf16[136,768]{1,0:T(8,128)(2,1)S(1)}, bf16[136,768]{1,0:T(8,128)(2,1)S(1)}, u32[]{:S(2)}, u32[]{:S(2)}) collective-permute-start(bf16[136,768]{1,0:T(8,128)(2,1)S(1)} %pad_maximum_fusion.4), channel_id=1, source_target_pairs={{0,1},{1,0},{2,3},{3,2},{4,5},{5,4},{6,7},{7,6},{8,9},{9,8},{10,11... | collective-permute-start | bytes 626696 | tf_op jit(solution)/shard_map/ppermute | solution.py:16
  14.8 6.6 %collective-permute-start.5 = (bf16[128,768]{1,0:T(8,128)(2,1)S(1)}, bf16[128,768]{1,0:T(8,128)(2,1)S(1)}, u32[]{:S(2)}, u32[]{:S(2)}) collective-permute-start(bf16[128,768]{1,0:T(8,128)(2,1)S(1)} %collective-permute-done.1), channel_id=1, source_target_pairs={{0,2},{1,3},{2,0},{3,1},{4,6},{5,7},{6,4},{7,5},{8,10},{9,11},{10,... | collective-permute-start | bytes 589832 | tf_op jit(solution)/shard_map/ppermute | solution.py:16
  15.6 10.9 %collective-permute-start.9 = (bf16[128,768]{1,0:T(8,128)(2,1)S(1)}, bf16[128,768]{1,0:T(8,128)(2,1)S(1)}, u32[]{:S(2)}, u32[]{:S(2)}) collective-permute-start(bf16[128,768]{1,0:T(8,128)(2,1)S(1)} %collective-permute-done.2), channel_id=1, source_target_pairs={{0,1},{1,0},{2,3},{3,2},{4,5},{5,4},{6,7},{7,6},{8,9},{9,8},{10,11... | collective-permute-start | bytes 589832 | tf_op jit(solution)/shard_map/ppermute | solution.py:16
  17.1 14.0 %collective-permute-start.11 = (bf16[128,768]{1,0:T(8,128)(2,1)S(1)}, bf16[128,768]{1,0:T(8,128)(2,1)S(1)}, u32[]{:S(2)}, u32[]{:S(2)}) collective-permute-start(bf16[128,768]{1,0:T(8,128)(2,1)S(1)} %collective-permute-done.1), channel_id=1, source_target_pairs={{0,1},{1,0},{2,3},{3,2},{4,5},{5,4},{6,7},{7,6},{8,9},{9,8},{10,11... | collective-permute-start | bytes 589832 | tf_op jit(solution)/shard_map/ppermute | solution.py:16
  18.3 3.4 %collective-permute-start.4 = (bf16[136,768]{1,0:T(8,128)(2,1)S(1)}, bf16[136,768]{1,0:T(8,128)(2,1)S(1)}, u32[]{:S(2)}, u32[]{:S(2)}) collective-permute-start(bf16[136,768]{1,0:T(8,128)(2,1)S(1)} %collective-permute-done.3), channel_id=1, source_target_pairs={{0,8},{8,0},{16,24},{24,16},{1,9},{9,1},{17,25},{25,17},{2,10},{10... | collective-permute-start | bytes 626696 | tf_op jit(solution)/shard_map/ppermute | solution.py:16
  22.8 3.7 %collective-permute-start.8 = (f32[1,2,2,128]{3,2,1,0:T(2,128)S(1)}, f32[1,2,2,128]{3,2,1,0:T(2,128)S(1)}, u32[]{:S(2)}, u32[]{:S(2)}) collective-permute-start(f32[1,2,2,128]{3,2,1,0:T(2,128)S(1)} %bitcast.133), channel_id=1, source_target_pairs={{0,2},{1,3},{2,0},{3,1},{4,6},{5,7},{6,4},{7,5},{8,10},{9,11},{10,... | collective-permute-start | bytes 6152 | tf_op jit(solution)/shard_map/ppermute | solution.py:16
  24.7 6.5 %collective-permute-start.12 = (bf16[128,768]{1,0:T(8,128)(2,1)}, bf16[128,768]{1,0:T(8,128)(2,1)S(1)}, u32[]{:S(2)}, u32[]{:S(2)}) collective-permute-start(bf16[128,768]{1,0:T(8,128)(2,1)} %slice.257), channel_id=1, source_target_pairs={{0,1},{1,0},{2,3},{3,2},{4,5},{5,4},{6,7},{7,6},{8,9},{9,8},{10,11... | collective-permute-start | bytes 589832 | tf_op jit(solution)/shard_map/ppermute | solution.py:16
  26.5 4.6 %collective-permute-start.10 = (f32[1,2,2,128]{3,2,1,0:T(2,128)S(1)}, f32[1,2,2,128]{3,2,1,0:T(2,128)S(1)}, u32[]{:S(2)}, u32[]{:S(2)}) collective-permute-start(f32[1,2,2,128]{3,2,1,0:T(2,128)S(1)} %log_add_fusion.6), channel_id=1, source_target_pairs={{0,4},{1,5},{2,6},{3,7},{4,0},{5,1},{6,2},{7,3},{8,12},{9,13},{10,... | collective-permute-start | bytes 6152 | tf_op jit(solution)/shard_map/ppermute | solution.py:16
  31.1 3.7 %collective-permute-start.13 = (f32[1,2,2,128]{3,2,1,0:T(2,128)S(1)}, f32[1,2,2,128]{3,2,1,0:T(2,128)S(1)}, u32[]{:S(2)}, u32[]{:S(2)}) collective-permute-start(f32[1,2,2,128]{3,2,1,0:T(2,128)S(1)} %log_add_fusion.5), channel_id=1, source_target_pairs={{0,1},{1,0},{2,3},{3,2},{4,5},{5,4},{6,7},{7,6},{8,9},{9,8},{10,11... | collective-permute-start | bytes 6152 | tf_op jit(solution)/shard_map/ppermute | solution.py:16
  35.8 1.4 %collective-permute-start.14 = (bf16[136,384]{1,0:T(8,128)(2,1)S(1)}, bf16[136,384]{1,0:T(8,128)(2,1)S(1)}, u32[]{:S(2)}, u32[]{:S(2)}) collective-permute-start(bf16[136,384]{1,0:T(8,128)(2,1)S(1)} %pad_maximum_fusion.5), channel_id=1, source_target_pairs={{0,8},{8,0},{16,24},{24,16},{1,9},{9,1},{17,25},{25,17},{2,10},{10... | collective-permute-start | bytes 313352 | tf_op jit(solution)/shard_map/ppermute | solution.py:16
  36.5 2.4 %collective-permute-start.17 = (bf16[128,384]{1,0:T(8,128)(2,1)S(1)}, bf16[128,384]{1,0:T(8,128)(2,1)S(1)}, u32[]{:S(2)}, u32[]{:S(2)}) collective-permute-start(bf16[128,384]{1,0:T(8,128)(2,1)S(1)} %select_convert_fusion.2), channel_id=1, source_target_pairs={{0,8},{8,0},{16,24},{24,16},{1,9},{9,1},{17,25},{25,17},{2,10},{10... | collective-permute-start | bytes 294920 | tf_op jit(solution)/shard_map/ppermute | solution.py:16
  37.2 5.8 %collective-permute-start.15 = (bf16[136,384]{1,0:T(8,128)(2,1)S(1)}, bf16[136,384]{1,0:T(8,128)(2,1)S(1)}, u32[]{:S(2)}, u32[]{:S(2)}) collective-permute-start(bf16[136,384]{1,0:T(8,128)(2,1)S(1)} %pad_maximum_fusion.6), channel_id=1, source_target_pairs={{0,16},{8,24},{16,0},{24,8},{1,17},{9,25},{17,1},{25,9},{2,18},{10... | collective-permute-start | bytes 313352 | tf_op jit(solution)/shard_map/ppermute | solution.py:16
  38.9 5.5 %collective-permute-start.18 = (bf16[128,384]{1,0:T(8,128)(2,1)S(1)}, bf16[128,384]{1,0:T(8,128)(2,1)S(1)}, u32[]{:S(2)}, u32[]{:S(2)}) collective-permute-start(bf16[128,384]{1,0:T(8,128)(2,1)S(1)} %add_convert_fusion.2), channel_id=1, source_target_pairs={{0,16},{8,24},{16,0},{24,8},{1,17},{9,25},{17,1},{25,9},{2,18},{10... | collective-permute-start | bytes 294920 | tf_op jit(solution)/shard_map/ppermute | solution.py:16
  43.2 1.5 %collective-permute-start.16 = (f32[128,384]{1,0:T(8,128)S(1)}, f32[128,384]{1,0:T(8,128)S(1)}, u32[]{:S(2)}, u32[]{:S(2)}) collective-permute-start(f32[128,384]{1,0:T(8,128)S(1)} %fusion.39), channel_id=1, source_target_pairs={{0,8},{8,0},{16,24},{24,16},{1,9},{9,1},{17,25},{25,17},{2,10},{10... | collective-permute-start | bytes 589832 | tf_op jit(solution)/shard_map/ppermute | solution.py:16
  44.5 1.5 %collective-permute-start.19 = (f32[128,384]{1,0:T(8,128)S(1)}, f32[128,384]{1,0:T(8,128)S(1)}, u32[]{:S(2)}, u32[]{:S(2)}) collective-permute-start(f32[128,384]{1,0:T(8,128)S(1)} %fusion.38), channel_id=1, source_target_pairs={{0,8},{8,0},{16,24},{24,16},{1,9},{9,1},{17,25},{25,17},{2,10},{10... | collective-permute-start | bytes 589832 | tf_op jit(solution)/shard_map/ppermute | solution.py:16
  47.3 6.6 %copy-start.4 = (s32[128]{0:T(128)S(1)}, s32[128]{0:T(128)}, u32[]{:S(2)}) copy-start(s32[128]{0:T(128)} %param.11) | copy-start | bytes 1540
  47.3 4.6 %collective-permute-start.20 = (f32[2,2,2,128]{3,2,1,0:T(2,128)S(1)}, f32[2,2,2,128]{3,2,1,0:T(2,128)S(1)}, u32[]{:S(2)}, u32[]{:S(2)}) collective-permute-start(f32[2,2,2,128]{3,2,1,0:T(2,128)S(1)} %pad_maximum_fusion.12), channel_id=1, source_target_pairs={{0,4},{1,5},{2,6},{3,7},{4,0},{5,1},{6,2},{7,3},{8,12},{9,13},{10,... | collective-permute-start | bytes 12296 | tf_op jit(solution)/shard_map/ppermute | solution.py:16
  52.2 3.6 %collective-permute-start.21 = (f32[2,2,2,128]{3,2,1,0:T(2,128)S(1)}, f32[2,2,2,128]{3,2,1,0:T(2,128)S(1)}, u32[]{:S(2)}, u32[]{:S(2)}) collective-permute-start(f32[2,2,2,128]{3,2,1,0:T(2,128)S(1)} %log_add_fusion.2), channel_id=1, source_target_pairs={{0,2},{1,3},{2,0},{3,1},{4,6},{5,7},{6,4},{7,5},{8,10},{9,11},{10,... | collective-permute-start | bytes 12296 | tf_op jit(solution)/shard_map/ppermute | solution.py:16
  55.9 3.7 %collective-permute-start.22 = (f32[2,2,2,128]{3,2,1,0:T(2,128)S(1)}, f32[2,2,2,128]{3,2,1,0:T(2,128)S(1)}, u32[]{:S(2)}, u32[]{:S(2)}) collective-permute-start(f32[2,2,2,128]{3,2,1,0:T(2,128)S(1)} %log_add_fusion.1), channel_id=1, source_target_pairs={{0,1},{1,0},{2,3},{3,2},{4,5},{5,4},{6,7},{7,6},{8,9},{9,8},{10,11... | collective-permute-start | bytes 12296 | tf_op jit(solution)/shard_map/ppermute | solution.py:16
  60.7 1.4 %collective-permute-start.23 = (bf16[136,384]{1,0:T(8,128)(2,1)S(1)}, bf16[136,384]{1,0:T(8,128)(2,1)S(1)}, u32[]{:S(2)}, u32[]{:S(2)}) collective-permute-start(bf16[136,384]{1,0:T(8,128)(2,1)S(1)} %pad_maximum_fusion.7), channel_id=1, source_target_pairs={{0,8},{8,0},{16,24},{24,16},{1,9},{9,1},{17,25},{25,17},{2,10},{10... | collective-permute-start | bytes 313352 | tf_op jit(solution)/shard_map/ppermute | solution.py:16
  61.4 2.5 %collective-permute-start.26 = (bf16[128,384]{1,0:T(8,128)(2,1)S(1)}, bf16[128,384]{1,0:T(8,128)(2,1)S(1)}, u32[]{:S(2)}, u32[]{:S(2)}) collective-permute-start(bf16[128,384]{1,0:T(8,128)(2,1)S(1)} %select_convert_fusion), channel_id=1, source_target_pairs={{0,8},{8,0},{16,24},{24,16},{1,9},{9,1},{17,25},{25,17},{2,10},{10... | collective-permute-start | bytes 294920 | tf_op jit(solution)/shard_map/ppermute | solution.py:16
  62.4 5.8 %collective-permute-start.24 = (bf16[136,384]{1,0:T(8,128)(2,1)S(1)}, bf16[136,384]{1,0:T(8,128)(2,1)S(1)}, u32[]{:S(2)}, u32[]{:S(2)}) collective-permute-start(bf16[136,384]{1,0:T(8,128)(2,1)S(1)} %pad_maximum_fusion.8), channel_id=1, source_target_pairs={{0,16},{8,24},{16,0},{24,8},{1,17},{9,25},{17,1},{25,9},{2,18},{10... | collective-permute-start | bytes 313352 | tf_op jit(solution)/shard_map/ppermute | solution.py:16
  64.0 5.5 %collective-permute-start.27 = (bf16[128,384]{1,0:T(8,128)(2,1)S(1)}, bf16[128,384]{1,0:T(8,128)(2,1)S(1)}, u32[]{:S(2)}, u32[]{:S(2)}) collective-permute-start(bf16[128,384]{1,0:T(8,128)(2,1)S(1)} %add_convert_fusion), channel_id=1, source_target_pairs={{0,16},{8,24},{16,0},{24,8},{1,17},{9,25},{17,1},{25,9},{2,18},{10... | collective-permute-start | bytes 294920 | tf_op jit(solution)/shard_map/ppermute | solution.py:16
  68.3 2.0 %collective-permute-start.25 = (f32[128,384]{1,0:T(8,128)S(1)}, f32[128,384]{1,0:T(8,128)S(1)}, u32[]{:S(2)}, u32[]{:S(2)}) collective-permute-start(f32[128,384]{1,0:T(8,128)S(1)} %fusion.37), channel_id=1, source_target_pairs={{0,8},{8,0},{16,24},{24,16},{1,9},{9,1},{17,25},{25,17},{2,10},{10... | collective-permute-start | bytes 589832 | tf_op jit(solution)/shard_map/ppermute | solution.py:16
  69.6 1.5 %collective-permute-start.28 = (f32[128,384]{1,0:T(8,128)S(1)}, f32[128,384]{1,0:T(8,128)S(1)}, u32[]{:S(2)}, u32[]{:S(2)}) collective-permute-start(f32[128,384]{1,0:T(8,128)S(1)} %fusion.36), channel_id=1, source_target_pairs={{0,8},{8,0},{16,24},{24,16},{1,9},{9,1},{17,25},{25,17},{2,10},{10... | collective-permute-start | bytes 589832 | tf_op jit(solution)/shard_map/ppermute | solution.py:16
  (2 other events, 7.2 us)
